TPU v7x, 256 devices: a whole 4x4x8 slice. The times are simulated.
256 devices in a mesh: dp: 4 (over z_hi, core), tm: 4 (over z_lo), height: 16 (over x, y).
Axes of the slice: x: 4, y: 4, z: 8 (z_hi: 2, z_lo: 4; z = z_hi * 4 + z_lo), core: 2. Of those that a mesh axis runs over, the one named last changes fastest.
Arguments:
- vit_cot: bfloat16 [4, 64, 256, 1280], P('dp', ('tm', 'height')), may hold values from -6 to 6
- vit_pre: bfloat16 [4, 64, 256, 1280], P('dp', ('tm', 'height')), may hold values from -6 to 6
- ln_gain: bfloat16 [1280], replicated, may hold values from 0.099609375 to 1.8984375
- patch_w: bfloat16 [588, 1280], replicated, may hold values from -0.25 to 0.25
- frame_owner: int32 [64], replicated, may hold values from 0 to 15, as said below
- conv_w: bfloat16 [81, 128], replicated, may hold values from -0.625 to 0.625
- join_w: bfloat16 [512, 3072], replicated, may hold values from -0.25 to 0.25
- token_order: int32 [16, 256], P('height', 'tm'), may hold values from 0 to 63, as said below
- queries: bfloat16 [4, 4096, 1536], P('dp', 'height', 'tm'), may hold values from -28 to 28
- keys: bfloat16 [4, 4096, 1536], P('dp', 'height', 'tm'), may hold values from -13 to 13
- values: bfloat16 [4, 4096, 1536], P('dp', 'height', 'tm'), may hold values from -6 to 6
- attn_out: bfloat16 [4, 4096, 1536], P('dp', 'height', 'tm'), may hold values from -6 to 6
- out_w: bfloat16 [1536, 3072], P('tm'), may hold values from -0.15625 to 0.15625
Outputs:
- query_grad: bfloat16 [4, 4096, 1536], P('dp', 'height', 'tm')
- key_grad: bfloat16 [4, 4096, 1536], P('dp', 'height', 'tm')
- value_grad: bfloat16 [4, 4096, 1536], P('dp', 'height', 'tm')
- weight_grad: float32 [3072, 1536], P(('dp', 'height'), 'tm')
Inputs may be any that keep to these rules, and one draw needn't show every extreme that they name: `frame_owner`: each aligned block of 16 entries holds every number of 0 to 15 once. `token_order`: each aligned block of 64 entries of a row holds every number of 0 to 63 once.
All inputs are finite; a program needn't handle non-finite values.
Results may differ from a plain program's by a relative error of at most 0.022.
Values may be sent and summed in bfloat16 or wider, within the bound.
No kernel may reach another device: no remote copies, remote signals or barrier semaphores. Data moves between devices by JAX's collectives and lax.ppermute only.
A program may use at most 128 MiB of HBM per device.

v0:
```python
import math

import jax
import jax.numpy as jnp
from jax import lax
from jax.sharding import PartitionSpec as P

HDIM = 128
IMG = 224
PATCH = 14
PW = 56


epsilon = 1e-05
pixel_std = (0.26862954, 0.26130258, 0.27577711)


def with_halo(block, sides, width):
    for axis, dim in sides:
        count = lax.axis_size(axis)
        forward = [(i, i + 1) for i in range(count - 1)]
        backward = [(target, source) for source, target in forward]
        low = lax.ppermute(
            lax.slice_in_dim(block, block.shape[dim] - width, None, axis=dim), axis, forward
        )
        high = lax.ppermute(lax.slice_in_dim(block, 0, width, axis=dim), axis, backward)
        block = jnp.concatenate([low, block, high], axis=dim)
    return block


def norm_backward(cotangent, inputs, gain):
    values32 = inputs.astype(jnp.float32)
    centered = values32 - jnp.mean(values32, axis=-1, keepdims=True)
    inverse = lax.rsqrt(jnp.mean(centered * centered, axis=-1, keepdims=True) + epsilon)
    normed = centered * inverse
    scaled = cotangent.astype(jnp.float32) * gain.astype(jnp.float32)
    return inverse * (
        scaled
        - jnp.mean(scaled, axis=-1, keepdims=True)
        - normed * jnp.mean(scaled * normed, axis=-1, keepdims=True)
    )


def patch_pixels(grad_rows, patch_w):
    flattened = jnp.dot(grad_rows, patch_w.T, preferred_element_type=jnp.float32)
    patches = flattened.reshape(flattened.shape[0], 3, PATCH, PATCH)
    deviation = jnp.array(pixel_std, dtype=jnp.float32)
    return patches / deviation[None, :, None, None]


def frame_image(cotangent, inputs, gain, patch_w):
    grad_rows = norm_backward(cotangent, inputs, gain).astype(jnp.bfloat16)
    patches = patch_pixels(grad_rows, patch_w)
    side_count = IMG // PATCH
    picture = patches.reshape(side_count, side_count, 3, PATCH, PATCH).transpose(2, 0, 3, 1, 4)
    return picture.reshape(3, IMG, IMG).astype(jnp.bfloat16)


def conv_adjoint(padded, conv_w, frame_count, row_count, col_count):
    shifted = [
        padded[
            :,
            shift_t : shift_t + frame_count,
            shift_r : shift_r + row_count,
            shift_c : shift_c + col_count,
        ]
        for shift_t in range(3)
        for shift_r in range(3)
        for shift_c in range(3)
    ]
    stacked = jnp.stack(shifted, axis=0).reshape(81, frame_count * row_count * col_count)
    return lax.dot_general(
        stacked, conv_w, (((0,), (0,)), ((), ())), preferred_element_type=jnp.float32
    )


def pool_tokens(cell_grads, frame_count, row_count, col_count):
    channels = cell_grads.shape[-1]
    pooled_grid = cell_grads.reshape(
        frame_count, row_count // PATCH, 2, PATCH // 2, col_count // PW, 2, PW // 2, channels
    )
    quarter_means = jnp.mean(pooled_grid, axis=(3, 6))
    ordered = quarter_means.transpose(0, 1, 3, 2, 4, 5)
    return ordered.reshape(
        frame_count * (row_count // PATCH) * (col_count // PW), 4 * channels
    ).astype(jnp.bfloat16)


def attention_terms(query_rows, grad_rows, key_rows, value_rows, log_totals, row_dots, score_scale):
    scores = (
        jnp.einsum("qhd,khd->hqk", query_rows, key_rows, preferred_element_type=jnp.float32)
        * score_scale
    )
    weights = jnp.exp(scores - log_totals[..., None])
    mixed_grads = jnp.einsum(
        "qhd,khd->hqk", grad_rows, value_rows, preferred_element_type=jnp.float32
    )
    dscore = (weights * (mixed_grads - row_dots[..., None])).astype(jnp.bfloat16)
    return (weights.astype(jnp.bfloat16), dscore)


def per_device(
    vit_cot,
    vit_pre,
    ln_gain,
    patch_w,
    frame_owner,
    conv_w,
    join_w,
    token_order,
    queries,
    keys,
    values,
    attn_out,
    out_w,
):
    height_count = lax.axis_size("height")
    clip_count = lax.axis_size("dp")
    row_count = IMG // height_count
    picture = frame_image(vit_cot[0, 0], vit_pre[0, 0], ln_gain, patch_w)
    received = lax.all_to_all(
        picture.reshape(3, height_count, row_count, IMG),
        "height",
        split_axis=1,
        concat_axis=1,
        tiled=True,
    )
    owners = lax.dynamic_slice_in_dim(
        frame_owner, lax.axis_index("tm") * height_count, height_count
    )
    slab_grads = jnp.take(received, owners, axis=1)
    bordered = with_halo(slab_grads, (("tm", 1), ("height", 2)), 1)
    padded = jnp.pad(bordered, ((0, 0), (0, 0), (0, 0), (1, 1)))
    cell_grads = conv_adjoint(padded, conv_w, height_count, row_count, IMG)
    pooled = pool_tokens(cell_grads, height_count, row_count, IMG)
    patch_grads = jnp.dot(pooled, join_w, preferred_element_type=jnp.float32).astype(jnp.bfloat16)
    token_grads = jnp.take(patch_grads, token_order[0], axis=0)
    all_grads = lax.all_gather(token_grads, "tm", axis=0, tiled=True)
    query_here = queries[0]
    key_here = keys[0]
    value_here = values[0]
    output_here = attn_out[0]
    grad_out = jnp.dot(all_grads, out_w.T, preferred_element_type=jnp.float32).astype(jnp.bfloat16)
    local_rows = query_here.shape[0]
    token_total = local_rows * height_count
    heads_here = query_here.shape[1] // HDIM
    score_scale = HDIM ** (-0.5)

    def head_view(matrix):
        return matrix.reshape(matrix.shape[0], heads_here, HDIM)

    query_heads = head_view(query_here)
    key_heads = head_view(key_here)
    value_heads = head_view(value_here)
    output_heads = head_view(output_here)
    grad_heads = head_view(grad_out)
    running_max = jnp.full((heads_here, local_rows), -1e30, jnp.float32)
    scores = (
        jnp.einsum(
            "qhd,khd->hqk",
            query_heads,
            head_view(lax.all_gather(key_here, "height", axis=0, tiled=True)),
            preferred_element_type=jnp.float32,
        )
        * score_scale
    )
    new_max = jnp.maximum(running_max, jnp.max(scores, axis=-1))
    new_sum = jnp.sum(jnp.exp(scores - new_max[..., None]), axis=-1)
    log_totals = new_max + jnp.log(new_sum)
    row_dots = jnp.sum(grad_heads.astype(jnp.float32) * output_heads.astype(jnp.float32), axis=-1).T
    fragments = (
        lax.all_gather(key_here, "height", axis=0, tiled=True),
        lax.all_gather(value_here, "height", axis=0, tiled=True),
    )
    key_rows = head_view(fragments[0])
    value_rows = head_view(fragments[1])
    weights, dscore = attention_terms(
        query_heads, grad_heads, key_rows, value_rows, log_totals, row_dots, score_scale
    )
    query_acc = (
        jnp.einsum("hqk,khd->qhd", dscore, key_rows, preferred_element_type=jnp.float32)
        * score_scale
    )
    fragments = (
        lax.all_gather(query_here.astype(jnp.float32), "height", axis=0, tiled=True).astype(
            jnp.bfloat16
        ),
        lax.all_gather(grad_out.astype(jnp.float32), "height", axis=0, tiled=True).astype(
            jnp.bfloat16
        ),
        lax.all_gather(log_totals.T, "height", axis=0, tiled=True),
        lax.all_gather(row_dots.T, "height", axis=0, tiled=True),
    )
    query_rows = head_view(fragments[0])
    grad_rows = head_view(fragments[1])
    weights, dscore = attention_terms(
        query_rows, grad_rows, key_heads, value_heads, fragments[2].T, fragments[3].T, score_scale
    )
    key_sum = (
        jnp.einsum("hqk,qhd->khd", dscore, query_rows, preferred_element_type=jnp.float32)
        * score_scale
    )
    value_sum = jnp.einsum("hqk,qhd->khd", weights, grad_rows, preferred_element_type=jnp.float32)
    root = math.sqrt(token_total)

    def finish(grads):
        return (grads * root).reshape(local_rows, -1).astype(jnp.bfloat16)

    inv_root = 1.0 / math.sqrt(token_total * clip_count)
    weight_grad = lax.psum_scatter(
        jnp.einsum("td,th->dh", all_grads, output_here, preferred_element_type=jnp.float32)
        * inv_root,
        ("dp", "height"),
        scatter_dimension=0,
        tiled=True,
    )
    return (finish(query_acc)[None], finish(key_sum)[None], finish(value_sum)[None], weight_grad)


def solution(mesh):
    placed = (
        P("dp", ("tm", "height"), None, None),
        P("dp", ("tm", "height"), None, None),
        P(),
        P(),
        P(),
        P(),
        P(),
        P("height", "tm"),
        P("dp", "height", "tm"),
        P("dp", "height", "tm"),
        P("dp", "height", "tm"),
        P("dp", "height", "tm"),
        P("tm", None),
    )
    return jax.shard_map(
        per_device,
        mesh=mesh,
        in_specs=placed,
        out_specs=(
            P("dp", "height", "tm"),
            P("dp", "height", "tm"),
            P("dp", "height", "tm"),
            P(("dp", "height"), "tm"),
        ),
        check_vma=False,
    )
```

profile of v0, /device:TPU:24, one launch (start us, length us, event | category | flops | bytes accessed | tf_op | source)
XLA Modules:
  0.0 601.4 jit_solution(6633362850029942855)
XLA Ops:
  10.7 3.4 dot_general.42
  15.8 2.8 fusion.21
  20.8 4.2 convert_element_type.150
  25.8 7.2 %all-to-all-start = ((bf16[3,16,14,224]{3,2,0,1:T(8,128)(2,1)}), bf16[3,16,14,224]{3,2,0,1:T(8,128)(2,1)S(1)}, u32[]{:S(2)}, u32[]{:S(2)}) async-start(bf16[3,16,14,224]{3,2,0,1:T(8,128)(2,1)} %copy.79), calls=%async_computation | async-start | bytes 786432 | tf_op jit(solution)/shard_map/all_to_all | solution.py:121
  33.2 7.5 %all-to-all-done = bf16[3,16,14,224]{3,2,0,1:T(8,128)(2,1)S(1)} async-done(((bf16[3,16,14,224]{3,2,0,1:T(8,128)(2,1)}), bf16[3,16,14,224]{3,2,0,1:T(8,128)(2,1)S(1)}, u32[]{:S(2)}, u32[]{:S(2)}) %all-to-all-start) | async-done | bytes 301088 | tf_op jit(solution)/shard_map/all_to_all | solution.py:121
  43.1 3.8 collective-permute-start
  48.9 3.8 collective-permute-done.1
  52.8 3.7 collective-permute-start.2
  56.5 2.3 collective-permute-start.3
  58.8 5.8 collective-permute-done.3
  69.6 5.0 copy.83
  74.5 18.1 %reshape.220 = bf16[81,50176]{1,0:T(8,128)(2,1)} reshape(bf16[27,3,16,14,224]{4,3,2,1,0:T(8,128)(2,1)} %copy.83) | data formatting | bytes 16257024 | tf_op jit(solution)/shard_map/reshape | solution.py:71
  92.7 14.0 %copy.84 = bf16[50176,81]{1,0:T(8,128)(2,1)} copy(bf16[50176,81]{0,1:T(8,128)(2,1)} %bitcast.209) | data formatting | bytes 16257024 | tf_op jit(solution)/shard_map/dot_general | solution.py:72
  106.7 20.7 %reshape.221 = bf16[16,2,7,4,2,28,81]{6,5,4,3,2,1,0:T(8,128)(2,1)} reshape(bf16[50176,81]{1,0:T(8,128)(2,1)} %copy.84) | data formatting | bytes 16257024 | tf_op jit(solution)/shard_map/reshape.93
  127.3 7.3 %convolution_reduce_fusion = f32[16,2,4,2,128]{4,3,2,1,0:T(2,128)S(1)} fusion(bf16[16,2,7,4,2,28,81]{6,5,4,3,2,1,0:T(8,128)(2,1)} %reshape.221, bf16[81,128]{1,0:T(8,128)(2,1)S(1)} %copy-done.13), kind=kOutput, calls=%fused_computation.11 | convolution fusion | flops 1046839296 | bytes 8280320 | tf_op jit(solution)/shard_map/dot_general | solution.py:72
  144.2 37.6 %all-gather.9.cloned.1.call-done = bf16[256,3072]{1,0:T(8,128)(2,1)} async-done(((bf16[64,3072]{1,0:T(8,128)(2,1)}), bf16[256,3072]{1,0:T(8,128)(2,1)}) %all-gather.9.cloned.1.call-update) | async-done | bytes 1572880 | tf_op jit(solution)/shard_map/all_gather | solution.py:138
  181.8 3.8 convolution_convert_fusion.1
  185.9 4.6 convolution_multiply_fusion
  190.9 25.0 %all_gather.28 = f32[4096,3]{0,1:T(4,128)} all-gather(f32[256,3]{0,1:T(4,128)S(1)} %fusion.73), channel_id=1, replica_groups=mesh['dp'=4,'tm'=4,'height'=16] {'height'}, dimensions={0}, use_global_device_ids=true | all-gather | bytes 52224 | tf_op jit(solution)/shard_map/all_gather | solution.py:192
  215.9 25.6 %all-gather.13.cloned.1.call-done = bf16[1,4096,384]{1,2,0:T(8,128)(2,1)} async-done(((bf16[1,256,384]{1,2,0:T(8,128)(2,1)}), bf16[1,4096,384]{1,2,0:T(8,128)(2,1)}) %all-gather.13.cloned.1.call-update) | async-done | bytes 3145744 | tf_op jit(solution)/shard_map/all_gather | solution.py:172
  241.5 4.0 multiply_reduce_fusion
  245.5 4.6 copy-done.2
  252.3 48.7 %all-gather.15.cloned.1.call-done = bf16[1,4096,384]{1,2,0:T(8,128)(2,1)} async-done(((bf16[1,256,384]{1,2,0:T(8,128)(2,1)}), bf16[1,4096,384]{1,2,0:T(8,128)(2,1)}) %all-gather.15.cloned.1.call-update) | async-done | bytes 3145744 | tf_op jit(solution)/shard_map/all_gather | solution.py:173
  300.9 11.1 %fusion.31 = bf16[3,256,128]{1,2,0:T(8,128)(2,1)} fusion(bf16[4096,3,128]{0,2,1:T(8,128)(2,1)S(1)} %bitcast.216, f32[3,256,4096]{2,1,0:T(8,128)} %copy-done.2, bf16[256,3,128]{0,2,1:T(8,128)(2,1)S(1)} %bitcast.224, bf16[4096,3,128]{0,2,1:T(8,128)(2,1)} %bitcast.231, f32[3,256]{1,0:T(4,128)S(1)} %bitcast.229, f32[3,256]{1,0:T(4,128)S(1)} %log_add_fusion), kind=kOutput, calls=%fused_computation.45 | convolution fusion | flops 1626537984 | bytes 19273728 | tf_op jit(solution)/shard_map/hqk,khd->qhd/dot_general | solution.py:181
  313.8 21.7 %all_gather.26 = f32[4096,3]{0,1:T(4,128)S(1)} all-gather(f32[256,3]{0,1:T(4,128)S(1)} %bitcast.230), channel_id=1, replica_groups=mesh['dp'=4,'tm'=4,'height'=16] {'height'}, dimensions={0}, use_global_device_ids=true | all-gather | bytes 52224 | tf_op jit(solution)/shard_map/all_gather | solution.py:191
  335.5 25.3 %all-gather.17.cloned.1.call-done = bf16[1,4096,384]{1,2,0:T(8,128)(2,1)} async-done(((bf16[1,256,384]{1,2,0:T(8,128)(2,1)}), bf16[1,4096,384]{1,2,0:T(8,128)(2,1)}) %all-gather.17.cloned.1.call-update) | async-done | bytes 3145744 | tf_op jit(solution)/shard_map/all_gather | solution.py:185
  360.8 8.3 %fusion.83 = f32[3,4096,256]{2,1,0:T(8,128)} fusion(bf16[4096,3,128]{0,2,1:T(8,128)(2,1)} %bitcast.213, bf16[256,3,128]{0,2,1:T(8,128)(2,1)S(1)} %bitcast.217), kind=kOutput, calls=%fused_computation.147 | convolution fusion | flops 805306368 | bytes 15925248 | tf_op jit(solution)/shard_map/qhd,khd->hqk/dot_general | solution.py:91
  369.2 46.0 %all-gather.11.cloned.1.call-done = bf16[4096,384]{1,0:T(8,128)(2,1)} async-done(((bf16[256,384]{1,0:T(8,128)(2,1)}), bf16[4096,384]{1,0:T(8,128)(2,1)}) %all-gather.11.cloned.1.call-update) | async-done | bytes 3145744 | tf_op jit(solution)/shard_map/all_gather | solution.py:188
  415.2 3.2 copy.95
  418.4 7.7 %fusion.27 = bf16[3,128,256]{2,1,0:T(8,128)(2,1)S(1)} fusion(bf16[4096,3,128]{0,2,1:T(8,128)(2,1)S(1)} %bitcast.210, f32[3,4096,256]{2,1,0:T(8,128)} %fusion.83, f32[3,4096]{1,0:T(4,128)S(1)} %bitcast.219), kind=kOutput, calls=%fused_computation.43 | convolution fusion | flops 814940160 | bytes 15974400 | tf_op jit(solution)/shard_map/hqk,qhd->khd/dot_general | solution.py:203
  426.9 9.3 %fusion.30 = bf16[3,256,128]{1,2,0:T(8,128)(2,1)S(1)} fusion(bf16[4096,3,128]{0,2,1:T(8,128)(2,1)} %bitcast.214, f32[3,4096,256]{2,1,0:T(8,128)} %fusion.83, bf16[4096,3,128]{0,2,1:T(8,128)(2,1)} %bitcast.211, bf16[256,3,128]{0,2,1:T(8,128)(2,1)} %bitcast.222, f32[3,4096]{1,0:T(4,128)S(1)} %bitcast.228, f32[3,4096]{1,0:T(4,128)S(1)} %bitcast.220), kind=kOutput, calls=%fused_computation.44 | convolution fusion | flops 1626537984 | bytes 19365888 | tf_op jit(solution)/shard_map/hqk,qhd->khd/dot_general | solution.py:200
  437.0 157.6 %reduce-scatter.2.cloned.1.call-done = f32[48,384]{1,0:T(8,128)} async-done(((f32[3072,384]{1,0:T(8,128)}), f32[48,384]{1,0:T(8,128)}) %reduce-scatter.2.cloned.1.call-update) | async-done | bytes 73744 | tf_op jit(solution)/shard_map/reduce_scatter | solution.py:210
  (110 shorter events, 33.4 us)
Async XLA Ops:
  7.2 128.3 %copy-start = (bf16[512,3072]{1,0:T(8,128)(2,1)S(1)}, bf16[512,3072]{1,0:T(8,128)(2,1)}, u32[]{:S(2)}) copy-start(bf16[512,3072]{1,0:T(8,128)(2,1)} %param.20) | copy-start | bytes 9437188
  7.2 25.9 %copy-start.12 = (s32[64]{0:T(128)S(1)}, s32[64]{0:T(128)}, u32[]{:S(2)}) copy-start(s32[64]{0:T(128)} %param.18) | copy-start | bytes 772
  7.2 26.0 %copy-start.14 = (s32[1,64]{1,0:T(1,128)S(1)}, s32[1,64]{1,0:T(1,128)}, u32[]{:S(2)}) copy-start(s32[1,64]{1,0:T(1,128)} %param.21) | copy-start | bytes 772
  25.8 14.8 %all-to-all-start = ((bf16[3,16,14,224]{3,2,0,1:T(8,128)(2,1)}), bf16[3,16,14,224]{3,2,0,1:T(8,128)(2,1)S(1)}, u32[]{:S(2)}, u32[]{:S(2)}) async-start(bf16[3,16,14,224]{3,2,0,1:T(8,128)(2,1)} %copy.79), calls=%async_computation | async-start | bytes 786432 | tf_op jit(solution)/shard_map/all_to_all | solution.py:121
  33.0 148.8 %all-gather.9.cloned.1.call-start = ((), (), s32[]{:S(2)}) async-start(), calls=%async_computation.2 | async-start | bytes 1966080 | tf_op jit(solution)/shard_map/all_gather | solution.py:138
  43.1 5.8 collective-permute-start
  46.9 5.7 collective-permute-start.1
  52.8 6.1 %collective-permute-start.2 = (bf16[3,18,1,224]{3,2,0,1:T(2,128)(2,1)S(1)}, bf16[3,18,1,224]{3,2,0,1:T(2,128)(2,1)S(1)}, u32[]{:S(2)}, u32[]{:S(2)}) collective-permute-start(bf16[3,18,1,224]{3,2,0,1:T(2,128)(2,1)S(1)} %get-tuple-element.22), channel_id=1, source_target_pairs={{0,1},{1,2},{2,3},{3,4},{4,5},{5,6},{6,7},{7,8},{8,9},{9,10},{10,1... | collective-permute-start | bytes 72584 | tf_op jit(solution)/shard_map/ppermute | solution.py:23
  56.5 8.2 %collective-permute-start.3 = (bf16[3,18,1,224]{3,2,0,1:T(2,128)(2,1)S(1)}, bf16[3,18,1,224]{3,2,0,1:T(2,128)(2,1)S(1)}, u32[]{:S(2)}, u32[]{:S(2)}) collective-permute-start(bf16[3,18,1,224]{3,2,0,1:T(2,128)(2,1)S(1)} %get-tuple-element.23), channel_id=1, source_target_pairs={{1,0},{2,1},{3,2},{4,3},{5,4},{6,5},{7,6},{8,7},{9,8},{10,9},{11,1... | collective-permute-start | bytes 72584 | tf_op jit(solution)/shard_map/ppermute | solution.py:26
  106.7 20.7 %copy-start.13 = (bf16[81,128]{1,0:T(8,128)(2,1)S(1)}, bf16[81,128]{1,0:T(8,128)(2,1)}, u32[]{:S(2)}) copy-start(bf16[81,128]{1,0:T(8,128)(2,1)} %param.19) | copy-start | bytes 62212
  138.6 51.9 %copy-start.10 = (bf16[1,256,384]{2,1,0:T(8,128)(2,1)S(1)}, bf16[1,256,384]{2,1,0:T(8,128)(2,1)}, u32[]{:S(2)}) copy-start(bf16[1,256,384]{2,1,0:T(8,128)(2,1)} %param.25) | copy-start | bytes 589828
  138.6 102.8 %all-gather.13.cloned.1.call-start = ((), (), s32[]{:S(2)}) async-start(), calls=%async_computation.5 | async-start | bytes 3342336 | tf_op jit(solution)/shard_map/all_gather | solution.py:172
  140.5 160.4 %all-gather.15.cloned.1.call-start = ((), (), s32[]{:S(2)}) async-start(), calls=%async_computation.6 | async-start | bytes 3342336 | tf_op jit(solution)/shard_map/all_gather | solution.py:173
  142.3 218.5 %all-gather.17.cloned.1.call-start = ((), (), s32[]{:S(2)}) async-start(), calls=%async_computation.7 | async-start | bytes 3342336 | tf_op jit(solution)/shard_map/all_gather | solution.py:185
  144.1 97.3 %copy-start.6 = (bf16[1,256,384]{1,2,0:T(8,128)(2,1)S(1)}, bf16[1,256,384]{1,2,0:T(8,128)(2,1)}, u32[]{:S(2)}) copy-start(bf16[1,256,384]{1,2,0:T(8,128)(2,1)} %copy.74) | copy-start | bytes 589828
  144.1 271.0 %all-gather.11.cloned.1.call-start = ((), (), s32[]{:S(2)}) async-start(), calls=%async_computation.3 | async-start | bytes 3342336 | tf_op jit(solution)/shard_map/all_gather | solution.py:188
  185.6 5.0 copy-start.7
  185.6 409.0 %reduce-scatter.2.cloned.1.call-start = ((), (), s32[]{:S(2)}) async-start(), calls=%async_computation.4 | async-start | bytes 4792320 | tf_op jit(solution)/shard_map/reduce_scatter | solution.py:210
  190.8 50.6 %copy-start.8 = (bf16[256,384]{0,1:T(8,128)(2,1)}, bf16[256,384]{0,1:T(8,128)(2,1)S(1)}, u32[]{:S(2)}) copy-start(bf16[256,384]{0,1:T(8,128)(2,1)S(1)} %copy.86) | copy-start | bytes 589828
  241.5 59.5 %copy-start.4 = (bf16[1,4096,384]{1,2,0:T(8,128)(2,1)S(1)}, bf16[1,4096,384]{1,2,0:T(8,128)(2,1)}, u32[]{:S(2)}) copy-start(bf16[1,4096,384]{1,2,0:T(8,128)(2,1)} %all-gather.13.cloned.1.call-done) | copy-start | bytes 9437188
  245.5 4.6 copy-start.2
  245.5 55.5 %copy-start.9 = (bf16[256,384]{0,1:T(8,128)(2,1)S(1)}, bf16[256,384]{0,1:T(8,128)(2,1)}, u32[]{:S(2)}) copy-start(bf16[256,384]{0,1:T(8,128)(2,1)} %copy-done.8) | copy-start | bytes 589828
  300.9 59.9 %copy-start.5 = (bf16[1,256,384]{1,2,0:T(8,128)(2,1)S(1)}, bf16[1,256,384]{1,2,0:T(8,128)(2,1)}, u32[]{:S(2)}) copy-start(bf16[1,256,384]{1,2,0:T(8,128)(2,1)} %copy.75) | copy-start | bytes 589828
  418.3 7.7 %copy-start.3 = (bf16[4096,384]{0,1:T(8,128)(2,1)}, bf16[4096,384]{0,1:T(8,128)(2,1)S(1)}, u32[]{:S(2)}) copy-start(bf16[4096,384]{0,1:T(8,128)(2,1)S(1)} %copy.95) | copy-start | bytes 9437188
  418.4 8.6 %copy-start.11 = (f32[4096,3]{0,1:T(4,128)S(1)}, f32[4096,3]{0,1:T(4,128)}, u32[]{:S(2)}) copy-start(f32[4096,3]{0,1:T(4,128)} %all_gather.28) | copy-start | bytes 147460
  426.9 167.7 %copy-start.1 = (bf16[512,3072]{1,0:T(8,128)(2,1)S(1)}, bf16[512,3072]{1,0:T(8,128)(2,1)}, u32[]{:S(2)}) copy-start(bf16[512,3072]{1,0:T(8,128)(2,1)} %param.20) | copy-start | bytes 9437188
Sparse Core Ops, SparseCore 0:
  138.8 43.0 all-gather.8
  184.8 56.6 all-gather.12
  243.9 57.0 all-gather.14
  303.8 57.0 all-gather.16
  363.2 51.9 all-gather.10
  421.4 173.1 reduce-scatter.1
where the time goes:
time: 604 us; the launch traced here: 601 us
  waiting for transfers between devices  358 us (59%)
  local copies, waits for them, and re-layouts  92.4 us (15%)
  matrix products  60.4 us (10%)
  blocking collectives  46.7 us (8%)
  starting transfers between devices  18.8 us (3%)
  between operations  14.6 us (2%)
  other arithmetic  10.7 us (2%)
    reduce_scatter x1, waiting for transfers between devices, per_device(): lax.psum_scatter(jnp.einsum('td,th->dh', all_grads, output_here, preferre...  158 us
    all_gather x1, waiting for transfers between devices, per_device(): lax.all_gather(value_here, 'height', axis=0, tiled=True)  48.7 us
    all_gather x1, waiting for transfers between devices, per_device(): lax.all_gather(grad_out.astype(jnp.float32), 'height', axis=0, tiled=True)  46 us
    all_gather x1, waiting for transfers between devices, per_device(): all_grads = lax.all_gather(token_grads, 'tm', axis=0, tiled=True)  37.6 us
    all_gather x1, waiting for transfers between devices, per_device(): lax.all_gather(key_here, 'height', axis=0, tiled=True)  25.6 us
    all_gather x1, waiting for transfers between devices, per_device(): lax.all_gather(query_here.astype(jnp.float32), 'height', axis=0, tiled=True)  25.3 us
    all_gather x1, blocking collectives, per_device(): lax.all_gather(row_dots.T, 'height', axis=0, tiled=True)  25 us
    all_gather x1, blocking collectives, per_device(): lax.all_gather(log_totals.T, 'height', axis=0, tiled=True)  21.7 us
  transfers between devices with their start and end apart: 11, of which 9 were waited for; matrix products, arithmetic and copies ran while one was open for 11% of the time, Pallas kernels for 0%

commit v1 on v0

v1 whole, which is shorter than its diff:
```python
import functools
import math

import jax
import jax.numpy as jnp
import numpy as np
from jax import lax
from jax.experimental import pallas as pl
from jax.experimental.pallas import tpu as pltpu
from jax.sharding import Mesh
from jax.sharding import PartitionSpec as P

HDIM = 128
IMG = 224
PATCH = 14
SIDE = IMG // PATCH
GRID = 4
HEADS_HERE = 3
ROWS_HERE = 256
FEATS = HEADS_HERE * HDIM
BLOCK = GRID * ROWS_HERE
FRAMES = 64
LANES = 128
QUARTERS = 4
QUARTER_LANES = 32
TAPS = 27
ORDER_LANE = TAPS
QUARTER_CELLS = (PATCH // 2) * (2 * PATCH)

epsilon = 1e-05
pixel_std = (0.26862954, 0.26130258, 0.27577711)

f32 = jnp.float32
bf16 = jnp.bfloat16
VMEM_LIMIT = 56 * 1024 * 1024
HIGHEST = lax.Precision.HIGHEST
LOG2E = math.log2(math.e)
SCORE_SCALE = HDIM ** (-0.5)


def row_masks():
    masks = np.zeros((8, PATCH), np.float32)
    for half in range(2):
        for shift in range(3):
            low = half * 7 + shift - 1
            masks[half * 3 + shift, max(low, 0) : min(low + 7, PATCH)] = 1
    masks[6, 0] = 1
    masks[7, PATCH - 1] = 1
    return masks


def basis_matrix():
    rows = row_masks()
    columns = np.zeros((3, PATCH), np.float32)
    columns[0] = 1
    columns[1, 0] = 1
    columns[2, PATCH - 1] = 1
    basis = np.zeros((LANES, 3, PATCH, PATCH), np.float32)
    for col in range(3):
        for row in range(8):
            for channel in range(3):
                basis[col * 24 + row * 3 + channel, channel] = np.outer(rows[row], columns[col])
    return basis.reshape(LANES, 3 * PATCH * PATCH)


def basis_scale():
    scale = np.zeros((LANES, 1), np.float32)
    for lane in range(72):
        scale[lane, 0] = 1.0 / (pixel_std[lane % 3] * QUARTER_CELLS)
    return scale


def spread_matrix():
    spread = np.zeros((6, LANES, LANES), np.float32)
    for half in range(2):
        for side in range(2):
            first = 2 * side + 1
            terms = {
                0: [(first - 1, 2, 1), (first, 0, 1), (first + 1, 0, 1), (first + 1, 2, -1)],
                1: [(first, 0, 1), (first + 1, 0, 1)],
                2: [(first, 0, 1), (first, 1, -1), (first + 1, 0, 1), (first + 2, 1, 1)],
            }
            for shift in range(3):
                groups = [half * 3 + shift]
                if (half, shift) == (0, 0):
                    groups.append(7)
                if (half, shift) == (1, 2):
                    groups.append(6)
                for offset in range(3):
                    for channel in range(3):
                        lane = (half * 2 + side) * QUARTER_LANES + (shift * 3 + offset) * 3 + channel
                        for place, col, sign in terms[offset]:
                            for row in groups:
                                spread[place, col * 24 + row * 3 + channel, lane] += sign
    return spread.reshape(6 * LANES, LANES)


def window_kernel(
    cot_ref, pre_ref, gain_ref, patch_ref, basis_ref, scale_ref, spread_ref, order_ref, out_ref, sums
):
    pre = pre_ref[...].astype(f32)
    centered = pre - jnp.mean(pre, axis=-1, keepdims=True)
    inverse = lax.rsqrt(jnp.mean(centered * centered, axis=-1, keepdims=True) + epsilon)
    normed = centered * inverse
    scaled = cot_ref[...].astype(f32) * gain_ref[...].astype(f32)
    grad_rows = inverse * (
        scaled
        - jnp.mean(scaled, axis=-1, keepdims=True)
        - normed * jnp.mean(scaled * normed, axis=-1, keepdims=True)
    )
    grad_rows = grad_rows.astype(bf16)
    weights = (
        jnp.dot(basis_ref[...], patch_ref[...], preferred_element_type=f32) * scale_ref[...]
    )
    high = weights.astype(bf16)
    low = (weights - high.astype(f32)).astype(bf16)
    both = lax.dot_general(
        grad_rows,
        jnp.concatenate([high, low], axis=0),
        (((1,), (1,)), ((), ())),
        preferred_element_type=f32,
    )
    patch_sums = both[:, :LANES] + both[:, LANES:]
    group = (lax.broadcasted_iota(jnp.int32, (SIDE * SIDE, LANES), 1) // 3) % 8
    edge = jnp.zeros((SIDE, LANES), f32)
    above = jnp.concatenate([edge, patch_sums[:-SIDE]], axis=0)
    below = jnp.concatenate([patch_sums[SIDE:], edge], axis=0)
    patch_sums = jnp.where(group == 7, above, jnp.where(group == 6, below, patch_sums))
    sums[pl.ds(0, 8), :] = jnp.zeros((8, LANES), f32)
    sums[pl.ds(8 + SIDE * SIDE, 8), :] = jnp.zeros((8, LANES), f32)
    sums[pl.ds(8, SIDE * SIDE), :] = patch_sums
    column = lax.broadcasted_iota(jnp.int32, (SIDE * GRID, LANES), 0) % GRID
    total = jnp.zeros((SIDE * GRID, LANES), f32)
    for place in range(6):
        picked = sums[pl.ds(7 + place, SIDE * GRID, stride=GRID), :]
        if place == 0:
            picked = jnp.where(column == 0, 0.0, picked)
        if place == 5:
            picked = jnp.where(column == GRID - 1, 0.0, picked)
        total = total + jnp.dot(
            picked,
            spread_ref[pl.ds(place * LANES, LANES), :],
            preferred_element_type=f32,
            precision=HIGHEST,
        )
    windows = total.astype(bf16)
    for target_x in range(GRID):
        block = windows[target_x * 16 : (target_x + 1) * 16] + order_ref[...]
        for target_t in range(GRID):
            for target_y in range(GRID):
                out_ref[(target_t * GRID + target_x) * GRID + target_y] = block


def token_kernel(
    place_ref, owner_ref, recv_ref, conv_ref, joint_ref, *refs
):
    out_refs, (grad_ref, dots_ref, outer_ref, frames, conv_big, ordered) = refs[:GRID], refs[GRID:]
    here_x = place_ref[0]
    here_y = place_ref[1]
    frames[0] = jnp.zeros((16, LANES), bf16)
    frames[FRAMES + 1] = jnp.zeros((16, LANES), bf16)

    def fetch(frame, carry):
        frames[frame + 1] = recv_ref[(frame // 16) * 16 + owner_ref[frame]]
        return carry

    lax.fori_loop(0, FRAMES, fetch, 0, unroll=8)
    conv_big[...] = jnp.zeros_like(conv_big)
    for quarter in range(QUARTERS):
        for shift in range(3):
            conv_big[
                pl.ds(shift * LANES + quarter * QUARTER_LANES, QUARTER_LANES),
                pl.ds(quarter * LANES, LANES),
            ] = conv_ref[shift]
    lane = lax.broadcasted_iota(jnp.int32, (16, ROWS_HERE), 1)
    for slab_t in range(GRID):
        pooled = jnp.zeros((ROWS_HERE, QUARTERS * LANES), f32)
        for shift in range(3):
            window = frames[pl.ds(slab_t * 16 + shift, 16)].reshape(ROWS_HERE, LANES)
            pooled = pooled + jnp.dot(
                window, conv_big[pl.ds(shift * LANES, LANES), :], preferred_element_type=f32
            )
        pooled = pooled.astype(bf16)
        pieces = []
        for piece in range(GRID):
            slab = lax.rem(here_y + piece, GRID)
            block = recv_ref[slab_t * 16 + here_x * GRID + slab].astype(f32)
            for part in range(4):
                order = block[:, ORDER_LANE + part : ORDER_LANE + part + 1].astype(jnp.int32)
                target = (order // 4) * 16 + slab * 4 + lax.rem(order, 4)
                pieces.append(jnp.where(lane == target, 1.0, 0.0).astype(bf16))
        chosen = jnp.dot(
            jnp.concatenate(pieces, axis=0), pooled, preferred_element_type=f32
        ).astype(bf16)
        for piece in range(GRID):
            ordered[pl.ds(piece * ROWS_HERE + slab_t * 64, 64), :] = chosen[
                piece * 64 : (piece + 1) * 64
            ]
    outer = jnp.zeros((QUARTERS * LANES, FEATS), f32)
    ones = jnp.ones((8, HDIM), f32)
    for piece in range(GRID):
        rows = ordered[pl.ds(piece * ROWS_HERE, ROWS_HERE), :]
        grads = jnp.dot(rows, joint_ref[...], preferred_element_type=f32).astype(bf16)
        grad_ref[piece] = grads
        outs = out_refs[piece][...]
        products = grads.astype(f32) * outs.astype(f32)
        for head in range(HEADS_HERE):
            dots = lax.dot_general(
                ones,
                products[:, head * HDIM : (head + 1) * HDIM],
                (((1,), (1,)), ((), ())),
                preferred_element_type=f32,
                precision=HIGHEST,
            )
            dots_ref[head, :, pl.ds(piece * ROWS_HERE, ROWS_HERE)] = dots
        outer = outer + lax.dot_general(
            rows, outs, (((0,), (0,)), ((), ())), preferred_element_type=f32
        )
    outer_ref[...] = outer.astype(bf16)


def totals_kernel(*refs):
    query_refs, key_refs, out_ref = refs[:GRID], refs[GRID : 2 * GRID], refs[2 * GRID]

    def one_head(head, carry):
        columns = pl.ds(pl.multiple_of(head * HDIM, HDIM), HDIM)
        for piece in range(GRID):
            query = query_refs[piece][:, columns]
            scores = [
                lax.dot_general(
                    key_ref[:, columns],
                    query,
                    (((1,), (1,)), ((), ())),
                    preferred_element_type=f32,
                )
                for key_ref in key_refs
            ]
            top = functools.reduce(
                jnp.maximum, [jnp.max(tile, axis=0, keepdims=True) for tile in scores]
            )
            shifted = top * (SCORE_SCALE * LOG2E)
            total = sum(
                jnp.sum(
                    jnp.exp2(tile * (SCORE_SCALE * LOG2E) - shifted), axis=0, keepdims=True
                )
                for tile in scores
            )
            out_ref[head, :, pl.ds(piece * ROWS_HERE, ROWS_HERE)] = jnp.broadcast_to(
                shifted + jnp.log2(total), (8, ROWS_HERE)
            )
        return carry

    lax.fori_loop(0, HEADS_HERE, one_head, 0)


def grads_kernel(*refs):
    query_refs, key_refs, value_refs, total_refs = (
        refs[GRID * i : GRID * (i + 1)] for i in range(4)
    )
    grad_ref, dots_ref = refs[4 * GRID : 4 * GRID + 2]
    rest = refs[4 * GRID + 2 :]
    query_out, pair_out, (key_sums, value_sums) = rest[:GRID], rest[GRID : 2 * GRID], rest[2 * GRID :]
    root = math.sqrt(FRAMES * 64)

    def one_head(head, carry):
        columns = pl.ds(pl.multiple_of(head * HDIM, HDIM), HDIM)
        for piece in range(GRID):
            parts = [
                total_refs[step][
                    head, 0:1, pl.ds(((piece - step) % GRID) * ROWS_HERE, ROWS_HERE)
                ]
                for step in range(GRID)
            ]
            top = functools.reduce(jnp.maximum, parts)
            totals = top + jnp.log2(sum(jnp.exp2(part - top) for part in parts))
            dots = dots_ref[head, 0:1, pl.ds(piece * ROWS_HERE, ROWS_HERE)]
            query = query_refs[piece][:, columns]
            grad = grad_ref[piece, :, columns]
            query_sum = jnp.zeros((ROWS_HERE, HDIM), f32)
            for other in range(GRID):
                key = key_refs[other][:, columns]
                scores = lax.dot_general(
                    key, query, (((1,), (1,)), ((), ())), preferred_element_type=f32
                )
                weights = jnp.exp2(scores * (SCORE_SCALE * LOG2E) - totals)
                mixed = lax.dot_general(
                    value_refs[other][:, columns],
                    grad,
                    (((1,), (1,)), ((), ())),
                    preferred_element_type=f32,
                )
                dscore = (weights * (mixed - dots)).astype(bf16)
                value_part = jnp.dot(weights.astype(bf16), grad, preferred_element_type=f32)
                key_part = jnp.dot(dscore, query, preferred_element_type=f32)
                query_sum = query_sum + lax.dot_general(
                    dscore, key, (((0,), (0,)), ((), ())), preferred_element_type=f32
                )
                if piece == 0:
                    value_sums[other] = value_part
                    key_sums[other] = key_part
                else:
                    value_sums[other] += value_part
                    key_sums[other] += key_part
            query_out[piece][:, columns] = (query_sum * (root * SCORE_SCALE)).astype(bf16)
        for other in range(GRID):
            pair_out[other][0, :, columns] = (key_sums[other] * (root * SCORE_SCALE)).astype(bf16)
            pair_out[other][1, :, columns] = (value_sums[other] * root).astype(bf16)
        return carry

    lax.fori_loop(0, HEADS_HERE, one_head, 0)


def call(kernel, out_shape, scratch=(), scalars=0, operands=0, flops=0, moved=0):
    vmem = pl.BlockSpec(memory_space=pltpu.VMEM)
    smem = pl.BlockSpec(memory_space=pltpu.SMEM)
    return pl.pallas_call(
        kernel,
        out_shape=out_shape,
        in_specs=[smem] * scalars + [vmem] * operands,
        out_specs=jax.tree.map(lambda _: vmem, out_shape),
        scratch_shapes=list(scratch),
        compiler_params=pltpu.CompilerParams(vmem_limit_bytes=VMEM_LIMIT),
        cost_estimate=pl.CostEstimate(flops=flops, bytes_accessed=moved, transcendentals=0),
    )


def shape(dims, dtype):
    return jax.ShapeDtypeStruct(dims, dtype)


def from_ahead(block, axis, step):
    return lax.ppermute(block, axis, [(i, (i - step) % GRID) for i in range(GRID)])


def to_ahead(block, axis, step):
    return lax.ppermute(block, axis, [(i, (i + step) % GRID) for i in range(GRID)])


def per_device(
    vit_cot,
    vit_pre,
    ln_gain,
    patch_w,
    frame_owner,
    conv_w,
    join_w,
    token_order,
    queries,
    keys,
    values,
    attn_out,
    out_w,
):
    here_x = lax.axis_index("hx")
    here_y = lax.axis_index("hy")
    place = jnp.stack([here_x, here_y]).astype(jnp.int32)

    def gather(block, axis):
        return [block] + [from_ahead(block, axis, step) for step in range(1, GRID)]

    key_pieces = gather(keys[0], "hx")
    query_pieces = gather(queries[0], "hy")
    value_pieces = gather(values[0], "hx")
    out_pieces = gather(attn_out[0], "hy")

    order_lanes = jnp.pad(
        token_order.reshape(4, 16).T.astype(bf16),
        ((0, 0), (ORDER_LANE, LANES - ORDER_LANE - 4)),
    )
    windows = call(
        window_kernel,
        shape((FRAMES, 16, LANES), bf16),
        scratch=[pltpu.VMEM((SIDE * SIDE + 16, LANES), f32)],
        operands=8,
        flops=400 * 10**6,
        moved=3 * 10**6,
    )(
        vit_cot[0, 0],
        vit_pre[0, 0],
        ln_gain[None],
        patch_w,
        jnp.asarray(basis_matrix(), bf16),
        jnp.asarray(basis_scale(), f32),
        jnp.asarray(spread_matrix(), f32),
        order_lanes,
    )
    received = lax.all_to_all(
        windows, ("tm", "hx", "hy"), split_axis=0, concat_axis=0, tiled=True
    )

    totals = call(
        totals_kernel,
        shape((HEADS_HERE, 8, BLOCK), f32),
        operands=2 * GRID,
        flops=8 * 10**8,
        moved=2 * 10**6,
    )(*query_pieces, *key_pieces)
    total_pieces = gather(totals, "hy")

    joint = lax.dot_general(
        join_w, out_w, (((1,), (1,)), ((), ())), preferred_element_type=f32
    ).astype(bf16)
    conv_rows = jnp.pad(
        conv_w.reshape(3, TAPS, LANES), ((0, 0), (0, QUARTER_LANES - TAPS), (0, 0))
    )
    grad_out, row_dots, outer = call(
        token_kernel,
        (
            shape((GRID, ROWS_HERE, FEATS), bf16),
            shape((HEADS_HERE, 8, BLOCK), f32),
            shape((QUARTERS * LANES, FEATS), bf16),
        ),
        scratch=[
            pltpu.VMEM((FRAMES + 2, 16, LANES), bf16),
            pltpu.VMEM((3 * LANES, QUARTERS * LANES), bf16),
            pltpu.VMEM((BLOCK, QUARTERS * LANES), bf16),
        ],
        scalars=2,
        operands=3 + GRID,
        flops=2 * 10**9,
        moved=3 * 10**6,
    )(place, frame_owner, received, conv_rows, joint, *out_pieces)

    weight_part = lax.dot_general(
        join_w, outer, (((0,), (0,)), ((), ())), preferred_element_type=f32
    ) * (1.0 / math.sqrt(FRAMES * 64 * 4))
    weight_part = weight_part.astype(bf16).reshape(2, 2, GRID, GRID, 48, FEATS)
    weight_part = lax.dynamic_index_in_dim(weight_part, here_y, 3, keepdims=False)
    weight_part = weight_part.transpose(1, 2, 0, 3, 4).reshape(8, 2, 48, FEATS)
    weight_parts = lax.all_to_all(
        weight_part, ("core", "hx"), split_axis=0, concat_axis=0, tiled=True
    )
    weight_half = jnp.sum(weight_parts.astype(f32), axis=0)
    here_z = lax.axis_index("zh")
    weight_other = lax.ppermute(
        lax.dynamic_index_in_dim(weight_half, 1 - here_z, 0, keepdims=False),
        "zh",
        [(0, 1), (1, 0)],
    )
    weight_grad = lax.dynamic_index_in_dim(weight_half, here_z, 0, keepdims=False) + weight_other

    outs = call(
        grads_kernel,
        tuple([shape((ROWS_HERE, FEATS), bf16)] * GRID)
        + tuple([shape((2, ROWS_HERE, FEATS), bf16)] * GRID),
        scratch=[pltpu.VMEM((GRID, ROWS_HERE, HDIM), f32)] * 2,
        operands=4 * GRID + 2,
        flops=8 * 10**9,
        moved=6 * 10**6,
    )(*query_pieces, *key_pieces, *value_pieces, *total_pieces, grad_out, row_dots)
    query_parts, pair_parts = outs[:GRID], outs[GRID:]
    pair_back = [pair_parts[0]] + [
        to_ahead(pair_parts[step], "hx", step) for step in range(1, GRID)
    ]
    query_back = [query_parts[0]] + [
        to_ahead(query_parts[step], "hy", step) for step in range(1, GRID)
    ]

    def total(parts):
        return sum(part.astype(f32) for part in parts).astype(bf16)

    query_grad = total(query_back)
    key_grad = total([part[0] for part in pair_back])
    value_grad = total([part[1] for part in pair_back])
    return (query_grad[None], key_grad[None], value_grad[None], weight_grad)


def solution(mesh):
    fine = Mesh(
        mesh.devices.reshape(2, 2, GRID, GRID, GRID), ("zh", "core", "tm", "hx", "hy")
    )
    dp, height = ("zh", "core"), ("hx", "hy")
    rows = P(dp, height, "tm")
    slots = P(dp, ("tm",) + height, None, None)
    placed = (
        slots,
        slots,
        P(),
        P(),
        P(),
        P(),
        P(),
        P(height, "tm"),
        rows,
        rows,
        rows,
        rows,
        P("tm", None),
    )
    return jax.shard_map(
        per_device,
        mesh=fine,
        in_specs=placed,
        out_specs=(rows, rows, rows, P(dp + height, "tm")),
        check_vma=False,
    )
```

time: 604 us -> 123 us (0.20)
  the two profiles are of different devices: /device:TPU:24 before, /device:TPU:2 now
where the time goes in v1:
time: 123 us; the launch traced here: 122 us
  starting transfers between devices  49.8 us (40%)
  Pallas kernels  34.8 us (28%)
  waiting for transfers between devices  11.3 us (9%)
  local copies, waits for them, and re-layouts  10.5 us (9%)
  matrix products  8.08 us (7%)
  other arithmetic  7.33 us (6%)
    ppermute x15, starting transfers between devices, from_ahead(): lax.ppermute(block, axis, [(i, (i - step) % GRID) for i in range(GRID)])  22.4 us
    pallas_call x1, Pallas kernels, per_device(): call(grads_kernel, tuple([shape((ROWS_HERE, FEATS), bf16)] * GRID) + tupl...  17.4 us
    all_to_all x1, starting transfers between devices, per_device(): lax.all_to_all(windows, ('tm', 'hx', 'hy'), split_axis=0, concat_axis=0,...  11.5 us
    ppermute x6, waiting for transfers between devices, to_ahead(): lax.ppermute(block, axis, [(i, (i + step) % GRID) for i in range(GRID)])  11.2 us
    pallas_call x1, Pallas kernels, per_device(): call(token_kernel, (shape((GRID, ROWS_HERE, FEATS), bf16), shape((HEADS_H...  7.05 us
    ppermute x6, starting transfers between devices, to_ahead(): lax.ppermute(block, axis, [(i, (i + step) % GRID) for i in range(GRID)])  6.39 us
    pallas_call x1, Pallas kernels, per_device(): call(totals_kernel, shape((HEADS_HERE, 8, BLOCK), f32), operands=2 * GRID...  5.82 us
    all_to_all x1, starting transfers between devices, per_device(): lax.all_to_all(weight_part, ('core', 'hx'), split_axis=0, concat_axis=0,...  4.94 us
  transfers between devices with their start and end apart: 24, of which 3 were waited for; matrix products, arithmetic and copies ran while one was open for 19% of the time, Pallas kernels for 28%

profile of v1, /device:TPU:2, one launch (start us, length us, event | category | flops | bytes accessed | tf_op | source)
XLA Modules:
  0.0 122.5 jit_solution(11179597426902396751)
XLA Ops:
  0.6 3.1 %collective-permute-start = (bf16[256,384]{1,0:T(8,128)(2,1)}, bf16[256,384]{1,0:T(8,128)(2,1)}, u32[]{:S(2)}, u32[]{:S(2)}) collective-permute-start(bf16[256,384]{1,0:T(8,128)(2,1)} %bitcast.36), channel_id=1, source_target_pairs={{0,3},{1,0},{2,1},{3,2},{4,7},{5,4},{6,5},{7,6},{8,11},{9,8},{10,9... | collective-permute-start | bytes 589832 | tf_op jit(solution)/shard_map/ppermute | solution.py:332
  4.4 1.0 collective-permute-start.2
  5.9 2.4 %collective-permute-start.4 = (bf16[256,384]{1,0:T(8,128)(2,1)}, bf16[256,384]{1,0:T(8,128)(2,1)}, u32[]{:S(2)}, u32[]{:S(2)}) collective-permute-start(bf16[256,384]{1,0:T(8,128)(2,1)} %bitcast.42), channel_id=1, source_target_pairs={{0,8},{4,12},{8,0},{12,4},{1,9},{5,13},{9,1},{13,5},{2,10},{6,14},... | collective-permute-start | bytes 589832 | tf_op jit(solution)/shard_map/ppermute | solution.py:332
  9.2 1.3 %broadcast_in_dim.8.gain_ref = bf16[1,1280]{1,0:T(2,128)(2,1)} reshape(bf16[1280]{0:T(1024)(128)(2,1)} %param.18) | data formatting | bytes 5120 | tf_op jit(solution)/shard_map/broadcast_in_dim | solution.py:380
  11.1 4.6 %shard_map.184 = bf16[64,16,128]{2,1,0:T(8,128)(2,1)} custom-call(bf16[256,1280]{1,0:T(8,128)(2,1)} %bitcast.29, bf16[256,1280]{1,0:T(8,128)(2,1)} %bitcast.30, bf16[1,1280]{1,0:T(2,128)(2,1)} %broadcast_in_dim.8.gain_ref, bf16[588,1280]{1,0:T(8,128)(2,1)} %patch_ref.1, bf16[128,588]{1,0:T(8,128)(2,1)} %constant.43.clone.basis_ref, ...), custom_call_target="tpu_custom_call" | custom-call | flops 400000000 | bytes 3000000 | tf_op jit(solution)/shard_map/pallas_call | solution.py:370
  15.7 11.5 %all-to-all-start = ((bf16[64,16,128]{2,1,0:T(8,128)(2,1)}), bf16[64,16,128]{2,1,0:T(8,128)(2,1)S(1)}, u32[]{:S(2)}, u32[]{:S(2)}) async-start(bf16[64,16,128]{2,1,0:T(8,128)(2,1)} %shard_map.184), calls=%async_computation | async-start | bytes 524288 | tf_op jit(solution)/shard_map/all_to_all | solution.py:387
  27.1 1.5 %collective-permute-start.5 = (bf16[256,384]{1,0:T(8,128)(2,1)}, bf16[256,384]{1,0:T(8,128)(2,1)}, u32[]{:S(2)}, u32[]{:S(2)}) collective-permute-start(bf16[256,384]{1,0:T(8,128)(2,1)} %bitcast.43), channel_id=1, source_target_pairs={{0,4},{4,8},{8,12},{12,0},{1,5},{5,9},{9,13},{13,1},{2,6},{6,10},{... | collective-permute-start | bytes 589832 | tf_op jit(solution)/shard_map/ppermute | solution.py:332
  28.7 2.7 %collective-permute-start.12 = (bf16[256,384]{1,0:T(8,128)(2,1)}, bf16[256,384]{1,0:T(8,128)(2,1)}, u32[]{:S(2)}, u32[]{:S(2)}) collective-permute-start(bf16[256,384]{1,0:T(8,128)(2,1)} %bitcast.32), channel_id=1, source_target_pairs={{0,3},{1,0},{2,1},{3,2},{4,7},{5,4},{6,5},{7,6},{8,11},{9,8},{10,9... | collective-permute-start | bytes 589832 | tf_op jit(solution)/shard_map/ppermute | solution.py:332
  32.2 0.9 collective-permute-start.14
  33.1 4.2 %convolution_convert_fusion.joint_ref = bf16[512,384]{1,0:T(8,128)(2,1)} fusion(bf16[512,3072]{1,0:T(8,128)(2,1)S(1)} %copy-done, bf16[384,3072]{1,0:T(8,128)(2,1)} %param.28), kind=kOutput, calls=%fused_computation.2 | convolution fusion | flops 1208156160 | bytes 5898240 | tf_op jit(solution)/shard_map/dot_general | solution.py:400
  39.1 2.1 %collective-permute-start.7 = (bf16[256,384]{1,0:T(8,128)(2,1)}, bf16[256,384]{1,0:T(8,128)(2,1)}, u32[]{:S(2)}, u32[]{:S(2)}) collective-permute-start(bf16[256,384]{1,0:T(8,128)(2,1)} %bitcast.47), channel_id=1, source_target_pairs={{0,8},{4,12},{8,0},{12,4},{1,9},{5,13},{9,1},{13,5},{2,10},{6,14},... | collective-permute-start | bytes 589832 | tf_op jit(solution)/shard_map/ppermute | solution.py:332
  41.2 5.8 %shard_map.183.refs_12_ = f32[3,8,1024]{2,1,0:T(8,128)} custom-call(bf16[256,384]{1,0:T(8,128)(2,1)} %bitcast.39, bf16[256,384]{1,0:T(8,128)(2,1)} %collective-permute-done.refs_1_, bf16[256,384]{1,0:T(8,128)(2,1)} %collective-permute-done.1.refs_2_, bf16[256,384]{1,0:T(8,128)(2,1)} %collective-permute-done.2.refs_3_, bf16[256,384]{1,0:T(8,128)(2,1)} %bitcast.44, ...), custom_call_target="tpu_custom_call" | custom-call | flops 800000000 | bytes 2000000 | tf_op jit(solution)/shard_map/pallas_call | solution.py:391
  47.0 1.2 collective-permute-start.8
  48.2 1.8 %collective-permute-start.10 = (f32[3,8,1024]{2,1,0:T(8,128)}, f32[3,8,1024]{2,1,0:T(8,128)S(1)}, u32[]{:S(2)}, u32[]{:S(2)}) collective-permute-start(f32[3,8,1024]{2,1,0:T(8,128)} %shard_map.183.refs_12_), channel_id=1, source_target_pairs={{0,2},{1,3},{2,0},{3,1},{4,6},{5,7},{6,4},{7,5},{8,10},{9,11},{10,... | collective-permute-start | bytes 294920 | tf_op jit(solution)/shard_map/ppermute | solution.py:332
  50.0 1.4 %collective-permute-start.11 = (f32[3,8,1024]{2,1,0:T(8,128)}, f32[3,8,1024]{2,1,0:T(8,128)}, u32[]{:S(2)}, u32[]{:S(2)}) collective-permute-start(f32[3,8,1024]{2,1,0:T(8,128)} %shard_map.183.refs_12_), channel_id=1, source_target_pairs={{0,1},{1,2},{2,3},{3,0},{4,5},{5,6},{6,7},{7,4},{8,9},{9,10},{10,1... | collective-permute-start | bytes 294920 | tf_op jit(solution)/shard_map/ppermute | solution.py:332
  52.1 7.0 %shard_map.185 = (bf16[4,256,384]{2,1,0:T(8,128)(2,1)}, f32[3,8,1024]{2,1,0:T(8,128)}, bf16[512,384]{1,0:T(8,128)(2,1)}) custom-call(s32[2]{0:T(128)} %pad_add_fusion.place_ref, s32[64]{0:T(128)} %owner_ref.1, bf16[64,16,128]{2,1,0:T(8,128)(2,1)} %copy-done.1, bf16[3,32,128]{2,1,0:T(8,128)(2,1)} %pad.9.conv_ref, ...), custom_call_target="tpu_custom_call" | custom-call | flops 2000000000 | bytes 3000000 | tf_op jit(solution)/shard_map/pallas_call | solution.py:406
  59.2 3.9 %fusion = bf16[3072,384]{0,1:T(8,128)(2,1)} fusion(bf16[512,384]{1,0:T(8,128)(2,1)} %get-tuple-element.25, bf16[512,3072]{1,0:T(8,128)(2,1)S(1)} %copy-done), kind=kOutput, calls=%fused_computation.1 | convolution fusion | flops 1210318848 | bytes 5898240 | tf_op jit(solution)/shard_map/dot_general | solution.py:424
  63.0 4.3 %copy.24 = bf16[3072,384]{1,0:T(8,128)(2,1)} copy(bf16[3072,384]{0,1:T(8,128)(2,1)} %fusion) | data formatting | bytes 4718592 | tf_op jit(solution)/shard_map/convert_element_type | solution.py:427
  67.3 1.8 %collective-permute-start.9 = (f32[3,8,1024]{2,1,0:T(8,128)S(1)}, f32[3,8,1024]{2,1,0:T(8,128)S(1)}, u32[]{:S(2)}, u32[]{:S(2)}) collective-permute-start(f32[3,8,1024]{2,1,0:T(8,128)S(1)} %copy-done.3), channel_id=1, source_target_pairs={{0,3},{1,0},{2,1},{3,2},{4,7},{5,4},{6,5},{7,6},{8,11},{9,8},{10,9... | collective-permute-start | bytes 294920 | tf_op jit(solution)/shard_map/ppermute | solution.py:332
  69.2 1.1 constant_dynamic-slice_fusion
  70.3 0.9 copy.25
  71.2 4.9 %all-to-all-start.1 = ((bf16[8,2,48,384]{3,2,1,0:T(8,128)(2,1)}), bf16[8,2,48,384]{3,2,1,0:T(8,128)(2,1)}, u32[]{:S(2)}, u32[]{:S(2)}) async-start(bf16[8,2,48,384]{3,2,1,0:T(8,128)(2,1)} %copy.25), calls=%async_computation.1 | async-start | bytes 1179648 | tf_op jit(solution)/shard_map/all_to_all | solution.py:430
  76.8 17.4 %shard_map.186 = (bf16[256,384]{1,0:T(8,128)(2,1)}, bf16[256,384]{1,0:T(8,128)(2,1)}, bf16[256,384]{1,0:T(8,128)(2,1)}, bf16[256,384]{1,0:T(8,128)(2,1)}, bf16[2...) custom-call(bf16[256,384]{1,0:T(8,128)(2,1)} %bitcast.40, ...), custom_call_target="tpu_custom_call" | custom-call | flops 8000000000 | bytes 6000000 | tf_op jit(solution)/shard_map/pallas_call | solution.py:442
  94.5 2.7 %collective-permute-start.16 = (bf16[256,384]{1,0:T(8,128)(2,1)}, bf16[256,384]{1,0:T(8,128)(2,1)}, u32[]{:S(2)}, u32[]{:S(2)}) collective-permute-start(bf16[256,384]{1,0:T(8,128)(2,1)} %get-tuple-element.19), channel_id=1, source_target_pairs={{0,2},{1,3},{2,0},{3,1},{4,6},{5,7},{6,4},{7,5},{8,10},{9,11},{10,... | collective-permute-start | bytes 589832 | tf_op jit(solution)/shard_map/ppermute | solution.py:336
  97.8 1.5 %collective-permute-start.18 = (bf16[2,256,384]{2,1,0:T(8,128)(2,1)}, bf16[2,256,384]{2,1,0:T(8,128)(2,1)S(1)}, u32[]{:S(2)}, u32[]{:S(2)}) collective-permute-start(bf16[2,256,384]{2,1,0:T(8,128)(2,1)} %get-tuple-element.22), channel_id=1, source_target_pairs={{0,4},{4,8},{8,12},{12,0},{1,5},{5,9},{9,13},{13,1},{2,6},{6,10},{... | collective-permute-start | bytes 1179656 | tf_op jit(solution)/shard_map/ppermute | solution.py:336
  99.2 1.0 collective-permute-start.19
  100.2 6.8 %collective-permute-done.15 = bf16[256,384]{1,0:T(8,128)(2,1)} collective-permute-done((bf16[256,384]{1,0:T(8,128)(2,1)}, bf16[256,384]{1,0:T(8,128)(2,1)}, u32[]{:S(2)}, u32[]{:S(2)}) %collective-permute-start.15) | collective-permute-done | bytes 196640 | tf_op jit(solution)/shard_map/ppermute | solution.py:336
  107.6 2.0 %fusion.1 = bf16[1,256,384]{2,1,0:T(8,128)(2,1)} fusion(bf16[256,384]{1,0:T(8,128)(2,1)} %collective-permute-done.17, bf16[256,384]{1,0:T(8,128)(2,1)} %collective-permute-done.16, bf16[256,384]{1,0:T(8,128)(2,1)} %collective-permute-done.15, bf16[256,384]{1,0:T(8,128)(2,1)} %get-tuple-element.17), kind=kLoop, calls=%fused_computation.7 | loop fusion | flops 786432 | bytes 983040 | tf_op jit(solution)/shard_map/broadcast_in_dim | solution.py:465
  109.6 1.2 convert_reduce_fusion
  110.8 4.6 %collective-permute-start.21 = (f32[48,384]{1,0:T(8,128)S(1)}, f32[48,384]{1,0:T(8,128)S(1)}, u32[]{:S(2)}, u32[]{:S(2)}) collective-permute-start(f32[48,384]{1,0:T(8,128)S(1)} %dynamic-slice_bitcast_fusion), channel_id=1, source_target_pairs={{0,128},{128,0},{1,129},{129,1},{2,130},{130,2},{3,131},{131,3},{4... | collective-permute-start | bytes 221192 | tf_op jit(solution)/shard_map/ppermute | solution.py:435
  115.4 4.2 %collective-permute-done.20 = bf16[2,256,384]{2,1,0:T(8,128)(2,1)} collective-permute-done((bf16[2,256,384]{2,1,0:T(8,128)(2,1)}, bf16[2,256,384]{2,1,0:T(8,128)(2,1)}, u32[]{:S(2)}, u32[]{:S(2)}) %collective-permute-start.20) | collective-permute-done | bytes 393248 | tf_op jit(solution)/shard_map/ppermute | solution.py:336
  119.6 2.3 %add_convert_fusion = (bf16[1,256,384]{2,1,0:T(8,128)(2,1)}, bf16[1,256,384]{2,1,0:T(8,128)(2,1)}) fusion(bf16[2,256,384]{2,1,0:T(8,128)(2,1)} %collective-permute-done.20, bf16[2,256,384]{2,1,0:T(8,128)(2,1)} %collective-permute-done.19, bf16[2,256,384]{2,1,0:T(8,128)(2,1)S(1)} %collective-permute-done.18, bf16[2,256,384]{2,1,0:T(8,128)(2,1)} %get-tuple-element.21), kind=kLoop, calls=%fused_computation.4 | loop fusion | flops 1572864 | bytes 1966080 | tf_op jit(solution)/shard_map/convert_element_type | solution.py:460
  (50 shorter events, 8.9 us)
Async XLA Ops:
  0.6 32.5 %copy-start = (bf16[512,3072]{1,0:T(8,128)(2,1)S(1)}, bf16[512,3072]{1,0:T(8,128)(2,1)}, u32[]{:S(2)}) copy-start(bf16[512,3072]{1,0:T(8,128)(2,1)} %param.22) | copy-start | bytes 9437188
  0.6 26.5 %collective-permute-start = (bf16[256,384]{1,0:T(8,128)(2,1)}, bf16[256,384]{1,0:T(8,128)(2,1)}, u32[]{:S(2)}, u32[]{:S(2)}) collective-permute-start(bf16[256,384]{1,0:T(8,128)(2,1)} %bitcast.36), channel_id=1, source_target_pairs={{0,3},{1,0},{2,1},{3,2},{4,7},{5,4},{6,5},{7,6},{8,11},{9,8},{10,9... | collective-permute-start | bytes 589832 | tf_op jit(solution)/shard_map/ppermute | solution.py:332
  3.7 25.0 %collective-permute-start.1 = (bf16[256,384]{1,0:T(8,128)(2,1)}, bf16[256,384]{1,0:T(8,128)(2,1)}, u32[]{:S(2)}, u32[]{:S(2)}) collective-permute-start(bf16[256,384]{1,0:T(8,128)(2,1)} %bitcast.37), channel_id=1, source_target_pairs={{0,2},{1,3},{2,0},{3,1},{4,6},{5,7},{6,4},{7,5},{8,10},{9,11},{10,... | collective-permute-start | bytes 589832 | tf_op jit(solution)/shard_map/ppermute | solution.py:332
  4.4 27.0 %collective-permute-start.2 = (bf16[256,384]{1,0:T(8,128)(2,1)}, bf16[256,384]{1,0:T(8,128)(2,1)}, u32[]{:S(2)}, u32[]{:S(2)}) collective-permute-start(bf16[256,384]{1,0:T(8,128)(2,1)} %bitcast.38), channel_id=1, source_target_pairs={{0,1},{1,2},{2,3},{3,0},{4,5},{5,6},{6,7},{7,4},{8,9},{9,10},{10,1... | collective-permute-start | bytes 589832 | tf_op jit(solution)/shard_map/ppermute | solution.py:332
  5.3 26.9 %collective-permute-start.3 = (bf16[256,384]{1,0:T(8,128)(2,1)}, bf16[256,384]{1,0:T(8,128)(2,1)}, u32[]{:S(2)}, u32[]{:S(2)}) collective-permute-start(bf16[256,384]{1,0:T(8,128)(2,1)} %bitcast.41), channel_id=1, source_target_pairs={{0,12},{4,0},{8,4},{12,8},{1,13},{5,1},{9,5},{13,9},{2,14},{6,2},{... | collective-permute-start | bytes 589832 | tf_op jit(solution)/shard_map/ppermute | solution.py:332
  5.9 32.7 %collective-permute-start.4 = (bf16[256,384]{1,0:T(8,128)(2,1)}, bf16[256,384]{1,0:T(8,128)(2,1)}, u32[]{:S(2)}, u32[]{:S(2)}) collective-permute-start(bf16[256,384]{1,0:T(8,128)(2,1)} %bitcast.42), channel_id=1, source_target_pairs={{0,8},{4,12},{8,0},{12,4},{1,9},{5,13},{9,1},{13,5},{2,10},{6,14},... | collective-permute-start | bytes 589832 | tf_op jit(solution)/shard_map/ppermute | solution.py:332
  15.7 35.8 %all-to-all-start = ((bf16[64,16,128]{2,1,0:T(8,128)(2,1)}), bf16[64,16,128]{2,1,0:T(8,128)(2,1)S(1)}, u32[]{:S(2)}, u32[]{:S(2)}) async-start(bf16[64,16,128]{2,1,0:T(8,128)(2,1)} %shard_map.184), calls=%async_computation | async-start | bytes 524288 | tf_op jit(solution)/shard_map/all_to_all | solution.py:387
  27.1 12.0 %collective-permute-start.5 = (bf16[256,384]{1,0:T(8,128)(2,1)}, bf16[256,384]{1,0:T(8,128)(2,1)}, u32[]{:S(2)}, u32[]{:S(2)}) collective-permute-start(bf16[256,384]{1,0:T(8,128)(2,1)} %bitcast.43), channel_id=1, source_target_pairs={{0,4},{4,8},{8,12},{12,0},{1,5},{5,9},{9,13},{13,1},{2,6},{6,10},{... | collective-permute-start | bytes 589832 | tf_op jit(solution)/shard_map/ppermute | solution.py:332
  28.7 8.6 %copy-start.2 = (bf16[81,128]{1,0:T(8,128)(2,1)S(1)}, bf16[81,128]{1,0:T(8,128)(2,1)}, u32[]{:S(2)}) copy-start(bf16[81,128]{1,0:T(8,128)(2,1)} %param.21) | copy-start | bytes 62212
  28.7 18.3 %collective-permute-start.12 = (bf16[256,384]{1,0:T(8,128)(2,1)}, bf16[256,384]{1,0:T(8,128)(2,1)}, u32[]{:S(2)}, u32[]{:S(2)}) collective-permute-start(bf16[256,384]{1,0:T(8,128)(2,1)} %bitcast.32), channel_id=1, source_target_pairs={{0,3},{1,0},{2,1},{3,2},{4,7},{5,4},{6,5},{7,6},{8,11},{9,8},{10,9... | collective-permute-start | bytes 589832 | tf_op jit(solution)/shard_map/ppermute | solution.py:332
  31.4 16.8 %collective-permute-start.13 = (bf16[256,384]{1,0:T(8,128)(2,1)}, bf16[256,384]{1,0:T(8,128)(2,1)}, u32[]{:S(2)}, u32[]{:S(2)}) collective-permute-start(bf16[256,384]{1,0:T(8,128)(2,1)} %bitcast.33), channel_id=1, source_target_pairs={{0,2},{1,3},{2,0},{3,1},{4,6},{5,7},{6,4},{7,5},{8,10},{9,11},{10,... | collective-permute-start | bytes 589832 | tf_op jit(solution)/shard_map/ppermute | solution.py:332
  32.2 17.8 %collective-permute-start.14 = (bf16[256,384]{1,0:T(8,128)(2,1)}, bf16[256,384]{1,0:T(8,128)(2,1)}, u32[]{:S(2)}, u32[]{:S(2)}) collective-permute-start(bf16[256,384]{1,0:T(8,128)(2,1)} %bitcast.34), channel_id=1, source_target_pairs={{0,1},{1,2},{2,3},{3,0},{4,5},{5,6},{6,7},{7,4},{8,9},{9,10},{10,1... | collective-permute-start | bytes 589832 | tf_op jit(solution)/shard_map/ppermute | solution.py:332
  38.6 28.8 %collective-permute-start.6 = (bf16[256,384]{1,0:T(8,128)(2,1)}, bf16[256,384]{1,0:T(8,128)(2,1)}, u32[]{:S(2)}, u32[]{:S(2)}) collective-permute-start(bf16[256,384]{1,0:T(8,128)(2,1)} %bitcast.46), channel_id=1, source_target_pairs={{0,12},{4,0},{8,4},{12,8},{1,13},{5,1},{9,5},{13,9},{2,14},{6,2},{... | collective-permute-start | bytes 589832 | tf_op jit(solution)/shard_map/ppermute | solution.py:332
  39.1 37.0 %collective-permute-start.7 = (bf16[256,384]{1,0:T(8,128)(2,1)}, bf16[256,384]{1,0:T(8,128)(2,1)}, u32[]{:S(2)}, u32[]{:S(2)}) collective-permute-start(bf16[256,384]{1,0:T(8,128)(2,1)} %bitcast.47), channel_id=1, source_target_pairs={{0,8},{4,12},{8,0},{12,4},{1,9},{5,13},{9,1},{13,5},{2,10},{6,14},... | collective-permute-start | bytes 589832 | tf_op jit(solution)/shard_map/ppermute | solution.py:332
  47.0 29.1 %collective-permute-start.8 = (bf16[256,384]{1,0:T(8,128)(2,1)}, bf16[256,384]{1,0:T(8,128)(2,1)}, u32[]{:S(2)}, u32[]{:S(2)}) collective-permute-start(bf16[256,384]{1,0:T(8,128)(2,1)} %bitcast.48), channel_id=1, source_target_pairs={{0,4},{4,8},{8,12},{12,0},{1,5},{5,9},{9,13},{13,1},{2,6},{6,10},{... | collective-permute-start | bytes 589832 | tf_op jit(solution)/shard_map/ppermute | solution.py:332
  48.2 27.9 %collective-permute-start.10 = (f32[3,8,1024]{2,1,0:T(8,128)}, f32[3,8,1024]{2,1,0:T(8,128)S(1)}, u32[]{:S(2)}, u32[]{:S(2)}) collective-permute-start(f32[3,8,1024]{2,1,0:T(8,128)} %shard_map.183.refs_12_), channel_id=1, source_target_pairs={{0,2},{1,3},{2,0},{3,1},{4,6},{5,7},{6,4},{7,5},{8,10},{9,11},{10,... | collective-permute-start | bytes 294920 | tf_op jit(solution)/shard_map/ppermute | solution.py:332
  50.0 26.1 %collective-permute-start.11 = (f32[3,8,1024]{2,1,0:T(8,128)}, f32[3,8,1024]{2,1,0:T(8,128)}, u32[]{:S(2)}, u32[]{:S(2)}) collective-permute-start(f32[3,8,1024]{2,1,0:T(8,128)} %shard_map.183.refs_12_), channel_id=1, source_target_pairs={{0,1},{1,2},{2,3},{3,0},{4,5},{5,6},{6,7},{7,4},{8,9},{9,10},{10,1... | collective-permute-start | bytes 294920 | tf_op jit(solution)/shard_map/ppermute | solution.py:332
  51.4 0.7 copy-start.1
  63.0 4.3 %copy-start.3 = (f32[3,8,1024]{2,1,0:T(8,128)S(1)}, f32[3,8,1024]{2,1,0:T(8,128)}, u32[]{:S(2)}) copy-start(f32[3,8,1024]{2,1,0:T(8,128)} %shard_map.183.refs_12_) | copy-start | bytes 294916
  67.3 8.8 %collective-permute-start.9 = (f32[3,8,1024]{2,1,0:T(8,128)S(1)}, f32[3,8,1024]{2,1,0:T(8,128)S(1)}, u32[]{:S(2)}, u32[]{:S(2)}) collective-permute-start(f32[3,8,1024]{2,1,0:T(8,128)S(1)} %copy-done.3), channel_id=1, source_target_pairs={{0,3},{1,0},{2,1},{3,2},{4,7},{5,4},{6,5},{7,6},{8,11},{9,8},{10,9... | collective-permute-start | bytes 294920 | tf_op jit(solution)/shard_map/ppermute | solution.py:332
  71.2 38.4 %all-to-all-start.1 = ((bf16[8,2,48,384]{3,2,1,0:T(8,128)(2,1)}), bf16[8,2,48,384]{3,2,1,0:T(8,128)(2,1)}, u32[]{:S(2)}, u32[]{:S(2)}) async-start(bf16[8,2,48,384]{3,2,1,0:T(8,128)(2,1)} %copy.25), calls=%async_computation.1 | async-start | bytes 1179648 | tf_op jit(solution)/shard_map/all_to_all | solution.py:430
  76.1 0.6 copy-start.4
  76.2 0.6 copy-start.5
  94.2 12.8 %collective-permute-start.15 = (bf16[256,384]{1,0:T(8,128)(2,1)}, bf16[256,384]{1,0:T(8,128)(2,1)}, u32[]{:S(2)}, u32[]{:S(2)}) collective-permute-start(bf16[256,384]{1,0:T(8,128)(2,1)} %get-tuple-element.18), channel_id=1, source_target_pairs={{0,1},{1,2},{2,3},{3,0},{4,5},{5,6},{6,7},{7,4},{8,9},{9,10},{10,1... | collective-permute-start | bytes 589832 | tf_op jit(solution)/shard_map/ppermute | solution.py:336
  94.5 12.9 %collective-permute-start.16 = (bf16[256,384]{1,0:T(8,128)(2,1)}, bf16[256,384]{1,0:T(8,128)(2,1)}, u32[]{:S(2)}, u32[]{:S(2)}) collective-permute-start(bf16[256,384]{1,0:T(8,128)(2,1)} %get-tuple-element.19), channel_id=1, source_target_pairs={{0,2},{1,3},{2,0},{3,1},{4,6},{5,7},{6,4},{7,5},{8,10},{9,11},{10,... | collective-permute-start | bytes 589832 | tf_op jit(solution)/shard_map/ppermute | solution.py:336
  97.2 10.5 %collective-permute-start.17 = (bf16[256,384]{1,0:T(8,128)(2,1)}, bf16[256,384]{1,0:T(8,128)(2,1)}, u32[]{:S(2)}, u32[]{:S(2)}) collective-permute-start(bf16[256,384]{1,0:T(8,128)(2,1)} %get-tuple-element.20), channel_id=1, source_target_pairs={{0,3},{1,0},{2,1},{3,2},{4,7},{5,4},{6,5},{7,6},{8,11},{9,8},{10,9... | collective-permute-start | bytes 589832 | tf_op jit(solution)/shard_map/ppermute | solution.py:336
  97.8 17.6 %collective-permute-start.18 = (bf16[2,256,384]{2,1,0:T(8,128)(2,1)}, bf16[2,256,384]{2,1,0:T(8,128)(2,1)S(1)}, u32[]{:S(2)}, u32[]{:S(2)}) collective-permute-start(bf16[2,256,384]{2,1,0:T(8,128)(2,1)} %get-tuple-element.22), channel_id=1, source_target_pairs={{0,4},{4,8},{8,12},{12,0},{1,5},{5,9},{9,13},{13,1},{2,6},{6,10},{... | collective-permute-start | bytes 1179656 | tf_op jit(solution)/shard_map/ppermute | solution.py:336
  99.2 16.1 %collective-permute-start.19 = (bf16[2,256,384]{2,1,0:T(8,128)(2,1)}, bf16[2,256,384]{2,1,0:T(8,128)(2,1)}, u32[]{:S(2)}, u32[]{:S(2)}) collective-permute-start(bf16[2,256,384]{2,1,0:T(8,128)(2,1)} %get-tuple-element.23), channel_id=1, source_target_pairs={{0,8},{4,12},{8,0},{12,4},{1,9},{5,13},{9,1},{13,5},{2,10},{6,14},... | collective-permute-start | bytes 1179656 | tf_op jit(solution)/shard_map/ppermute | solution.py:336
  107.0 12.6 %collective-permute-start.20 = (bf16[2,256,384]{2,1,0:T(8,128)(2,1)}, bf16[2,256,384]{2,1,0:T(8,128)(2,1)}, u32[]{:S(2)}, u32[]{:S(2)}) collective-permute-start(bf16[2,256,384]{2,1,0:T(8,128)(2,1)} %get-tuple-element.24), channel_id=1, source_target_pairs={{0,12},{4,0},{8,4},{12,8},{1,13},{5,1},{9,5},{13,9},{2,14},{6,2},{... | collective-permute-start | bytes 1179656 | tf_op jit(solution)/shard_map/ppermute | solution.py:336
  110.8 11.1 %collective-permute-start.21 = (f32[48,384]{1,0:T(8,128)S(1)}, f32[48,384]{1,0:T(8,128)S(1)}, u32[]{:S(2)}, u32[]{:S(2)}) collective-permute-start(f32[48,384]{1,0:T(8,128)S(1)} %dynamic-slice_bitcast_fusion), channel_id=1, source_target_pairs={{0,128},{128,0},{1,129},{129,1},{2,130},{130,2},{3,131},{131,3},{4... | collective-permute-start | bytes 221192 | tf_op jit(solution)/shard_map/ppermute | solution.py:435

commit v2 on v1

v2 whole, which is shorter than its diff:
```python
import functools
import math

import jax
import jax.numpy as jnp
import numpy as np
from jax import lax
from jax.experimental import pallas as pl
from jax.experimental.pallas import tpu as pltpu
from jax.sharding import Mesh
from jax.sharding import PartitionSpec as P

HDIM = 128
IMG = 224
PATCH = 14
SIDE = IMG // PATCH
GRID = 4
HEADS_HERE = 3
ROWS_HERE = 256
FEATS = HEADS_HERE * HDIM
BLOCK = GRID * ROWS_HERE
FRAMES = 64
LANES = 128
QUARTERS = 4
QUARTER_LANES = 32
TAPS = 27
ORDER_LANE = TAPS
QUARTER_CELLS = (PATCH // 2) * (2 * PATCH)

epsilon = 1e-05
pixel_std = (0.26862954, 0.26130258, 0.27577711)

f32 = jnp.float32
bf16 = jnp.bfloat16
MIB = 1024 * 1024
HIGHEST = lax.Precision.HIGHEST
LOG2E = math.log2(math.e)
SCORE_SCALE = HDIM ** (-0.5)


def row_masks():
    masks = np.zeros((8, PATCH), np.float32)
    for half in range(2):
        for shift in range(3):
            low = half * 7 + shift - 1
            masks[half * 3 + shift, max(low, 0) : min(low + 7, PATCH)] = 1
    masks[6, 0] = 1
    masks[7, PATCH - 1] = 1
    return masks


def basis_matrix():
    rows = row_masks()
    columns = np.zeros((3, PATCH), np.float32)
    columns[0] = 1
    columns[1, 0] = 1
    columns[2, PATCH - 1] = 1
    basis = np.zeros((LANES, 3, PATCH, PATCH), np.float32)
    for col in range(3):
        for row in range(8):
            for channel in range(3):
                basis[col * 24 + row * 3 + channel, channel] = np.outer(rows[row], columns[col])
    return basis.reshape(LANES, 3 * PATCH * PATCH)


def spread_matrix():
    spread = np.zeros((6, LANES, LANES), np.float32)
    for half in range(2):
        for side in range(2):
            first = 2 * side + 1
            terms = {
                0: [(first - 1, 2, 1), (first, 0, 1), (first + 1, 0, 1), (first + 1, 2, -1)],
                1: [(first, 0, 1), (first + 1, 0, 1)],
                2: [(first, 0, 1), (first, 1, -1), (first + 1, 0, 1), (first + 2, 1, 1)],
            }
            for shift in range(3):
                groups = [half * 3 + shift]
                if (half, shift) == (0, 0):
                    groups.append(7)
                if (half, shift) == (1, 2):
                    groups.append(6)
                for offset in range(3):
                    for channel in range(3):
                        lane = (half * 2 + side) * QUARTER_LANES + (shift * 3 + offset) * 3 + channel
                        for place, col, sign in terms[offset]:
                            for row in groups:
                                spread[place, col * 24 + row * 3 + channel, lane] += sign
    return spread.reshape(6 * LANES, LANES)


NN = (((1,), (0,)), ((), ()))
NT = (((1,), (1,)), ((), ()))
TN = (((0,), (0,)), ((), ()))


def dot(left, right, dims=NN):
    return lax.dot_general(left, right, dims, preferred_element_type=f32)


def one_hot(condition):
    return jnp.where(condition, 1.0, 0.0).astype(bf16)


def iota(dims, axis):
    return lax.broadcasted_iota(jnp.int32, dims, axis)


def fetch_halves(refs, column, held, arrived):
    copies = [
        pltpu.make_async_copy(
            ref.at[:, pl.ds(column * FEATS, FEATS)], held.at[place], arrived.at[place]
        )
        for place, ref in enumerate(refs)
    ]
    for copy in copies:
        copy.start()
    return copies


def window_kernel(
    cot_ref, pre_ref, gain_ref, patch_ref, basis_ref, spread_ref, order_ref, out_ref, sums
):
    pre = pre_ref[...].astype(f32)
    centered = pre - jnp.mean(pre, axis=-1, keepdims=True)
    inverse = lax.rsqrt(jnp.mean(centered * centered, axis=-1, keepdims=True) + epsilon)
    normed = centered * inverse
    scaled = cot_ref[...].astype(f32) * gain_ref[...].astype(f32).reshape(1, -1)
    grad_rows = inverse * (
        scaled
        - jnp.mean(scaled, axis=-1, keepdims=True)
        - normed * jnp.mean(scaled * normed, axis=-1, keepdims=True)
    )
    grad_rows = grad_rows.astype(bf16)
    channel = iota((LANES, 1), 0) % 3
    scale = jnp.where(
        channel == 0, 1.0 / pixel_std[0], jnp.where(channel == 1, 1.0 / pixel_std[1], 1.0 / pixel_std[2])
    ) * (1.0 / QUARTER_CELLS)
    weights = dot(basis_ref[...], patch_ref[...]) * scale
    high = weights.astype(bf16)
    low = (weights - high.astype(f32)).astype(bf16)
    both = dot(grad_rows, jnp.concatenate([high, low], axis=0), NT)
    patch_sums = both[:, :LANES] + both[:, LANES:]
    group = (iota((SIDE * SIDE, LANES), 1) // 3) % 8
    edge = jnp.zeros((SIDE, LANES), f32)
    above = jnp.concatenate([edge, patch_sums[:-SIDE]], axis=0)
    below = jnp.concatenate([patch_sums[SIDE:], edge], axis=0)
    patch_sums = jnp.where(group == 7, above, jnp.where(group == 6, below, patch_sums))
    sums[pl.ds(0, 8), :] = jnp.zeros((8, LANES), f32)
    sums[pl.ds(8 + SIDE * SIDE, 8), :] = jnp.zeros((8, LANES), f32)
    sums[pl.ds(8, SIDE * SIDE), :] = patch_sums
    column = iota((SIDE * GRID, LANES), 0) % GRID
    total = jnp.zeros((SIDE * GRID, LANES), f32)
    for place in range(6):
        picked = sums[pl.ds(7 + place, SIDE * GRID, stride=GRID), :]
        if place == 0:
            picked = jnp.where(column == 0, 0.0, picked)
        if place == 5:
            picked = jnp.where(column == GRID - 1, 0.0, picked)
        high = picked.astype(bf16)
        low = (picked - high.astype(f32)).astype(bf16)
        both = dot(
            jnp.concatenate([high, low], axis=0), spread_ref[pl.ds(place * LANES, LANES), :]
        )
        total = total + (both[: SIDE * GRID] + both[SIDE * GRID :])
    windows = total.astype(bf16)
    entries = jnp.where(
        iota((16, 64), 1) % 16 == iota((16, 64), 0), order_ref[...].astype(f32), 0.0
    ).astype(bf16)
    order = dot(entries, one_hot(iota((64, LANES), 1) == ORDER_LANE + iota((64, LANES), 0) // 16))
    order = order.astype(bf16)
    for target_x in range(GRID):
        block = windows[target_x * 16 : (target_x + 1) * 16] + order
        for target_t in range(GRID):
            for target_y in range(GRID):
                out_ref[(target_t * GRID + target_x) * GRID + target_y] = block


def weights_kernel(join_ref, out_w_ref, joint_ref, picked_ref):
    here_y = lax.axis_index("hy")
    joint_ref[...] = dot(join_ref[...], out_w_ref[...], NT).astype(bf16)
    row, column = iota((96, 384), 0), iota((96, 384), 1)
    half = row // 48
    pick = one_hot(column == half * 192 + here_y * 48 + (row - half * 48))
    for pair in range(8):
        rows = dot(pick, join_ref[:, pl.ds(pair * 384, 384)], NT).astype(bf16)
        z, core, x = pair // 4, (pair % 4) // 2, (pair % 2) * 2
        for step in range(2):
            picked_ref[pl.ds((core * GRID + x + step) * 96 + z * 48, 48), :] = rows[
                step * 48 : (step + 1) * 48
            ]


def token_kernel(owner_ref, recv_ref, conv_ref, joint_ref, picked_ref, *refs):
    grad_ref, dots_ref, weight_ref, frames, conv_big, ordered, held, arrived = refs[GRID:]
    copies = fetch_halves(refs[:GRID], 1, held, arrived)
    here_x = lax.axis_index("hx")
    here_y = lax.axis_index("hy")
    frames[0] = jnp.zeros((16, LANES), bf16)
    frames[FRAMES + 1] = jnp.zeros((16, LANES), bf16)

    def fetch(frame, carry):
        frames[frame + 1] = recv_ref[(frame // 16) * 16 + owner_ref[frame]]
        return carry

    lax.fori_loop(0, FRAMES, fetch, 0, unroll=8)
    row, column = iota((3 * QUARTER_LANES, 3 * TAPS), 0), iota((3 * QUARTER_LANES, 3 * TAPS), 1)
    tap = row % QUARTER_LANES
    conv = dot(
        one_hot((tap < TAPS) & (column == (row // QUARTER_LANES) * TAPS + tap)), conv_ref[...]
    ).astype(bf16)
    conv_big[...] = jnp.zeros_like(conv_big)
    for quarter in range(QUARTERS):
        for shift in range(3):
            conv_big[
                pl.ds(shift * LANES + quarter * QUARTER_LANES, QUARTER_LANES),
                pl.ds(quarter * LANES, LANES),
            ] = conv[shift * QUARTER_LANES : (shift + 1) * QUARTER_LANES]
    lane = iota((16, ROWS_HERE), 1)
    for slab_t in range(GRID):
        pooled = sum(
            dot(
                frames[pl.ds(slab_t * 16 + shift, 16)].reshape(ROWS_HERE, LANES),
                conv_big[pl.ds(shift * LANES, LANES), :],
            )
            for shift in range(3)
        ).astype(bf16)
        pieces = []
        for piece in range(GRID):
            slab = lax.rem(here_y + piece, GRID)
            block = recv_ref[slab_t * 16 + here_x * GRID + slab].astype(f32)
            for part in range(4):
                order = block[:, ORDER_LANE + part : ORDER_LANE + part + 1].astype(jnp.int32)
                target = (order // 4) * 16 + slab * 4 + lax.rem(order, 4)
                pieces.append(one_hot(lane == target))
        chosen = dot(jnp.concatenate(pieces, axis=0), pooled).astype(bf16)
        for piece in range(GRID):
            ordered[pl.ds(piece * ROWS_HERE + slab_t * 64, 64), :] = chosen[
                piece * 64 : (piece + 1) * 64
            ]
    ones = jnp.ones((8, HDIM), f32)
    outer = jnp.zeros((QUARTERS * LANES, FEATS), f32)
    for piece in range(GRID):
        rows = ordered[pl.ds(piece * ROWS_HERE, ROWS_HERE), :]
        copies[piece].wait()
        outs = held[piece]
        grads = dot(rows, joint_ref[...]).astype(bf16)
        grad_ref[piece] = grads
        products = grads.astype(f32) * outs.astype(f32)
        for head in range(HEADS_HERE):
            dots_ref[head, :, pl.ds(piece * ROWS_HERE, ROWS_HERE)] = lax.dot_general(
                ones,
                products[:, head * HDIM : (head + 1) * HDIM],
                NT,
                preferred_element_type=f32,
                precision=HIGHEST,
            )
        outer = outer + dot(rows, outs, TN)
    weight_ref[...] = (
        dot(picked_ref[...], outer.astype(bf16)) * (1.0 / math.sqrt(FRAMES * 64 * 4))
    ).astype(bf16)


def totals_kernel(*refs):
    out_ref, query_held, key_held, query_arrived, key_arrived = refs[2 * GRID :]
    key_copies = fetch_halves(refs[GRID : 2 * GRID], 0, key_held, key_arrived)
    query_copies = fetch_halves(refs[:GRID], 0, query_held, query_arrived)
    for copy in key_copies + query_copies:
        copy.wait()
    for head in range(HEADS_HERE):
        columns = pl.ds(head * HDIM, HDIM)
        for piece in range(GRID):
            query = query_held[piece, :, columns]
            scores = [dot(key_held[other, :, columns], query, NT) for other in range(GRID)]
            top = functools.reduce(
                jnp.maximum, [jnp.max(tile, axis=0, keepdims=True) for tile in scores]
            ) * (SCORE_SCALE * LOG2E)
            total = sum(
                jnp.sum(jnp.exp2(tile * (SCORE_SCALE * LOG2E) - top), axis=0, keepdims=True)
                for tile in scores
            )
            out_ref[pl.ds(head, 1), pl.ds(piece * ROWS_HERE, ROWS_HERE)] = top + jnp.log2(total)
    out_ref[pl.ds(HEADS_HERE, 8 - HEADS_HERE), :] = jnp.zeros((8 - HEADS_HERE, BLOCK), f32)


def grads_kernel(*refs):
    pair_refs, total_refs = refs[GRID : 2 * GRID], refs[2 * GRID : 3 * GRID]
    grad_ref, dots_ref = refs[3 * GRID : 3 * GRID + 2]
    rest = refs[3 * GRID + 2 :]
    query_out, pair_out = rest[:GRID], rest[GRID : 2 * GRID]
    sums, query_held, key_held, value_held, query_arrived, key_arrived, value_arrived = rest[
        2 * GRID :
    ]
    query_copies = fetch_halves(refs[:GRID], 0, query_held, query_arrived)
    key_copies = fetch_halves(pair_refs, 0, key_held, key_arrived)
    value_copies = fetch_halves(pair_refs, 1, value_held, value_arrived)
    for copy in query_copies:
        copy.wait()
    root = math.sqrt(FRAMES * 64)
    for head in range(HEADS_HERE):
        columns = pl.ds(head * HDIM, HDIM)
        totals = []
        for piece in range(GRID):
            parts = [
                total_refs[step][
                    pl.ds(head, 1), pl.ds(((piece - step) % GRID) * ROWS_HERE, ROWS_HERE)
                ]
                for step in range(GRID)
            ]
            top = functools.reduce(jnp.maximum, parts)
            totals.append(top + jnp.log2(sum(jnp.exp2(part - top) for part in parts)))
        totals = jnp.concatenate(totals, axis=1)
        dots = dots_ref[head, 0:1, :]
        query = query_held[:, :, columns].reshape(BLOCK, HDIM)
        grad = grad_ref[:, :, columns].reshape(BLOCK, HDIM)
        for other in range(GRID):
            if head == 0:
                key_copies[other].wait()
                value_copies[other].wait()
            key = key_held[other, :, columns]
            value = value_held[other, :, columns]
            weights = jnp.exp2(dot(key, query, NT) * (SCORE_SCALE * LOG2E) - totals)
            dscore = (weights * (dot(value, grad, NT) - dots)).astype(bf16)
            pair_out[other][1, :, columns] = (dot(weights.astype(bf16), grad) * root).astype(bf16)
            pair_out[other][0, :, columns] = (
                dot(dscore, query) * (root * SCORE_SCALE)
            ).astype(bf16)
            part = dot(key.T, dscore)
            if other == 0:
                sums[...] = part
            else:
                sums[...] += part
        for piece in range(GRID):
            query_out[piece][:, columns] = (
                sums[:, pl.ds(piece * ROWS_HERE, ROWS_HERE)].T * (root * SCORE_SCALE)
            ).astype(bf16)


def call(kernel, out_shape, in_specs, scratch=(), limit=16, flops=0, moved=0):
    return pl.pallas_call(
        kernel,
        out_shape=out_shape,
        in_specs=in_specs,
        out_specs=jax.tree.map(lambda _: VMEM, out_shape),
        scratch_shapes=list(scratch),
        compiler_params=pltpu.CompilerParams(vmem_limit_bytes=limit * MIB),
        cost_estimate=pl.CostEstimate(flops=flops, bytes_accessed=moved, transcendentals=0),
    )


VMEM = pl.BlockSpec(memory_space=pltpu.VMEM)
SMEM = pl.BlockSpec(memory_space=pltpu.SMEM)
ANY = pl.BlockSpec(memory_space=pl.ANY)
HELD = [pltpu.VMEM((GRID, ROWS_HERE, FEATS), bf16)]
ARRIVED = [pltpu.SemaphoreType.DMA((GRID,))]


def shape(dims, dtype):
    return jax.ShapeDtypeStruct(dims, dtype)


def from_ahead(block, axis, step):
    return lax.ppermute(block, axis, [(i, (i - step) % GRID) for i in range(GRID)])


def to_ahead(block, axis, step):
    return lax.ppermute(block, axis, [(i, (i + step) % GRID) for i in range(GRID)])


def gather(block, axis):
    return [block] + [from_ahead(block, axis, step) for step in range(1, GRID)]


def per_device(
    vit_cot,
    vit_pre,
    ln_gain,
    patch_w,
    frame_owner,
    conv_w,
    join_w,
    token_order,
    queries,
    keys,
    values,
    attn_out,
    out_w,
):
    key_values = gather(jnp.concatenate([keys[0], values[0]], axis=1), "hx")
    query_outs = gather(jnp.concatenate([queries[0], attn_out[0]], axis=1), "hy")
    windows = call(
        window_kernel,
        shape((FRAMES, 16, LANES), bf16),
        [VMEM] * 7,
        scratch=[pltpu.VMEM((SIDE * SIDE + 16, LANES), f32)],
        flops=400 * 10**6,
        moved=3 * 10**6,
    )(
        vit_cot[0, 0],
        vit_pre[0, 0],
        ln_gain,
        patch_w,
        jnp.asarray(basis_matrix(), bf16),
        jnp.asarray(spread_matrix(), bf16),
        token_order,
    )
    received = lax.all_to_all(
        windows, ("tm", "hx", "hy"), split_axis=0, concat_axis=0, tiled=True
    )
    joint, picked = call(
        weights_kernel,
        (shape((QUARTERS * LANES, FEATS), bf16), shape((768, QUARTERS * LANES), bf16)),
        [VMEM] * 2,
        flops=2 * 10**9,
        moved=6 * 10**6,
    )(join_w, out_w)
    totals = call(
        totals_kernel,
        shape((8, BLOCK), f32),
        [ANY] * (2 * GRID),
        scratch=HELD * 2 + ARRIVED * 2,
        flops=8 * 10**8,
        moved=2 * 10**6,
    )(*query_outs, *key_values)
    total_pieces = gather(totals, "hy")
    grad_out, row_dots, weight_part = call(
        token_kernel,
        (
            shape((GRID, ROWS_HERE, FEATS), bf16),
            shape((HEADS_HERE, 8, BLOCK), f32),
            shape((768, FEATS), bf16),
        ),
        [SMEM] + [VMEM] * 4 + [ANY] * GRID,
        scratch=[
            pltpu.VMEM((FRAMES + 2, 16, LANES), bf16),
            pltpu.VMEM((3 * LANES, QUARTERS * LANES), bf16),
            pltpu.VMEM((BLOCK, QUARTERS * LANES), bf16),
        ]
        + HELD
        + ARRIVED,
        flops=2 * 10**9,
        moved=3 * 10**6,
    )(frame_owner, received, conv_w, joint, picked, *query_outs)
    weight_parts = lax.all_to_all(
        weight_part.reshape(8, 2, 48, FEATS),
        ("core", "hx"),
        split_axis=0,
        concat_axis=0,
        tiled=True,
    )
    weight_half = jnp.sum(weight_parts.astype(f32), axis=0)
    here_z = lax.axis_index("zh")
    weight_other = lax.ppermute(
        lax.dynamic_index_in_dim(weight_half, 1 - here_z, 0, keepdims=False),
        "zh",
        [(0, 1), (1, 0)],
    )
    weight_grad = lax.dynamic_index_in_dim(weight_half, here_z, 0, keepdims=False) + weight_other

    outs = call(
        grads_kernel,
        tuple([shape((ROWS_HERE, FEATS), bf16)] * GRID)
        + tuple([shape((2, ROWS_HERE, FEATS), bf16)] * GRID),
        [ANY] * (2 * GRID) + [VMEM] * (GRID + 2),
        scratch=[pltpu.VMEM((HDIM, BLOCK), f32)] + HELD * 3 + ARRIVED * 3,
        limit=24,
        flops=8 * 10**9,
        moved=6 * 10**6,
    )(*query_outs, *key_values, *total_pieces, grad_out, row_dots)
    query_parts, pair_parts = outs[:GRID], outs[GRID:]
    pair_back = [pair_parts[0]] + [
        to_ahead(pair_parts[step], "hx", step) for step in range(1, GRID)
    ]
    query_back = [query_parts[0]] + [
        to_ahead(query_parts[step], "hy", step) for step in range(1, GRID)
    ]

    def total(parts):
        return sum(part.astype(f32) for part in parts).astype(bf16)

    query_grad = total(query_back)
    key_grad = total([part[0] for part in pair_back])
    value_grad = total([part[1] for part in pair_back])
    return (query_grad[None], key_grad[None], value_grad[None], weight_grad)


def solution(mesh):
    fine = Mesh(
        mesh.devices.reshape(2, 2, GRID, GRID, GRID), ("zh", "core", "tm", "hx", "hy")
    )
    dp, height = ("zh", "core"), ("hx", "hy")
    rows = P(dp, height, "tm")
    slots = P(dp, ("tm",) + height, None, None)
    placed = (
        slots,
        slots,
        P(),
        P(),
        P(),
        P(),
        P(),
        P(height, "tm"),
        rows,
        rows,
        rows,
        rows,
        P("tm", None),
    )
    return jax.shard_map(
        per_device,
        mesh=fine,
        in_specs=placed,
        out_specs=(rows, rows, rows, P(dp + height, "tm")),
        check_vma=False,
    )
```

time: 123 us -> 124 us (level)
  the two profiles are of different devices: /device:TPU:2 before, /device:TPU:24 now
where the time goes in v2:
time: 124 us; the launch traced here: 122 us
  starting transfers between devices  45.7 us (37%)
  Pallas kernels  25.6 us (21%)
  local copies, waits for them, and re-layouts  24.6 us (20%)
  waiting for transfers between devices  19.4 us (16%)
  other arithmetic  5.58 us (4%)
    unnamed x66, local copies, waits for them, and re-layouts  24.6 us
    ppermute x9, starting transfers between devices, from_ahead(): lax.ppermute(block, axis, [(i, (i - step) % GRID) for i in range(GRID)])  12.8 us
    ppermute x9, waiting for transfers between devices, from_ahead(): lax.ppermute(block, axis, [(i, (i - step) % GRID) for i in range(GRID)])  12.7 us
    ppermute x6, starting transfers between devices, to_ahead(): lax.ppermute(block, axis, [(i, (i + step) % GRID) for i in range(GRID)])  12.6 us
    all_to_all x1, starting transfers between devices, per_device(): lax.all_to_all(windows, ('tm', 'hx', 'hy'), split_axis=0, concat_axis=0,...  11.6 us
    pallas_call x1, Pallas kernels, per_device(): call(grads_kernel, tuple([shape((ROWS_HERE, FEATS), bf16)] * GRID) + tupl...  9.49 us
    pallas_call x1, Pallas kernels, per_device(): call(token_kernel, (shape((GRID, ROWS_HERE, FEATS), bf16), shape((HEADS_H...  7.85 us
    ppermute x6, waiting for transfers between devices, to_ahead(): lax.ppermute(block, axis, [(i, (i + step) % GRID) for i in range(GRID)])  6.76 us
  transfers between devices with their start and end apart: 18, of which 4 were waited for; matrix products, arithmetic and copies ran while one was open for 3% of the time, Pallas kernels for 21%

profile of v2, /device:TPU:24, one launch (start us, length us, event | category | flops | bytes accessed | tf_op | source)
XLA Modules:
  0.0 121.8 jit_solution(15655558383660952966)
XLA Ops:
  0.7 1.1 pad_maximum_fusion.refs_0_
  2.6 2.7 %collective-permute-start.1 = (bf16[256,768]{1,0:T(8,128)(2,1)S(1)}, bf16[256,768]{1,0:T(8,128)(2,1)S(1)}, u32[]{:S(2)}, u32[]{:S(2)}) collective-permute-start(bf16[256,768]{1,0:T(8,128)(2,1)S(1)} %pad_maximum_fusion.refs_0_), channel_id=1, source_target_pairs={{0,2},{1,3},{2,0},{3,1},{4,6},{5,7},{6,4},{7,5},{8,10},{9,11},{10,... | collective-permute-start | bytes 1179656 | tf_op jit(solution)/shard_map/ppermute | solution.py:362
  5.7 1.4 %copy-done = bf16[588,1280]{1,0:T(8,128)(2,1)S(1)} copy-done((bf16[588,1280]{1,0:T(8,128)(2,1)S(1)}, bf16[588,1280]{1,0:T(8,128)(2,1)}, u32[]{:S(2)}) %copy-start) | copy-done | bytes 1505304
  7.1 1.1 copy-done.1
  8.2 1.1 copy-done.2
  12.5 2.2 %shard_map.175 = bf16[64,16,128]{2,1,0:T(8,128)(2,1)} custom-call(bf16[256,1280]{1,0:T(8,128)(2,1)S(1)} %bitcast.13, bf16[256,1280]{1,0:T(8,128)(2,1)S(1)} %bitcast.14, bf16[1280]{0:T(1024)(128)(2,1)S(1)} %copy-done.8, bf16[588,1280]{1,0:T(8,128)(2,1)S(1)} %copy-done, bf16[128,588]{1,0:T(8,128)(2,1)S(1)} %copy-done.5, bf16[768,128]{1,0:T(8,128)(2,1)S(1)} %copy-done.3, ...), custom_call_target="tpu_custom_call" | custom-call | flops 400000000 | bytes 3000000 | tf_op jit(solution)/shard_map/pallas_call | solution.py:390
  14.7 11.6 %all-to-all-start = ((bf16[64,16,128]{2,1,0:T(8,128)(2,1)}), bf16[64,16,128]{2,1,0:T(8,128)(2,1)S(1)}, u32[]{:S(2)}, u32[]{:S(2)}) async-start(bf16[64,16,128]{2,1,0:T(8,128)(2,1)} %shard_map.175), calls=%async_computation | async-start | bytes 524288 | tf_op jit(solution)/shard_map/all_to_all | solution.py:406
  26.4 2.8 %collective-permute-start.3 = (bf16[256,768]{1,0:T(8,128)(2,1)S(1)}, bf16[256,768]{1,0:T(8,128)(2,1)S(1)}, u32[]{:S(2)}, u32[]{:S(2)}) collective-permute-start(bf16[256,768]{1,0:T(8,128)(2,1)S(1)} %pad_maximum_fusion.1.refs_4_), channel_id=1, source_target_pairs={{0,12},{4,0},{8,4},{12,8},{1,13},{5,1},{9,5},{13,9},{2,14},{6,2},{... | collective-permute-start | bytes 1179656 | tf_op jit(solution)/shard_map/ppermute | solution.py:362
  30.8 1.9 %copy-done.10 = bf16[512,3072]{1,0:T(8,128)(2,1)S(1)} copy-done((bf16[512,3072]{1,0:T(8,128)(2,1)S(1)}, bf16[512,3072]{1,0:T(8,128)(2,1)}, u32[]{:S(2)}) %copy-start.10) | copy-done | bytes 3145752
  32.7 1.7 %copy-done.11 = bf16[384,3072]{1,0:T(8,128)(2,1)S(1)} copy-done((bf16[384,3072]{1,0:T(8,128)(2,1)S(1)}, bf16[384,3072]{1,0:T(8,128)(2,1)}, u32[]{:S(2)}) %copy-start.11) | copy-done | bytes 2359320
  34.4 2.6 %shard_map.176 = (bf16[512,384]{1,0:T(8,128)(2,1)S(1)}, bf16[768,512]{1,0:T(8,128)(2,1)S(1)}) custom-call(bf16[512,3072]{1,0:T(8,128)(2,1)S(1)} %copy-done.10, bf16[384,3072]{1,0:T(8,128)(2,1)S(1)} %copy-done.11), custom_call_target="tpu_custom_call" | custom-call | flops 2000000000 | bytes 6000000 | tf_op jit(solution)/shard_map/pallas_call | solution.py:409
  37.1 9.4 %collective-permute-done.3.refs_5_ = bf16[256,768]{1,0:T(8,128)(2,1)S(1)} collective-permute-done((bf16[256,768]{1,0:T(8,128)(2,1)S(1)}, bf16[256,768]{1,0:T(8,128)(2,1)S(1)}, u32[]{:S(2)}, u32[]{:S(2)}) %collective-permute-start.3) | collective-permute-done | bytes 393248 | tf_op jit(solution)/shard_map/ppermute | solution.py:362
  46.5 3.2 %collective-permute-done.5.refs_7_ = bf16[256,768]{1,0:T(8,128)(2,1)S(1)} collective-permute-done((bf16[256,768]{1,0:T(8,128)(2,1)S(1)}, bf16[256,768]{1,0:T(8,128)(2,1)S(1)}, u32[]{:S(2)}, u32[]{:S(2)}) %collective-permute-start.5) | collective-permute-done | bytes 393248 | tf_op jit(solution)/shard_map/ppermute | solution.py:362
  49.7 3.4 %shard_map.174.refs_8_ = f32[8,1024]{1,0:T(8,128)S(1)} custom-call(bf16[256,768]{1,0:T(8,128)(2,1)S(1)} %pad_maximum_fusion.refs_0_, bf16[256,768]{1,0:T(8,128)(2,1)S(1)} %collective-permute-done.refs_1_, bf16[256,768]{1,0:T(8,128)(2,1)S(1)} %collective-permute-done.1.refs_2_, bf16[256,768]{1,0:T(8,128)(2,1)S(1)} %collective-permute-done.2.refs_3_, ...), custom_call_target="tpu_custom_call" | custom-call | flops 800000000 | bytes 2000000 | tf_op jit(solution)/shard_map/pallas_call | solution.py:416
  53.2 1.1 collective-permute-start.6
  54.3 1.1 collective-permute-start.7
  55.4 2.1 %collective-permute-start.8 = (f32[8,1024]{1,0:T(8,128)S(1)}, f32[8,1024]{1,0:T(8,128)S(1)}, u32[]{:S(2)}, u32[]{:S(2)}) collective-permute-start(f32[8,1024]{1,0:T(8,128)S(1)} %shard_map.174.refs_8_), channel_id=1, source_target_pairs={{0,1},{1,2},{2,3},{3,0},{4,5},{5,6},{6,7},{7,4},{8,9},{9,10},{10,1... | collective-permute-start | bytes 98312 | tf_op jit(solution)/shard_map/ppermute | solution.py:362
  58.3 1.1 copy-done.24
  59.4 1.0 copy-done.26
  60.4 7.8 %shard_map.177 = (bf16[4,256,384]{2,1,0:T(8,128)(2,1)S(1)}, f32[3,8,1024]{2,1,0:T(8,128)S(1)}, bf16[768,384]{1,0:T(8,128)(2,1)}) custom-call(s32[64]{0:T(128)S(1)} %copy-done.22, bf16[64,16,128]{2,1,0:T(8,128)(2,1)S(1)} %all-to-all-done.recv_ref, bf16[81,128]{1,0:T(8,128)(2,1)S(1)} %copy-done.21, bf16[512,384]{1,0:T(8,128)(2,1)S(1)} %copy-done.26, ...), custom_call_target="tpu_custom_call" | custom-call | flops 2000000000 | bytes 3000000 | tf_op jit(solution)/shard_map/pallas_call | solution.py:425
  69.8 4.2 %all-to-all-start.1 = ((bf16[8,2,48,384]{3,2,1,0:T(8,128)(2,1)}), bf16[8,2,48,384]{3,2,1,0:T(8,128)(2,1)}, u32[]{:S(2)}, u32[]{:S(2)}) async-start(bf16[8,2,48,384]{3,2,1,0:T(8,128)(2,1)} %bitcast.7), calls=%async_computation.1 | async-start | bytes 1179648 | tf_op jit(solution)/shard_map/all_to_all | solution.py:443
  78.9 1.1 copy-done.28
  80.9 9.5 %shard_map.178 = (bf16[256,384]{1,0:T(8,128)(2,1)S(1)}, bf16[256,384]{1,0:T(8,128)(2,1)}, bf16[256,384]{1,0:T(8,128)(2,1)}, bf16[256,384]{1,0:T(8,128)(2,1)}, bf...) custom-call(bf16[256,768]{1,0:T(8,128)(2,1)S(1)} %pad_maximum_fusion, ...), custom_call_target="tpu_custom_call" | custom-call | flops 8000000000 | bytes 6000000 | tf_op jit(solution)/shard_map/pallas_call | solution.py:459
  93.4 2.1 %collective-permute-start.10 = (bf16[256,384]{1,0:T(8,128)(2,1)}, bf16[256,384]{1,0:T(8,128)(2,1)S(1)}, u32[]{:S(2)}, u32[]{:S(2)}) collective-permute-start(bf16[256,384]{1,0:T(8,128)(2,1)} %get-tuple-element.23), channel_id=1, source_target_pairs={{0,2},{1,3},{2,0},{3,1},{4,6},{5,7},{6,4},{7,5},{8,10},{9,11},{10,... | collective-permute-start | bytes 589832 | tf_op jit(solution)/shard_map/ppermute | solution.py:366
  95.5 3.2 %collective-permute-start.9 = (bf16[256,384]{1,0:T(8,128)(2,1)}, bf16[256,384]{1,0:T(8,128)(2,1)S(1)}, u32[]{:S(2)}, u32[]{:S(2)}) collective-permute-start(bf16[256,384]{1,0:T(8,128)(2,1)} %get-tuple-element.22), channel_id=1, source_target_pairs={{0,1},{1,2},{2,3},{3,0},{4,5},{5,6},{6,7},{7,4},{8,9},{9,10},{10,1... | collective-permute-start | bytes 589832 | tf_op jit(solution)/shard_map/ppermute | solution.py:366
  98.7 1.9 %collective-permute-start.12 = (bf16[2,256,384]{2,1,0:T(8,128)(2,1)}, bf16[2,256,384]{2,1,0:T(8,128)(2,1)S(1)}, u32[]{:S(2)}, u32[]{:S(2)}) collective-permute-start(bf16[2,256,384]{2,1,0:T(8,128)(2,1)} %copy-done.14), channel_id=1, source_target_pairs={{0,4},{4,8},{8,12},{12,0},{1,5},{5,9},{9,13},{13,1},{2,6},{6,10},{... | collective-permute-start | bytes 1179656 | tf_op jit(solution)/shard_map/ppermute | solution.py:366
  100.6 2.7 %collective-permute-start.13 = (bf16[2,256,384]{2,1,0:T(8,128)(2,1)}, bf16[2,256,384]{2,1,0:T(8,128)(2,1)S(1)}, u32[]{:S(2)}, u32[]{:S(2)}) collective-permute-start(bf16[2,256,384]{2,1,0:T(8,128)(2,1)} %copy-done.13), channel_id=1, source_target_pairs={{0,8},{4,12},{8,0},{12,4},{1,9},{5,13},{9,1},{13,5},{2,10},{6,14},... | collective-permute-start | bytes 1179656 | tf_op jit(solution)/shard_map/ppermute | solution.py:366
  103.3 2.7 %collective-permute-start.14 = (bf16[2,256,384]{2,1,0:T(8,128)(2,1)}, bf16[2,256,384]{2,1,0:T(8,128)(2,1)S(1)}, u32[]{:S(2)}, u32[]{:S(2)}) collective-permute-start(bf16[2,256,384]{2,1,0:T(8,128)(2,1)} %copy-done.12), channel_id=1, source_target_pairs={{0,12},{4,0},{8,4},{12,8},{1,13},{5,1},{9,5},{13,9},{2,14},{6,2},{... | collective-permute-start | bytes 1179656 | tf_op jit(solution)/shard_map/ppermute | solution.py:366
  106.5 1.7 %fusion = bf16[1,256,384]{2,1,0:T(8,128)(2,1)} fusion(bf16[256,384]{1,0:T(8,128)(2,1)S(1)} %collective-permute-done.11, bf16[256,384]{1,0:T(8,128)(2,1)S(1)} %collective-permute-done.10, bf16[256,384]{1,0:T(8,128)(2,1)S(1)} %collective-permute-done.9, bf16[256,384]{1,0:T(8,128)(2,1)} %copy-done.4), kind=kLoop, calls=%fused_computation.6 | loop fusion | flops 786432 | bytes 983040 | tf_op jit(solution)/shard_map/broadcast_in_dim | solution.py:483
  108.2 1.2 convert_reduce_fusion
  109.4 4.6 %collective-permute-start.15 = (f32[48,384]{1,0:T(8,128)S(1)}, f32[48,384]{1,0:T(8,128)S(1)}, u32[]{:S(2)}, u32[]{:S(2)}) collective-permute-start(f32[48,384]{1,0:T(8,128)S(1)} %dynamic-slice_bitcast_fusion), channel_id=1, source_target_pairs={{0,128},{128,0},{1,129},{129,1},{2,130},{130,2},{3,131},{131,3},{4... | collective-permute-start | bytes 221192 | tf_op jit(solution)/shard_map/ppermute | solution.py:452
  114.0 6.2 %collective-permute-done.13 = bf16[2,256,384]{2,1,0:T(8,128)(2,1)S(1)} collective-permute-done((bf16[2,256,384]{2,1,0:T(8,128)(2,1)}, bf16[2,256,384]{2,1,0:T(8,128)(2,1)S(1)}, u32[]{:S(2)}, u32[]{:S(2)}) %collective-permute-start.13) | collective-permute-done | bytes 393248 | tf_op jit(solution)/shard_map/ppermute | solution.py:366
  (82 shorter events, 19.4 us)
Async XLA Ops:
  0.6 25.7 %copy-start.31 = (bf16[1,256,384]{2,1,0:T(8,128)(2,1)S(1)}, bf16[1,256,384]{2,1,0:T(8,128)(2,1)}, u32[]{:S(2)}) copy-start(bf16[1,256,384]{2,1,0:T(8,128)(2,1)} %param.25) | copy-start | bytes 589828
  0.6 25.7 %copy-start.32 = (bf16[1,256,384]{2,1,0:T(8,128)(2,1)S(1)}, bf16[1,256,384]{2,1,0:T(8,128)(2,1)}, u32[]{:S(2)}) copy-start(bf16[1,256,384]{2,1,0:T(8,128)(2,1)} %param.24) | copy-start | bytes 589828
  1.8 28.2 %collective-permute-start = (bf16[256,768]{1,0:T(8,128)(2,1)S(1)}, bf16[256,768]{1,0:T(8,128)(2,1)S(1)}, u32[]{:S(2)}, u32[]{:S(2)}) collective-permute-start(bf16[256,768]{1,0:T(8,128)(2,1)S(1)} %pad_maximum_fusion.refs_0_), channel_id=1, source_target_pairs={{0,3},{1,0},{2,1},{3,2},{4,7},{5,4},{6,5},{7,6},{8,11},{9,8},{10,9... | collective-permute-start | bytes 1179656 | tf_op jit(solution)/shard_map/ppermute | solution.py:362
  2.6 34.5 %collective-permute-start.1 = (bf16[256,768]{1,0:T(8,128)(2,1)S(1)}, bf16[256,768]{1,0:T(8,128)(2,1)S(1)}, u32[]{:S(2)}, u32[]{:S(2)}) collective-permute-start(bf16[256,768]{1,0:T(8,128)(2,1)S(1)} %pad_maximum_fusion.refs_0_), channel_id=1, source_target_pairs={{0,2},{1,3},{2,0},{3,1},{4,6},{5,7},{6,4},{7,5},{8,10},{9,11},{10,... | collective-permute-start | bytes 1179656 | tf_op jit(solution)/shard_map/ppermute | solution.py:362
  5.3 31.8 %collective-permute-start.2 = (bf16[256,768]{1,0:T(8,128)(2,1)S(1)}, bf16[256,768]{1,0:T(8,128)(2,1)S(1)}, u32[]{:S(2)}, u32[]{:S(2)}) collective-permute-start(bf16[256,768]{1,0:T(8,128)(2,1)S(1)} %pad_maximum_fusion.refs_0_), channel_id=1, source_target_pairs={{0,1},{1,2},{2,3},{3,0},{4,5},{5,6},{6,7},{7,4},{8,9},{9,10},{10,1... | collective-permute-start | bytes 1179656 | tf_op jit(solution)/shard_map/ppermute | solution.py:362
  5.7 1.4 %copy-start = (bf16[588,1280]{1,0:T(8,128)(2,1)S(1)}, bf16[588,1280]{1,0:T(8,128)(2,1)}, u32[]{:S(2)}) copy-start(bf16[588,1280]{1,0:T(8,128)(2,1)} %patch_ref.1) | copy-start | bytes 4515844
  7.1 1.1 copy-start.1
  8.2 1.1 copy-start.2
  14.7 42.8 %all-to-all-start = ((bf16[64,16,128]{2,1,0:T(8,128)(2,1)}), bf16[64,16,128]{2,1,0:T(8,128)(2,1)S(1)}, u32[]{:S(2)}, u32[]{:S(2)}) async-start(bf16[64,16,128]{2,1,0:T(8,128)(2,1)} %shard_map.175), calls=%async_computation | async-start | bytes 524288 | tf_op jit(solution)/shard_map/all_to_all | solution.py:406
  26.4 20.1 %collective-permute-start.3 = (bf16[256,768]{1,0:T(8,128)(2,1)S(1)}, bf16[256,768]{1,0:T(8,128)(2,1)S(1)}, u32[]{:S(2)}, u32[]{:S(2)}) collective-permute-start(bf16[256,768]{1,0:T(8,128)(2,1)S(1)} %pad_maximum_fusion.1.refs_4_), channel_id=1, source_target_pairs={{0,12},{4,0},{8,4},{12,8},{1,13},{5,1},{9,5},{13,9},{2,14},{6,2},{... | collective-permute-start | bytes 1179656 | tf_op jit(solution)/shard_map/ppermute | solution.py:362
  29.1 17.4 %collective-permute-start.4 = (bf16[256,768]{1,0:T(8,128)(2,1)S(1)}, bf16[256,768]{1,0:T(8,128)(2,1)S(1)}, u32[]{:S(2)}, u32[]{:S(2)}) collective-permute-start(bf16[256,768]{1,0:T(8,128)(2,1)S(1)} %pad_maximum_fusion.1.refs_4_), channel_id=1, source_target_pairs={{0,8},{4,12},{8,0},{12,4},{1,9},{5,13},{9,1},{13,5},{2,10},{6,14},... | collective-permute-start | bytes 1179656 | tf_op jit(solution)/shard_map/ppermute | solution.py:362
  30.0 19.7 %collective-permute-start.5 = (bf16[256,768]{1,0:T(8,128)(2,1)S(1)}, bf16[256,768]{1,0:T(8,128)(2,1)S(1)}, u32[]{:S(2)}, u32[]{:S(2)}) collective-permute-start(bf16[256,768]{1,0:T(8,128)(2,1)S(1)} %pad_maximum_fusion.1.refs_4_), channel_id=1, source_target_pairs={{0,4},{4,8},{8,12},{12,0},{1,5},{5,9},{9,13},{13,1},{2,6},{6,10},{... | collective-permute-start | bytes 1179656 | tf_op jit(solution)/shard_map/ppermute | solution.py:362
  30.8 1.9 %copy-start.10 = (bf16[512,3072]{1,0:T(8,128)(2,1)S(1)}, bf16[512,3072]{1,0:T(8,128)(2,1)}, u32[]{:S(2)}) copy-start(bf16[512,3072]{1,0:T(8,128)(2,1)} %join_ref.1) | copy-start | bytes 9437188
  32.7 1.7 %copy-start.11 = (bf16[384,3072]{1,0:T(8,128)(2,1)S(1)}, bf16[384,3072]{1,0:T(8,128)(2,1)}, u32[]{:S(2)}) copy-start(bf16[384,3072]{1,0:T(8,128)(2,1)} %out_w_ref.1) | copy-start | bytes 7077892
  37.0 18.4 %copy-start.23 = (bf16[768,512]{1,0:T(8,128)(2,1)}, bf16[768,512]{1,0:T(8,128)(2,1)S(1)}, u32[]{:S(2)}) copy-start(bf16[768,512]{1,0:T(8,128)(2,1)S(1)} %get-tuple-element.18.picked_ref) | copy-start | bytes 2359300
  37.0 18.4 %copy-start.25 = (bf16[512,384]{1,0:T(8,128)(2,1)}, bf16[512,384]{1,0:T(8,128)(2,1)S(1)}, u32[]{:S(2)}) copy-start(bf16[512,384]{1,0:T(8,128)(2,1)S(1)} %get-tuple-element.17.joint_ref) | copy-start | bytes 1179652
  37.0 20.5 %copy-start.22 = (s32[64]{0:T(128)S(1)}, s32[64]{0:T(128)}, u32[]{:S(2)}) copy-start(s32[64]{0:T(128)} %owner_ref.1) | copy-start | bytes 772
  53.2 15.1 %copy-start.6 = (f32[8,1024]{1,0:T(8,128)}, f32[8,1024]{1,0:T(8,128)S(1)}, u32[]{:S(2)}) copy-start(f32[8,1024]{1,0:T(8,128)S(1)} %shard_map.174.refs_8_) | copy-start | bytes 98308
  53.2 20.8 %collective-permute-start.6 = (f32[8,1024]{1,0:T(8,128)S(1)}, f32[8,1024]{1,0:T(8,128)S(1)}, u32[]{:S(2)}, u32[]{:S(2)}) collective-permute-start(f32[8,1024]{1,0:T(8,128)S(1)} %shard_map.174.refs_8_), channel_id=1, source_target_pairs={{0,3},{1,0},{2,1},{3,2},{4,7},{5,4},{6,5},{7,6},{8,11},{9,8},{10,9... | collective-permute-start | bytes 98312 | tf_op jit(solution)/shard_map/ppermute | solution.py:362
  54.3 20.3 %collective-permute-start.7 = (f32[8,1024]{1,0:T(8,128)S(1)}, f32[8,1024]{1,0:T(8,128)S(1)}, u32[]{:S(2)}, u32[]{:S(2)}) collective-permute-start(f32[8,1024]{1,0:T(8,128)S(1)} %shard_map.174.refs_8_), channel_id=1, source_target_pairs={{0,2},{1,3},{2,0},{3,1},{4,6},{5,7},{6,4},{7,5},{8,10},{9,11},{10,... | collective-permute-start | bytes 98312 | tf_op jit(solution)/shard_map/ppermute | solution.py:362
  55.4 19.8 %collective-permute-start.8 = (f32[8,1024]{1,0:T(8,128)S(1)}, f32[8,1024]{1,0:T(8,128)S(1)}, u32[]{:S(2)}, u32[]{:S(2)}) collective-permute-start(f32[8,1024]{1,0:T(8,128)S(1)} %shard_map.174.refs_8_), channel_id=1, source_target_pairs={{0,1},{1,2},{2,3},{3,0},{4,5},{5,6},{6,7},{7,4},{8,9},{9,10},{10,1... | collective-permute-start | bytes 98312 | tf_op jit(solution)/shard_map/ppermute | solution.py:362
  58.3 1.1 copy-start.24
  59.4 1.0 copy-start.26
  69.8 38.4 %all-to-all-start.1 = ((bf16[8,2,48,384]{3,2,1,0:T(8,128)(2,1)}), bf16[8,2,48,384]{3,2,1,0:T(8,128)(2,1)}, u32[]{:S(2)}, u32[]{:S(2)}) async-start(bf16[8,2,48,384]{3,2,1,0:T(8,128)(2,1)} %bitcast.7), calls=%async_computation.1 | async-start | bytes 1179648 | tf_op jit(solution)/shard_map/all_to_all | solution.py:443
  78.9 1.1 copy-start.28
  93.4 9.9 %collective-permute-start.10 = (bf16[256,384]{1,0:T(8,128)(2,1)}, bf16[256,384]{1,0:T(8,128)(2,1)S(1)}, u32[]{:S(2)}, u32[]{:S(2)}) collective-permute-start(bf16[256,384]{1,0:T(8,128)(2,1)} %get-tuple-element.23), channel_id=1, source_target_pairs={{0,2},{1,3},{2,0},{3,1},{4,6},{5,7},{6,4},{7,5},{8,10},{9,11},{10,... | collective-permute-start | bytes 589832 | tf_op jit(solution)/shard_map/ppermute | solution.py:366
  95.5 11.0 %collective-permute-start.11 = (bf16[256,384]{1,0:T(8,128)(2,1)}, bf16[256,384]{1,0:T(8,128)(2,1)S(1)}, u32[]{:S(2)}, u32[]{:S(2)}) collective-permute-start(bf16[256,384]{1,0:T(8,128)(2,1)} %get-tuple-element.24), channel_id=1, source_target_pairs={{0,3},{1,0},{2,1},{3,2},{4,7},{5,4},{6,5},{7,6},{8,11},{9,8},{10,9... | collective-permute-start | bytes 589832 | tf_op jit(solution)/shard_map/ppermute | solution.py:366
  95.5 11.0 %collective-permute-start.9 = (bf16[256,384]{1,0:T(8,128)(2,1)}, bf16[256,384]{1,0:T(8,128)(2,1)S(1)}, u32[]{:S(2)}, u32[]{:S(2)}) collective-permute-start(bf16[256,384]{1,0:T(8,128)(2,1)} %get-tuple-element.22), channel_id=1, source_target_pairs={{0,1},{1,2},{2,3},{3,0},{4,5},{5,6},{6,7},{7,4},{8,9},{9,10},{10,1... | collective-permute-start | bytes 589832 | tf_op jit(solution)/shard_map/ppermute | solution.py:366
  98.7 15.3 %collective-permute-start.12 = (bf16[2,256,384]{2,1,0:T(8,128)(2,1)}, bf16[2,256,384]{2,1,0:T(8,128)(2,1)S(1)}, u32[]{:S(2)}, u32[]{:S(2)}) collective-permute-start(bf16[2,256,384]{2,1,0:T(8,128)(2,1)} %copy-done.14), channel_id=1, source_target_pairs={{0,4},{4,8},{8,12},{12,0},{1,5},{5,9},{9,13},{13,1},{2,6},{6,10},{... | collective-permute-start | bytes 1179656 | tf_op jit(solution)/shard_map/ppermute | solution.py:366
  100.6 19.6 %collective-permute-start.13 = (bf16[2,256,384]{2,1,0:T(8,128)(2,1)}, bf16[2,256,384]{2,1,0:T(8,128)(2,1)S(1)}, u32[]{:S(2)}, u32[]{:S(2)}) collective-permute-start(bf16[2,256,384]{2,1,0:T(8,128)(2,1)} %copy-done.13), channel_id=1, source_target_pairs={{0,8},{4,12},{8,0},{12,4},{1,9},{5,13},{9,1},{13,5},{2,10},{6,14},... | collective-permute-start | bytes 1179656 | tf_op jit(solution)/shard_map/ppermute | solution.py:366
  103.3 17.0 %collective-permute-start.14 = (bf16[2,256,384]{2,1,0:T(8,128)(2,1)}, bf16[2,256,384]{2,1,0:T(8,128)(2,1)S(1)}, u32[]{:S(2)}, u32[]{:S(2)}) collective-permute-start(bf16[2,256,384]{2,1,0:T(8,128)(2,1)} %copy-done.12), channel_id=1, source_target_pairs={{0,12},{4,0},{8,4},{12,8},{1,13},{5,1},{9,5},{13,9},{2,14},{6,2},{... | collective-permute-start | bytes 1179656 | tf_op jit(solution)/shard_map/ppermute | solution.py:366
  109.4 11.8 %collective-permute-start.15 = (f32[48,384]{1,0:T(8,128)S(1)}, f32[48,384]{1,0:T(8,128)S(1)}, u32[]{:S(2)}, u32[]{:S(2)}) collective-permute-start(f32[48,384]{1,0:T(8,128)S(1)} %dynamic-slice_bitcast_fusion), channel_id=1, source_target_pairs={{0,128},{128,0},{1,129},{129,1},{2,130},{130,2},{3,131},{131,3},{4... | collective-permute-start | bytes 221192 | tf_op jit(solution)/shard_map/ppermute | solution.py:452
  (19 other events, 14.2 us)

commit v3 on v2

--- a/solution.py
+++ b/solution.py
@@ -105,21 +105,34 @@
     return lax.broadcasted_iota(jnp.int32, dims, axis)
 
 
-def fetch_halves(refs, column, held, arrived):
-    copies = [
-        pltpu.make_async_copy(
-            ref.at[:, pl.ds(column * FEATS, FEATS)], held.at[place], arrived.at[place]
-        )
-        for place, ref in enumerate(refs)
-    ]
+def start(copies):
     for copy in copies:
         copy.start()
+
+
+def fetch(refs, held, arrived):
+    copies = [
+        pltpu.make_async_copy(ref, kept, arrived.at[place])
+        for place, (ref, kept) in enumerate(zip(refs, held))
+    ]
+    start(copies)
     return copies
 
 
-def window_kernel(
-    cot_ref, pre_ref, gain_ref, patch_ref, basis_ref, spread_ref, order_ref, out_ref, sums
-):
+def fetch_halves(refs, column, held, arrived):
+    return fetch(
+        [ref.at[:, pl.ds(column * FEATS, FEATS)] for ref in refs],
+        [held.at[place] for place in range(len(refs))],
+        arrived,
+    )
+
+
+def window_kernel(gain_ref, order_ref, *refs):
+    out_ref, cot_ref, pre_ref, patch_ref, basis_ref, spread_ref, sums, arrived = refs[5:]
+    held = (pre_ref, cot_ref, basis_ref, patch_ref, spread_ref)
+    copies = fetch(refs[:5], held, arrived)
+    copies[0].wait()
+    copies[1].wait()
     pre = pre_ref[...].astype(f32)
     centered = pre - jnp.mean(pre, axis=-1, keepdims=True)
     inverse = lax.rsqrt(jnp.mean(centered * centered, axis=-1, keepdims=True) + epsilon)
@@ -135,6 +148,8 @@
     scale = jnp.where(
         channel == 0, 1.0 / pixel_std[0], jnp.where(channel == 1, 1.0 / pixel_std[1], 1.0 / pixel_std[2])
     ) * (1.0 / QUARTER_CELLS)
+    copies[2].wait()
+    copies[3].wait()
     weights = dot(basis_ref[...], patch_ref[...]) * scale
     high = weights.astype(bf16)
     low = (weights - high.astype(f32)).astype(bf16)
@@ -148,6 +163,7 @@
     sums[pl.ds(0, 8), :] = jnp.zeros((8, LANES), f32)
     sums[pl.ds(8 + SIDE * SIDE, 8), :] = jnp.zeros((8, LANES), f32)
     sums[pl.ds(8, SIDE * SIDE), :] = patch_sums
+    copies[4].wait()
     column = iota((SIDE * GRID, LANES), 0) % GRID
     total = jnp.zeros((SIDE * GRID, LANES), f32)
     for place in range(6):
@@ -175,8 +191,11 @@
                 out_ref[(target_t * GRID + target_x) * GRID + target_y] = block
 
 
-def weights_kernel(join_ref, out_w_ref, joint_ref, picked_ref):
+def weights_kernel(join_from, out_w_from, joint_ref, picked_ref, join_ref, out_w_ref, arrived):
     here_y = lax.axis_index("hy")
+    copies = fetch([join_from, out_w_from], [join_ref, out_w_ref], arrived)
+    copies[0].wait()
+    copies[1].wait()
     joint_ref[...] = dot(join_ref[...], out_w_ref[...], NT).astype(bf16)
     row, column = iota((96, 384), 0), iota((96, 384), 1)
     half = row // 48
@@ -190,19 +209,18 @@
             ]
 
 
-def token_kernel(owner_ref, recv_ref, conv_ref, joint_ref, picked_ref, *refs):
-    grad_ref, dots_ref, weight_ref, frames, conv_big, ordered, held, arrived = refs[GRID:]
-    copies = fetch_halves(refs[:GRID], 1, held, arrived)
+def token_kernel(owner_ref, conv_ref, recv_from, joint_from, picked_from, *refs):
+    grad_ref, dots_ref, weight_ref, frames, conv_big, ordered, *rest = refs[GRID:]
+    recv_ref, joint_ref, picked_ref, held, arrived, held_arrived = rest
+    firsts = fetch(
+        [recv_from, joint_from, picked_from], [recv_ref, joint_ref, picked_ref], arrived
+    )
+    copies = fetch_halves(refs[:GRID], 1, held, held_arrived)
     here_x = lax.axis_index("hx")
     here_y = lax.axis_index("hy")
     frames[0] = jnp.zeros((16, LANES), bf16)
     frames[FRAMES + 1] = jnp.zeros((16, LANES), bf16)
 
-    def fetch(frame, carry):
-        frames[frame + 1] = recv_ref[(frame // 16) * 16 + owner_ref[frame]]
-        return carry
-
-    lax.fori_loop(0, FRAMES, fetch, 0, unroll=8)
     row, column = iota((3 * QUARTER_LANES, 3 * TAPS), 0), iota((3 * QUARTER_LANES, 3 * TAPS), 1)
     tap = row % QUARTER_LANES
     conv = dot(
@@ -215,6 +233,13 @@
                 pl.ds(shift * LANES + quarter * QUARTER_LANES, QUARTER_LANES),
                 pl.ds(quarter * LANES, LANES),
             ] = conv[shift * QUARTER_LANES : (shift + 1) * QUARTER_LANES]
+    firsts[0].wait()
+
+    def place_frame(frame, carry):
+        frames[frame + 1] = recv_ref[(frame // 16) * 16 + owner_ref[frame]]
+        return carry
+
+    lax.fori_loop(0, FRAMES, place_frame, 0, unroll=8)
     lane = iota((16, ROWS_HERE), 1)
     for slab_t in range(GRID):
         pooled = sum(
@@ -237,6 +262,7 @@
             ordered[pl.ds(piece * ROWS_HERE + slab_t * 64, 64), :] = chosen[
                 piece * 64 : (piece + 1) * 64
             ]
+    firsts[1].wait()
     ones = jnp.ones((8, HDIM), f32)
     outer = jnp.zeros((QUARTERS * LANES, FEATS), f32)
     for piece in range(GRID):
@@ -255,6 +281,7 @@
                 precision=HIGHEST,
             )
         outer = outer + dot(rows, outs, TN)
+    firsts[2].wait()
     weight_ref[...] = (
         dot(picked_ref[...], outer.astype(bf16)) * (1.0 / math.sqrt(FRAMES * 64 * 4))
     ).astype(bf16)
@@ -264,11 +291,13 @@
     out_ref, query_held, key_held, query_arrived, key_arrived = refs[2 * GRID :]
     key_copies = fetch_halves(refs[GRID : 2 * GRID], 0, key_held, key_arrived)
     query_copies = fetch_halves(refs[:GRID], 0, query_held, query_arrived)
-    for copy in key_copies + query_copies:
+    for copy in key_copies:
         copy.wait()
     for head in range(HEADS_HERE):
         columns = pl.ds(head * HDIM, HDIM)
         for piece in range(GRID):
+            if head == 0:
+                query_copies[piece].wait()
             query = query_held[piece, :, columns]
             scores = [dot(key_held[other, :, columns], query, NT) for other in range(GRID)]
             top = functools.reduce(
@@ -283,67 +312,102 @@
 
 
 def grads_kernel(*refs):
-    pair_refs, total_refs = refs[GRID : 2 * GRID], refs[2 * GRID : 3 * GRID]
-    grad_ref, dots_ref = refs[3 * GRID : 3 * GRID + 2]
+    query_refs, pair_refs, total_refs = (refs[GRID * i : GRID * (i + 1)] for i in range(3))
+    grad_from, dots_ref = refs[3 * GRID : 3 * GRID + 2]
     rest = refs[3 * GRID + 2 :]
     query_out, pair_out = rest[:GRID], rest[GRID : 2 * GRID]
-    sums, query_held, key_held, value_held, query_arrived, key_arrived, value_arrived = rest[
-        2 * GRID :
+    (
+        sums,
+        query_held,
+        key_held,
+        value_held,
+        grad_ref,
+        query_made,
+        pair_made,
+        query_arrived,
+        key_arrived,
+        value_arrived,
+        grad_arrived,
+        query_sent,
+        pair_sent,
+    ) = rest[2 * GRID :]
+    sends_order = (2, 1, 3, 0)
+    query_copies = fetch_halves(query_refs, 0, query_held, query_arrived)
+    (grad_copy,) = fetch([grad_from], [grad_ref], grad_arrived)
+    pair_copies = [
+        (
+            pltpu.make_async_copy(
+                pair_refs[other].at[:, pl.ds(0, FEATS)], key_held.at[other], key_arrived.at[other]
+            ),
+            pltpu.make_async_copy(
+                pair_refs[other].at[:, pl.ds(FEATS, FEATS)],
+                value_held.at[other],
+                value_arrived.at[other],
+            ),
+        )
+        for other in range(GRID)
     ]
-    query_copies = fetch_halves(refs[:GRID], 0, query_held, query_arrived)
-    key_copies = fetch_halves(pair_refs, 0, key_held, key_arrived)
-    value_copies = fetch_halves(pair_refs, 1, value_held, value_arrived)
-    for copy in query_copies:
+    for other in sends_order:
+        start(pair_copies[other])
+    root = math.sqrt(FRAMES * 64)
+    totals = []
+    for piece in range(GRID):
+        parts = [
+            total_refs[step][:, pl.ds(((piece - step) % GRID) * ROWS_HERE, ROWS_HERE)]
+            for step in range(GRID)
+        ]
+        top = functools.reduce(jnp.maximum, parts)
+        totals.append(top + jnp.log2(sum(jnp.exp2(part - top) for part in parts)))
+    totals = jnp.concatenate(totals, axis=1)
+    for copy in query_copies + [grad_copy]:
         copy.wait()
-    root = math.sqrt(FRAMES * 64)
-    for head in range(HEADS_HERE):
-        columns = pl.ds(head * HDIM, HDIM)
-        totals = []
-        for piece in range(GRID):
-            parts = [
-                total_refs[step][
-                    pl.ds(head, 1), pl.ds(((piece - step) % GRID) * ROWS_HERE, ROWS_HERE)
-                ]
-                for step in range(GRID)
-            ]
-            top = functools.reduce(jnp.maximum, parts)
-            totals.append(top + jnp.log2(sum(jnp.exp2(part - top) for part in parts)))
-        totals = jnp.concatenate(totals, axis=1)
-        dots = dots_ref[head, 0:1, :]
-        query = query_held[:, :, columns].reshape(BLOCK, HDIM)
-        grad = grad_ref[:, :, columns].reshape(BLOCK, HDIM)
-        for other in range(GRID):
-            if head == 0:
-                key_copies[other].wait()
-                value_copies[other].wait()
+    sends = []
+    for other in sends_order:
+        for copy in pair_copies[other]:
+            copy.wait()
+        for head in range(HEADS_HERE):
+            columns = pl.ds(head * HDIM, HDIM)
+            query = query_held[:, :, columns].reshape(BLOCK, HDIM)
+            grad = grad_ref[:, :, columns].reshape(BLOCK, HDIM)
             key = key_held[other, :, columns]
             value = value_held[other, :, columns]
-            weights = jnp.exp2(dot(key, query, NT) * (SCORE_SCALE * LOG2E) - totals)
-            dscore = (weights * (dot(value, grad, NT) - dots)).astype(bf16)
-            pair_out[other][1, :, columns] = (dot(weights.astype(bf16), grad) * root).astype(bf16)
-            pair_out[other][0, :, columns] = (
+            weights = jnp.exp2(
+                dot(key, query, NT) * (SCORE_SCALE * LOG2E) - totals[head : head + 1]
+            )
+            dscore = (weights * (dot(value, grad, NT) - dots_ref[head, 0:1, :])).astype(bf16)
+            pair_made[other, 1, :, columns] = (dot(weights.astype(bf16), grad) * root).astype(bf16)
+            pair_made[other, 0, :, columns] = (
                 dot(dscore, query) * (root * SCORE_SCALE)
             ).astype(bf16)
             part = dot(key.T, dscore)
-            if other == 0:
-                sums[...] = part
+            if other == sends_order[0]:
+                sums[head] = part
             else:
-                sums[...] += part
-        for piece in range(GRID):
-            query_out[piece][:, columns] = (
-                sums[:, pl.ds(piece * ROWS_HERE, ROWS_HERE)].T * (root * SCORE_SCALE)
+                sums[head] += part
+        send = pltpu.make_async_copy(pair_made.at[other], pair_out[other], pair_sent.at[other])
+        send.start()
+        sends.append(send)
+    for piece in sends_order:
+        for head in range(HEADS_HERE):
+            query_made[piece, :, pl.ds(head * HDIM, HDIM)] = (
+                sums[head, :, pl.ds(piece * ROWS_HERE, ROWS_HERE)].T * (root * SCORE_SCALE)
             ).astype(bf16)
-
-
-def call(kernel, out_shape, in_specs, scratch=(), limit=16, flops=0, moved=0):
+        send = pltpu.make_async_copy(query_made.at[piece], query_out[piece], query_sent.at[piece])
+        send.start()
+        sends.append(send)
+    for send in sends:
+        send.wait()
+
+
+def call(kernel, out_shape, in_specs, scratch=(), out_spec=None):
     return pl.pallas_call(
         kernel,
         out_shape=out_shape,
         in_specs=in_specs,
-        out_specs=jax.tree.map(lambda _: VMEM, out_shape),
+        out_specs=jax.tree.map(lambda _: out_spec or VMEM, out_shape),
         scratch_shapes=list(scratch),
-        compiler_params=pltpu.CompilerParams(vmem_limit_bytes=limit * MIB),
-        cost_estimate=pl.CostEstimate(flops=flops, bytes_accessed=moved, transcendentals=0),
+        compiler_params=pltpu.CompilerParams(vmem_limit_bytes=56 * MIB),
+        cost_estimate=pl.CostEstimate(flops=10**6, bytes_accessed=10**5, transcendentals=0),
     )
 
 
@@ -390,18 +454,24 @@
     windows = call(
         window_kernel,
         shape((FRAMES, 16, LANES), bf16),
-        [VMEM] * 7,
-        scratch=[pltpu.VMEM((SIDE * SIDE + 16, LANES), f32)],
-        flops=400 * 10**6,
-        moved=3 * 10**6,
+        [VMEM] * 2 + [ANY] * 5,
+        scratch=[
+            pltpu.VMEM(vit_cot.shape[2:], bf16),
+            pltpu.VMEM(vit_pre.shape[2:], bf16),
+            pltpu.VMEM(patch_w.shape, bf16),
+            pltpu.VMEM((LANES, patch_w.shape[0]), bf16),
+            pltpu.VMEM((6 * LANES, LANES), bf16),
+            pltpu.VMEM((SIDE * SIDE + 16, LANES), f32),
+            pltpu.SemaphoreType.DMA((5,)),
+        ],
     )(
+        ln_gain,
+        token_order,
+        vit_pre[0, 0],
         vit_cot[0, 0],
-        vit_pre[0, 0],
-        ln_gain,
+        jnp.asarray(basis_matrix(), bf16),
         patch_w,
-        jnp.asarray(basis_matrix(), bf16),
         jnp.asarray(spread_matrix(), bf16),
-        token_order,
     )
     received = lax.all_to_all(
         windows, ("tm", "hx", "hy"), split_axis=0, concat_axis=0, tiled=True
@@ -409,17 +479,18 @@
     joint, picked = call(
         weights_kernel,
         (shape((QUARTERS * LANES, FEATS), bf16), shape((768, QUARTERS * LANES), bf16)),
-        [VMEM] * 2,
-        flops=2 * 10**9,
-        moved=6 * 10**6,
+        [ANY] * 2,
+        scratch=[
+            pltpu.VMEM(join_w.shape, bf16),
+            pltpu.VMEM(out_w.shape, bf16),
+            pltpu.SemaphoreType.DMA((2,)),
+        ],
     )(join_w, out_w)
     totals = call(
         totals_kernel,
         shape((8, BLOCK), f32),
         [ANY] * (2 * GRID),
         scratch=HELD * 2 + ARRIVED * 2,
-        flops=8 * 10**8,
-        moved=2 * 10**6,
     )(*query_outs, *key_values)
     total_pieces = gather(totals, "hy")
     grad_out, row_dots, weight_part = call(
@@ -429,17 +500,21 @@
             shape((HEADS_HERE, 8, BLOCK), f32),
             shape((768, FEATS), bf16),
         ),
-        [SMEM] + [VMEM] * 4 + [ANY] * GRID,
+        [SMEM, VMEM] + [ANY] * (3 + GRID),
         scratch=[
             pltpu.VMEM((FRAMES + 2, 16, LANES), bf16),
             pltpu.VMEM((3 * LANES, QUARTERS * LANES), bf16),
             pltpu.VMEM((BLOCK, QUARTERS * LANES), bf16),
         ]
+        + [
+            pltpu.VMEM((FRAMES, 16, LANES), bf16),
+            pltpu.VMEM((QUARTERS * LANES, FEATS), bf16),
+            pltpu.VMEM((768, QUARTERS * LANES), bf16),
+        ]
         + HELD
+        + [pltpu.SemaphoreType.DMA((3,))]
         + ARRIVED,
-        flops=2 * 10**9,
-        moved=3 * 10**6,
-    )(frame_owner, received, conv_w, joint, picked, *query_outs)
+    )(frame_owner, conv_w, received, joint, picked, *query_outs)
     weight_parts = lax.all_to_all(
         weight_part.reshape(8, 2, 48, FEATS),
         ("core", "hx"),
@@ -460,11 +535,14 @@
         grads_kernel,
         tuple([shape((ROWS_HERE, FEATS), bf16)] * GRID)
         + tuple([shape((2, ROWS_HERE, FEATS), bf16)] * GRID),
-        [ANY] * (2 * GRID) + [VMEM] * (GRID + 2),
-        scratch=[pltpu.VMEM((HDIM, BLOCK), f32)] + HELD * 3 + ARRIVED * 3,
-        limit=24,
-        flops=8 * 10**9,
-        moved=6 * 10**6,
+        [ANY] * (2 * GRID) + [VMEM] * GRID + [ANY, VMEM],
+        scratch=[pltpu.VMEM((HEADS_HERE, HDIM, BLOCK), f32)]
+        + HELD * 5
+        + [pltpu.VMEM((GRID, 2, ROWS_HERE, FEATS), bf16)]
+        + ARRIVED * 3
+        + [pltpu.SemaphoreType.DMA((1,))]
+        + ARRIVED * 2,
+        out_spec=ANY,
     )(*query_outs, *key_values, *total_pieces, grad_out, row_dots)
     query_parts, pair_parts = outs[:GRID], outs[GRID:]
     pair_back = [pair_parts[0]] + [

time: 124 us -> 111 us (0.90); the launches traced: 122 us -> 110 us
  local copies, waits for them, and re-layouts: 24.6 us -> 3.14 us
  Pallas kernels: 25.6 us -> 38.1 us
  waiting for transfers between devices: 19.4 us -> 15.6 us
    unnamed x66 -> x28, local copies, waits for them, and re-layouts: 24.6 us -> 3.13 us
    pallas_call x1, Pallas kernels: 2.62 us -> 6.17 us  [per_device(): call(weights_kernel, (shape((QUARTERS * LANES, FEATS), bf16), shape((768,...]
    ppermute x9, waiting for transfers between devices: 12.7 us -> 9.57 us  [from_ahead(): lax.ppermute(block, axis, [(i, (i - step) % GRID) for i in range(GRID)])]
    pallas_call x1, Pallas kernels: 9.49 us -> 12.4 us  [per_device(): call(grads_kernel, tuple([shape((ROWS_HERE, FEATS), bf16)] * GRID) + tupl...]
    pallas_call x1, Pallas kernels: 3.45 us -> 5.97 us  [per_device(): call(totals_kernel, shape((8, BLOCK), f32), [ANY] * (2 * GRID), scratch=H...]
    pallas_call x1, Pallas kernels: 2.23 us -> 4.59 us  [per_device(): call(window_kernel, shape((FRAMES, 16, LANES), bf16), [VMEM] * 2 + [ANY]...]
    ppermute x9, starting transfers between devices: 12.8 us -> 14.2 us  [from_ahead(): lax.ppermute(block, axis, [(i, (i - step) % GRID) for i in range(GRID)])]
  transfers between devices with their start and end apart: 18 -> 18, of which waited for: 4 -> 6; matrix products, arithmetic and copies ran while one was open for 3% -> 3% of each run, Pallas kernels for 21% -> 35%
where the time goes in v3:
time: 111 us; the launch traced here: 110 us
  starting transfers between devices  46.8 us (42%)
  Pallas kernels  38.1 us (34%)
  waiting for transfers between devices  15.6 us (14%)
  other arithmetic  5.52 us (5%)
  local copies, waits for them, and re-layouts  3.14 us (3%)
    ppermute x9, starting transfers between devices, from_ahead(): lax.ppermute(block, axis, [(i, (i - step) % GRID) for i in range(GRID)])  14.2 us
    ppermute x6, starting transfers between devices, to_ahead(): lax.ppermute(block, axis, [(i, (i + step) % GRID) for i in range(GRID)])  12.6 us
    pallas_call x1, Pallas kernels, per_device(): call(grads_kernel, tuple([shape((ROWS_HERE, FEATS), bf16)] * GRID) + tupl...  12.4 us
    all_to_all x1, starting transfers between devices, per_device(): lax.all_to_all(windows, ('tm', 'hx', 'hy'), split_axis=0, concat_axis=0,...  11.6 us
    ppermute x9, waiting for transfers between devices, from_ahead(): lax.ppermute(block, axis, [(i, (i - step) % GRID) for i in range(GRID)])  9.57 us
    pallas_call x1, Pallas kernels, per_device(): call(token_kernel, (shape((GRID, ROWS_HERE, FEATS), bf16), shape((HEADS_H...  8.95 us
    pallas_call x1, Pallas kernels, per_device(): call(weights_kernel, (shape((QUARTERS * LANES, FEATS), bf16), shape((768,...  6.17 us
    ppermute x6, waiting for transfers between devices, to_ahead(): lax.ppermute(block, axis, [(i, (i + step) % GRID) for i in range(GRID)])  6.04 us
  transfers between devices with their start and end apart: 18, of which 6 were waited for; matrix products, arithmetic and copies ran while one was open for 3% of the time, Pallas kernels for 35%

profile of v3, /device:TPU:24, one launch (start us, length us, event | category | flops | bytes accessed | tf_op | source)
XLA Modules:
  0.0 110.1 jit_solution(11100920477460133314)
XLA Ops:
  0.7 1.1 %pad_maximum_fusion.refs_0_ = bf16[256,768]{1,0:T(8,128)(2,1)S(1)} fusion(bf16[256,384]{1,0:T(8,128)(2,1)} %bitcast.16, bf16[256,384]{1,0:T(8,128)(2,1)} %bitcast.17), kind=kLoop, calls=%fused_computation.1 | loop fusion | flops 786432 | bytes 786432 | tf_op jit(solution)/shard_map/concatenate | solution.py:453
  1.8 0.8 collective-permute-start
  2.6 4.6 %shard_map.175 = bf16[64,16,128]{2,1,0:T(8,128)(2,1)} custom-call(bf16[1280]{0:T(1024)(128)(2,1)} %gain_ref.1, s32[1,64]{1,0:T(1,128)} %order_ref.1, bf16[256,1280]{1,0:T(8,128)(2,1)} %bitcast.13, bf16[256,1280]{1,0:T(8,128)(2,1)} %bitcast.14, bf16[128,588]{1,0:T(8,128)(2,1)} %constant.24.clone.refs_2_, bf16[588,1280]{1,0:T(8,128)(2,1)} %refs_3_.1, ...), custom_call_target="tpu_custom_call" | custom-call | flops 1000000 | bytes 100000 | tf_op jit(solution)/shard_map/pallas_call | solution.py:454
  7.2 11.6 %all-to-all-start = ((bf16[64,16,128]{2,1,0:T(8,128)(2,1)}), bf16[64,16,128]{2,1,0:T(8,128)(2,1)S(1)}, u32[]{:S(2)}, u32[]{:S(2)}) async-start(bf16[64,16,128]{2,1,0:T(8,128)(2,1)} %shard_map.175), calls=%async_computation | async-start | bytes 524288 | tf_op jit(solution)/shard_map/all_to_all | solution.py:476
  18.8 1.5 %collective-permute-start.1 = (bf16[256,768]{1,0:T(8,128)(2,1)S(1)}, bf16[256,768]{1,0:T(8,128)(2,1)S(1)}, u32[]{:S(2)}, u32[]{:S(2)}) collective-permute-start(bf16[256,768]{1,0:T(8,128)(2,1)S(1)} %pad_maximum_fusion.refs_0_), channel_id=1, source_target_pairs={{0,2},{1,3},{2,0},{3,1},{4,6},{5,7},{6,4},{7,5},{8,10},{9,11},{10,... | collective-permute-start | bytes 1179656 | tf_op jit(solution)/shard_map/ppermute | solution.py:426
  20.3 2.1 %collective-permute-start.2 = (bf16[256,768]{1,0:T(8,128)(2,1)S(1)}, bf16[256,768]{1,0:T(8,128)(2,1)S(1)}, u32[]{:S(2)}, u32[]{:S(2)}) collective-permute-start(bf16[256,768]{1,0:T(8,128)(2,1)S(1)} %pad_maximum_fusion.refs_0_), channel_id=1, source_target_pairs={{0,1},{1,2},{2,3},{3,0},{4,5},{5,6},{6,7},{7,4},{8,9},{9,10},{10,1... | collective-permute-start | bytes 1179656 | tf_op jit(solution)/shard_map/ppermute | solution.py:426
  22.5 2.8 %collective-permute-start.3 = (bf16[256,768]{1,0:T(8,128)(2,1)S(1)}, bf16[256,768]{1,0:T(8,128)(2,1)S(1)}, u32[]{:S(2)}, u32[]{:S(2)}) collective-permute-start(bf16[256,768]{1,0:T(8,128)(2,1)S(1)} %pad_maximum_fusion.1.refs_4_), channel_id=1, source_target_pairs={{0,12},{4,0},{8,4},{12,8},{1,13},{5,1},{9,5},{13,9},{2,14},{6,2},{... | collective-permute-start | bytes 1179656 | tf_op jit(solution)/shard_map/ppermute | solution.py:426
  25.2 0.9 collective-permute-start.4
  26.1 0.9 collective-permute-start.5
  27.0 6.2 %shard_map.176 = (bf16[512,384]{1,0:T(8,128)(2,1)}, bf16[768,512]{1,0:T(8,128)(2,1)}) custom-call(bf16[512,3072]{1,0:T(8,128)(2,1)} %join_from.1, bf16[384,3072]{1,0:T(8,128)(2,1)} %out_w_from.1), custom_call_target="tpu_custom_call" | custom-call | flops 1000000 | bytes 100000 | tf_op jit(solution)/shard_map/pallas_call | solution.py:479
  33.2 6.5 %collective-permute-done.2.refs_3_ = bf16[256,768]{1,0:T(8,128)(2,1)S(1)} collective-permute-done((bf16[256,768]{1,0:T(8,128)(2,1)S(1)}, bf16[256,768]{1,0:T(8,128)(2,1)S(1)}, u32[]{:S(2)}, u32[]{:S(2)}) %collective-permute-start.2) | collective-permute-done | bytes 393248 | tf_op jit(solution)/shard_map/ppermute | solution.py:426
  40.5 9.0 %shard_map.177 = (bf16[4,256,384]{2,1,0:T(8,128)(2,1)}, f32[3,8,1024]{2,1,0:T(8,128)}, bf16[768,384]{1,0:T(8,128)(2,1)}) custom-call(s32[64]{0:T(128)} %owner_ref.1, bf16[81,128]{1,0:T(8,128)(2,1)} %conv_ref.1, bf16[64,16,128]{2,1,0:T(8,128)(2,1)} %copy-done.8, bf16[512,384]{1,0:T(8,128)(2,1)} %get-tuple-element.17.joint_from, ...), custom_call_target="tpu_custom_call" | custom-call | flops 1000000 | bytes 100000 | tf_op jit(solution)/shard_map/pallas_call | solution.py:496
  49.4 3.9 %all-to-all-start.1 = ((bf16[8,2,48,384]{3,2,1,0:T(8,128)(2,1)}), bf16[8,2,48,384]{3,2,1,0:T(8,128)(2,1)S(1)}, u32[]{:S(2)}, u32[]{:S(2)}) async-start(bf16[8,2,48,384]{3,2,1,0:T(8,128)(2,1)} %bitcast.15), calls=%async_computation.1 | async-start | bytes 1179648 | tf_op jit(solution)/shard_map/all_to_all | solution.py:518
  53.4 0.7 copy-done.5
  54.3 0.8 copy-done.7
  55.0 6.0 %shard_map.174.refs_8_ = f32[8,1024]{1,0:T(8,128)} custom-call(bf16[256,768]{1,0:T(8,128)(2,1)} %copy-done, bf16[256,768]{1,0:T(8,128)(2,1)} %copy-done.2, bf16[256,768]{1,0:T(8,128)(2,1)} %copy-done.3, bf16[256,768]{1,0:T(8,128)(2,1)} %copy-done.4, bf16[256,768]{1,0:T(8,128)(2,1)} %copy-done.1, bf16[256,768]{1,0:T(8,128)(2,1)} %copy-done.5, ...), custom_call_target="tpu_custom_call" | custom-call | flops 1000000 | bytes 100000 | tf_op jit(solution)/shard_map/pallas_call | solution.py:489
  61.0 1.5 %collective-permute-start.6 = (f32[8,1024]{1,0:T(8,128)}, f32[8,1024]{1,0:T(8,128)S(1)}, u32[]{:S(2)}, u32[]{:S(2)}) collective-permute-start(f32[8,1024]{1,0:T(8,128)} %shard_map.174.refs_8_), channel_id=1, source_target_pairs={{0,3},{1,0},{2,1},{3,2},{4,7},{5,4},{6,5},{7,6},{8,11},{9,8},{10,9... | collective-permute-start | bytes 98312 | tf_op jit(solution)/shard_map/ppermute | solution.py:426
  62.5 2.7 %collective-permute-start.7 = (f32[8,1024]{1,0:T(8,128)}, f32[8,1024]{1,0:T(8,128)S(1)}, u32[]{:S(2)}, u32[]{:S(2)}) collective-permute-start(f32[8,1024]{1,0:T(8,128)} %shard_map.174.refs_8_), channel_id=1, source_target_pairs={{0,2},{1,3},{2,0},{3,1},{4,6},{5,7},{6,4},{7,5},{8,10},{9,11},{10,... | collective-permute-start | bytes 98312 | tf_op jit(solution)/shard_map/ppermute | solution.py:426
  65.2 1.0 collective-permute-start.8
  66.4 1.7 %collective-permute-done.7.refs_10_ = f32[8,1024]{1,0:T(8,128)S(1)} collective-permute-done((f32[8,1024]{1,0:T(8,128)}, f32[8,1024]{1,0:T(8,128)S(1)}, u32[]{:S(2)}, u32[]{:S(2)}) %collective-permute-start.7) | collective-permute-done | bytes 32800 | tf_op jit(solution)/shard_map/ppermute | solution.py:426
  68.1 1.2 %collective-permute-done.8.refs_11_ = f32[8,1024]{1,0:T(8,128)S(1)} collective-permute-done((f32[8,1024]{1,0:T(8,128)}, f32[8,1024]{1,0:T(8,128)S(1)}, u32[]{:S(2)}, u32[]{:S(2)}) %collective-permute-start.8) | collective-permute-done | bytes 32800 | tf_op jit(solution)/shard_map/ppermute | solution.py:426
  70.0 12.4 %shard_map.178 = (bf16[256,384]{1,0:T(8,128)(2,1)}, bf16[256,384]{1,0:T(8,128)(2,1)}, bf16[256,384]{1,0:T(8,128)(2,1)}, bf16[256,384]{1,0:T(8,128)(2,1)}, bf16[2...) custom-call(bf16[256,768]{1,0:T(8,128)(2,1)} %copy-done, ...), custom_call_target="tpu_custom_call" | custom-call | flops 1000000 | bytes 100000 | tf_op jit(solution)/shard_map/pallas_call | solution.py:534
  82.4 1.6 %collective-permute-start.10 = (bf16[256,384]{1,0:T(8,128)(2,1)}, bf16[256,384]{1,0:T(8,128)(2,1)S(1)}, u32[]{:S(2)}, u32[]{:S(2)}) collective-permute-start(bf16[256,384]{1,0:T(8,128)(2,1)} %get-tuple-element.23), channel_id=1, source_target_pairs={{0,2},{1,3},{2,0},{3,1},{4,6},{5,7},{6,4},{7,5},{8,10},{9,11},{10,... | collective-permute-start | bytes 589832 | tf_op jit(solution)/shard_map/ppermute | solution.py:430
  84.0 1.6 %collective-permute-start.11 = (bf16[256,384]{1,0:T(8,128)(2,1)}, bf16[256,384]{1,0:T(8,128)(2,1)S(1)}, u32[]{:S(2)}, u32[]{:S(2)}) collective-permute-start(bf16[256,384]{1,0:T(8,128)(2,1)} %get-tuple-element.24), channel_id=1, source_target_pairs={{0,3},{1,0},{2,1},{3,2},{4,7},{5,4},{6,5},{7,6},{8,11},{9,8},{10,9... | collective-permute-start | bytes 589832 | tf_op jit(solution)/shard_map/ppermute | solution.py:430
  85.6 1.6 %collective-permute-start.9 = (bf16[256,384]{1,0:T(8,128)(2,1)}, bf16[256,384]{1,0:T(8,128)(2,1)S(1)}, u32[]{:S(2)}, u32[]{:S(2)}) collective-permute-start(bf16[256,384]{1,0:T(8,128)(2,1)} %get-tuple-element.22), channel_id=1, source_target_pairs={{0,1},{1,2},{2,3},{3,0},{4,5},{5,6},{6,7},{7,4},{8,9},{9,10},{10,1... | collective-permute-start | bytes 589832 | tf_op jit(solution)/shard_map/ppermute | solution.py:430
  87.2 2.0 %collective-permute-start.12 = (bf16[2,256,384]{2,1,0:T(8,128)(2,1)}, bf16[2,256,384]{2,1,0:T(8,128)(2,1)S(1)}, u32[]{:S(2)}, u32[]{:S(2)}) collective-permute-start(bf16[2,256,384]{2,1,0:T(8,128)(2,1)} %get-tuple-element.26), channel_id=1, source_target_pairs={{0,4},{4,8},{8,12},{12,0},{1,5},{5,9},{9,13},{13,1},{2,6},{6,10},{... | collective-permute-start | bytes 1179656 | tf_op jit(solution)/shard_map/ppermute | solution.py:430
  89.3 2.7 %collective-permute-start.13 = (bf16[2,256,384]{2,1,0:T(8,128)(2,1)}, bf16[2,256,384]{2,1,0:T(8,128)(2,1)S(1)}, u32[]{:S(2)}, u32[]{:S(2)}) collective-permute-start(bf16[2,256,384]{2,1,0:T(8,128)(2,1)} %get-tuple-element.27), channel_id=1, source_target_pairs={{0,8},{4,12},{8,0},{12,4},{1,9},{5,13},{9,1},{13,5},{2,10},{6,14},... | collective-permute-start | bytes 1179656 | tf_op jit(solution)/shard_map/ppermute | solution.py:430
  92.0 3.1 %collective-permute-start.14 = (bf16[2,256,384]{2,1,0:T(8,128)(2,1)}, bf16[2,256,384]{2,1,0:T(8,128)(2,1)S(1)}, u32[]{:S(2)}, u32[]{:S(2)}) collective-permute-start(bf16[2,256,384]{2,1,0:T(8,128)(2,1)} %get-tuple-element.28), channel_id=1, source_target_pairs={{0,12},{4,0},{8,4},{12,8},{1,13},{5,1},{9,5},{13,9},{2,14},{6,2},{... | collective-permute-start | bytes 1179656 | tf_op jit(solution)/shard_map/ppermute | solution.py:430
  95.1 1.7 %fusion = bf16[1,256,384]{2,1,0:T(8,128)(2,1)} fusion(bf16[256,384]{1,0:T(8,128)(2,1)S(1)} %collective-permute-done.11, bf16[256,384]{1,0:T(8,128)(2,1)S(1)} %collective-permute-done.10, bf16[256,384]{1,0:T(8,128)(2,1)S(1)} %collective-permute-done.9, bf16[256,384]{1,0:T(8,128)(2,1)} %get-tuple-element.21), kind=kLoop, calls=%fused_computation.6 | loop fusion | flops 786432 | bytes 983040 | tf_op jit(solution)/shard_map/broadcast_in_dim | solution.py:561
  96.9 4.6 %collective-permute-start.15 = (f32[48,384]{1,0:T(8,128)S(1)}, f32[48,384]{1,0:T(8,128)S(1)}, u32[]{:S(2)}, u32[]{:S(2)}) collective-permute-start(f32[48,384]{1,0:T(8,128)S(1)} %dynamic-slice_bitcast_fusion), channel_id=1, source_target_pairs={{0,128},{128,0},{1,129},{129,1},{2,130},{130,2},{3,131},{131,3},{4... | collective-permute-start | bytes 221192 | tf_op jit(solution)/shard_map/ppermute | solution.py:527
  101.5 5.9 %collective-permute-done.13 = bf16[2,256,384]{2,1,0:T(8,128)(2,1)S(1)} collective-permute-done((bf16[2,256,384]{2,1,0:T(8,128)(2,1)}, bf16[2,256,384]{2,1,0:T(8,128)(2,1)S(1)}, u32[]{:S(2)}, u32[]{:S(2)}) %collective-permute-start.13) | collective-permute-done | bytes 393248 | tf_op jit(solution)/shard_map/ppermute | solution.py:430
  107.5 2.0 %add_convert_fusion = (bf16[1,256,384]{2,1,0:T(8,128)(2,1)}, bf16[1,256,384]{2,1,0:T(8,128)(2,1)}) fusion(bf16[2,256,384]{2,1,0:T(8,128)(2,1)S(1)} %collective-permute-done.14, bf16[2,256,384]{2,1,0:T(8,128)(2,1)S(1)} %collective-permute-done.13, bf16[2,256,384]{2,1,0:T(8,128)(2,1)S(1)} %collective-permute-done.12, bf16[2,256,384]{2,1,0:T(8,128)(2,1)} %get-tuple-element.25), kind=kLoop, calls=%fused_computation.3 | loop fusion | flops 1572864 | bytes 1966080 | tf_op jit(solution)/shard_map/convert_element_type | solution.py:556
  (44 shorter events, 2.6 us)
Async XLA Ops:
  0.6 21.8 %copy-start.9 = (bf16[1,256,384]{2,1,0:T(8,128)(2,1)S(1)}, bf16[1,256,384]{2,1,0:T(8,128)(2,1)}, u32[]{:S(2)}) copy-start(bf16[1,256,384]{2,1,0:T(8,128)(2,1)} %param.25) | copy-start | bytes 589828
  0.6 21.8 %copy-start.10 = (bf16[1,256,384]{2,1,0:T(8,128)(2,1)S(1)}, bf16[1,256,384]{2,1,0:T(8,128)(2,1)}, u32[]{:S(2)}) copy-start(bf16[1,256,384]{2,1,0:T(8,128)(2,1)} %param.24) | copy-start | bytes 589828
  1.8 20.7 %copy-start = (bf16[256,768]{1,0:T(8,128)(2,1)}, bf16[256,768]{1,0:T(8,128)(2,1)S(1)}, u32[]{:S(2)}) copy-start(bf16[256,768]{1,0:T(8,128)(2,1)S(1)} %pad_maximum_fusion.refs_0_) | copy-start | bytes 1179652
  1.8 24.3 %collective-permute-start = (bf16[256,768]{1,0:T(8,128)(2,1)S(1)}, bf16[256,768]{1,0:T(8,128)(2,1)S(1)}, u32[]{:S(2)}, u32[]{:S(2)}) collective-permute-start(bf16[256,768]{1,0:T(8,128)(2,1)S(1)} %pad_maximum_fusion.refs_0_), channel_id=1, source_target_pairs={{0,3},{1,0},{2,1},{3,2},{4,7},{5,4},{6,5},{7,6},{8,11},{9,8},{10,9... | collective-permute-start | bytes 1179656 | tf_op jit(solution)/shard_map/ppermute | solution.py:426
  7.2 32.5 %all-to-all-start = ((bf16[64,16,128]{2,1,0:T(8,128)(2,1)}), bf16[64,16,128]{2,1,0:T(8,128)(2,1)S(1)}, u32[]{:S(2)}, u32[]{:S(2)}) async-start(bf16[64,16,128]{2,1,0:T(8,128)(2,1)} %shard_map.175), calls=%async_computation | async-start | bytes 524288 | tf_op jit(solution)/shard_map/all_to_all | solution.py:476
  18.8 14.4 %collective-permute-start.1 = (bf16[256,768]{1,0:T(8,128)(2,1)S(1)}, bf16[256,768]{1,0:T(8,128)(2,1)S(1)}, u32[]{:S(2)}, u32[]{:S(2)}) collective-permute-start(bf16[256,768]{1,0:T(8,128)(2,1)S(1)} %pad_maximum_fusion.refs_0_), channel_id=1, source_target_pairs={{0,2},{1,3},{2,0},{3,1},{4,6},{5,7},{6,4},{7,5},{8,10},{9,11},{10,... | collective-permute-start | bytes 1179656 | tf_op jit(solution)/shard_map/ppermute | solution.py:426
  20.3 19.3 %collective-permute-start.2 = (bf16[256,768]{1,0:T(8,128)(2,1)S(1)}, bf16[256,768]{1,0:T(8,128)(2,1)S(1)}, u32[]{:S(2)}, u32[]{:S(2)}) collective-permute-start(bf16[256,768]{1,0:T(8,128)(2,1)S(1)} %pad_maximum_fusion.refs_0_), channel_id=1, source_target_pairs={{0,1},{1,2},{2,3},{3,0},{4,5},{5,6},{6,7},{7,4},{8,9},{9,10},{10,1... | collective-permute-start | bytes 1179656 | tf_op jit(solution)/shard_map/ppermute | solution.py:426
  22.5 10.7 %copy-start.1 = (bf16[256,768]{1,0:T(8,128)(2,1)}, bf16[256,768]{1,0:T(8,128)(2,1)S(1)}, u32[]{:S(2)}) copy-start(bf16[256,768]{1,0:T(8,128)(2,1)S(1)} %pad_maximum_fusion.1.refs_4_) | copy-start | bytes 1179652
  22.5 30.8 %collective-permute-start.3 = (bf16[256,768]{1,0:T(8,128)(2,1)S(1)}, bf16[256,768]{1,0:T(8,128)(2,1)S(1)}, u32[]{:S(2)}, u32[]{:S(2)}) collective-permute-start(bf16[256,768]{1,0:T(8,128)(2,1)S(1)} %pad_maximum_fusion.1.refs_4_), channel_id=1, source_target_pairs={{0,12},{4,0},{8,4},{12,8},{1,13},{5,1},{9,5},{13,9},{2,14},{6,2},{... | collective-permute-start | bytes 1179656 | tf_op jit(solution)/shard_map/ppermute | solution.py:426
  25.2 28.1 %collective-permute-start.4 = (bf16[256,768]{1,0:T(8,128)(2,1)S(1)}, bf16[256,768]{1,0:T(8,128)(2,1)S(1)}, u32[]{:S(2)}, u32[]{:S(2)}) collective-permute-start(bf16[256,768]{1,0:T(8,128)(2,1)S(1)} %pad_maximum_fusion.1.refs_4_), channel_id=1, source_target_pairs={{0,8},{4,12},{8,0},{12,4},{1,9},{5,13},{9,1},{13,5},{2,10},{6,14},... | collective-permute-start | bytes 1179656 | tf_op jit(solution)/shard_map/ppermute | solution.py:426
  26.1 7.1 %copy-start.2 = (bf16[256,768]{1,0:T(8,128)(2,1)}, bf16[256,768]{1,0:T(8,128)(2,1)S(1)}, u32[]{:S(2)}) copy-start(bf16[256,768]{1,0:T(8,128)(2,1)S(1)} %collective-permute-done.refs_1_) | copy-start | bytes 1179652
  26.1 27.3 %collective-permute-start.5 = (bf16[256,768]{1,0:T(8,128)(2,1)S(1)}, bf16[256,768]{1,0:T(8,128)(2,1)S(1)}, u32[]{:S(2)}, u32[]{:S(2)}) collective-permute-start(bf16[256,768]{1,0:T(8,128)(2,1)S(1)} %pad_maximum_fusion.1.refs_4_), channel_id=1, source_target_pairs={{0,4},{4,8},{8,12},{12,0},{1,5},{5,9},{9,13},{13,1},{2,6},{6,10},{... | collective-permute-start | bytes 1179656 | tf_op jit(solution)/shard_map/ppermute | solution.py:426
  33.2 6.5 %copy-start.3 = (bf16[256,768]{1,0:T(8,128)(2,1)}, bf16[256,768]{1,0:T(8,128)(2,1)S(1)}, u32[]{:S(2)}) copy-start(bf16[256,768]{1,0:T(8,128)(2,1)S(1)} %collective-permute-done.1.refs_2_) | copy-start | bytes 1179652
  39.7 0.7 copy-start.4
  39.7 0.8 copy-start.8
  49.4 47.4 %all-to-all-start.1 = ((bf16[8,2,48,384]{3,2,1,0:T(8,128)(2,1)}), bf16[8,2,48,384]{3,2,1,0:T(8,128)(2,1)S(1)}, u32[]{:S(2)}, u32[]{:S(2)}) async-start(bf16[8,2,48,384]{3,2,1,0:T(8,128)(2,1)} %bitcast.15), calls=%async_computation.1 | async-start | bytes 1179648 | tf_op jit(solution)/shard_map/all_to_all | solution.py:518
  53.3 0.8 copy-start.5
  53.3 0.9 copy-start.6
  54.3 0.8 copy-start.7
  61.0 5.4 %collective-permute-start.6 = (f32[8,1024]{1,0:T(8,128)}, f32[8,1024]{1,0:T(8,128)S(1)}, u32[]{:S(2)}, u32[]{:S(2)}) collective-permute-start(f32[8,1024]{1,0:T(8,128)} %shard_map.174.refs_8_), channel_id=1, source_target_pairs={{0,3},{1,0},{2,1},{3,2},{4,7},{5,4},{6,5},{7,6},{8,11},{9,8},{10,9... | collective-permute-start | bytes 98312 | tf_op jit(solution)/shard_map/ppermute | solution.py:426
  62.5 5.6 %collective-permute-start.7 = (f32[8,1024]{1,0:T(8,128)}, f32[8,1024]{1,0:T(8,128)S(1)}, u32[]{:S(2)}, u32[]{:S(2)}) collective-permute-start(f32[8,1024]{1,0:T(8,128)} %shard_map.174.refs_8_), channel_id=1, source_target_pairs={{0,2},{1,3},{2,0},{3,1},{4,6},{5,7},{6,4},{7,5},{8,10},{9,11},{10,... | collective-permute-start | bytes 98312 | tf_op jit(solution)/shard_map/ppermute | solution.py:426
  65.2 4.1 %collective-permute-start.8 = (f32[8,1024]{1,0:T(8,128)}, f32[8,1024]{1,0:T(8,128)S(1)}, u32[]{:S(2)}, u32[]{:S(2)}) collective-permute-start(f32[8,1024]{1,0:T(8,128)} %shard_map.174.refs_8_), channel_id=1, source_target_pairs={{0,1},{1,2},{2,3},{3,0},{4,5},{5,6},{6,7},{7,4},{8,9},{9,10},{10,1... | collective-permute-start | bytes 98312 | tf_op jit(solution)/shard_map/ppermute | solution.py:426
  66.4 2.9 %copy-start.11 = (f32[8,1024]{1,0:T(8,128)}, f32[8,1024]{1,0:T(8,128)S(1)}, u32[]{:S(2)}) copy-start(f32[8,1024]{1,0:T(8,128)S(1)} %collective-permute-done.6.refs_9_) | copy-start | bytes 98308
  68.1 1.2 %copy-start.12 = (f32[8,1024]{1,0:T(8,128)}, f32[8,1024]{1,0:T(8,128)S(1)}, u32[]{:S(2)}) copy-start(f32[8,1024]{1,0:T(8,128)S(1)} %collective-permute-done.7.refs_10_) | copy-start | bytes 98308
  69.4 0.6 copy-start.13
  82.4 9.6 %collective-permute-start.10 = (bf16[256,384]{1,0:T(8,128)(2,1)}, bf16[256,384]{1,0:T(8,128)(2,1)S(1)}, u32[]{:S(2)}, u32[]{:S(2)}) collective-permute-start(bf16[256,384]{1,0:T(8,128)(2,1)} %get-tuple-element.23), channel_id=1, source_target_pairs={{0,2},{1,3},{2,0},{3,1},{4,6},{5,7},{6,4},{7,5},{8,10},{9,11},{10,... | collective-permute-start | bytes 589832 | tf_op jit(solution)/shard_map/ppermute | solution.py:430
  84.0 11.1 %collective-permute-start.11 = (bf16[256,384]{1,0:T(8,128)(2,1)}, bf16[256,384]{1,0:T(8,128)(2,1)S(1)}, u32[]{:S(2)}, u32[]{:S(2)}) collective-permute-start(bf16[256,384]{1,0:T(8,128)(2,1)} %get-tuple-element.24), channel_id=1, source_target_pairs={{0,3},{1,0},{2,1},{3,2},{4,7},{5,4},{6,5},{7,6},{8,11},{9,8},{10,9... | collective-permute-start | bytes 589832 | tf_op jit(solution)/shard_map/ppermute | solution.py:430
  85.6 9.5 %collective-permute-start.9 = (bf16[256,384]{1,0:T(8,128)(2,1)}, bf16[256,384]{1,0:T(8,128)(2,1)S(1)}, u32[]{:S(2)}, u32[]{:S(2)}) collective-permute-start(bf16[256,384]{1,0:T(8,128)(2,1)} %get-tuple-element.22), channel_id=1, source_target_pairs={{0,1},{1,2},{2,3},{3,0},{4,5},{5,6},{6,7},{7,4},{8,9},{9,10},{10,1... | collective-permute-start | bytes 589832 | tf_op jit(solution)/shard_map/ppermute | solution.py:430
  87.2 14.3 %collective-permute-start.12 = (bf16[2,256,384]{2,1,0:T(8,128)(2,1)}, bf16[2,256,384]{2,1,0:T(8,128)(2,1)S(1)}, u32[]{:S(2)}, u32[]{:S(2)}) collective-permute-start(bf16[2,256,384]{2,1,0:T(8,128)(2,1)} %get-tuple-element.26), channel_id=1, source_target_pairs={{0,4},{4,8},{8,12},{12,0},{1,5},{5,9},{9,13},{13,1},{2,6},{6,10},{... | collective-permute-start | bytes 1179656 | tf_op jit(solution)/shard_map/ppermute | solution.py:430
  89.3 18.2 %collective-permute-start.13 = (bf16[2,256,384]{2,1,0:T(8,128)(2,1)}, bf16[2,256,384]{2,1,0:T(8,128)(2,1)S(1)}, u32[]{:S(2)}, u32[]{:S(2)}) collective-permute-start(bf16[2,256,384]{2,1,0:T(8,128)(2,1)} %get-tuple-element.27), channel_id=1, source_target_pairs={{0,8},{4,12},{8,0},{12,4},{1,9},{5,13},{9,1},{13,5},{2,10},{6,14},... | collective-permute-start | bytes 1179656 | tf_op jit(solution)/shard_map/ppermute | solution.py:430
  92.0 15.4 %collective-permute-start.14 = (bf16[2,256,384]{2,1,0:T(8,128)(2,1)}, bf16[2,256,384]{2,1,0:T(8,128)(2,1)S(1)}, u32[]{:S(2)}, u32[]{:S(2)}) collective-permute-start(bf16[2,256,384]{2,1,0:T(8,128)(2,1)} %get-tuple-element.28), channel_id=1, source_target_pairs={{0,12},{4,0},{8,4},{12,8},{1,13},{5,1},{9,5},{13,9},{2,14},{6,2},{... | collective-permute-start | bytes 1179656 | tf_op jit(solution)/shard_map/ppermute | solution.py:430
  96.9 12.5 %collective-permute-start.15 = (f32[48,384]{1,0:T(8,128)S(1)}, f32[48,384]{1,0:T(8,128)S(1)}, u32[]{:S(2)}, u32[]{:S(2)}) collective-permute-start(f32[48,384]{1,0:T(8,128)S(1)} %dynamic-slice_bitcast_fusion), channel_id=1, source_target_pairs={{0,128},{128,0},{1,129},{129,1},{2,130},{130,2},{3,131},{131,3},{4... | collective-permute-start | bytes 221192 | tf_op jit(solution)/shard_map/ppermute | solution.py:527

commit v4 on v3

--- a/solution.py
+++ b/solution.py
@@ -209,18 +209,35 @@
             ]
 
 
-def token_kernel(owner_ref, conv_ref, recv_from, joint_from, picked_from, *refs):
-    grad_ref, dots_ref, weight_ref, frames, conv_big, ordered, *rest = refs[GRID:]
-    recv_ref, joint_ref, picked_ref, held, arrived, held_arrived = rest
-    firsts = fetch(
-        [recv_from, joint_from, picked_from], [recv_ref, joint_ref, picked_ref], arrived
-    )
-    copies = fetch_halves(refs[:GRID], 1, held, held_arrived)
+def totals_kernel(*refs):
+    out_ref, query_held, key_held, query_arrived, key_arrived = refs[2 * GRID :]
+    key_copies = fetch_halves(refs[GRID : 2 * GRID], 0, key_held, key_arrived)
+    query_copies = fetch_halves(refs[:GRID], 0, query_held, query_arrived)
+    for copy in key_copies:
+        copy.wait()
+    for head in range(HEADS_HERE):
+        columns = pl.ds(head * HDIM, HDIM)
+        for piece in range(GRID):
+            if head == 0:
+                query_copies[piece].wait()
+            query = query_held[piece, :, columns]
+            scores = [dot(key_held[other, :, columns], query, NT) for other in range(GRID)]
+            top = functools.reduce(
+                jnp.maximum, [jnp.max(tile, axis=0, keepdims=True) for tile in scores]
+            ) * (SCORE_SCALE * LOG2E)
+            total = sum(
+                jnp.sum(jnp.exp2(tile * (SCORE_SCALE * LOG2E) - top), axis=0, keepdims=True)
+                for tile in scores
+            )
+            out_ref[pl.ds(head, 1), pl.ds(piece * ROWS_HERE, ROWS_HERE)] = top + jnp.log2(total)
+    out_ref[pl.ds(HEADS_HERE, 8 - HEADS_HERE), :] = jnp.zeros((8 - HEADS_HERE, BLOCK), f32)
+
+
+def token_part(owner_ref, conv_ref, recv_ref, arrivals, frames, conv_big, ordered):
     here_x = lax.axis_index("hx")
     here_y = lax.axis_index("hy")
     frames[0] = jnp.zeros((16, LANES), bf16)
     frames[FRAMES + 1] = jnp.zeros((16, LANES), bf16)
-
     row, column = iota((3 * QUARTER_LANES, 3 * TAPS), 0), iota((3 * QUARTER_LANES, 3 * TAPS), 1)
     tap = row % QUARTER_LANES
     conv = dot(
@@ -233,7 +250,7 @@
                 pl.ds(shift * LANES + quarter * QUARTER_LANES, QUARTER_LANES),
                 pl.ds(quarter * LANES, LANES),
             ] = conv[shift * QUARTER_LANES : (shift + 1) * QUARTER_LANES]
-    firsts[0].wait()
+    arrivals.wait()
 
     def place_frame(frame, carry):
         frames[frame + 1] = recv_ref[(frame // 16) * 16 + owner_ref[frame]]
@@ -262,93 +279,70 @@
             ordered[pl.ds(piece * ROWS_HERE + slab_t * 64, 64), :] = chosen[
                 piece * 64 : (piece + 1) * 64
             ]
-    firsts[1].wait()
-    ones = jnp.ones((8, HDIM), f32)
-    outer = jnp.zeros((QUARTERS * LANES, FEATS), f32)
-    for piece in range(GRID):
-        rows = ordered[pl.ds(piece * ROWS_HERE, ROWS_HERE), :]
-        copies[piece].wait()
-        outs = held[piece]
-        grads = dot(rows, joint_ref[...]).astype(bf16)
-        grad_ref[piece] = grads
-        products = grads.astype(f32) * outs.astype(f32)
-        for head in range(HEADS_HERE):
-            dots_ref[head, :, pl.ds(piece * ROWS_HERE, ROWS_HERE)] = lax.dot_general(
-                ones,
-                products[:, head * HDIM : (head + 1) * HDIM],
-                NT,
-                preferred_element_type=f32,
-                precision=HIGHEST,
-            )
-        outer = outer + dot(rows, outs, TN)
-    firsts[2].wait()
-    weight_ref[...] = (
-        dot(picked_ref[...], outer.astype(bf16)) * (1.0 / math.sqrt(FRAMES * 64 * 4))
-    ).astype(bf16)
-
-
-def totals_kernel(*refs):
-    out_ref, query_held, key_held, query_arrived, key_arrived = refs[2 * GRID :]
-    key_copies = fetch_halves(refs[GRID : 2 * GRID], 0, key_held, key_arrived)
-    query_copies = fetch_halves(refs[:GRID], 0, query_held, query_arrived)
-    for copy in key_copies:
-        copy.wait()
-    for head in range(HEADS_HERE):
-        columns = pl.ds(head * HDIM, HDIM)
-        for piece in range(GRID):
-            if head == 0:
-                query_copies[piece].wait()
-            query = query_held[piece, :, columns]
-            scores = [dot(key_held[other, :, columns], query, NT) for other in range(GRID)]
-            top = functools.reduce(
-                jnp.maximum, [jnp.max(tile, axis=0, keepdims=True) for tile in scores]
-            ) * (SCORE_SCALE * LOG2E)
-            total = sum(
-                jnp.sum(jnp.exp2(tile * (SCORE_SCALE * LOG2E) - top), axis=0, keepdims=True)
-                for tile in scores
-            )
-            out_ref[pl.ds(head, 1), pl.ds(piece * ROWS_HERE, ROWS_HERE)] = top + jnp.log2(total)
-    out_ref[pl.ds(HEADS_HERE, 8 - HEADS_HERE), :] = jnp.zeros((8 - HEADS_HERE, BLOCK), f32)
-
-
-def grads_kernel(*refs):
-    query_refs, pair_refs, total_refs = (refs[GRID * i : GRID * (i + 1)] for i in range(3))
-    grad_from, dots_ref = refs[3 * GRID : 3 * GRID + 2]
-    rest = refs[3 * GRID + 2 :]
-    query_out, pair_out = rest[:GRID], rest[GRID : 2 * GRID]
+
+
+def grads_kernel(owner_ref, conv_ref, *refs):
+    total_refs, (recv_from, joint_from, picked_from) = refs[:GRID], refs[GRID : GRID + 3]
+    query_refs, pair_refs = refs[GRID + 3 : 2 * GRID + 3], refs[2 * GRID + 3 : 3 * GRID + 3]
+    rest = refs[3 * GRID + 3 :]
+    query_out, pair_out, weight_out = rest[:GRID], rest[GRID : 2 * GRID], rest[2 * GRID]
     (
+        frames,
+        conv_big,
+        ordered,
+        recv_ref,
+        joint_ref,
+        picked_ref,
+        weight_made,
+        dots_ref,
         sums,
+        out_held,
         query_held,
         key_held,
         value_held,
         grad_ref,
         query_made,
         pair_made,
+        first_arrived,
+        out_arrived,
         query_arrived,
         key_arrived,
         value_arrived,
-        grad_arrived,
         query_sent,
         pair_sent,
-    ) = rest[2 * GRID :]
+        weight_sent,
+    ) = rest[2 * GRID + 1 :]
     sends_order = (2, 1, 3, 0)
+    firsts = fetch(
+        [recv_from, joint_from, picked_from], [recv_ref, joint_ref, picked_ref], first_arrived
+    )
+    out_copies = fetch_halves(query_refs, 1, out_held, out_arrived)
     query_copies = fetch_halves(query_refs, 0, query_held, query_arrived)
-    (grad_copy,) = fetch([grad_from], [grad_ref], grad_arrived)
-    pair_copies = [
-        (
-            pltpu.make_async_copy(
-                pair_refs[other].at[:, pl.ds(0, FEATS)], key_held.at[other], key_arrived.at[other]
-            ),
-            pltpu.make_async_copy(
-                pair_refs[other].at[:, pl.ds(FEATS, FEATS)],
-                value_held.at[other],
-                value_arrived.at[other],
-            ),
-        )
-        for other in range(GRID)
-    ]
-    for other in sends_order:
-        start(pair_copies[other])
+    key_copies = fetch_halves(pair_refs, 0, key_held, key_arrived)
+    value_copies = fetch_halves(pair_refs, 1, value_held, value_arrived)
+    token_part(owner_ref, conv_ref, recv_ref, firsts[0], frames, conv_big, ordered)
+    firsts[1].wait()
+    ones = jnp.ones((8, 2 * HDIM), bf16)
+    outer = jnp.zeros((QUARTERS * LANES, FEATS), f32)
+    for piece in range(GRID):
+        rows = ordered[pl.ds(piece * ROWS_HERE, ROWS_HERE), :]
+        grads = dot(rows, joint_ref[...]).astype(bf16)
+        grad_ref[piece] = grads
+        out_copies[piece].wait()
+        outs = out_held[piece]
+        products = grads.astype(f32) * outs.astype(f32)
+        high = products.astype(bf16)
+        low = (products - high.astype(f32)).astype(bf16)
+        for head in range(HEADS_HERE):
+            columns = slice(head * HDIM, (head + 1) * HDIM)
+            both = jnp.concatenate([high[:, columns], low[:, columns]], axis=1)
+            dots_ref[head, :, pl.ds(piece * ROWS_HERE, ROWS_HERE)] = dot(ones, both, NT)
+        outer = outer + dot(rows, outs, TN)
+    firsts[2].wait()
+    weight_made[...] = (
+        dot(picked_ref[...], outer.astype(bf16)) * (1.0 / math.sqrt(FRAMES * 64 * 4))
+    ).astype(bf16)
+    sends = fetch([weight_made], [weight_out], weight_sent)
     root = math.sqrt(FRAMES * 64)
     totals = []
     for piece in range(GRID):
@@ -359,12 +353,11 @@
         top = functools.reduce(jnp.maximum, parts)
         totals.append(top + jnp.log2(sum(jnp.exp2(part - top) for part in parts)))
     totals = jnp.concatenate(totals, axis=1)
-    for copy in query_copies + [grad_copy]:
+    for copy in query_copies:
         copy.wait()
-    sends = []
     for other in sends_order:
-        for copy in pair_copies[other]:
-            copy.wait()
+        key_copies[other].wait()
+        value_copies[other].wait()
         for head in range(HEADS_HERE):
             columns = pl.ds(head * HDIM, HDIM)
             query = query_held[:, :, columns].reshape(BLOCK, HDIM)
@@ -473,9 +466,7 @@
         patch_w,
         jnp.asarray(spread_matrix(), bf16),
     )
-    received = lax.all_to_all(
-        windows, ("tm", "hx", "hy"), split_axis=0, concat_axis=0, tiled=True
-    )
+    join_late, windows = lax.optimization_barrier((join_w, windows))
     joint, picked = call(
         weights_kernel,
         (shape((QUARTERS * LANES, FEATS), bf16), shape((768, QUARTERS * LANES), bf16)),
@@ -485,7 +476,13 @@
             pltpu.VMEM(out_w.shape, bf16),
             pltpu.SemaphoreType.DMA((2,)),
         ],
-    )(join_w, out_w)
+    )(join_late, out_w)
+    windows, joint, picked, query_outs, key_values = lax.optimization_barrier(
+        (windows, joint, picked, query_outs, key_values)
+    )
+    received = lax.all_to_all(
+        windows, ("tm", "hx", "hy"), split_axis=0, concat_axis=0, tiled=True
+    )
     totals = call(
         totals_kernel,
         shape((8, BLOCK), f32),
@@ -493,28 +490,30 @@
         scratch=HELD * 2 + ARRIVED * 2,
     )(*query_outs, *key_values)
     total_pieces = gather(totals, "hy")
-    grad_out, row_dots, weight_part = call(
-        token_kernel,
-        (
-            shape((GRID, ROWS_HERE, FEATS), bf16),
-            shape((HEADS_HERE, 8, BLOCK), f32),
-            shape((768, FEATS), bf16),
-        ),
-        [SMEM, VMEM] + [ANY] * (3 + GRID),
+    outs = call(
+        grads_kernel,
+        tuple([shape((ROWS_HERE, FEATS), bf16)] * GRID)
+        + tuple([shape((2, ROWS_HERE, FEATS), bf16)] * GRID)
+        + (shape((768, FEATS), bf16),),
+        [SMEM] + [VMEM] * (1 + GRID) + [ANY] * (3 + 2 * GRID),
         scratch=[
             pltpu.VMEM((FRAMES + 2, 16, LANES), bf16),
             pltpu.VMEM((3 * LANES, QUARTERS * LANES), bf16),
             pltpu.VMEM((BLOCK, QUARTERS * LANES), bf16),
-        ]
-        + [
             pltpu.VMEM((FRAMES, 16, LANES), bf16),
             pltpu.VMEM((QUARTERS * LANES, FEATS), bf16),
             pltpu.VMEM((768, QUARTERS * LANES), bf16),
+            pltpu.VMEM((768, FEATS), bf16),
+            pltpu.VMEM((HEADS_HERE, 8, BLOCK), f32),
+            pltpu.VMEM((HEADS_HERE, HDIM, BLOCK), f32),
         ]
-        + HELD
-        + [pltpu.SemaphoreType.DMA((3,))]
-        + ARRIVED,
-    )(frame_owner, conv_w, received, joint, picked, *query_outs)
+        + HELD * 6
+        + [pltpu.VMEM((GRID, 2, ROWS_HERE, FEATS), bf16), pltpu.SemaphoreType.DMA((3,))]
+        + ARRIVED * 6
+        + [pltpu.SemaphoreType.DMA((1,))],
+        out_spec=ANY,
+    )(frame_owner, conv_w, *total_pieces, received, joint, picked, *query_outs, *key_values)
+    query_parts, pair_parts, weight_part = outs[:GRID], outs[GRID : 2 * GRID], outs[2 * GRID]
     weight_parts = lax.all_to_all(
         weight_part.reshape(8, 2, 48, FEATS),
         ("core", "hx"),
@@ -531,20 +530,6 @@
     )
     weight_grad = lax.dynamic_index_in_dim(weight_half, here_z, 0, keepdims=False) + weight_other
 
-    outs = call(
-        grads_kernel,
-        tuple([shape((ROWS_HERE, FEATS), bf16)] * GRID)
-        + tuple([shape((2, ROWS_HERE, FEATS), bf16)] * GRID),
-        [ANY] * (2 * GRID) + [VMEM] * GRID + [ANY, VMEM],
-        scratch=[pltpu.VMEM((HEADS_HERE, HDIM, BLOCK), f32)]
-        + HELD * 5
-        + [pltpu.VMEM((GRID, 2, ROWS_HERE, FEATS), bf16)]
-        + ARRIVED * 3
-        + [pltpu.SemaphoreType.DMA((1,))]
-        + ARRIVED * 2,
-        out_spec=ANY,
-    )(*query_outs, *key_values, *total_pieces, grad_out, row_dots)
-    query_parts, pair_parts = outs[:GRID], outs[GRID:]
     pair_back = [pair_parts[0]] + [
         to_ahead(pair_parts[step], "hx", step) for step in range(1, GRID)
     ]

time: 111 us -> 115 us (1.036)
  the two profiles are of different devices: /device:TPU:24 before, /device:TPU:1 now
where the time goes in v4:
time: 115 us; the launch traced here: 114 us
  starting transfers between devices  45.5 us (40%)
  Pallas kernels  33.7 us (29%)
  waiting for transfers between devices  27.3 us (24%)
  other arithmetic  5.47 us (5%)
  local copies, waits for them, and re-layouts  1.36 us (1%)
    pallas_call x1, Pallas kernels, per_device(): call(grads_kernel, tuple([shape((ROWS_HERE, FEATS), bf16)] * GRID) + tupl...  16.9 us
    ppermute x9, waiting for transfers between devices, from_ahead(): lax.ppermute(block, axis, [(i, (i - step) % GRID) for i in range(GRID)])  14.9 us
    all_to_all x1, starting transfers between devices, per_device(): lax.all_to_all(windows, ('tm', 'hx', 'hy'), split_axis=0, concat_axis=0,...  13.4 us
    ppermute x6, waiting for transfers between devices, to_ahead(): lax.ppermute(block, axis, [(i, (i + step) % GRID) for i in range(GRID)])  12.4 us
    ppermute x9, starting transfers between devices, from_ahead(): lax.ppermute(block, axis, [(i, (i - step) % GRID) for i in range(GRID)])  11 us
    ppermute x6, starting transfers between devices, to_ahead(): lax.ppermute(block, axis, [(i, (i + step) % GRID) for i in range(GRID)])  8.61 us
    all_to_all x1, starting transfers between devices, per_device(): lax.all_to_all(weight_part.reshape(8, 2, 48, FEATS), ('core', 'hx'), spli...  8.07 us
    pallas_call x1, Pallas kernels, per_device(): call(weights_kernel, (shape((QUARTERS * LANES, FEATS), bf16), shape((768,...  6.16 us
  transfers between devices with their start and end apart: 18, of which 7 were waited for; matrix products, arithmetic and copies ran while one was open for 3% of the time, Pallas kernels for 15%

profile of v4, /device:TPU:1, one launch (start us, length us, event | category | flops | bytes accessed | tf_op | source)
XLA Modules:
  0.0 114.1 jit_solution(2775708209581720474)
XLA Ops:
  0.6 1.1 pad_maximum_fusion.refs_0_.refs_7_
  1.7 3.6 %collective-permute-start = (bf16[256,768]{1,0:T(8,128)(2,1)S(1)}, bf16[256,768]{1,0:T(8,128)(2,1)S(1)}, u32[]{:S(2)}, u32[]{:S(2)}) collective-permute-start(bf16[256,768]{1,0:T(8,128)(2,1)S(1)} %pad_maximum_fusion.refs_0_.refs_7_), channel_id=1, source_target_pairs={{0,3},{1,0},{2,1},{3,2},{4,7},{5,4},{6,5},{7,6},{8,11},{9,8},{10,9... | collective-permute-start | bytes 1179656 | tf_op jit(solution)/shard_map/ppermute | solution.py:419
  5.3 0.3 collective-permute-start.1
  5.7 0.7 collective-permute-start.2
  6.4 1.1 pad_maximum_fusion.1.refs_4_.refs_11_
  7.5 2.6 %collective-permute-start.3 = (bf16[256,768]{1,0:T(8,128)(2,1)S(1)}, bf16[256,768]{1,0:T(8,128)(2,1)S(1)}, u32[]{:S(2)}, u32[]{:S(2)}) collective-permute-start(bf16[256,768]{1,0:T(8,128)(2,1)S(1)} %pad_maximum_fusion.1.refs_4_.refs_11_), channel_id=1, source_target_pairs={{0,12},{4,0},{8,4},{12,8},{1,13},{5,1},{9,5},{13,9},{2,14},{6,2},{... | collective-permute-start | bytes 1179656 | tf_op jit(solution)/shard_map/ppermute | solution.py:419
  10.0 0.5 collective-permute-start.4
  10.5 10.9 %collective-permute-done.refs_1_.refs_8_ = bf16[256,768]{1,0:T(8,128)(2,1)S(1)} collective-permute-done((bf16[256,768]{1,0:T(8,128)(2,1)S(1)}, bf16[256,768]{1,0:T(8,128)(2,1)S(1)}, u32[]{:S(2)}, u32[]{:S(2)}) %collective-permute-start) | collective-permute-done | bytes 393248 | tf_op jit(solution)/shard_map/ppermute | solution.py:419
  21.4 4.6 %shard_map.174 = bf16[64,16,128]{2,1,0:T(8,128)(2,1)} custom-call(bf16[1280]{0:T(1024)(128)(2,1)} %gain_ref.1, s32[1,64]{1,0:T(1,128)} %order_ref.1, bf16[256,1280]{1,0:T(8,128)(2,1)} %bitcast.13, bf16[256,1280]{1,0:T(8,128)(2,1)} %bitcast.14, bf16[128,588]{1,0:T(8,128)(2,1)} %constant.24.clone.refs_2_, bf16[588,1280]{1,0:T(8,128)(2,1)} %refs_3_.1, ...), custom_call_target="tpu_custom_call" | custom-call | flops 1000000 | bytes 100000 | tf_op jit(solution)/shard_map/pallas_call | solution.py:447
  26.0 6.2 %shard_map.175 = (bf16[512,384]{1,0:T(8,128)(2,1)}, bf16[768,512]{1,0:T(8,128)(2,1)}) custom-call(bf16[512,3072]{1,0:T(8,128)(2,1)} %join_from, bf16[384,3072]{1,0:T(8,128)(2,1)} %out_w_from.1), custom_call_target="tpu_custom_call" | custom-call | flops 1000000 | bytes 100000 | tf_op jit(solution)/shard_map/pallas_call | solution.py:470
  32.3 13.4 %all-to-all-start = ((bf16[64,16,128]{2,1,0:T(8,128)(2,1)}), bf16[64,16,128]{2,1,0:T(8,128)(2,1)S(1)}, u32[]{:S(2)}, u32[]{:S(2)}) async-start(bf16[64,16,128]{2,1,0:T(8,128)(2,1)} %shard_map.174), calls=%async_computation | async-start | bytes 524288 | tf_op jit(solution)/shard_map/all_to_all | solution.py:483
  45.8 6.0 %shard_map.176.refs_0_ = f32[8,1024]{1,0:T(8,128)} custom-call(bf16[256,768]{1,0:T(8,128)(2,1)} %copy-done, bf16[256,768]{1,0:T(8,128)(2,1)} %copy-done.2, bf16[256,768]{1,0:T(8,128)(2,1)} %copy-done.3, bf16[256,768]{1,0:T(8,128)(2,1)} %copy-done.4, bf16[256,768]{1,0:T(8,128)(2,1)} %copy-done.1, bf16[256,768]{1,0:T(8,128)(2,1)} %copy-done.5, ...), custom_call_target="tpu_custom_call" | custom-call | flops 1000000 | bytes 100000 | tf_op jit(solution)/shard_map/pallas_call | solution.py:486
  51.8 2.1 %collective-permute-start.6 = (f32[8,1024]{1,0:T(8,128)}, f32[8,1024]{1,0:T(8,128)S(1)}, u32[]{:S(2)}, u32[]{:S(2)}) collective-permute-start(f32[8,1024]{1,0:T(8,128)} %shard_map.176.refs_0_), channel_id=1, source_target_pairs={{0,3},{1,0},{2,1},{3,2},{4,7},{5,4},{6,5},{7,6},{8,11},{9,8},{10,9... | collective-permute-start | bytes 98312 | tf_op jit(solution)/shard_map/ppermute | solution.py:419
  54.0 0.6 collective-permute-start.7
  54.5 0.6 collective-permute-start.8
  55.4 3.4 %collective-permute-done.7.refs_2_ = f32[8,1024]{1,0:T(8,128)S(1)} collective-permute-done((f32[8,1024]{1,0:T(8,128)}, f32[8,1024]{1,0:T(8,128)S(1)}, u32[]{:S(2)}, u32[]{:S(2)}) %collective-permute-start.7) | collective-permute-done | bytes 32800 | tf_op jit(solution)/shard_map/ppermute | solution.py:419
  59.7 0.7 copy-done.8
  60.4 16.9 %shard_map.177 = (bf16[256,384]{1,0:T(8,128)(2,1)}, bf16[256,384]{1,0:T(8,128)(2,1)}, bf16[256,384]{1,0:T(8,128)(2,1)}, bf16[256,384]{1,0:T(8,128)(2,1)}, bf16[2...) custom-call(s32[64]{0:T(128)} %owner_ref.1, ...), custom_call_target="tpu_custom_call" | custom-call | flops 1000000 | bytes 100000 | tf_op jit(solution)/shard_map/pallas_call | solution.py:493
  77.4 8.1 %all-to-all-start.1 = ((bf16[8,2,48,384]{3,2,1,0:T(8,128)(2,1)}), bf16[8,2,48,384]{3,2,1,0:T(8,128)(2,1)S(1)}, u32[]{:S(2)}, u32[]{:S(2)}) async-start(bf16[8,2,48,384]{3,2,1,0:T(8,128)(2,1)} %bitcast.15), calls=%async_computation.1 | async-start | bytes 1179648 | tf_op jit(solution)/shard_map/all_to_all | solution.py:517
  85.5 1.2 %collective-permute-start.10 = (bf16[256,384]{1,0:T(8,128)(2,1)}, bf16[256,384]{1,0:T(8,128)(2,1)S(1)}, u32[]{:S(2)}, u32[]{:S(2)}) collective-permute-start(bf16[256,384]{1,0:T(8,128)(2,1)} %get-tuple-element.45), channel_id=1, source_target_pairs={{0,2},{1,3},{2,0},{3,1},{4,6},{5,7},{6,4},{7,5},{8,10},{9,11},{10,... | collective-permute-start | bytes 589832 | tf_op jit(solution)/shard_map/ppermute | solution.py:423
  86.6 0.6 collective-permute-start.11
  87.2 0.9 collective-permute-start.9
  88.1 1.4 %collective-permute-start.12 = (bf16[2,256,384]{2,1,0:T(8,128)(2,1)}, bf16[2,256,384]{2,1,0:T(8,128)(2,1)S(1)}, u32[]{:S(2)}, u32[]{:S(2)}) collective-permute-start(bf16[2,256,384]{2,1,0:T(8,128)(2,1)} %get-tuple-element.48), channel_id=1, source_target_pairs={{0,4},{4,8},{8,12},{12,0},{1,5},{5,9},{9,13},{13,1},{2,6},{6,10},{... | collective-permute-start | bytes 1179656 | tf_op jit(solution)/shard_map/ppermute | solution.py:423
  89.5 2.4 %collective-permute-start.13 = (bf16[2,256,384]{2,1,0:T(8,128)(2,1)}, bf16[2,256,384]{2,1,0:T(8,128)(2,1)S(1)}, u32[]{:S(2)}, u32[]{:S(2)}) collective-permute-start(bf16[2,256,384]{2,1,0:T(8,128)(2,1)} %get-tuple-element.49), channel_id=1, source_target_pairs={{0,8},{4,12},{8,0},{12,4},{1,9},{5,13},{9,1},{13,5},{2,10},{6,14},... | collective-permute-start | bytes 1179656 | tf_op jit(solution)/shard_map/ppermute | solution.py:423
  91.9 1.9 %collective-permute-done.10 = bf16[256,384]{1,0:T(8,128)(2,1)S(1)} collective-permute-done((bf16[256,384]{1,0:T(8,128)(2,1)}, bf16[256,384]{1,0:T(8,128)(2,1)S(1)}, u32[]{:S(2)}, u32[]{:S(2)}) %collective-permute-start.10) | collective-permute-done | bytes 196640 | tf_op jit(solution)/shard_map/ppermute | solution.py:423
  93.8 2.2 %collective-permute-start.14 = (bf16[2,256,384]{2,1,0:T(8,128)(2,1)}, bf16[2,256,384]{2,1,0:T(8,128)(2,1)S(1)}, u32[]{:S(2)}, u32[]{:S(2)}) collective-permute-start(bf16[2,256,384]{2,1,0:T(8,128)(2,1)} %get-tuple-element.50), channel_id=1, source_target_pairs={{0,12},{4,0},{8,4},{12,8},{1,13},{5,1},{9,5},{13,9},{2,14},{6,2},{... | collective-permute-start | bytes 1179656 | tf_op jit(solution)/shard_map/ppermute | solution.py:423
  95.9 2.3 %collective-permute-done.9 = bf16[256,384]{1,0:T(8,128)(2,1)S(1)} collective-permute-done((bf16[256,384]{1,0:T(8,128)(2,1)}, bf16[256,384]{1,0:T(8,128)(2,1)S(1)}, u32[]{:S(2)}, u32[]{:S(2)}) %collective-permute-start.9) | collective-permute-done | bytes 196640 | tf_op jit(solution)/shard_map/ppermute | solution.py:423
  98.2 1.7 %fusion = bf16[1,256,384]{2,1,0:T(8,128)(2,1)} fusion(bf16[256,384]{1,0:T(8,128)(2,1)S(1)} %collective-permute-done.11, bf16[256,384]{1,0:T(8,128)(2,1)S(1)} %collective-permute-done.10, bf16[256,384]{1,0:T(8,128)(2,1)S(1)} %collective-permute-done.9, bf16[256,384]{1,0:T(8,128)(2,1)} %get-tuple-element.43), kind=kLoop, calls=%fused_computation.6 | loop fusion | flops 786432 | bytes 983040 | tf_op jit(solution)/shard_map/broadcast_in_dim | solution.py:546
  100.0 4.3 %collective-permute-start.15 = (f32[48,384]{1,0:T(8,128)S(1)}, f32[48,384]{1,0:T(8,128)S(1)}, u32[]{:S(2)}, u32[]{:S(2)}) collective-permute-start(f32[48,384]{1,0:T(8,128)S(1)} %dynamic-slice_bitcast_fusion), channel_id=1, source_target_pairs={{0,128},{128,0},{1,129},{129,1},{2,130},{130,2},{3,131},{131,3},{4... | collective-permute-start | bytes 221192 | tf_op jit(solution)/shard_map/ppermute | solution.py:526
  104.3 8.2 %collective-permute-done.13 = bf16[2,256,384]{2,1,0:T(8,128)(2,1)S(1)} collective-permute-done((bf16[2,256,384]{2,1,0:T(8,128)(2,1)}, bf16[2,256,384]{2,1,0:T(8,128)(2,1)S(1)}, u32[]{:S(2)}, u32[]{:S(2)}) %collective-permute-start.13) | collective-permute-done | bytes 393248 | tf_op jit(solution)/shard_map/ppermute | solution.py:423
  112.6 0.9 add_convert_fusion
  113.5 0.6 bitcast_add_fusion
  (41 shorter events, 1.4 us)
Async XLA Ops:
  1.7 30.5 %copy-start = (bf16[256,768]{1,0:T(8,128)(2,1)}, bf16[256,768]{1,0:T(8,128)(2,1)S(1)}, u32[]{:S(2)}) copy-start(bf16[256,768]{1,0:T(8,128)(2,1)S(1)} %pad_maximum_fusion.refs_0_.refs_7_) | copy-start | bytes 1179652
  1.7 19.7 %collective-permute-start = (bf16[256,768]{1,0:T(8,128)(2,1)S(1)}, bf16[256,768]{1,0:T(8,128)(2,1)S(1)}, u32[]{:S(2)}, u32[]{:S(2)}) collective-permute-start(bf16[256,768]{1,0:T(8,128)(2,1)S(1)} %pad_maximum_fusion.refs_0_.refs_7_), channel_id=1, source_target_pairs={{0,3},{1,0},{2,1},{3,2},{4,7},{5,4},{6,5},{7,6},{8,11},{9,8},{10,9... | collective-permute-start | bytes 1179656 | tf_op jit(solution)/shard_map/ppermute | solution.py:419
  5.3 26.9 %collective-permute-start.1 = (bf16[256,768]{1,0:T(8,128)(2,1)S(1)}, bf16[256,768]{1,0:T(8,128)(2,1)S(1)}, u32[]{:S(2)}, u32[]{:S(2)}) collective-permute-start(bf16[256,768]{1,0:T(8,128)(2,1)S(1)} %pad_maximum_fusion.refs_0_.refs_7_), channel_id=1, source_target_pairs={{0,2},{1,3},{2,0},{3,1},{4,6},{5,7},{6,4},{7,5},{8,10},{9,11},{10,... | collective-permute-start | bytes 1179656 | tf_op jit(solution)/shard_map/ppermute | solution.py:419
  5.7 26.6 %collective-permute-start.2 = (bf16[256,768]{1,0:T(8,128)(2,1)S(1)}, bf16[256,768]{1,0:T(8,128)(2,1)S(1)}, u32[]{:S(2)}, u32[]{:S(2)}) collective-permute-start(bf16[256,768]{1,0:T(8,128)(2,1)S(1)} %pad_maximum_fusion.refs_0_.refs_7_), channel_id=1, source_target_pairs={{0,1},{1,2},{2,3},{3,0},{4,5},{5,6},{6,7},{7,4},{8,9},{9,10},{10,1... | collective-permute-start | bytes 1179656 | tf_op jit(solution)/shard_map/ppermute | solution.py:419
  7.4 24.8 %copy-start.1 = (bf16[256,768]{1,0:T(8,128)(2,1)}, bf16[256,768]{1,0:T(8,128)(2,1)S(1)}, u32[]{:S(2)}) copy-start(bf16[256,768]{1,0:T(8,128)(2,1)S(1)} %pad_maximum_fusion.1.refs_4_.refs_11_) | copy-start | bytes 1179652
  7.5 24.8 %collective-permute-start.3 = (bf16[256,768]{1,0:T(8,128)(2,1)S(1)}, bf16[256,768]{1,0:T(8,128)(2,1)S(1)}, u32[]{:S(2)}, u32[]{:S(2)}) collective-permute-start(bf16[256,768]{1,0:T(8,128)(2,1)S(1)} %pad_maximum_fusion.1.refs_4_.refs_11_), channel_id=1, source_target_pairs={{0,12},{4,0},{8,4},{12,8},{1,13},{5,1},{9,5},{13,9},{2,14},{6,2},{... | collective-permute-start | bytes 1179656 | tf_op jit(solution)/shard_map/ppermute | solution.py:419
  10.0 22.3 %collective-permute-start.4 = (bf16[256,768]{1,0:T(8,128)(2,1)S(1)}, bf16[256,768]{1,0:T(8,128)(2,1)S(1)}, u32[]{:S(2)}, u32[]{:S(2)}) collective-permute-start(bf16[256,768]{1,0:T(8,128)(2,1)S(1)} %pad_maximum_fusion.1.refs_4_.refs_11_), channel_id=1, source_target_pairs={{0,8},{4,12},{8,0},{12,4},{1,9},{5,13},{9,1},{13,5},{2,10},{6,14},... | collective-permute-start | bytes 1179656 | tf_op jit(solution)/shard_map/ppermute | solution.py:419
  21.4 10.8 %copy-start.2 = (bf16[256,768]{1,0:T(8,128)(2,1)}, bf16[256,768]{1,0:T(8,128)(2,1)S(1)}, u32[]{:S(2)}) copy-start(bf16[256,768]{1,0:T(8,128)(2,1)S(1)} %collective-permute-done.refs_1_.refs_8_) | copy-start | bytes 1179652
  21.4 10.9 %collective-permute-start.5 = (bf16[256,768]{1,0:T(8,128)(2,1)S(1)}, bf16[256,768]{1,0:T(8,128)(2,1)S(1)}, u32[]{:S(2)}, u32[]{:S(2)}) collective-permute-start(bf16[256,768]{1,0:T(8,128)(2,1)S(1)} %pad_maximum_fusion.1.refs_4_.refs_11_), channel_id=1, source_target_pairs={{0,4},{4,8},{8,12},{12,0},{1,5},{5,9},{9,13},{13,1},{2,6},{6,10},{... | collective-permute-start | bytes 1179656 | tf_op jit(solution)/shard_map/ppermute | solution.py:419
  32.3 13.5 %copy-start.3 = (bf16[256,768]{1,0:T(8,128)(2,1)}, bf16[256,768]{1,0:T(8,128)(2,1)S(1)}, u32[]{:S(2)}) copy-start(bf16[256,768]{1,0:T(8,128)(2,1)S(1)} %collective-permute-done.1.refs_2_.refs_9_) | copy-start | bytes 1179652
  32.3 13.5 %copy-start.4 = (bf16[256,768]{1,0:T(8,128)(2,1)}, bf16[256,768]{1,0:T(8,128)(2,1)S(1)}, u32[]{:S(2)}) copy-start(bf16[256,768]{1,0:T(8,128)(2,1)S(1)} %collective-permute-done.2.refs_3_.refs_10_) | copy-start | bytes 1179652
  32.3 13.5 %copy-start.5 = (bf16[256,768]{1,0:T(8,128)(2,1)}, bf16[256,768]{1,0:T(8,128)(2,1)S(1)}, u32[]{:S(2)}) copy-start(bf16[256,768]{1,0:T(8,128)(2,1)S(1)} %collective-permute-done.3.refs_5_.refs_12_) | copy-start | bytes 1179652
  32.3 13.5 %copy-start.6 = (bf16[256,768]{1,0:T(8,128)(2,1)}, bf16[256,768]{1,0:T(8,128)(2,1)S(1)}, u32[]{:S(2)}) copy-start(bf16[256,768]{1,0:T(8,128)(2,1)S(1)} %collective-permute-done.4.refs_6_.refs_13_) | copy-start | bytes 1179652
  32.3 13.5 %copy-start.7 = (bf16[256,768]{1,0:T(8,128)(2,1)}, bf16[256,768]{1,0:T(8,128)(2,1)S(1)}, u32[]{:S(2)}) copy-start(bf16[256,768]{1,0:T(8,128)(2,1)S(1)} %collective-permute-done.5.refs_7_.refs_14_) | copy-start | bytes 1179652
  32.3 26.8 %all-to-all-start = ((bf16[64,16,128]{2,1,0:T(8,128)(2,1)}), bf16[64,16,128]{2,1,0:T(8,128)(2,1)S(1)}, u32[]{:S(2)}, u32[]{:S(2)}) async-start(bf16[64,16,128]{2,1,0:T(8,128)(2,1)} %shard_map.174), calls=%async_computation | async-start | bytes 524288 | tf_op jit(solution)/shard_map/all_to_all | solution.py:483
  51.8 3.6 %collective-permute-start.6 = (f32[8,1024]{1,0:T(8,128)}, f32[8,1024]{1,0:T(8,128)S(1)}, u32[]{:S(2)}, u32[]{:S(2)}) collective-permute-start(f32[8,1024]{1,0:T(8,128)} %shard_map.176.refs_0_), channel_id=1, source_target_pairs={{0,3},{1,0},{2,1},{3,2},{4,7},{5,4},{6,5},{7,6},{8,11},{9,8},{10,9... | collective-permute-start | bytes 98312 | tf_op jit(solution)/shard_map/ppermute | solution.py:419
  54.0 4.9 %collective-permute-start.7 = (f32[8,1024]{1,0:T(8,128)}, f32[8,1024]{1,0:T(8,128)S(1)}, u32[]{:S(2)}, u32[]{:S(2)}) collective-permute-start(f32[8,1024]{1,0:T(8,128)} %shard_map.176.refs_0_), channel_id=1, source_target_pairs={{0,2},{1,3},{2,0},{3,1},{4,6},{5,7},{6,4},{7,5},{8,10},{9,11},{10,... | collective-permute-start | bytes 98312 | tf_op jit(solution)/shard_map/ppermute | solution.py:419
  54.5 4.6 %collective-permute-start.8 = (f32[8,1024]{1,0:T(8,128)}, f32[8,1024]{1,0:T(8,128)S(1)}, u32[]{:S(2)}, u32[]{:S(2)}) collective-permute-start(f32[8,1024]{1,0:T(8,128)} %shard_map.176.refs_0_), channel_id=1, source_target_pairs={{0,1},{1,2},{2,3},{3,0},{4,5},{5,6},{6,7},{7,4},{8,9},{9,10},{10,1... | collective-permute-start | bytes 98312 | tf_op jit(solution)/shard_map/ppermute | solution.py:419
  55.4 3.7 %copy-start.10 = (f32[8,1024]{1,0:T(8,128)}, f32[8,1024]{1,0:T(8,128)S(1)}, u32[]{:S(2)}) copy-start(f32[8,1024]{1,0:T(8,128)S(1)} %collective-permute-done.6.refs_1_) | copy-start | bytes 98308
  58.8 0.6 copy-start.11
  59.1 0.6 copy-start.12
  59.7 0.7 copy-start.8
  77.4 35.2 %copy-start.9 = (bf16[2,256,384]{2,1,0:T(8,128)(2,1)S(1)}, bf16[2,256,384]{2,1,0:T(8,128)(2,1)}, u32[]{:S(2)}) copy-start(bf16[2,256,384]{2,1,0:T(8,128)(2,1)} %get-tuple-element.47) | copy-start | bytes 1179652
  77.4 22.5 %all-to-all-start.1 = ((bf16[8,2,48,384]{3,2,1,0:T(8,128)(2,1)}), bf16[8,2,48,384]{3,2,1,0:T(8,128)(2,1)S(1)}, u32[]{:S(2)}, u32[]{:S(2)}) async-start(bf16[8,2,48,384]{3,2,1,0:T(8,128)(2,1)} %bitcast.15), calls=%async_computation.1 | async-start | bytes 1179648 | tf_op jit(solution)/shard_map/all_to_all | solution.py:517
  85.5 8.3 %collective-permute-start.10 = (bf16[256,384]{1,0:T(8,128)(2,1)}, bf16[256,384]{1,0:T(8,128)(2,1)S(1)}, u32[]{:S(2)}, u32[]{:S(2)}) collective-permute-start(bf16[256,384]{1,0:T(8,128)(2,1)} %get-tuple-element.45), channel_id=1, source_target_pairs={{0,2},{1,3},{2,0},{3,1},{4,6},{5,7},{6,4},{7,5},{8,10},{9,11},{10,... | collective-permute-start | bytes 589832 | tf_op jit(solution)/shard_map/ppermute | solution.py:423
  86.6 9.3 %collective-permute-start.11 = (bf16[256,384]{1,0:T(8,128)(2,1)}, bf16[256,384]{1,0:T(8,128)(2,1)S(1)}, u32[]{:S(2)}, u32[]{:S(2)}) collective-permute-start(bf16[256,384]{1,0:T(8,128)(2,1)} %get-tuple-element.46), channel_id=1, source_target_pairs={{0,3},{1,0},{2,1},{3,2},{4,7},{5,4},{6,5},{7,6},{8,11},{9,8},{10,9... | collective-permute-start | bytes 589832 | tf_op jit(solution)/shard_map/ppermute | solution.py:423
  87.2 11.0 %collective-permute-start.9 = (bf16[256,384]{1,0:T(8,128)(2,1)}, bf16[256,384]{1,0:T(8,128)(2,1)S(1)}, u32[]{:S(2)}, u32[]{:S(2)}) collective-permute-start(bf16[256,384]{1,0:T(8,128)(2,1)} %get-tuple-element.44), channel_id=1, source_target_pairs={{0,1},{1,2},{2,3},{3,0},{4,5},{5,6},{6,7},{7,4},{8,9},{9,10},{10,1... | collective-permute-start | bytes 589832 | tf_op jit(solution)/shard_map/ppermute | solution.py:423
  88.1 16.2 %collective-permute-start.12 = (bf16[2,256,384]{2,1,0:T(8,128)(2,1)}, bf16[2,256,384]{2,1,0:T(8,128)(2,1)S(1)}, u32[]{:S(2)}, u32[]{:S(2)}) collective-permute-start(bf16[2,256,384]{2,1,0:T(8,128)(2,1)} %get-tuple-element.48), channel_id=1, source_target_pairs={{0,4},{4,8},{8,12},{12,0},{1,5},{5,9},{9,13},{13,1},{2,6},{6,10},{... | collective-permute-start | bytes 1179656 | tf_op jit(solution)/shard_map/ppermute | solution.py:423
  89.5 23.0 %collective-permute-start.13 = (bf16[2,256,384]{2,1,0:T(8,128)(2,1)}, bf16[2,256,384]{2,1,0:T(8,128)(2,1)S(1)}, u32[]{:S(2)}, u32[]{:S(2)}) collective-permute-start(bf16[2,256,384]{2,1,0:T(8,128)(2,1)} %get-tuple-element.49), channel_id=1, source_target_pairs={{0,8},{4,12},{8,0},{12,4},{1,9},{5,13},{9,1},{13,5},{2,10},{6,14},... | collective-permute-start | bytes 1179656 | tf_op jit(solution)/shard_map/ppermute | solution.py:423
  93.8 18.8 %collective-permute-start.14 = (bf16[2,256,384]{2,1,0:T(8,128)(2,1)}, bf16[2,256,384]{2,1,0:T(8,128)(2,1)S(1)}, u32[]{:S(2)}, u32[]{:S(2)}) collective-permute-start(bf16[2,256,384]{2,1,0:T(8,128)(2,1)} %get-tuple-element.50), channel_id=1, source_target_pairs={{0,12},{4,0},{8,4},{12,8},{1,13},{5,1},{9,5},{13,9},{2,14},{6,2},{... | collective-permute-start | bytes 1179656 | tf_op jit(solution)/shard_map/ppermute | solution.py:423
  100.0 13.5 %collective-permute-start.15 = (f32[48,384]{1,0:T(8,128)S(1)}, f32[48,384]{1,0:T(8,128)S(1)}, u32[]{:S(2)}, u32[]{:S(2)}) collective-permute-start(f32[48,384]{1,0:T(8,128)S(1)} %dynamic-slice_bitcast_fusion), channel_id=1, source_target_pairs={{0,128},{128,0},{1,129},{129,1},{2,130},{130,2},{3,131},{131,3},{4... | collective-permute-start | bytes 221192 | tf_op jit(solution)/shard_map/ppermute | solution.py:526

commit v5 on v4

--- a/solution.py
+++ b/solution.py
@@ -392,14 +392,35 @@
         send.wait()
 
 
-def call(kernel, out_shape, in_specs, scratch=(), out_spec=None):
+def half_kernel(parts_ref, kept_ref, sent_ref):
+    here_z = lax.axis_index("zh")
+    for out_ref, half in ((kept_ref, here_z), (sent_ref, 1 - here_z)):
+        out_ref[...] = sum(parts_ref[source, half].astype(f32) for source in range(2 * GRID))
+
+
+def sum_kernel(kept_ref, other_ref, *refs):
+    pair_refs, query_refs = refs[:GRID], refs[GRID : 2 * GRID]
+    query_out, key_out, value_out, weight_out, query_held, pair_held, *arrived = refs[2 * GRID :]
+    pair_copies = fetch(pair_refs, [pair_held.at[step] for step in range(GRID)], arrived[1])
+    query_copies = fetch(query_refs, [query_held.at[step] for step in range(GRID)], arrived[0])
+    weight_out[...] = kept_ref[...] + other_ref[...]
+    for copy in query_copies:
+        copy.wait()
+    query_out[0] = sum(query_held[step].astype(f32) for step in range(GRID)).astype(bf16)
+    for copy in pair_copies:
+        copy.wait()
+    for place, out_ref in enumerate((key_out, value_out)):
+        out_ref[0] = sum(pair_held[step, place].astype(f32) for step in range(GRID)).astype(bf16)
+
+
+def call(kernel, out_shape, in_specs, scratch=(), out_spec=None, limit=56):
     return pl.pallas_call(
         kernel,
         out_shape=out_shape,
         in_specs=in_specs,
         out_specs=jax.tree.map(lambda _: out_spec or VMEM, out_shape),
         scratch_shapes=list(scratch),
-        compiler_params=pltpu.CompilerParams(vmem_limit_bytes=56 * MIB),
+        compiler_params=pltpu.CompilerParams(vmem_limit_bytes=limit * MIB),
         cost_estimate=pl.CostEstimate(flops=10**6, bytes_accessed=10**5, transcendentals=0),
     )
 
@@ -466,7 +487,6 @@
         patch_w,
         jnp.asarray(spread_matrix(), bf16),
     )
-    join_late, windows = lax.optimization_barrier((join_w, windows))
     joint, picked = call(
         weights_kernel,
         (shape((QUARTERS * LANES, FEATS), bf16), shape((768, QUARTERS * LANES), bf16)),
@@ -476,18 +496,17 @@
             pltpu.VMEM(out_w.shape, bf16),
             pltpu.SemaphoreType.DMA((2,)),
         ],
-    )(join_late, out_w)
-    windows, joint, picked, query_outs, key_values = lax.optimization_barrier(
-        (windows, joint, picked, query_outs, key_values)
-    )
+    )(join_w, out_w)
     received = lax.all_to_all(
         windows, ("tm", "hx", "hy"), split_axis=0, concat_axis=0, tiled=True
     )
+    joint, picked, key_values[0] = lax.optimization_barrier((joint, picked, key_values[0]))
     totals = call(
         totals_kernel,
         shape((8, BLOCK), f32),
         [ANY] * (2 * GRID),
         scratch=HELD * 2 + ARRIVED * 2,
+        limit=24,
     )(*query_outs, *key_values)
     total_pieces = gather(totals, "hy")
     outs = call(
@@ -512,6 +531,7 @@
         + ARRIVED * 6
         + [pltpu.SemaphoreType.DMA((1,))],
         out_spec=ANY,
+        limit=40,
     )(frame_owner, conv_w, *total_pieces, received, joint, picked, *query_outs, *key_values)
     query_parts, pair_parts, weight_part = outs[:GRID], outs[GRID : 2 * GRID], outs[2 * GRID]
     weight_parts = lax.all_to_all(
@@ -521,15 +541,13 @@
         concat_axis=0,
         tiled=True,
     )
-    weight_half = jnp.sum(weight_parts.astype(f32), axis=0)
-    here_z = lax.axis_index("zh")
-    weight_other = lax.ppermute(
-        lax.dynamic_index_in_dim(weight_half, 1 - here_z, 0, keepdims=False),
-        "zh",
-        [(0, 1), (1, 0)],
-    )
-    weight_grad = lax.dynamic_index_in_dim(weight_half, here_z, 0, keepdims=False) + weight_other
-
+    weight_kept, weight_sent = call(
+        half_kernel,
+        (shape((48, FEATS), f32), shape((48, FEATS), f32)),
+        [VMEM],
+        limit=8,
+    )(weight_parts)
+    weight_other = lax.ppermute(weight_sent, "zh", [(0, 1), (1, 0)])
     pair_back = [pair_parts[0]] + [
         to_ahead(pair_parts[step], "hx", step) for step in range(1, GRID)
     ]
@@ -537,13 +555,14 @@
         to_ahead(query_parts[step], "hy", step) for step in range(1, GRID)
     ]
 
-    def total(parts):
-        return sum(part.astype(f32) for part in parts).astype(bf16)
-
-    query_grad = total(query_back)
-    key_grad = total([part[0] for part in pair_back])
-    value_grad = total([part[1] for part in pair_back])
-    return (query_grad[None], key_grad[None], value_grad[None], weight_grad)
+    rows = shape((1, ROWS_HERE, FEATS), bf16)
+    return call(
+        sum_kernel,
+        (rows, rows, rows, shape((48, FEATS), f32)),
+        [VMEM] * 2 + [ANY] * (2 * GRID),
+        scratch=HELD + [pltpu.VMEM((GRID, 2, ROWS_HERE, FEATS), bf16)] + ARRIVED * 2,
+        limit=8,
+    )(weight_kept, weight_other, *pair_back, *query_back)
 
 
 def solution(mesh):

time: 115 us -> 121 us (1.052)
  the two profiles are of different devices: /device:TPU:1 before, /device:TPU:24 now
where the time goes in v5:
time: 121 us; the launch traced here: 120 us
  starting transfers between devices  38.4 us (32%)
  Pallas kernels  35.7 us (30%)
  waiting for transfers between devices  32.2 us (27%)
  local copies, waits for them, and re-layouts  11.4 us (9%)
    pallas_call x1, Pallas kernels, per_device(): call(grads_kernel, tuple([shape((ROWS_HERE, FEATS), bf16)] * GRID) + tupl...  17.9 us
    ppermute x9, waiting for transfers between devices, from_ahead(): lax.ppermute(block, axis, [(i, (i - step) % GRID) for i in range(GRID)])  17.5 us
    ppermute x6, waiting for transfers between devices, to_ahead(): lax.ppermute(block, axis, [(i, (i + step) % GRID) for i in range(GRID)])  12.7 us
    ppermute x9, starting transfers between devices, from_ahead(): lax.ppermute(block, axis, [(i, (i - step) % GRID) for i in range(GRID)])  12.2 us
    unnamed x34, local copies, waits for them, and re-layouts  11.4 us
    all_to_all x1, starting transfers between devices, per_device(): lax.all_to_all(windows, ('tm', 'hx', 'hy'), split_axis=0, concat_axis=0,...  9.35 us
    ppermute x6, starting transfers between devices, to_ahead(): lax.ppermute(block, axis, [(i, (i + step) % GRID) for i in range(GRID)])  8.5 us
    pallas_call x1, Pallas kernels, per_device(): call(weights_kernel, (shape((QUARTERS * LANES, FEATS), bf16), shape((768,...  6.14 us
  transfers between devices with their start and end apart: 18, of which 9 were waited for; matrix products, arithmetic and copies ran while one was open for 0% of the time, Pallas kernels for 12%

profile of v5, /device:TPU:24, one launch (start us, length us, event | category | flops | bytes accessed | tf_op | source)
XLA Modules:
  0.0 119.8 jit_solution(1800984375260586567)
XLA Ops:
  0.7 1.1 pad_maximum_fusion.1.refs_4_.refs_11_
  1.8 1.6 %collective-permute-start.5 = (bf16[256,768]{1,0:T(8,128)(2,1)S(1)}, bf16[256,768]{1,0:T(8,128)(2,1)S(1)}, u32[]{:S(2)}, u32[]{:S(2)}) collective-permute-start(bf16[256,768]{1,0:T(8,128)(2,1)S(1)} %pad_maximum_fusion.1.refs_4_.refs_11_), channel_id=1, source_target_pairs={{0,4},{4,8},{8,12},{12,0},{1,5},{5,9},{9,13},{13,1},{2,6},{6,10},{... | collective-permute-start | bytes 1179656 | tf_op jit(solution)/shard_map/ppermute | solution.py:440
  3.3 2.7 %collective-permute-start.4 = (bf16[256,768]{1,0:T(8,128)(2,1)S(1)}, bf16[256,768]{1,0:T(8,128)(2,1)S(1)}, u32[]{:S(2)}, u32[]{:S(2)}) collective-permute-start(bf16[256,768]{1,0:T(8,128)(2,1)S(1)} %pad_maximum_fusion.1.refs_4_.refs_11_), channel_id=1, source_target_pairs={{0,8},{4,12},{8,0},{12,4},{1,9},{5,13},{9,1},{13,5},{2,10},{6,14},... | collective-permute-start | bytes 1179656 | tf_op jit(solution)/shard_map/ppermute | solution.py:440
  6.1 1.4 %collective-permute-start.3 = (bf16[256,768]{1,0:T(8,128)(2,1)S(1)}, bf16[256,768]{1,0:T(8,128)(2,1)S(1)}, u32[]{:S(2)}, u32[]{:S(2)}) collective-permute-start(bf16[256,768]{1,0:T(8,128)(2,1)S(1)} %pad_maximum_fusion.1.refs_4_.refs_11_), channel_id=1, source_target_pairs={{0,12},{4,0},{8,4},{12,8},{1,13},{5,1},{9,5},{13,9},{2,14},{6,2},{... | collective-permute-start | bytes 1179656 | tf_op jit(solution)/shard_map/ppermute | solution.py:440
  7.5 4.6 %shard_map.176 = bf16[64,16,128]{2,1,0:T(8,128)(2,1)} custom-call(bf16[1280]{0:T(1024)(128)(2,1)} %gain_ref.1, s32[1,64]{1,0:T(1,128)} %order_ref.1, bf16[256,1280]{1,0:T(8,128)(2,1)} %bitcast.8, bf16[256,1280]{1,0:T(8,128)(2,1)} %bitcast.9, bf16[128,588]{1,0:T(8,128)(2,1)} %constant.4.clone.refs_2_, bf16[588,1280]{1,0:T(8,128)(2,1)} %refs_3_.1, ...), custom_call_target="tpu_custom_call" | custom-call | flops 1000000 | bytes 100000 | tf_op jit(solution)/shard_map/pallas_call | solution.py:468
  12.1 9.4 %all-to-all-start = ((bf16[64,16,128]{2,1,0:T(8,128)(2,1)}), bf16[64,16,128]{2,1,0:T(8,128)(2,1)S(1)}, u32[]{:S(2)}, u32[]{:S(2)}) async-start(bf16[64,16,128]{2,1,0:T(8,128)(2,1)} %shard_map.176), calls=%async_computation | async-start | bytes 524288 | tf_op jit(solution)/shard_map/all_to_all | solution.py:500
  22.0 2.5 %collective-permute-start.1 = (bf16[256,768]{1,0:T(8,128)(2,1)S(1)}, bf16[256,768]{1,0:T(8,128)(2,1)S(1)}, u32[]{:S(2)}, u32[]{:S(2)}) collective-permute-start(bf16[256,768]{1,0:T(8,128)(2,1)S(1)} %pad_maximum_fusion.refs_0_.refs_7_), channel_id=1, source_target_pairs={{0,2},{1,3},{2,0},{3,1},{4,6},{5,7},{6,4},{7,5},{8,10},{9,11},{10,... | collective-permute-start | bytes 1179656 | tf_op jit(solution)/shard_map/ppermute | solution.py:440
  24.5 6.1 %shard_map.174 = (bf16[512,384]{1,0:T(8,128)(2,1)}, bf16[768,512]{1,0:T(8,128)(2,1)}) custom-call(bf16[512,3072]{1,0:T(8,128)(2,1)} %join_from.1, bf16[384,3072]{1,0:T(8,128)(2,1)} %out_w_from.1), custom_call_target="tpu_custom_call" | custom-call | flops 1000000 | bytes 100000 | tf_op jit(solution)/shard_map/pallas_call | solution.py:490
  30.7 4.8 %collective-permute-done.2.refs_3_.refs_10_ = bf16[256,768]{1,0:T(8,128)(2,1)S(1)} collective-permute-done((bf16[256,768]{1,0:T(8,128)(2,1)S(1)}, bf16[256,768]{1,0:T(8,128)(2,1)S(1)}, u32[]{:S(2)}, u32[]{:S(2)}) %collective-permute-start.2) | collective-permute-done | bytes 393248 | tf_op jit(solution)/shard_map/ppermute | solution.py:440
  35.4 1.4 %collective-permute-done.1.refs_2_.refs_9_ = bf16[256,768]{1,0:T(8,128)(2,1)S(1)} collective-permute-done((bf16[256,768]{1,0:T(8,128)(2,1)S(1)}, bf16[256,768]{1,0:T(8,128)(2,1)S(1)}, u32[]{:S(2)}, u32[]{:S(2)}) %collective-permute-start.1) | collective-permute-done | bytes 393248 | tf_op jit(solution)/shard_map/ppermute | solution.py:440
  36.8 6.8 %collective-permute-done.refs_1_.refs_8_ = bf16[256,768]{1,0:T(8,128)(2,1)S(1)} collective-permute-done((bf16[256,768]{1,0:T(8,128)(2,1)S(1)}, bf16[256,768]{1,0:T(8,128)(2,1)S(1)}, u32[]{:S(2)}, u32[]{:S(2)}) %collective-permute-start) | collective-permute-done | bytes 393248 | tf_op jit(solution)/shard_map/ppermute | solution.py:440
  43.6 4.1 %shard_map.175.refs_0_ = f32[8,1024]{1,0:T(8,128)S(1)} custom-call(bf16[256,768]{1,0:T(8,128)(2,1)S(1)} %pad_maximum_fusion.refs_0_.refs_7_, bf16[256,768]{1,0:T(8,128)(2,1)S(1)} %collective-permute-done.refs_1_.refs_8_, bf16[256,768]{1,0:T(8,128)(2,1)S(1)} %collective-permute-done.1.refs_2_.refs_9_, ...), custom_call_target="tpu_custom_call" | custom-call | flops 1000000 | bytes 100000 | tf_op jit(solution)/shard_map/pallas_call | solution.py:504
  47.7 1.3 %collective-permute-start.8 = (f32[8,1024]{1,0:T(8,128)S(1)}, f32[8,1024]{1,0:T(8,128)S(1)}, u32[]{:S(2)}, u32[]{:S(2)}) collective-permute-start(f32[8,1024]{1,0:T(8,128)S(1)} %shard_map.175.refs_0_), channel_id=1, source_target_pairs={{0,1},{1,2},{2,3},{3,0},{4,5},{5,6},{6,7},{7,4},{8,9},{9,10},{10,1... | collective-permute-start | bytes 98312 | tf_op jit(solution)/shard_map/ppermute | solution.py:440
  49.0 1.7 %collective-permute-start.7 = (f32[8,1024]{1,0:T(8,128)S(1)}, f32[8,1024]{1,0:T(8,128)S(1)}, u32[]{:S(2)}, u32[]{:S(2)}) collective-permute-start(f32[8,1024]{1,0:T(8,128)S(1)} %shard_map.175.refs_0_), channel_id=1, source_target_pairs={{0,2},{1,3},{2,0},{3,1},{4,6},{5,7},{6,4},{7,5},{8,10},{9,11},{10,... | collective-permute-start | bytes 98312 | tf_op jit(solution)/shard_map/ppermute | solution.py:440
  52.0 2.7 %collective-permute-done.7.refs_2_ = f32[8,1024]{1,0:T(8,128)S(1)} collective-permute-done((f32[8,1024]{1,0:T(8,128)S(1)}, f32[8,1024]{1,0:T(8,128)S(1)}, u32[]{:S(2)}, u32[]{:S(2)}) %collective-permute-start.7) | collective-permute-done | bytes 32800 | tf_op jit(solution)/shard_map/ppermute | solution.py:440
  54.7 1.1 collective-permute-done.6.refs_1_
  55.8 1.1 copy-done
  57.0 1.0 copy-done.4
  58.7 17.9 %shard_map.177 = (bf16[256,384]{1,0:T(8,128)(2,1)S(1)}, bf16[256,384]{1,0:T(8,128)(2,1)S(1)}, bf16[256,384]{1,0:T(8,128)(2,1)S(1)}, bf16[256,384]{1,0:T(8,128)(2...) custom-call(s32[64]{0:T(128)S(1)} %copy-done.8, ...), custom_call_target="tpu_custom_call" | custom-call | flops 1000000 | bytes 100000 | tf_op jit(solution)/shard_map/pallas_call | solution.py:512
  76.6 0.8 copy-done.1
  83.2 3.7 %all-to-all-start.1 = ((bf16[8,2,48,384]{3,2,1,0:T(8,128)(2,1)}), bf16[8,2,48,384]{3,2,1,0:T(8,128)(2,1)S(1)}, u32[]{:S(2)}, u32[]{:S(2)}) async-start(bf16[8,2,48,384]{3,2,1,0:T(8,128)(2,1)} %bitcast.7), calls=%async_computation.1 | async-start | bytes 1179648 | tf_op jit(solution)/shard_map/all_to_all | solution.py:537
  87.5 2.0 %collective-permute-start.10 = (bf16[2,256,384]{2,1,0:T(8,128)(2,1)}, bf16[2,256,384]{2,1,0:T(8,128)(2,1)S(1)}, u32[]{:S(2)}, u32[]{:S(2)}) collective-permute-start(bf16[2,256,384]{2,1,0:T(8,128)(2,1)} %copy-done.11), channel_id=1, source_target_pairs={{0,4},{4,8},{8,12},{12,0},{1,5},{5,9},{9,13},{13,1},{2,6},{6,10},{... | collective-permute-start | bytes 1179656 | tf_op jit(solution)/shard_map/ppermute | solution.py:444
  89.5 2.7 %collective-permute-start.11 = (bf16[2,256,384]{2,1,0:T(8,128)(2,1)}, bf16[2,256,384]{2,1,0:T(8,128)(2,1)S(1)}, u32[]{:S(2)}, u32[]{:S(2)}) collective-permute-start(bf16[2,256,384]{2,1,0:T(8,128)(2,1)} %copy-done.10), channel_id=1, source_target_pairs={{0,8},{4,12},{8,0},{12,4},{1,9},{5,13},{9,1},{13,5},{2,10},{6,14},... | collective-permute-start | bytes 1179656 | tf_op jit(solution)/shard_map/ppermute | solution.py:444
  92.2 1.5 %collective-permute-start.12 = (bf16[2,256,384]{2,1,0:T(8,128)(2,1)}, bf16[2,256,384]{2,1,0:T(8,128)(2,1)S(1)}, u32[]{:S(2)}, u32[]{:S(2)}) collective-permute-start(bf16[2,256,384]{2,1,0:T(8,128)(2,1)} %copy-done.9), channel_id=1, source_target_pairs={{0,12},{4,0},{8,4},{12,8},{1,13},{5,1},{9,5},{13,9},{2,14},{6,2},{... | collective-permute-start | bytes 1179656 | tf_op jit(solution)/shard_map/ppermute | solution.py:444
  93.7 0.9 collective-permute-start.14
  95.4 1.9 %all-to-all-done.1.parts_ref = bf16[8,2,48,384]{3,2,1,0:T(8,128)(2,1)S(1)} async-done(((bf16[8,2,48,384]{3,2,1,0:T(8,128)(2,1)}), bf16[8,2,48,384]{3,2,1,0:T(8,128)(2,1)S(1)}, u32[]{:S(2)}, u32[]{:S(2)}) %all-to-all-start.1) | async-done | bytes 589856 | tf_op jit(solution)/shard_map/all_to_all | solution.py:537
  97.4 5.9 %collective-permute-done.14.refs_6_ = bf16[256,384]{1,0:T(8,128)(2,1)S(1)} collective-permute-done((bf16[256,384]{1,0:T(8,128)(2,1)}, bf16[256,384]{1,0:T(8,128)(2,1)S(1)}, u32[]{:S(2)}, u32[]{:S(2)}) %collective-permute-start.14) | collective-permute-done | bytes 196640 | tf_op jit(solution)/shard_map/ppermute | solution.py:444
  103.2 4.7 %collective-permute-start.9 = (f32[48,384]{1,0:T(8,128)S(1)}, f32[48,384]{1,0:T(8,128)S(1)}, u32[]{:S(2)}, u32[]{:S(2)}) collective-permute-start(f32[48,384]{1,0:T(8,128)S(1)} %get-tuple-element.27), channel_id=1, source_target_pairs={{0,128},{128,0},{1,129},{129,1},{2,130},{130,2},{3,131},{131,3},{4... | collective-permute-start | bytes 221192 | tf_op jit(solution)/shard_map/ppermute | solution.py:550
  108.0 6.9 %collective-permute-done.11.refs_2_ = bf16[2,256,384]{2,1,0:T(8,128)(2,1)S(1)} collective-permute-done((bf16[2,256,384]{2,1,0:T(8,128)(2,1)}, bf16[2,256,384]{2,1,0:T(8,128)(2,1)S(1)}, u32[]{:S(2)}, u32[]{:S(2)}) %collective-permute-start.11) | collective-permute-done | bytes 393248 | tf_op jit(solution)/shard_map/ppermute | solution.py:444
  114.8 1.0 copy-done.3
  115.8 0.9 copy-done.6
  116.8 2.8 %shard_map.179 = (bf16[1,256,384]{2,1,0:T(8,128)(2,1)}, bf16[1,256,384]{2,1,0:T(8,128)(2,1)}, bf16[1,256,384]{2,1,0:T(8,128)(2,1)}, f32[48,384]{1,0:T(8,128)}) custom-call(f32[48,384]{1,0:T(8,128)S(1)} %get-tuple-element.26.kept_ref, f32[48,384]{1,0:T(8,128)S(1)} %collective-permute-done.9.other_ref, bf16[2,256,384]{2,1,0:T(8,128)(2,1)S(1)} %copy-done.3, ...), custom_call_target="tpu_custom_call" | custom-call | flops 1000000 | bytes 100000 | tf_op jit(solution)/shard_map/pallas_call | solution.py:559
  (46 shorter events, 9.9 us)
Async XLA Ops:
  0.6 20.8 %copy-start.15 = (bf16[1,256,384]{2,1,0:T(8,128)(2,1)S(1)}, bf16[1,256,384]{2,1,0:T(8,128)(2,1)}, u32[]{:S(2)}) copy-start(bf16[1,256,384]{2,1,0:T(8,128)(2,1)} %param.26) | copy-start | bytes 589828
  0.6 20.8 %copy-start.16 = (bf16[1,256,384]{2,1,0:T(8,128)(2,1)S(1)}, bf16[1,256,384]{2,1,0:T(8,128)(2,1)}, u32[]{:S(2)}) copy-start(bf16[1,256,384]{2,1,0:T(8,128)(2,1)} %param.23) | copy-start | bytes 589828
  1.8 22.7 %collective-permute-start.5 = (bf16[256,768]{1,0:T(8,128)(2,1)S(1)}, bf16[256,768]{1,0:T(8,128)(2,1)S(1)}, u32[]{:S(2)}, u32[]{:S(2)}) collective-permute-start(bf16[256,768]{1,0:T(8,128)(2,1)S(1)} %pad_maximum_fusion.1.refs_4_.refs_11_), channel_id=1, source_target_pairs={{0,4},{4,8},{8,12},{12,0},{1,5},{5,9},{9,13},{13,1},{2,6},{6,10},{... | collective-permute-start | bytes 1179656 | tf_op jit(solution)/shard_map/ppermute | solution.py:440
  3.3 27.3 %collective-permute-start.4 = (bf16[256,768]{1,0:T(8,128)(2,1)S(1)}, bf16[256,768]{1,0:T(8,128)(2,1)S(1)}, u32[]{:S(2)}, u32[]{:S(2)}) collective-permute-start(bf16[256,768]{1,0:T(8,128)(2,1)S(1)} %pad_maximum_fusion.1.refs_4_.refs_11_), channel_id=1, source_target_pairs={{0,8},{4,12},{8,0},{12,4},{1,9},{5,13},{9,1},{13,5},{2,10},{6,14},... | collective-permute-start | bytes 1179656 | tf_op jit(solution)/shard_map/ppermute | solution.py:440
  6.1 24.6 %collective-permute-start.3 = (bf16[256,768]{1,0:T(8,128)(2,1)S(1)}, bf16[256,768]{1,0:T(8,128)(2,1)S(1)}, u32[]{:S(2)}, u32[]{:S(2)}) collective-permute-start(bf16[256,768]{1,0:T(8,128)(2,1)S(1)} %pad_maximum_fusion.1.refs_4_.refs_11_), channel_id=1, source_target_pairs={{0,12},{4,0},{8,4},{12,8},{1,13},{5,1},{9,5},{13,9},{2,14},{6,2},{... | collective-permute-start | bytes 1179656 | tf_op jit(solution)/shard_map/ppermute | solution.py:440
  12.1 43.7 %all-to-all-start = ((bf16[64,16,128]{2,1,0:T(8,128)(2,1)}), bf16[64,16,128]{2,1,0:T(8,128)(2,1)S(1)}, u32[]{:S(2)}, u32[]{:S(2)}) async-start(bf16[64,16,128]{2,1,0:T(8,128)(2,1)} %shard_map.176), calls=%async_computation | async-start | bytes 524288 | tf_op jit(solution)/shard_map/all_to_all | solution.py:500
  21.5 13.9 %collective-permute-start.2 = (bf16[256,768]{1,0:T(8,128)(2,1)S(1)}, bf16[256,768]{1,0:T(8,128)(2,1)S(1)}, u32[]{:S(2)}, u32[]{:S(2)}) collective-permute-start(bf16[256,768]{1,0:T(8,128)(2,1)S(1)} %pad_maximum_fusion.refs_0_.refs_7_), channel_id=1, source_target_pairs={{0,1},{1,2},{2,3},{3,0},{4,5},{5,6},{6,7},{7,4},{8,9},{9,10},{10,1... | collective-permute-start | bytes 1179656 | tf_op jit(solution)/shard_map/ppermute | solution.py:440
  22.0 14.8 %collective-permute-start.1 = (bf16[256,768]{1,0:T(8,128)(2,1)S(1)}, bf16[256,768]{1,0:T(8,128)(2,1)S(1)}, u32[]{:S(2)}, u32[]{:S(2)}) collective-permute-start(bf16[256,768]{1,0:T(8,128)(2,1)S(1)} %pad_maximum_fusion.refs_0_.refs_7_), channel_id=1, source_target_pairs={{0,2},{1,3},{2,0},{3,1},{4,6},{5,7},{6,4},{7,5},{8,10},{9,11},{10,... | collective-permute-start | bytes 1179656 | tf_op jit(solution)/shard_map/ppermute | solution.py:440
  24.5 19.1 %collective-permute-start = (bf16[256,768]{1,0:T(8,128)(2,1)S(1)}, bf16[256,768]{1,0:T(8,128)(2,1)S(1)}, u32[]{:S(2)}, u32[]{:S(2)}) collective-permute-start(bf16[256,768]{1,0:T(8,128)(2,1)S(1)} %pad_maximum_fusion.refs_0_.refs_7_), channel_id=1, source_target_pairs={{0,3},{1,0},{2,1},{3,2},{4,7},{5,4},{6,5},{7,6},{8,11},{9,8},{10,9... | collective-permute-start | bytes 1179656 | tf_op jit(solution)/shard_map/ppermute | solution.py:440
  30.7 25.2 %copy-start.8 = (s32[64]{0:T(128)S(1)}, s32[64]{0:T(128)}, u32[]{:S(2)}) copy-start(s32[64]{0:T(128)} %owner_ref.1) | copy-start | bytes 772
  47.7 4.2 %collective-permute-start.8 = (f32[8,1024]{1,0:T(8,128)S(1)}, f32[8,1024]{1,0:T(8,128)S(1)}, u32[]{:S(2)}, u32[]{:S(2)}) collective-permute-start(f32[8,1024]{1,0:T(8,128)S(1)} %shard_map.175.refs_0_), channel_id=1, source_target_pairs={{0,1},{1,2},{2,3},{3,0},{4,5},{5,6},{6,7},{7,4},{8,9},{9,10},{10,1... | collective-permute-start | bytes 98312 | tf_op jit(solution)/shard_map/ppermute | solution.py:440
  49.0 5.7 %collective-permute-start.7 = (f32[8,1024]{1,0:T(8,128)S(1)}, f32[8,1024]{1,0:T(8,128)S(1)}, u32[]{:S(2)}, u32[]{:S(2)}) collective-permute-start(f32[8,1024]{1,0:T(8,128)S(1)} %shard_map.175.refs_0_), channel_id=1, source_target_pairs={{0,2},{1,3},{2,0},{3,1},{4,6},{5,7},{6,4},{7,5},{8,10},{9,11},{10,... | collective-permute-start | bytes 98312 | tf_op jit(solution)/shard_map/ppermute | solution.py:440
  50.7 5.1 %collective-permute-start.6 = (f32[8,1024]{1,0:T(8,128)S(1)}, f32[8,1024]{1,0:T(8,128)S(1)}, u32[]{:S(2)}, u32[]{:S(2)}) collective-permute-start(f32[8,1024]{1,0:T(8,128)S(1)} %shard_map.175.refs_0_), channel_id=1, source_target_pairs={{0,3},{1,0},{2,1},{3,2},{4,7},{5,4},{6,5},{7,6},{8,11},{9,8},{10,9... | collective-permute-start | bytes 98312 | tf_op jit(solution)/shard_map/ppermute | solution.py:440
  55.8 1.1 copy-start
  57.0 1.0 copy-start.4
  58.0 0.7 copy-start.7
  76.6 0.8 copy-start.1
  77.4 0.8 copy-start.2
  78.2 0.7 copy-start.5
  78.9 0.7 copy-start.9
  79.6 0.8 copy-start.10
  80.4 0.7 copy-start.11
  83.2 14.1 %all-to-all-start.1 = ((bf16[8,2,48,384]{3,2,1,0:T(8,128)(2,1)}), bf16[8,2,48,384]{3,2,1,0:T(8,128)(2,1)S(1)}, u32[]{:S(2)}, u32[]{:S(2)}) async-start(bf16[8,2,48,384]{3,2,1,0:T(8,128)(2,1)} %bitcast.7), calls=%async_computation.1 | async-start | bytes 1179648 | tf_op jit(solution)/shard_map/all_to_all | solution.py:537
  86.9 7.7 %collective-permute-start.13 = (bf16[256,384]{1,0:T(8,128)(2,1)}, bf16[256,384]{1,0:T(8,128)(2,1)S(1)}, u32[]{:S(2)}, u32[]{:S(2)}) collective-permute-start(bf16[256,384]{1,0:T(8,128)(2,1)} %copy-done.14), channel_id=1, source_target_pairs={{0,1},{1,2},{2,3},{3,0},{4,5},{5,6},{6,7},{7,4},{8,9},{9,10},{10,1... | collective-permute-start | bytes 589832 | tf_op jit(solution)/shard_map/ppermute | solution.py:444
  87.5 20.4 %collective-permute-start.10 = (bf16[2,256,384]{2,1,0:T(8,128)(2,1)}, bf16[2,256,384]{2,1,0:T(8,128)(2,1)S(1)}, u32[]{:S(2)}, u32[]{:S(2)}) collective-permute-start(bf16[2,256,384]{2,1,0:T(8,128)(2,1)} %copy-done.11), channel_id=1, source_target_pairs={{0,4},{4,8},{8,12},{12,0},{1,5},{5,9},{9,13},{13,1},{2,6},{6,10},{... | collective-permute-start | bytes 1179656 | tf_op jit(solution)/shard_map/ppermute | solution.py:444
  89.5 25.3 %collective-permute-start.11 = (bf16[2,256,384]{2,1,0:T(8,128)(2,1)}, bf16[2,256,384]{2,1,0:T(8,128)(2,1)S(1)}, u32[]{:S(2)}, u32[]{:S(2)}) collective-permute-start(bf16[2,256,384]{2,1,0:T(8,128)(2,1)} %copy-done.10), channel_id=1, source_target_pairs={{0,8},{4,12},{8,0},{12,4},{1,9},{5,13},{9,1},{13,5},{2,10},{6,14},... | collective-permute-start | bytes 1179656 | tf_op jit(solution)/shard_map/ppermute | solution.py:444
  92.2 22.6 %collective-permute-start.12 = (bf16[2,256,384]{2,1,0:T(8,128)(2,1)}, bf16[2,256,384]{2,1,0:T(8,128)(2,1)S(1)}, u32[]{:S(2)}, u32[]{:S(2)}) collective-permute-start(bf16[2,256,384]{2,1,0:T(8,128)(2,1)} %copy-done.9), channel_id=1, source_target_pairs={{0,12},{4,0},{8,4},{12,8},{1,13},{5,1},{9,5},{13,9},{2,14},{6,2},{... | collective-permute-start | bytes 1179656 | tf_op jit(solution)/shard_map/ppermute | solution.py:444
  93.7 9.6 %collective-permute-start.14 = (bf16[256,384]{1,0:T(8,128)(2,1)}, bf16[256,384]{1,0:T(8,128)(2,1)S(1)}, u32[]{:S(2)}, u32[]{:S(2)}) collective-permute-start(bf16[256,384]{1,0:T(8,128)(2,1)} %copy-done.13), channel_id=1, source_target_pairs={{0,2},{1,3},{2,0},{3,1},{4,6},{5,7},{6,4},{7,5},{8,10},{9,11},{10,... | collective-permute-start | bytes 589832 | tf_op jit(solution)/shard_map/ppermute | solution.py:444
  94.6 13.4 %collective-permute-start.15 = (bf16[256,384]{1,0:T(8,128)(2,1)}, bf16[256,384]{1,0:T(8,128)(2,1)S(1)}, u32[]{:S(2)}, u32[]{:S(2)}) collective-permute-start(bf16[256,384]{1,0:T(8,128)(2,1)} %copy-done.12), channel_id=1, source_target_pairs={{0,3},{1,0},{2,1},{3,2},{4,7},{5,4},{6,5},{7,6},{8,11},{9,8},{10,9... | collective-permute-start | bytes 589832 | tf_op jit(solution)/shard_map/ppermute | solution.py:444
  103.2 11.6 %collective-permute-start.9 = (f32[48,384]{1,0:T(8,128)S(1)}, f32[48,384]{1,0:T(8,128)S(1)}, u32[]{:S(2)}, u32[]{:S(2)}) collective-permute-start(f32[48,384]{1,0:T(8,128)S(1)} %get-tuple-element.27), channel_id=1, source_target_pairs={{0,128},{128,0},{1,129},{129,1},{2,130},{130,2},{3,131},{131,3},{4... | collective-permute-start | bytes 221192 | tf_op jit(solution)/shard_map/ppermute | solution.py:550
  114.8 1.0 copy-start.3
  115.8 0.9 copy-start.6
  (3 other events, 2.0 us)

commit v6 on v5

--- a/solution.py
+++ b/solution.py
@@ -463,8 +463,10 @@
     attn_out,
     out_w,
 ):
-    key_values = gather(jnp.concatenate([keys[0], values[0]], axis=1), "hx")
-    query_outs = gather(jnp.concatenate([queries[0], attn_out[0]], axis=1), "hy")
+    key_value = jnp.concatenate([keys[0], values[0]], axis=1)
+    query_out = jnp.concatenate([queries[0], attn_out[0]], axis=1)
+    sides = [from_ahead(key_value, "hx", step) for step in (1, 3)]
+    sides += [from_ahead(query_out, "hy", step) for step in (1, 3)]
     windows = call(
         window_kernel,
         shape((FRAMES, 16, LANES), bf16),
@@ -487,6 +489,11 @@
         patch_w,
         jnp.asarray(spread_matrix(), bf16),
     )
+    windows, join_w, key_value, query_out, sides = lax.optimization_barrier(
+        (windows, join_w, key_value, query_out, sides)
+    )
+    key_values = [key_value, sides[0], from_ahead(key_value, "hx", 2), sides[1]]
+    query_outs = [query_out, sides[2], from_ahead(query_out, "hy", 2), sides[3]]
     joint, picked = call(
         weights_kernel,
         (shape((QUARTERS * LANES, FEATS), bf16), shape((768, QUARTERS * LANES), bf16)),
@@ -497,10 +504,12 @@
             pltpu.SemaphoreType.DMA((2,)),
         ],
     )(join_w, out_w)
+    windows, joint, picked, key_values, query_outs = lax.optimization_barrier(
+        (windows, joint, picked, key_values, query_outs)
+    )
     received = lax.all_to_all(
         windows, ("tm", "hx", "hy"), split_axis=0, concat_axis=0, tiled=True
     )
-    joint, picked, key_values[0] = lax.optimization_barrier((joint, picked, key_values[0]))
     totals = call(
         totals_kernel,
         shape((8, BLOCK), f32),
@@ -531,7 +540,7 @@
         + ARRIVED * 6
         + [pltpu.SemaphoreType.DMA((1,))],
         out_spec=ANY,
-        limit=40,
+        limit=56,
     )(frame_owner, conv_w, *total_pieces, received, joint, picked, *query_outs, *key_values)
     query_parts, pair_parts, weight_part = outs[:GRID], outs[GRID : 2 * GRID], outs[2 * GRID]
     weight_parts = lax.all_to_all(

time: 121 us -> 110 us (0.909)
  local copies, waits for them, and re-layouts: 11.4 us -> 3.24 us
  waiting for transfers between devices: 32.2 us -> 28.4 us
    unnamed x34 -> x30, local copies, waits for them, and re-layouts: 11.4 us -> 3.24 us
    ppermute x9, waiting for transfers between devices: 17.5 us -> 13.2 us  [from_ahead(): lax.ppermute(block, axis, [(i, (i - step) % GRID) for i in range(GRID)])]
  transfers between devices with their start and end apart: 18 -> 18, of which waited for: 9 -> 11; matrix products, arithmetic and copies ran while one was open for 0% -> 1% of each run, Pallas kernels for 12% -> 14%
where the time goes in v6:
time: 110 us; the launch traced here: 108 us
  starting transfers between devices  38.7 us (35%)
  Pallas kernels  34.7 us (32%)
  waiting for transfers between devices  28.4 us (26%)
  local copies, waits for them, and re-layouts  3.24 us (3%)
  other arithmetic  2.11 us (2%)
    pallas_call x1, Pallas kernels, per_device(): call(grads_kernel, tuple([shape((ROWS_HERE, FEATS), bf16)] * GRID) + tupl...  16.9 us
    ppermute x9, waiting for transfers between devices, from_ahead(): lax.ppermute(block, axis, [(i, (i - step) % GRID) for i in range(GRID)])  13.2 us
    ppermute x6, waiting for transfers between devices, to_ahead(): lax.ppermute(block, axis, [(i, (i + step) % GRID) for i in range(GRID)])  12.9 us
    ppermute x9, starting transfers between devices, from_ahead(): lax.ppermute(block, axis, [(i, (i - step) % GRID) for i in range(GRID)])  11.5 us
    all_to_all x1, starting transfers between devices, per_device(): lax.all_to_all(windows, ('tm', 'hx', 'hy'), split_axis=0, concat_axis=0,...  10.3 us
    ppermute x6, starting transfers between devices, to_ahead(): lax.ppermute(block, axis, [(i, (i + step) % GRID) for i in range(GRID)])  8.19 us
    pallas_call x1, Pallas kernels, per_device(): call(weights_kernel, (shape((QUARTERS * LANES, FEATS), bf16), shape((768,...  6.14 us
    pallas_call x1, Pallas kernels, per_device(): call(window_kernel, shape((FRAMES, 16, LANES), bf16), [VMEM] * 2 + [ANY]...  4.57 us
  transfers between devices with their start and end apart: 18, of which 11 were waited for; matrix products, arithmetic and copies ran while one was open for 1% of the time, Pallas kernels for 14%

profile of v6, /device:TPU:24, one launch (start us, length us, event | category | flops | bytes accessed | tf_op | source)
XLA Modules:
  0.0 108.1 jit_solution(15122889849050683711)
XLA Ops:
  0.6 1.1 pad_maximum_fusion.refs_4_.refs_11_
  1.7 1.6 %collective-permute-start.1 = (bf16[256,768]{1,0:T(8,128)(2,1)S(1)}, bf16[256,768]{1,0:T(8,128)(2,1)S(1)}, u32[]{:S(2)}, u32[]{:S(2)}) collective-permute-start(bf16[256,768]{1,0:T(8,128)(2,1)S(1)} %pad_maximum_fusion.refs_4_.refs_11_), channel_id=1, source_target_pairs={{0,4},{4,8},{8,12},{12,0},{1,5},{5,9},{9,13},{13,1},{2,6},{6,10},{... | collective-permute-start | bytes 1179656 | tf_op jit(solution)/shard_map/ppermute | solution.py:440
  3.3 1.7 %collective-permute-start = (bf16[256,768]{1,0:T(8,128)(2,1)S(1)}, bf16[256,768]{1,0:T(8,128)(2,1)S(1)}, u32[]{:S(2)}, u32[]{:S(2)}) collective-permute-start(bf16[256,768]{1,0:T(8,128)(2,1)S(1)} %pad_maximum_fusion.refs_4_.refs_11_), channel_id=1, source_target_pairs={{0,12},{4,0},{8,4},{12,8},{1,13},{5,1},{9,5},{13,9},{2,14},{6,2},{... | collective-permute-start | bytes 1179656 | tf_op jit(solution)/shard_map/ppermute | solution.py:440
  5.0 1.1 pad_maximum_fusion.1.refs_0_.refs_7_
  6.1 2.0 %collective-permute-start.3 = (bf16[256,768]{1,0:T(8,128)(2,1)S(1)}, bf16[256,768]{1,0:T(8,128)(2,1)S(1)}, u32[]{:S(2)}, u32[]{:S(2)}) collective-permute-start(bf16[256,768]{1,0:T(8,128)(2,1)S(1)} %pad_maximum_fusion.1.refs_0_.refs_7_), channel_id=1, source_target_pairs={{0,1},{1,2},{2,3},{3,0},{4,5},{5,6},{6,7},{7,4},{8,9},{9,10},{10,1... | collective-permute-start | bytes 1179656 | tf_op jit(solution)/shard_map/ppermute | solution.py:440
  8.2 4.6 %shard_map.174 = bf16[64,16,128]{2,1,0:T(8,128)(2,1)} custom-call(bf16[1280]{0:T(1024)(128)(2,1)} %gain_ref.1, s32[1,64]{1,0:T(1,128)} %order_ref.1, bf16[256,1280]{1,0:T(8,128)(2,1)} %bitcast.7, bf16[256,1280]{1,0:T(8,128)(2,1)} %bitcast.8, bf16[128,588]{1,0:T(8,128)(2,1)} %constant.4.clone.refs_2_, bf16[588,1280]{1,0:T(8,128)(2,1)} %refs_3_.1, ...), custom_call_target="tpu_custom_call" | custom-call | flops 1000000 | bytes 100000 | tf_op jit(solution)/shard_map/pallas_call | solution.py:470
  12.8 1.1 collective-permute-done.1.refs_7_.refs_14_
  13.9 2.6 %collective-permute-done.3.refs_3_.refs_10_ = bf16[256,768]{1,0:T(8,128)(2,1)S(1)} collective-permute-done((bf16[256,768]{1,0:T(8,128)(2,1)S(1)}, bf16[256,768]{1,0:T(8,128)(2,1)S(1)}, u32[]{:S(2)}, u32[]{:S(2)}) %collective-permute-start.3) | collective-permute-done | bytes 393248 | tf_op jit(solution)/shard_map/ppermute | solution.py:440
  16.5 1.3 %collective-permute-done.2.refs_1_.refs_8_ = bf16[256,768]{1,0:T(8,128)(2,1)S(1)} collective-permute-done((bf16[256,768]{1,0:T(8,128)(2,1)S(1)}, bf16[256,768]{1,0:T(8,128)(2,1)S(1)}, u32[]{:S(2)}, u32[]{:S(2)}) %collective-permute-start.2) | collective-permute-done | bytes 393248 | tf_op jit(solution)/shard_map/ppermute | solution.py:440
  17.8 1.8 %collective-permute-start.4 = (bf16[256,768]{1,0:T(8,128)(2,1)S(1)}, bf16[256,768]{1,0:T(8,128)(2,1)S(1)}, u32[]{:S(2)}, u32[]{:S(2)}) collective-permute-start(bf16[256,768]{1,0:T(8,128)(2,1)S(1)} %pad_maximum_fusion.refs_4_.refs_11_), channel_id=1, source_target_pairs={{0,8},{4,12},{8,0},{12,4},{1,9},{5,13},{9,1},{13,5},{2,10},{6,14},... | collective-permute-start | bytes 1179656 | tf_op jit(solution)/shard_map/ppermute | solution.py:440
  19.6 1.2 %collective-permute-start.5 = (bf16[256,768]{1,0:T(8,128)(2,1)S(1)}, bf16[256,768]{1,0:T(8,128)(2,1)S(1)}, u32[]{:S(2)}, u32[]{:S(2)}) collective-permute-start(bf16[256,768]{1,0:T(8,128)(2,1)S(1)} %pad_maximum_fusion.1.refs_0_.refs_7_), channel_id=1, source_target_pairs={{0,2},{1,3},{2,0},{3,1},{4,6},{5,7},{6,4},{7,5},{8,10},{9,11},{10,... | collective-permute-start | bytes 1179656 | tf_op jit(solution)/shard_map/ppermute | solution.py:440
  20.8 6.1 %shard_map.175 = (bf16[512,384]{1,0:T(8,128)(2,1)}, bf16[768,512]{1,0:T(8,128)(2,1)}) custom-call(bf16[512,3072]{1,0:T(8,128)(2,1)} %join_from, bf16[384,3072]{1,0:T(8,128)(2,1)} %out_w_from.1), custom_call_target="tpu_custom_call" | custom-call | flops 1000000 | bytes 100000 | tf_op jit(solution)/shard_map/pallas_call | solution.py:497
  27.4 2.6 %collective-permute-done.5.refs_2_.refs_9_ = bf16[256,768]{1,0:T(8,128)(2,1)S(1)} collective-permute-done((bf16[256,768]{1,0:T(8,128)(2,1)S(1)}, bf16[256,768]{1,0:T(8,128)(2,1)S(1)}, u32[]{:S(2)}, u32[]{:S(2)}) %collective-permute-start.5) | collective-permute-done | bytes 393248 | tf_op jit(solution)/shard_map/ppermute | solution.py:440
  30.0 10.3 %all-to-all-start = ((bf16[64,16,128]{2,1,0:T(8,128)(2,1)}), bf16[64,16,128]{2,1,0:T(8,128)(2,1)S(1)}, u32[]{:S(2)}, u32[]{:S(2)}) async-start(bf16[64,16,128]{2,1,0:T(8,128)(2,1)} %shard_map.174), calls=%async_computation | async-start | bytes 524288 | tf_op jit(solution)/shard_map/all_to_all | solution.py:510
  40.4 4.1 %shard_map.176.refs_0_ = f32[8,1024]{1,0:T(8,128)S(1)} custom-call(bf16[256,768]{1,0:T(8,128)(2,1)S(1)} %pad_maximum_fusion.1.refs_0_.refs_7_, bf16[256,768]{1,0:T(8,128)(2,1)S(1)} %collective-permute-done.2.refs_1_.refs_8_, bf16[256,768]{1,0:T(8,128)(2,1)S(1)} %collective-permute-done.5.refs_2_.refs_9_, ...), custom_call_target="tpu_custom_call" | custom-call | flops 1000000 | bytes 100000 | tf_op jit(solution)/shard_map/pallas_call | solution.py:513
  45.3 2.3 %collective-permute-start.7 = (f32[8,1024]{1,0:T(8,128)S(1)}, f32[8,1024]{1,0:T(8,128)S(1)}, u32[]{:S(2)}, u32[]{:S(2)}) collective-permute-start(f32[8,1024]{1,0:T(8,128)S(1)} %shard_map.176.refs_0_), channel_id=1, source_target_pairs={{0,2},{1,3},{2,0},{3,1},{4,6},{5,7},{6,4},{7,5},{8,10},{9,11},{10,... | collective-permute-start | bytes 98312 | tf_op jit(solution)/shard_map/ppermute | solution.py:440
  47.6 1.1 collective-permute-done.8.refs_3_
  48.6 2.1 %collective-permute-done.7.refs_2_ = f32[8,1024]{1,0:T(8,128)S(1)} collective-permute-done((f32[8,1024]{1,0:T(8,128)S(1)}, f32[8,1024]{1,0:T(8,128)S(1)}, u32[]{:S(2)}, u32[]{:S(2)}) %collective-permute-start.7) | collective-permute-done | bytes 32800 | tf_op jit(solution)/shard_map/ppermute | solution.py:440
  50.7 2.0 %collective-permute-done.6.refs_1_ = f32[8,1024]{1,0:T(8,128)S(1)} collective-permute-done((f32[8,1024]{1,0:T(8,128)S(1)}, f32[8,1024]{1,0:T(8,128)S(1)}, u32[]{:S(2)}, u32[]{:S(2)}) %collective-permute-start.6) | collective-permute-done | bytes 32800 | tf_op jit(solution)/shard_map/ppermute | solution.py:440
  54.0 16.9 %shard_map.177 = (bf16[256,384]{1,0:T(8,128)(2,1)}, bf16[256,384]{1,0:T(8,128)(2,1)}, bf16[256,384]{1,0:T(8,128)(2,1)}, bf16[256,384]{1,0:T(8,128)(2,1)}, bf16[2...) custom-call(s32[64]{0:T(128)} %owner_ref.1, ...), custom_call_target="tpu_custom_call" | custom-call | flops 1000000 | bytes 100000 | tf_op jit(solution)/shard_map/pallas_call | solution.py:521
  71.0 4.2 %all-to-all-start.1 = ((bf16[8,2,48,384]{3,2,1,0:T(8,128)(2,1)}), bf16[8,2,48,384]{3,2,1,0:T(8,128)(2,1)S(1)}, u32[]{:S(2)}, u32[]{:S(2)}) async-start(bf16[8,2,48,384]{3,2,1,0:T(8,128)(2,1)} %bitcast.9), calls=%async_computation.1 | async-start | bytes 1179648 | tf_op jit(solution)/shard_map/all_to_all | solution.py:546
  75.8 2.0 %collective-permute-start.10 = (bf16[2,256,384]{2,1,0:T(8,128)(2,1)}, bf16[2,256,384]{2,1,0:T(8,128)(2,1)S(1)}, u32[]{:S(2)}, u32[]{:S(2)}) collective-permute-start(bf16[2,256,384]{2,1,0:T(8,128)(2,1)} %get-tuple-element.61), channel_id=1, source_target_pairs={{0,4},{4,8},{8,12},{12,0},{1,5},{5,9},{9,13},{13,1},{2,6},{6,10},{... | collective-permute-start | bytes 1179656 | tf_op jit(solution)/shard_map/ppermute | solution.py:444
  77.8 2.7 %collective-permute-start.11 = (bf16[2,256,384]{2,1,0:T(8,128)(2,1)}, bf16[2,256,384]{2,1,0:T(8,128)(2,1)S(1)}, u32[]{:S(2)}, u32[]{:S(2)}) collective-permute-start(bf16[2,256,384]{2,1,0:T(8,128)(2,1)} %get-tuple-element.62), channel_id=1, source_target_pairs={{0,8},{4,12},{8,0},{12,4},{1,9},{5,13},{9,1},{13,5},{2,10},{6,14},... | collective-permute-start | bytes 1179656 | tf_op jit(solution)/shard_map/ppermute | solution.py:444
  80.5 1.5 %collective-permute-start.12 = (bf16[2,256,384]{2,1,0:T(8,128)(2,1)}, bf16[2,256,384]{2,1,0:T(8,128)(2,1)S(1)}, u32[]{:S(2)}, u32[]{:S(2)}) collective-permute-start(bf16[2,256,384]{2,1,0:T(8,128)(2,1)} %get-tuple-element.63), channel_id=1, source_target_pairs={{0,12},{4,0},{8,4},{12,8},{1,13},{5,1},{9,5},{13,9},{2,14},{6,2},{... | collective-permute-start | bytes 1179656 | tf_op jit(solution)/shard_map/ppermute | solution.py:444
  81.9 0.9 collective-permute-start.14
  83.4 2.2 %all-to-all-done.1.parts_ref = bf16[8,2,48,384]{3,2,1,0:T(8,128)(2,1)S(1)} async-done(((bf16[8,2,48,384]{3,2,1,0:T(8,128)(2,1)}), bf16[8,2,48,384]{3,2,1,0:T(8,128)(2,1)S(1)}, u32[]{:S(2)}, u32[]{:S(2)}) %all-to-all-start.1) | async-done | bytes 589856 | tf_op jit(solution)/shard_map/all_to_all | solution.py:546
  85.7 5.8 %collective-permute-done.14.refs_6_ = bf16[256,384]{1,0:T(8,128)(2,1)S(1)} collective-permute-done((bf16[256,384]{1,0:T(8,128)(2,1)}, bf16[256,384]{1,0:T(8,128)(2,1)S(1)}, u32[]{:S(2)}, u32[]{:S(2)}) %collective-permute-start.14) | collective-permute-done | bytes 196640 | tf_op jit(solution)/shard_map/ppermute | solution.py:444
  91.5 4.5 %collective-permute-start.9 = (f32[48,384]{1,0:T(8,128)S(1)}, f32[48,384]{1,0:T(8,128)S(1)}, u32[]{:S(2)}, u32[]{:S(2)}) collective-permute-start(f32[48,384]{1,0:T(8,128)S(1)} %get-tuple-element.59), channel_id=1, source_target_pairs={{0,128},{128,0},{1,129},{129,1},{2,130},{130,2},{3,131},{131,3},{4... | collective-permute-start | bytes 221192 | tf_op jit(solution)/shard_map/ppermute | solution.py:559
  96.0 7.2 %collective-permute-done.11.refs_2_ = bf16[2,256,384]{2,1,0:T(8,128)(2,1)S(1)} collective-permute-done((bf16[2,256,384]{2,1,0:T(8,128)(2,1)}, bf16[2,256,384]{2,1,0:T(8,128)(2,1)S(1)}, u32[]{:S(2)}, u32[]{:S(2)}) %collective-permute-start.11) | collective-permute-done | bytes 393248 | tf_op jit(solution)/shard_map/ppermute | solution.py:444
  103.2 1.0 copy-done.8
  104.2 0.9 copy-done.9
  105.1 2.8 %shard_map.179 = (bf16[1,256,384]{2,1,0:T(8,128)(2,1)}, bf16[1,256,384]{2,1,0:T(8,128)(2,1)}, bf16[1,256,384]{2,1,0:T(8,128)(2,1)}, f32[48,384]{1,0:T(8,128)}) custom-call(f32[48,384]{1,0:T(8,128)S(1)} %get-tuple-element.58.kept_ref, f32[48,384]{1,0:T(8,128)S(1)} %collective-permute-done.9.other_ref, bf16[2,256,384]{2,1,0:T(8,128)(2,1)S(1)} %copy-done.8, ...), custom_call_target="tpu_custom_call" | custom-call | flops 1000000 | bytes 100000 | tf_op jit(solution)/shard_map/pallas_call | solution.py:568
  (42 shorter events, 3.8 us)
Async XLA Ops:
  1.7 38.6 %copy-start = (bf16[256,768]{1,0:T(8,128)(2,1)}, bf16[256,768]{1,0:T(8,128)(2,1)S(1)}, u32[]{:S(2)}) copy-start(bf16[256,768]{1,0:T(8,128)(2,1)S(1)} %pad_maximum_fusion.refs_4_.refs_11_) | copy-start | bytes 1179652
  1.7 12.1 %collective-permute-start.1 = (bf16[256,768]{1,0:T(8,128)(2,1)S(1)}, bf16[256,768]{1,0:T(8,128)(2,1)S(1)}, u32[]{:S(2)}, u32[]{:S(2)}) collective-permute-start(bf16[256,768]{1,0:T(8,128)(2,1)S(1)} %pad_maximum_fusion.refs_4_.refs_11_), channel_id=1, source_target_pairs={{0,4},{4,8},{8,12},{12,0},{1,5},{5,9},{9,13},{13,1},{2,6},{6,10},{... | collective-permute-start | bytes 1179656 | tf_op jit(solution)/shard_map/ppermute | solution.py:440
  3.3 10.6 %collective-permute-start = (bf16[256,768]{1,0:T(8,128)(2,1)S(1)}, bf16[256,768]{1,0:T(8,128)(2,1)S(1)}, u32[]{:S(2)}, u32[]{:S(2)}) collective-permute-start(bf16[256,768]{1,0:T(8,128)(2,1)S(1)} %pad_maximum_fusion.refs_4_.refs_11_), channel_id=1, source_target_pairs={{0,12},{4,0},{8,4},{12,8},{1,13},{5,1},{9,5},{13,9},{2,14},{6,2},{... | collective-permute-start | bytes 1179656 | tf_op jit(solution)/shard_map/ppermute | solution.py:440
  6.1 34.3 %copy-start.1 = (bf16[256,768]{1,0:T(8,128)(2,1)}, bf16[256,768]{1,0:T(8,128)(2,1)S(1)}, u32[]{:S(2)}) copy-start(bf16[256,768]{1,0:T(8,128)(2,1)S(1)} %pad_maximum_fusion.1.refs_0_.refs_7_) | copy-start | bytes 1179652
  6.1 10.4 %collective-permute-start.3 = (bf16[256,768]{1,0:T(8,128)(2,1)S(1)}, bf16[256,768]{1,0:T(8,128)(2,1)S(1)}, u32[]{:S(2)}, u32[]{:S(2)}) collective-permute-start(bf16[256,768]{1,0:T(8,128)(2,1)S(1)} %pad_maximum_fusion.1.refs_0_.refs_7_), channel_id=1, source_target_pairs={{0,1},{1,2},{2,3},{3,0},{4,5},{5,6},{6,7},{7,4},{8,9},{9,10},{10,1... | collective-permute-start | bytes 1179656 | tf_op jit(solution)/shard_map/ppermute | solution.py:440
  8.1 9.6 %collective-permute-start.2 = (bf16[256,768]{1,0:T(8,128)(2,1)S(1)}, bf16[256,768]{1,0:T(8,128)(2,1)S(1)}, u32[]{:S(2)}, u32[]{:S(2)}) collective-permute-start(bf16[256,768]{1,0:T(8,128)(2,1)S(1)} %pad_maximum_fusion.1.refs_0_.refs_7_), channel_id=1, source_target_pairs={{0,3},{1,0},{2,1},{3,2},{4,7},{5,4},{6,5},{7,6},{8,11},{9,8},{10,9... | collective-permute-start | bytes 1179656 | tf_op jit(solution)/shard_map/ppermute | solution.py:440
  13.8 26.5 %copy-start.2 = (bf16[256,768]{1,0:T(8,128)(2,1)}, bf16[256,768]{1,0:T(8,128)(2,1)S(1)}, u32[]{:S(2)}) copy-start(bf16[256,768]{1,0:T(8,128)(2,1)S(1)} %collective-permute-done.1.refs_7_.refs_14_) | copy-start | bytes 1179652
  13.8 26.5 %copy-start.3 = (bf16[256,768]{1,0:T(8,128)(2,1)}, bf16[256,768]{1,0:T(8,128)(2,1)S(1)}, u32[]{:S(2)}) copy-start(bf16[256,768]{1,0:T(8,128)(2,1)S(1)} %collective-permute-done.refs_5_.refs_12_) | copy-start | bytes 1179652
  16.5 23.9 %copy-start.4 = (bf16[256,768]{1,0:T(8,128)(2,1)}, bf16[256,768]{1,0:T(8,128)(2,1)S(1)}, u32[]{:S(2)}) copy-start(bf16[256,768]{1,0:T(8,128)(2,1)S(1)} %collective-permute-done.3.refs_3_.refs_10_) | copy-start | bytes 1179652
  17.8 22.6 %copy-start.5 = (bf16[256,768]{1,0:T(8,128)(2,1)}, bf16[256,768]{1,0:T(8,128)(2,1)S(1)}, u32[]{:S(2)}) copy-start(bf16[256,768]{1,0:T(8,128)(2,1)S(1)} %collective-permute-done.2.refs_1_.refs_8_) | copy-start | bytes 1179652
  17.8 9.7 %collective-permute-start.4 = (bf16[256,768]{1,0:T(8,128)(2,1)S(1)}, bf16[256,768]{1,0:T(8,128)(2,1)S(1)}, u32[]{:S(2)}, u32[]{:S(2)}) collective-permute-start(bf16[256,768]{1,0:T(8,128)(2,1)S(1)} %pad_maximum_fusion.refs_4_.refs_11_), channel_id=1, source_target_pairs={{0,8},{4,12},{8,0},{12,4},{1,9},{5,13},{9,1},{13,5},{2,10},{6,14},... | collective-permute-start | bytes 1179656 | tf_op jit(solution)/shard_map/ppermute | solution.py:440
  19.6 10.5 %collective-permute-start.5 = (bf16[256,768]{1,0:T(8,128)(2,1)S(1)}, bf16[256,768]{1,0:T(8,128)(2,1)S(1)}, u32[]{:S(2)}, u32[]{:S(2)}) collective-permute-start(bf16[256,768]{1,0:T(8,128)(2,1)S(1)} %pad_maximum_fusion.1.refs_0_.refs_7_), channel_id=1, source_target_pairs={{0,2},{1,3},{2,0},{3,1},{4,6},{5,7},{6,4},{7,5},{8,10},{9,11},{10,... | collective-permute-start | bytes 1179656 | tf_op jit(solution)/shard_map/ppermute | solution.py:440
  27.4 25.3 %copy-start.6 = (bf16[256,768]{1,0:T(8,128)(2,1)}, bf16[256,768]{1,0:T(8,128)(2,1)S(1)}, u32[]{:S(2)}) copy-start(bf16[256,768]{1,0:T(8,128)(2,1)S(1)} %collective-permute-done.4.refs_6_.refs_13_) | copy-start | bytes 1179652
  30.0 22.7 %copy-start.7 = (bf16[256,768]{1,0:T(8,128)(2,1)}, bf16[256,768]{1,0:T(8,128)(2,1)S(1)}, u32[]{:S(2)}) copy-start(bf16[256,768]{1,0:T(8,128)(2,1)S(1)} %collective-permute-done.5.refs_2_.refs_9_) | copy-start | bytes 1179652
  30.0 22.7 %all-to-all-start = ((bf16[64,16,128]{2,1,0:T(8,128)(2,1)}), bf16[64,16,128]{2,1,0:T(8,128)(2,1)S(1)}, u32[]{:S(2)}, u32[]{:S(2)}) async-start(bf16[64,16,128]{2,1,0:T(8,128)(2,1)} %shard_map.174), calls=%async_computation | async-start | bytes 524288 | tf_op jit(solution)/shard_map/all_to_all | solution.py:510
  44.5 8.2 %copy-start.10 = (f32[8,1024]{1,0:T(8,128)}, f32[8,1024]{1,0:T(8,128)S(1)}, u32[]{:S(2)}) copy-start(f32[8,1024]{1,0:T(8,128)S(1)} %shard_map.176.refs_0_) | copy-start | bytes 98308
  44.6 4.1 %collective-permute-start.8 = (f32[8,1024]{1,0:T(8,128)S(1)}, f32[8,1024]{1,0:T(8,128)S(1)}, u32[]{:S(2)}, u32[]{:S(2)}) collective-permute-start(f32[8,1024]{1,0:T(8,128)S(1)} %shard_map.176.refs_0_), channel_id=1, source_target_pairs={{0,1},{1,2},{2,3},{3,0},{4,5},{5,6},{6,7},{7,4},{8,9},{9,10},{10,1... | collective-permute-start | bytes 98312 | tf_op jit(solution)/shard_map/ppermute | solution.py:440
  45.3 5.4 %collective-permute-start.7 = (f32[8,1024]{1,0:T(8,128)S(1)}, f32[8,1024]{1,0:T(8,128)S(1)}, u32[]{:S(2)}, u32[]{:S(2)}) collective-permute-start(f32[8,1024]{1,0:T(8,128)S(1)} %shard_map.176.refs_0_), channel_id=1, source_target_pairs={{0,2},{1,3},{2,0},{3,1},{4,6},{5,7},{6,4},{7,5},{8,10},{9,11},{10,... | collective-permute-start | bytes 98312 | tf_op jit(solution)/shard_map/ppermute | solution.py:440
  47.6 5.1 %collective-permute-start.6 = (f32[8,1024]{1,0:T(8,128)S(1)}, f32[8,1024]{1,0:T(8,128)S(1)}, u32[]{:S(2)}, u32[]{:S(2)}) collective-permute-start(f32[8,1024]{1,0:T(8,128)S(1)} %shard_map.176.refs_0_), channel_id=1, source_target_pairs={{0,3},{1,0},{2,1},{3,2},{4,7},{5,4},{6,5},{7,6},{8,11},{9,8},{10,9... | collective-permute-start | bytes 98312 | tf_op jit(solution)/shard_map/ppermute | solution.py:440
  48.6 4.1 %copy-start.12 = (f32[8,1024]{1,0:T(8,128)}, f32[8,1024]{1,0:T(8,128)S(1)}, u32[]{:S(2)}) copy-start(f32[8,1024]{1,0:T(8,128)S(1)} %collective-permute-done.8.refs_3_) | copy-start | bytes 98308
  50.7 2.0 %copy-start.13 = (f32[8,1024]{1,0:T(8,128)}, f32[8,1024]{1,0:T(8,128)S(1)}, u32[]{:S(2)}) copy-start(f32[8,1024]{1,0:T(8,128)S(1)} %collective-permute-done.7.refs_2_) | copy-start | bytes 98308
  53.3 0.7 copy-start.11
  71.0 14.7 %all-to-all-start.1 = ((bf16[8,2,48,384]{3,2,1,0:T(8,128)(2,1)}), bf16[8,2,48,384]{3,2,1,0:T(8,128)(2,1)S(1)}, u32[]{:S(2)}, u32[]{:S(2)}) async-start(bf16[8,2,48,384]{3,2,1,0:T(8,128)(2,1)} %bitcast.9), calls=%async_computation.1 | async-start | bytes 1179648 | tf_op jit(solution)/shard_map/all_to_all | solution.py:546
  75.2 7.6 %collective-permute-start.13 = (bf16[256,384]{1,0:T(8,128)(2,1)}, bf16[256,384]{1,0:T(8,128)(2,1)S(1)}, u32[]{:S(2)}, u32[]{:S(2)}) collective-permute-start(bf16[256,384]{1,0:T(8,128)(2,1)} %get-tuple-element.65), channel_id=1, source_target_pairs={{0,1},{1,2},{2,3},{3,0},{4,5},{5,6},{6,7},{7,4},{8,9},{9,10},{10,1... | collective-permute-start | bytes 589832 | tf_op jit(solution)/shard_map/ppermute | solution.py:444
  75.8 20.2 %collective-permute-start.10 = (bf16[2,256,384]{2,1,0:T(8,128)(2,1)}, bf16[2,256,384]{2,1,0:T(8,128)(2,1)S(1)}, u32[]{:S(2)}, u32[]{:S(2)}) collective-permute-start(bf16[2,256,384]{2,1,0:T(8,128)(2,1)} %get-tuple-element.61), channel_id=1, source_target_pairs={{0,4},{4,8},{8,12},{12,0},{1,5},{5,9},{9,13},{13,1},{2,6},{6,10},{... | collective-permute-start | bytes 1179656 | tf_op jit(solution)/shard_map/ppermute | solution.py:444
  77.8 25.4 %collective-permute-start.11 = (bf16[2,256,384]{2,1,0:T(8,128)(2,1)}, bf16[2,256,384]{2,1,0:T(8,128)(2,1)S(1)}, u32[]{:S(2)}, u32[]{:S(2)}) collective-permute-start(bf16[2,256,384]{2,1,0:T(8,128)(2,1)} %get-tuple-element.62), channel_id=1, source_target_pairs={{0,8},{4,12},{8,0},{12,4},{1,9},{5,13},{9,1},{13,5},{2,10},{6,14},... | collective-permute-start | bytes 1179656 | tf_op jit(solution)/shard_map/ppermute | solution.py:444
  80.5 22.7 %collective-permute-start.12 = (bf16[2,256,384]{2,1,0:T(8,128)(2,1)}, bf16[2,256,384]{2,1,0:T(8,128)(2,1)S(1)}, u32[]{:S(2)}, u32[]{:S(2)}) collective-permute-start(bf16[2,256,384]{2,1,0:T(8,128)(2,1)} %get-tuple-element.63), channel_id=1, source_target_pairs={{0,12},{4,0},{8,4},{12,8},{1,13},{5,1},{9,5},{13,9},{2,14},{6,2},{... | collective-permute-start | bytes 1179656 | tf_op jit(solution)/shard_map/ppermute | solution.py:444
  81.9 9.6 %collective-permute-start.14 = (bf16[256,384]{1,0:T(8,128)(2,1)}, bf16[256,384]{1,0:T(8,128)(2,1)S(1)}, u32[]{:S(2)}, u32[]{:S(2)}) collective-permute-start(bf16[256,384]{1,0:T(8,128)(2,1)} %get-tuple-element.66), channel_id=1, source_target_pairs={{0,2},{1,3},{2,0},{3,1},{4,6},{5,7},{6,4},{7,5},{8,10},{9,11},{10,... | collective-permute-start | bytes 589832 | tf_op jit(solution)/shard_map/ppermute | solution.py:444
  82.9 13.1 %collective-permute-start.15 = (bf16[256,384]{1,0:T(8,128)(2,1)}, bf16[256,384]{1,0:T(8,128)(2,1)S(1)}, u32[]{:S(2)}, u32[]{:S(2)}) collective-permute-start(bf16[256,384]{1,0:T(8,128)(2,1)} %get-tuple-element.67), channel_id=1, source_target_pairs={{0,3},{1,0},{2,1},{3,2},{4,7},{5,4},{6,5},{7,6},{8,11},{9,8},{10,9... | collective-permute-start | bytes 589832 | tf_op jit(solution)/shard_map/ppermute | solution.py:444
  91.5 11.7 %collective-permute-start.9 = (f32[48,384]{1,0:T(8,128)S(1)}, f32[48,384]{1,0:T(8,128)S(1)}, u32[]{:S(2)}, u32[]{:S(2)}) collective-permute-start(f32[48,384]{1,0:T(8,128)S(1)} %get-tuple-element.59), channel_id=1, source_target_pairs={{0,128},{128,0},{1,129},{129,1},{2,130},{130,2},{3,131},{131,3},{4... | collective-permute-start | bytes 221192 | tf_op jit(solution)/shard_map/ppermute | solution.py:559
  103.2 1.0 copy-start.8
  104.2 0.9 copy-start.9
  (1 other events, 0.6 us)

commit v7 on v6

--- a/solution.py
+++ b/solution.py
@@ -281,12 +281,12 @@
             ]
 
 
-def grads_kernel(owner_ref, conv_ref, *refs):
-    total_refs, (recv_from, joint_from, picked_from) = refs[:GRID], refs[GRID : GRID + 3]
-    query_refs, pair_refs = refs[GRID + 3 : 2 * GRID + 3], refs[2 * GRID + 3 : 3 * GRID + 3]
-    rest = refs[3 * GRID + 3 :]
-    query_out, pair_out, weight_out = rest[:GRID], rest[GRID : 2 * GRID], rest[2 * GRID]
+def token_kernel(owner_ref, conv_ref, *refs):
+    recv_from, joint_from, picked_from = refs[:3]
     (
+        dots_ref,
+        grad_out,
+        weight_out,
         frames,
         conv_big,
         ordered,
@@ -294,40 +294,28 @@
         joint_ref,
         picked_ref,
         weight_made,
-        dots_ref,
-        sums,
         out_held,
-        query_held,
-        key_held,
-        value_held,
-        grad_ref,
-        query_made,
-        pair_made,
+        grad_made,
         first_arrived,
         out_arrived,
-        query_arrived,
-        key_arrived,
-        value_arrived,
-        query_sent,
-        pair_sent,
+        grad_sent,
         weight_sent,
-    ) = rest[2 * GRID + 1 :]
-    sends_order = (2, 1, 3, 0)
+    ) = refs[GRID + 3 :]
     firsts = fetch(
         [recv_from, joint_from, picked_from], [recv_ref, joint_ref, picked_ref], first_arrived
     )
-    out_copies = fetch_halves(query_refs, 1, out_held, out_arrived)
-    query_copies = fetch_halves(query_refs, 0, query_held, query_arrived)
-    key_copies = fetch_halves(pair_refs, 0, key_held, key_arrived)
-    value_copies = fetch_halves(pair_refs, 1, value_held, value_arrived)
+    out_copies = fetch_halves(refs[3 : GRID + 3], 1, out_held, out_arrived)
     token_part(owner_ref, conv_ref, recv_ref, firsts[0], frames, conv_big, ordered)
     firsts[1].wait()
     ones = jnp.ones((8, 2 * HDIM), bf16)
+    sends = []
+    dots_ref[...] = jnp.zeros_like(dots_ref)
     outer = jnp.zeros((QUARTERS * LANES, FEATS), f32)
     for piece in range(GRID):
         rows = ordered[pl.ds(piece * ROWS_HERE, ROWS_HERE), :]
         grads = dot(rows, joint_ref[...]).astype(bf16)
-        grad_ref[piece] = grads
+        grad_made[piece] = grads
+        sends += fetch([grad_made.at[piece]], [grad_out.at[piece]], grad_sent.at[pl.ds(piece, 1)])
         out_copies[piece].wait()
         outs = out_held[piece]
         products = grads.astype(f32) * outs.astype(f32)
@@ -336,13 +324,44 @@
         for head in range(HEADS_HERE):
             columns = slice(head * HDIM, (head + 1) * HDIM)
             both = jnp.concatenate([high[:, columns], low[:, columns]], axis=1)
-            dots_ref[head, :, pl.ds(piece * ROWS_HERE, ROWS_HERE)] = dot(ones, both, NT)
+            dots_ref[pl.ds(head, 1), pl.ds(piece * ROWS_HERE, ROWS_HERE)] = dot(ones, both, NT)[
+                0:1
+            ]
         outer = outer + dot(rows, outs, TN)
     firsts[2].wait()
     weight_made[...] = (
         dot(picked_ref[...], outer.astype(bf16)) * (1.0 / math.sqrt(FRAMES * 64 * 4))
     ).astype(bf16)
-    sends = fetch([weight_made], [weight_out], weight_sent)
+    sends += fetch([weight_made], [weight_out], weight_sent)
+    for send in sends:
+        send.wait()
+
+
+def grads_kernel(dots_ref, *refs):
+    total_refs, grad_from = refs[:GRID], refs[GRID]
+    query_refs, pair_refs = refs[GRID + 1 : 2 * GRID + 1], refs[2 * GRID + 1 : 3 * GRID + 1]
+    rest = refs[3 * GRID + 1 :]
+    query_out, pair_out = rest[:GRID], rest[GRID : 2 * GRID]
+    (
+        sums,
+        query_held,
+        key_held,
+        value_held,
+        grad_ref,
+        query_made,
+        pair_made,
+        query_arrived,
+        key_arrived,
+        value_arrived,
+        grad_arrived,
+        query_sent,
+        pair_sent,
+    ) = rest[2 * GRID :]
+    sends_order = (2, 1, 3, 0)
+    query_copies = fetch_halves(query_refs, 0, query_held, query_arrived)
+    query_copies += fetch([grad_from], [grad_ref], grad_arrived)
+    key_copies = fetch_halves(pair_refs, 0, key_held, key_arrived)
+    value_copies = fetch_halves(pair_refs, 1, value_held, value_arrived)
     root = math.sqrt(FRAMES * 64)
     totals = []
     for piece in range(GRID):
@@ -355,6 +374,7 @@
     totals = jnp.concatenate(totals, axis=1)
     for copy in query_copies:
         copy.wait()
+    sends = []
     for other in sends_order:
         key_copies[other].wait()
         value_copies[other].wait()
@@ -367,7 +387,7 @@
             weights = jnp.exp2(
                 dot(key, query, NT) * (SCORE_SCALE * LOG2E) - totals[head : head + 1]
             )
-            dscore = (weights * (dot(value, grad, NT) - dots_ref[head, 0:1, :])).astype(bf16)
+            dscore = (weights * (dot(value, grad, NT) - dots_ref[pl.ds(head, 1), :])).astype(bf16)
             pair_made[other, 1, :, columns] = (dot(weights.astype(bf16), grad) * root).astype(bf16)
             pair_made[other, 0, :, columns] = (
                 dot(dscore, query) * (root * SCORE_SCALE)
@@ -418,7 +438,7 @@
         kernel,
         out_shape=out_shape,
         in_specs=in_specs,
-        out_specs=jax.tree.map(lambda _: out_spec or VMEM, out_shape),
+        out_specs=out_spec or jax.tree.map(lambda _: VMEM, out_shape),
         scratch_shapes=list(scratch),
         compiler_params=pltpu.CompilerParams(vmem_limit_bytes=limit * MIB),
         cost_estimate=pl.CostEstimate(flops=10**6, bytes_accessed=10**5, transcendentals=0),
@@ -517,13 +537,16 @@
         scratch=HELD * 2 + ARRIVED * 2,
         limit=24,
     )(*query_outs, *key_values)
+    totals, received = lax.optimization_barrier((totals, received))
     total_pieces = gather(totals, "hy")
-    outs = call(
-        grads_kernel,
-        tuple([shape((ROWS_HERE, FEATS), bf16)] * GRID)
-        + tuple([shape((2, ROWS_HERE, FEATS), bf16)] * GRID)
-        + (shape((768, FEATS), bf16),),
-        [SMEM] + [VMEM] * (1 + GRID) + [ANY] * (3 + 2 * GRID),
+    row_dots, grad_out, weight_part = call(
+        token_kernel,
+        (
+            shape((8, BLOCK), f32),
+            shape((GRID, ROWS_HERE, FEATS), bf16),
+            shape((768, FEATS), bf16),
+        ),
+        [SMEM, VMEM] + [ANY] * (3 + GRID),
         scratch=[
             pltpu.VMEM((FRAMES + 2, 16, LANES), bf16),
             pltpu.VMEM((3 * LANES, QUARTERS * LANES), bf16),
@@ -532,17 +555,27 @@
             pltpu.VMEM((QUARTERS * LANES, FEATS), bf16),
             pltpu.VMEM((768, QUARTERS * LANES), bf16),
             pltpu.VMEM((768, FEATS), bf16),
-            pltpu.VMEM((HEADS_HERE, 8, BLOCK), f32),
-            pltpu.VMEM((HEADS_HERE, HDIM, BLOCK), f32),
         ]
-        + HELD * 6
-        + [pltpu.VMEM((GRID, 2, ROWS_HERE, FEATS), bf16), pltpu.SemaphoreType.DMA((3,))]
-        + ARRIVED * 6
+        + HELD * 2
+        + [pltpu.SemaphoreType.DMA((3,))]
+        + ARRIVED * 2
         + [pltpu.SemaphoreType.DMA((1,))],
-        out_spec=ANY,
-        limit=56,
-    )(frame_owner, conv_w, *total_pieces, received, joint, picked, *query_outs, *key_values)
-    query_parts, pair_parts, weight_part = outs[:GRID], outs[GRID : 2 * GRID], outs[2 * GRID]
+        out_spec=(VMEM, ANY, ANY),
+    )(frame_owner, conv_w, received, joint, picked, *query_outs)
+    outs = call(
+        grads_kernel,
+        tuple([shape((ROWS_HERE, FEATS), bf16)] * GRID)
+        + tuple([shape((2, ROWS_HERE, FEATS), bf16)] * GRID),
+        [VMEM] * (1 + GRID) + [ANY] * (1 + 2 * GRID),
+        scratch=[pltpu.VMEM((HEADS_HERE, HDIM, BLOCK), f32)]
+        + HELD * 5
+        + [pltpu.VMEM((GRID, 2, ROWS_HERE, FEATS), bf16)]
+        + ARRIVED * 3
+        + [pltpu.SemaphoreType.DMA((1,))]
+        + ARRIVED * 2,
+        out_spec=tuple([ANY] * (2 * GRID)),
+    )(row_dots, *total_pieces, grad_out, *query_outs, *key_values)
+    query_parts, pair_parts = outs[:GRID], outs[GRID:]
     weight_parts = lax.all_to_all(
         weight_part.reshape(8, 2, 48, FEATS),
         ("core", "hx"),

time: 110 us -> 113 us (1.027); the launches traced: 108 us -> 113 us
  Pallas kernels: 34.7 us -> 38.6 us
  starting transfers between devices: 38.7 us -> 40 us
    pallas_call x0 -> x1, Pallas kernels: none -> 8.45 us  [per_device(): call(token_kernel, (shape((8, BLOCK), f32), shape((GRID, ROWS_HERE, FEATS...]
    all_to_all x1, waiting for transfers between devices: 0.01 us -> 5.69 us  [per_device(): lax.all_to_all(windows, ('tm', 'hx', 'hy'), split_axis=0, concat_axis=0,...]
    ppermute x6, waiting for transfers between devices: 12.9 us -> 7.8 us  [to_ahead(): lax.ppermute(block, axis, [(i, (i + step) % GRID) for i in range(GRID)])]
    pallas_call x1, Pallas kernels: 16.9 us -> 12.4 us  [per_device(): call(grads_kernel, tuple([shape((ROWS_HERE, FEATS), bf16)] * GRID) + tupl...]
    all_to_all x1, waiting for transfers between devices: 2.24 us -> 0.01 us  [per_device(): lax.all_to_all(weight_part.reshape(8, 2, 48, FEATS), ('core', 'hx'), spli...]
    ppermute x1, waiting for transfers between devices: 0.01 us -> 1.93 us  [per_device(): weight_other = lax.ppermute(weight_sent, 'zh', [(0, 1), (1, 0)])]
    ppermute x6, starting transfers between devices: 8.19 us -> 9.33 us  [to_ahead(): lax.ppermute(block, axis, [(i, (i + step) % GRID) for i in range(GRID)])]
  transfers between devices with their start and end apart: 18 -> 18, of which waited for: 11 -> 12; matrix products, arithmetic and copies ran while one was open for 1% -> 1% of each run, Pallas kernels for 14% -> 24%
where the time goes in v7:
time: 113 us
  starting transfers between devices  40 us (35%)
  Pallas kernels  38.6 us (34%)
  waiting for transfers between devices  27.6 us (24%)
  local copies, waits for them, and re-layouts  3.27 us (3%)
  other arithmetic  2.11 us (2%)
    pallas_call x1, Pallas kernels, per_device(): call(grads_kernel, tuple([shape((ROWS_HERE, FEATS), bf16)] * GRID) + tupl...  12.4 us
    ppermute x9, starting transfers between devices, from_ahead(): lax.ppermute(block, axis, [(i, (i - step) % GRID) for i in range(GRID)])  12.3 us
    ppermute x9, waiting for transfers between devices, from_ahead(): lax.ppermute(block, axis, [(i, (i - step) % GRID) for i in range(GRID)])  12.2 us
    all_to_all x1, starting transfers between devices, per_device(): lax.all_to_all(windows, ('tm', 'hx', 'hy'), split_axis=0, concat_axis=0,...  10.3 us
    ppermute x6, starting transfers between devices, to_ahead(): lax.ppermute(block, axis, [(i, (i + step) % GRID) for i in range(GRID)])  9.33 us
    pallas_call x1, Pallas kernels, per_device(): call(token_kernel, (shape((8, BLOCK), f32), shape((GRID, ROWS_HERE, FEATS...  8.45 us
    ppermute x6, waiting for transfers between devices, to_ahead(): lax.ppermute(block, axis, [(i, (i + step) % GRID) for i in range(GRID)])  7.8 us
    pallas_call x1, Pallas kernels, per_device(): call(weights_kernel, (shape((QUARTERS * LANES, FEATS), bf16), shape((768,...  6.17 us
  transfers between devices with their start and end apart: 18, of which 12 were waited for; matrix products, arithmetic and copies ran while one was open for 1% of the time, Pallas kernels for 24%

profile of v7, /device:TPU:24, one launch (start us, length us, event | category | flops | bytes accessed | tf_op | source)
XLA Modules:
  0.0 112.6 jit_solution(6737941996683913197)
XLA Ops:
  0.6 1.1 pad_maximum_fusion.refs_4_.refs_9_
  1.7 1.6 %collective-permute-start.1 = (bf16[256,768]{1,0:T(8,128)(2,1)S(1)}, bf16[256,768]{1,0:T(8,128)(2,1)S(1)}, u32[]{:S(2)}, u32[]{:S(2)}) collective-permute-start(bf16[256,768]{1,0:T(8,128)(2,1)S(1)} %pad_maximum_fusion.refs_4_.refs_9_), channel_id=1, source_target_pairs={{0,4},{4,8},{8,12},{12,0},{1,5},{5,9},{9,13},{13,1},{2,6},{6,10},{... | collective-permute-start | bytes 1179656 | tf_op jit(solution)/shard_map/ppermute | solution.py:460
  3.3 1.7 %collective-permute-start = (bf16[256,768]{1,0:T(8,128)(2,1)S(1)}, bf16[256,768]{1,0:T(8,128)(2,1)S(1)}, u32[]{:S(2)}, u32[]{:S(2)}) collective-permute-start(bf16[256,768]{1,0:T(8,128)(2,1)S(1)} %pad_maximum_fusion.refs_4_.refs_9_), channel_id=1, source_target_pairs={{0,12},{4,0},{8,4},{12,8},{1,13},{5,1},{9,5},{13,9},{2,14},{6,2},{... | collective-permute-start | bytes 1179656 | tf_op jit(solution)/shard_map/ppermute | solution.py:460
  5.0 1.1 pad_maximum_fusion.1.refs_0_.refs_3_.refs_5_
  6.1 2.0 %collective-permute-start.3 = (bf16[256,768]{1,0:T(8,128)(2,1)S(1)}, bf16[256,768]{1,0:T(8,128)(2,1)S(1)}, u32[]{:S(2)}, u32[]{:S(2)}) collective-permute-start(bf16[256,768]{1,0:T(8,128)(2,1)S(1)} %pad_maximum_fusion.1.refs_0_.refs_3_.refs_5_), channel_id=1, source_target_pairs={{0,1},{1,2},{2,3},{3,0},{4,5},{5,6},{6,7},{7,4},{8,9},{9,10},{10,1... | collective-permute-start | bytes 1179656 | tf_op jit(solution)/shard_map/ppermute | solution.py:460
  8.2 4.6 %shard_map.174 = bf16[64,16,128]{2,1,0:T(8,128)(2,1)} custom-call(bf16[1280]{0:T(1024)(128)(2,1)} %gain_ref.1, s32[1,64]{1,0:T(1,128)} %order_ref.1, bf16[256,1280]{1,0:T(8,128)(2,1)} %bitcast.7, bf16[256,1280]{1,0:T(8,128)(2,1)} %bitcast.8, bf16[128,588]{1,0:T(8,128)(2,1)} %constant.4.clone.refs_2_, bf16[588,1280]{1,0:T(8,128)(2,1)} %refs_3_.1, ...), custom_call_target="tpu_custom_call" | custom-call | flops 1000000 | bytes 100000 | tf_op jit(solution)/shard_map/pallas_call | solution.py:490
  12.8 1.1 collective-permute-done.1.refs_7_.refs_12_
  13.9 2.6 %collective-permute-done.3.refs_3_.refs_6_.refs_8_ = bf16[256,768]{1,0:T(8,128)(2,1)S(1)} collective-permute-done((bf16[256,768]{1,0:T(8,128)(2,1)S(1)}, bf16[256,768]{1,0:T(8,128)(2,1)S(1)}, u32[]{:S(2)}, u32[]{:S(2)}) %collective-permute-start.3) | collective-permute-done | bytes 393248 | tf_op jit(solution)/shard_map/ppermute | solution.py:460
  16.5 1.3 %collective-permute-done.2.refs_1_.refs_4_.refs_6_ = bf16[256,768]{1,0:T(8,128)(2,1)S(1)} collective-permute-done((bf16[256,768]{1,0:T(8,128)(2,1)S(1)}, bf16[256,768]{1,0:T(8,128)(2,1)S(1)}, u32[]{:S(2)}, u32[]{:S(2)}) %collective-permute-start.2) | collective-permute-done | bytes 393248 | tf_op jit(solution)/shard_map/ppermute | solution.py:460
  17.8 1.8 %collective-permute-start.4 = (bf16[256,768]{1,0:T(8,128)(2,1)S(1)}, bf16[256,768]{1,0:T(8,128)(2,1)S(1)}, u32[]{:S(2)}, u32[]{:S(2)}) collective-permute-start(bf16[256,768]{1,0:T(8,128)(2,1)S(1)} %pad_maximum_fusion.refs_4_.refs_9_), channel_id=1, source_target_pairs={{0,8},{4,12},{8,0},{12,4},{1,9},{5,13},{9,1},{13,5},{2,10},{6,14},... | collective-permute-start | bytes 1179656 | tf_op jit(solution)/shard_map/ppermute | solution.py:460
  19.6 1.2 %collective-permute-start.5 = (bf16[256,768]{1,0:T(8,128)(2,1)S(1)}, bf16[256,768]{1,0:T(8,128)(2,1)S(1)}, u32[]{:S(2)}, u32[]{:S(2)}) collective-permute-start(bf16[256,768]{1,0:T(8,128)(2,1)S(1)} %pad_maximum_fusion.1.refs_0_.refs_3_.refs_5_), channel_id=1, source_target_pairs={{0,2},{1,3},{2,0},{3,1},{4,6},{5,7},{6,4},{7,5},{8,10},{9,11},{10,... | collective-permute-start | bytes 1179656 | tf_op jit(solution)/shard_map/ppermute | solution.py:460
  20.8 6.2 %shard_map.175 = (bf16[512,384]{1,0:T(8,128)(2,1)}, bf16[768,512]{1,0:T(8,128)(2,1)}) custom-call(bf16[512,3072]{1,0:T(8,128)(2,1)} %join_from, bf16[384,3072]{1,0:T(8,128)(2,1)} %out_w_from.1), custom_call_target="tpu_custom_call" | custom-call | flops 1000000 | bytes 100000 | tf_op jit(solution)/shard_map/pallas_call | solution.py:517
  27.4 2.6 %collective-permute-done.5.refs_2_.refs_5_.refs_7_ = bf16[256,768]{1,0:T(8,128)(2,1)S(1)} collective-permute-done((bf16[256,768]{1,0:T(8,128)(2,1)S(1)}, bf16[256,768]{1,0:T(8,128)(2,1)S(1)}, u32[]{:S(2)}, u32[]{:S(2)}) %collective-permute-start.5) | collective-permute-done | bytes 393248 | tf_op jit(solution)/shard_map/ppermute | solution.py:460
  30.0 10.3 %all-to-all-start = ((bf16[64,16,128]{2,1,0:T(8,128)(2,1)}), bf16[64,16,128]{2,1,0:T(8,128)(2,1)S(1)}, u32[]{:S(2)}, u32[]{:S(2)}) async-start(bf16[64,16,128]{2,1,0:T(8,128)(2,1)} %shard_map.174), calls=%async_computation | async-start | bytes 524288 | tf_op jit(solution)/shard_map/all_to_all | solution.py:530
  40.4 4.1 %shard_map.176.refs_0_ = f32[8,1024]{1,0:T(8,128)S(1)} custom-call(bf16[256,768]{1,0:T(8,128)(2,1)S(1)} %pad_maximum_fusion.1.refs_0_.refs_3_.refs_5_, bf16[256,768]{1,0:T(8,128)(2,1)S(1)} %collective-permute-done.2.refs_1_.refs_4_.refs_6_, bf16[256,768]{1,0:T(8,128)(2,1)S(1)} %collective-permute-done.5.refs_2_.refs_5_.refs_7_, ...), custom_call_target="tpu_custom_call" | custom-call | flops 1000000 | bytes 100000 | tf_op jit(solution)/shard_map/pallas_call | solution.py:533
  44.6 5.7 %all-to-all-done.refs_0_ = bf16[64,16,128]{2,1,0:T(8,128)(2,1)S(1)} async-done(((bf16[64,16,128]{2,1,0:T(8,128)(2,1)}), bf16[64,16,128]{2,1,0:T(8,128)(2,1)S(1)}, u32[]{:S(2)}, u32[]{:S(2)}) %all-to-all-start) | async-done | bytes 262176 | tf_op jit(solution)/shard_map/all_to_all | solution.py:530
  51.0 8.5 %shard_map.177 = (f32[8,1024]{1,0:T(8,128)}, bf16[4,256,384]{2,1,0:T(8,128)(2,1)}, bf16[768,384]{1,0:T(8,128)(2,1)}) custom-call(s32[64]{0:T(128)} %owner_ref.1, bf16[81,128]{1,0:T(8,128)(2,1)} %conv_ref.1, bf16[64,16,128]{2,1,0:T(8,128)(2,1)} %copy-done.11, bf16[512,384]{1,0:T(8,128)(2,1)} %get-tuple-element.60.refs_1_, ...), custom_call_target="tpu_custom_call" | custom-call | flops 1000000 | bytes 100000 | tf_op jit(solution)/shard_map/pallas_call | solution.py:542
  59.4 3.5 %all-to-all-start.1 = ((bf16[8,2,48,384]{3,2,1,0:T(8,128)(2,1)}), bf16[8,2,48,384]{3,2,1,0:T(8,128)(2,1)S(1)}, u32[]{:S(2)}, u32[]{:S(2)}) async-start(bf16[8,2,48,384]{3,2,1,0:T(8,128)(2,1)} %bitcast.9), calls=%async_computation.1 | async-start | bytes 1179648 | tf_op jit(solution)/shard_map/all_to_all | solution.py:579
  63.0 2.4 %collective-permute-start.9 = (f32[8,1024]{1,0:T(8,128)S(1)}, f32[8,1024]{1,0:T(8,128)S(1)}, u32[]{:S(2)}, u32[]{:S(2)}) collective-permute-start(f32[8,1024]{1,0:T(8,128)S(1)} %shard_map.176.refs_0_), channel_id=1, source_target_pairs={{0,1},{1,2},{2,3},{3,0},{4,5},{5,6},{6,7},{7,4},{8,9},{9,10},{10,1... | collective-permute-start | bytes 98312 | tf_op jit(solution)/shard_map/ppermute | solution.py:460
  65.5 1.3 %collective-permute-start.7 = (f32[8,1024]{1,0:T(8,128)S(1)}, f32[8,1024]{1,0:T(8,128)S(1)}, u32[]{:S(2)}, u32[]{:S(2)}) collective-permute-start(f32[8,1024]{1,0:T(8,128)S(1)} %shard_map.176.refs_0_), channel_id=1, source_target_pairs={{0,3},{1,0},{2,1},{3,2},{4,7},{5,4},{6,5},{7,6},{8,11},{9,8},{10,9... | collective-permute-start | bytes 98312 | tf_op jit(solution)/shard_map/ppermute | solution.py:460
  67.2 3.7 %collective-permute-done.8.refs_2_ = f32[8,1024]{1,0:T(8,128)S(1)} collective-permute-done((f32[8,1024]{1,0:T(8,128)S(1)}, f32[8,1024]{1,0:T(8,128)S(1)}, u32[]{:S(2)}, u32[]{:S(2)}) %collective-permute-start.8) | collective-permute-done | bytes 32800 | tf_op jit(solution)/shard_map/ppermute | solution.py:460
  71.6 12.4 %shard_map.179 = (bf16[256,384]{1,0:T(8,128)(2,1)}, bf16[256,384]{1,0:T(8,128)(2,1)}, bf16[256,384]{1,0:T(8,128)(2,1)}, bf16[256,384]{1,0:T(8,128)(2,1)}, bf16[2...) custom-call(f32[8,1024]{1,0:T(8,128)} %get-tuple-element.65.dots_ref, ...), custom_call_target="tpu_custom_call" | custom-call | flops 1000000 | bytes 100000 | tf_op jit(solution)/shard_map/pallas_call | solution.py:565
  84.8 1.8 %collective-permute-start.10 = (bf16[2,256,384]{2,1,0:T(8,128)(2,1)}, bf16[2,256,384]{2,1,0:T(8,128)(2,1)S(1)}, u32[]{:S(2)}, u32[]{:S(2)}) collective-permute-start(bf16[2,256,384]{2,1,0:T(8,128)(2,1)} %get-tuple-element.69), channel_id=1, source_target_pairs={{0,4},{4,8},{8,12},{12,0},{1,5},{5,9},{9,13},{13,1},{2,6},{6,10},{... | collective-permute-start | bytes 1179656 | tf_op jit(solution)/shard_map/ppermute | solution.py:464
  86.7 2.7 %collective-permute-start.11 = (bf16[2,256,384]{2,1,0:T(8,128)(2,1)}, bf16[2,256,384]{2,1,0:T(8,128)(2,1)S(1)}, u32[]{:S(2)}, u32[]{:S(2)}) collective-permute-start(bf16[2,256,384]{2,1,0:T(8,128)(2,1)} %get-tuple-element.70), channel_id=1, source_target_pairs={{0,8},{4,12},{8,0},{12,4},{1,9},{5,13},{9,1},{13,5},{2,10},{6,14},... | collective-permute-start | bytes 1179656 | tf_op jit(solution)/shard_map/ppermute | solution.py:464
  89.4 1.4 %collective-permute-start.12 = (bf16[2,256,384]{2,1,0:T(8,128)(2,1)}, bf16[2,256,384]{2,1,0:T(8,128)(2,1)S(1)}, u32[]{:S(2)}, u32[]{:S(2)}) collective-permute-start(bf16[2,256,384]{2,1,0:T(8,128)(2,1)} %get-tuple-element.71), channel_id=1, source_target_pairs={{0,12},{4,0},{8,4},{12,8},{1,13},{5,1},{9,5},{13,9},{2,14},{6,2},{... | collective-permute-start | bytes 1179656 | tf_op jit(solution)/shard_map/ppermute | solution.py:464
  90.8 1.2 %collective-permute-start.14 = (bf16[256,384]{1,0:T(8,128)(2,1)}, bf16[256,384]{1,0:T(8,128)(2,1)S(1)}, u32[]{:S(2)}, u32[]{:S(2)}) collective-permute-start(bf16[256,384]{1,0:T(8,128)(2,1)} %get-tuple-element.74), channel_id=1, source_target_pairs={{0,2},{1,3},{2,0},{3,1},{4,6},{5,7},{6,4},{7,5},{8,10},{9,11},{10,... | collective-permute-start | bytes 589832 | tf_op jit(solution)/shard_map/ppermute | solution.py:464
  92.0 1.3 %collective-permute-start.15 = (bf16[256,384]{1,0:T(8,128)(2,1)}, bf16[256,384]{1,0:T(8,128)(2,1)S(1)}, u32[]{:S(2)}, u32[]{:S(2)}) collective-permute-start(bf16[256,384]{1,0:T(8,128)(2,1)} %get-tuple-element.75), channel_id=1, source_target_pairs={{0,3},{1,0},{2,1},{3,2},{4,7},{5,4},{6,5},{7,6},{8,11},{9,8},{10,9... | collective-permute-start | bytes 589832 | tf_op jit(solution)/shard_map/ppermute | solution.py:464
  93.4 6.0 %collective-permute-done.14.refs_6_ = bf16[256,384]{1,0:T(8,128)(2,1)S(1)} collective-permute-done((bf16[256,384]{1,0:T(8,128)(2,1)}, bf16[256,384]{1,0:T(8,128)(2,1)S(1)}, u32[]{:S(2)}, u32[]{:S(2)}) %collective-permute-start.14) | collective-permute-done | bytes 196640 | tf_op jit(solution)/shard_map/ppermute | solution.py:464
  99.4 4.5 %collective-permute-start.6 = (f32[48,384]{1,0:T(8,128)S(1)}, f32[48,384]{1,0:T(8,128)S(1)}, u32[]{:S(2)}, u32[]{:S(2)}) collective-permute-start(f32[48,384]{1,0:T(8,128)S(1)} %get-tuple-element.64), channel_id=1, source_target_pairs={{0,128},{128,0},{1,129},{129,1},{2,130},{130,2},{3,131},{131,3},{4... | collective-permute-start | bytes 221192 | tf_op jit(solution)/shard_map/ppermute | solution.py:592
  103.9 1.8 %collective-permute-done.11.refs_2_ = bf16[2,256,384]{2,1,0:T(8,128)(2,1)S(1)} collective-permute-done((bf16[2,256,384]{2,1,0:T(8,128)(2,1)}, bf16[2,256,384]{2,1,0:T(8,128)(2,1)S(1)}, u32[]{:S(2)}, u32[]{:S(2)}) %collective-permute-start.11) | collective-permute-done | bytes 393248 | tf_op jit(solution)/shard_map/ppermute | solution.py:464
  105.7 1.9 %collective-permute-done.6.other_ref = f32[48,384]{1,0:T(8,128)S(1)} collective-permute-done((f32[48,384]{1,0:T(8,128)S(1)}, f32[48,384]{1,0:T(8,128)S(1)}, u32[]{:S(2)}, u32[]{:S(2)}) %collective-permute-start.6) | collective-permute-done | bytes 73760 | tf_op jit(solution)/shard_map/ppermute | solution.py:592
  109.6 2.8 %shard_map.180 = (bf16[1,256,384]{2,1,0:T(8,128)(2,1)}, bf16[1,256,384]{2,1,0:T(8,128)(2,1)}, bf16[1,256,384]{2,1,0:T(8,128)(2,1)}, f32[48,384]{1,0:T(8,128)}) custom-call(f32[48,384]{1,0:T(8,128)S(1)} %get-tuple-element.63.kept_ref, f32[48,384]{1,0:T(8,128)S(1)} %collective-permute-done.6.other_ref, bf16[2,256,384]{2,1,0:T(8,128)(2,1)S(1)} %copy-done.8, ...), custom_call_target="tpu_custom_call" | custom-call | flops 1000000 | bytes 100000 | tf_op jit(solution)/shard_map/pallas_call | solution.py:601
  (43 shorter events, 5.3 us)
Async XLA Ops:
  1.7 38.6 %copy-start.1 = (bf16[256,768]{1,0:T(8,128)(2,1)}, bf16[256,768]{1,0:T(8,128)(2,1)S(1)}, u32[]{:S(2)}) copy-start(bf16[256,768]{1,0:T(8,128)(2,1)S(1)} %pad_maximum_fusion.refs_4_.refs_9_) | copy-start | bytes 1179652
  1.7 12.1 %collective-permute-start.1 = (bf16[256,768]{1,0:T(8,128)(2,1)S(1)}, bf16[256,768]{1,0:T(8,128)(2,1)S(1)}, u32[]{:S(2)}, u32[]{:S(2)}) collective-permute-start(bf16[256,768]{1,0:T(8,128)(2,1)S(1)} %pad_maximum_fusion.refs_4_.refs_9_), channel_id=1, source_target_pairs={{0,4},{4,8},{8,12},{12,0},{1,5},{5,9},{9,13},{13,1},{2,6},{6,10},{... | collective-permute-start | bytes 1179656 | tf_op jit(solution)/shard_map/ppermute | solution.py:460
  3.3 10.6 %collective-permute-start = (bf16[256,768]{1,0:T(8,128)(2,1)S(1)}, bf16[256,768]{1,0:T(8,128)(2,1)S(1)}, u32[]{:S(2)}, u32[]{:S(2)}) collective-permute-start(bf16[256,768]{1,0:T(8,128)(2,1)S(1)} %pad_maximum_fusion.refs_4_.refs_9_), channel_id=1, source_target_pairs={{0,12},{4,0},{8,4},{12,8},{1,13},{5,1},{9,5},{13,9},{2,14},{6,2},{... | collective-permute-start | bytes 1179656 | tf_op jit(solution)/shard_map/ppermute | solution.py:460
  6.1 34.3 %copy-start = (bf16[256,768]{1,0:T(8,128)(2,1)}, bf16[256,768]{1,0:T(8,128)(2,1)S(1)}, u32[]{:S(2)}) copy-start(bf16[256,768]{1,0:T(8,128)(2,1)S(1)} %pad_maximum_fusion.1.refs_0_.refs_3_.refs_5_) | copy-start | bytes 1179652
  6.1 10.4 %collective-permute-start.3 = (bf16[256,768]{1,0:T(8,128)(2,1)S(1)}, bf16[256,768]{1,0:T(8,128)(2,1)S(1)}, u32[]{:S(2)}, u32[]{:S(2)}) collective-permute-start(bf16[256,768]{1,0:T(8,128)(2,1)S(1)} %pad_maximum_fusion.1.refs_0_.refs_3_.refs_5_), channel_id=1, source_target_pairs={{0,1},{1,2},{2,3},{3,0},{4,5},{5,6},{6,7},{7,4},{8,9},{9,10},{10,1... | collective-permute-start | bytes 1179656 | tf_op jit(solution)/shard_map/ppermute | solution.py:460
  8.1 9.6 %collective-permute-start.2 = (bf16[256,768]{1,0:T(8,128)(2,1)S(1)}, bf16[256,768]{1,0:T(8,128)(2,1)S(1)}, u32[]{:S(2)}, u32[]{:S(2)}) collective-permute-start(bf16[256,768]{1,0:T(8,128)(2,1)S(1)} %pad_maximum_fusion.1.refs_0_.refs_3_.refs_5_), channel_id=1, source_target_pairs={{0,3},{1,0},{2,1},{3,2},{4,7},{5,4},{6,5},{7,6},{8,11},{9,8},{10,9... | collective-permute-start | bytes 1179656 | tf_op jit(solution)/shard_map/ppermute | solution.py:460
  13.8 26.5 %copy-start.5 = (bf16[256,768]{1,0:T(8,128)(2,1)}, bf16[256,768]{1,0:T(8,128)(2,1)S(1)}, u32[]{:S(2)}) copy-start(bf16[256,768]{1,0:T(8,128)(2,1)S(1)} %collective-permute-done.1.refs_7_.refs_12_) | copy-start | bytes 1179652
  13.8 26.5 %copy-start.6 = (bf16[256,768]{1,0:T(8,128)(2,1)}, bf16[256,768]{1,0:T(8,128)(2,1)S(1)}, u32[]{:S(2)}) copy-start(bf16[256,768]{1,0:T(8,128)(2,1)S(1)} %collective-permute-done.refs_5_.refs_10_) | copy-start | bytes 1179652
  16.5 23.9 %copy-start.2 = (bf16[256,768]{1,0:T(8,128)(2,1)}, bf16[256,768]{1,0:T(8,128)(2,1)S(1)}, u32[]{:S(2)}) copy-start(bf16[256,768]{1,0:T(8,128)(2,1)S(1)} %collective-permute-done.3.refs_3_.refs_6_.refs_8_) | copy-start | bytes 1179652
  17.8 22.6 %copy-start.3 = (bf16[256,768]{1,0:T(8,128)(2,1)}, bf16[256,768]{1,0:T(8,128)(2,1)S(1)}, u32[]{:S(2)}) copy-start(bf16[256,768]{1,0:T(8,128)(2,1)S(1)} %collective-permute-done.2.refs_1_.refs_4_.refs_6_) | copy-start | bytes 1179652
  17.8 9.7 %collective-permute-start.4 = (bf16[256,768]{1,0:T(8,128)(2,1)S(1)}, bf16[256,768]{1,0:T(8,128)(2,1)S(1)}, u32[]{:S(2)}, u32[]{:S(2)}) collective-permute-start(bf16[256,768]{1,0:T(8,128)(2,1)S(1)} %pad_maximum_fusion.refs_4_.refs_9_), channel_id=1, source_target_pairs={{0,8},{4,12},{8,0},{12,4},{1,9},{5,13},{9,1},{13,5},{2,10},{6,14},... | collective-permute-start | bytes 1179656 | tf_op jit(solution)/shard_map/ppermute | solution.py:460
  19.6 10.5 %collective-permute-start.5 = (bf16[256,768]{1,0:T(8,128)(2,1)S(1)}, bf16[256,768]{1,0:T(8,128)(2,1)S(1)}, u32[]{:S(2)}, u32[]{:S(2)}) collective-permute-start(bf16[256,768]{1,0:T(8,128)(2,1)S(1)} %pad_maximum_fusion.1.refs_0_.refs_3_.refs_5_), channel_id=1, source_target_pairs={{0,2},{1,3},{2,0},{3,1},{4,6},{5,7},{6,4},{7,5},{8,10},{9,11},{10,... | collective-permute-start | bytes 1179656 | tf_op jit(solution)/shard_map/ppermute | solution.py:460
  27.4 32.0 %copy-start.7 = (bf16[256,768]{1,0:T(8,128)(2,1)}, bf16[256,768]{1,0:T(8,128)(2,1)S(1)}, u32[]{:S(2)}) copy-start(bf16[256,768]{1,0:T(8,128)(2,1)S(1)} %collective-permute-done.4.refs_6_.refs_11_) | copy-start | bytes 1179652
  30.0 20.2 %copy-start.4 = (bf16[256,768]{1,0:T(8,128)(2,1)}, bf16[256,768]{1,0:T(8,128)(2,1)S(1)}, u32[]{:S(2)}) copy-start(bf16[256,768]{1,0:T(8,128)(2,1)S(1)} %collective-permute-done.5.refs_2_.refs_5_.refs_7_) | copy-start | bytes 1179652
  30.0 20.2 %all-to-all-start = ((bf16[64,16,128]{2,1,0:T(8,128)(2,1)}), bf16[64,16,128]{2,1,0:T(8,128)(2,1)S(1)}, u32[]{:S(2)}, u32[]{:S(2)}) async-start(bf16[64,16,128]{2,1,0:T(8,128)(2,1)} %shard_map.174), calls=%async_computation | async-start | bytes 524288 | tf_op jit(solution)/shard_map/all_to_all | solution.py:530
  44.5 26.5 %copy-start.10 = (f32[8,1024]{1,0:T(8,128)}, f32[8,1024]{1,0:T(8,128)S(1)}, u32[]{:S(2)}) copy-start(f32[8,1024]{1,0:T(8,128)S(1)} %shard_map.176.refs_0_) | copy-start | bytes 98308
  50.2 0.7 copy-start.11
  59.4 33.9 %all-to-all-start.1 = ((bf16[8,2,48,384]{3,2,1,0:T(8,128)(2,1)}), bf16[8,2,48,384]{3,2,1,0:T(8,128)(2,1)S(1)}, u32[]{:S(2)}, u32[]{:S(2)}) async-start(bf16[8,2,48,384]{3,2,1,0:T(8,128)(2,1)} %bitcast.9), calls=%async_computation.1 | async-start | bytes 1179648 | tf_op jit(solution)/shard_map/all_to_all | solution.py:579
  63.0 4.2 %collective-permute-start.9 = (f32[8,1024]{1,0:T(8,128)S(1)}, f32[8,1024]{1,0:T(8,128)S(1)}, u32[]{:S(2)}, u32[]{:S(2)}) collective-permute-start(f32[8,1024]{1,0:T(8,128)S(1)} %shard_map.176.refs_0_), channel_id=1, source_target_pairs={{0,1},{1,2},{2,3},{3,0},{4,5},{5,6},{6,7},{7,4},{8,9},{9,10},{10,1... | collective-permute-start | bytes 98312 | tf_op jit(solution)/shard_map/ppermute | solution.py:460
  65.4 5.5 %collective-permute-start.8 = (f32[8,1024]{1,0:T(8,128)S(1)}, f32[8,1024]{1,0:T(8,128)S(1)}, u32[]{:S(2)}, u32[]{:S(2)}) collective-permute-start(f32[8,1024]{1,0:T(8,128)S(1)} %shard_map.176.refs_0_), channel_id=1, source_target_pairs={{0,2},{1,3},{2,0},{3,1},{4,6},{5,7},{6,4},{7,5},{8,10},{9,11},{10,... | collective-permute-start | bytes 98312 | tf_op jit(solution)/shard_map/ppermute | solution.py:460
  65.5 5.5 %collective-permute-start.7 = (f32[8,1024]{1,0:T(8,128)S(1)}, f32[8,1024]{1,0:T(8,128)S(1)}, u32[]{:S(2)}, u32[]{:S(2)}) collective-permute-start(f32[8,1024]{1,0:T(8,128)S(1)} %shard_map.176.refs_0_), channel_id=1, source_target_pairs={{0,3},{1,0},{2,1},{3,2},{4,7},{5,4},{6,5},{7,6},{8,11},{9,8},{10,9... | collective-permute-start | bytes 98312 | tf_op jit(solution)/shard_map/ppermute | solution.py:460
  67.2 3.8 %copy-start.12 = (f32[8,1024]{1,0:T(8,128)}, f32[8,1024]{1,0:T(8,128)S(1)}, u32[]{:S(2)}) copy-start(f32[8,1024]{1,0:T(8,128)S(1)} %collective-permute-done.9.refs_3_) | copy-start | bytes 98308
  70.9 0.6 copy-start.13
  84.0 8.0 %collective-permute-start.13 = (bf16[256,384]{1,0:T(8,128)(2,1)}, bf16[256,384]{1,0:T(8,128)(2,1)S(1)}, u32[]{:S(2)}, u32[]{:S(2)}) collective-permute-start(bf16[256,384]{1,0:T(8,128)(2,1)} %get-tuple-element.73), channel_id=1, source_target_pairs={{0,1},{1,2},{2,3},{3,0},{4,5},{5,6},{6,7},{7,4},{8,9},{9,10},{10,1... | collective-permute-start | bytes 589832 | tf_op jit(solution)/shard_map/ppermute | solution.py:464
  84.8 19.1 %collective-permute-start.10 = (bf16[2,256,384]{2,1,0:T(8,128)(2,1)}, bf16[2,256,384]{2,1,0:T(8,128)(2,1)S(1)}, u32[]{:S(2)}, u32[]{:S(2)}) collective-permute-start(bf16[2,256,384]{2,1,0:T(8,128)(2,1)} %get-tuple-element.69), channel_id=1, source_target_pairs={{0,4},{4,8},{8,12},{12,0},{1,5},{5,9},{9,13},{13,1},{2,6},{6,10},{... | collective-permute-start | bytes 1179656 | tf_op jit(solution)/shard_map/ppermute | solution.py:464
  86.7 19.1 %collective-permute-start.11 = (bf16[2,256,384]{2,1,0:T(8,128)(2,1)}, bf16[2,256,384]{2,1,0:T(8,128)(2,1)S(1)}, u32[]{:S(2)}, u32[]{:S(2)}) collective-permute-start(bf16[2,256,384]{2,1,0:T(8,128)(2,1)} %get-tuple-element.70), channel_id=1, source_target_pairs={{0,8},{4,12},{8,0},{12,4},{1,9},{5,13},{9,1},{13,5},{2,10},{6,14},... | collective-permute-start | bytes 1179656 | tf_op jit(solution)/shard_map/ppermute | solution.py:464
  89.4 16.4 %collective-permute-start.12 = (bf16[2,256,384]{2,1,0:T(8,128)(2,1)}, bf16[2,256,384]{2,1,0:T(8,128)(2,1)S(1)}, u32[]{:S(2)}, u32[]{:S(2)}) collective-permute-start(bf16[2,256,384]{2,1,0:T(8,128)(2,1)} %get-tuple-element.71), channel_id=1, source_target_pairs={{0,12},{4,0},{8,4},{12,8},{1,13},{5,1},{9,5},{13,9},{2,14},{6,2},{... | collective-permute-start | bytes 1179656 | tf_op jit(solution)/shard_map/ppermute | solution.py:464
  90.8 8.6 %collective-permute-start.14 = (bf16[256,384]{1,0:T(8,128)(2,1)}, bf16[256,384]{1,0:T(8,128)(2,1)S(1)}, u32[]{:S(2)}, u32[]{:S(2)}) collective-permute-start(bf16[256,384]{1,0:T(8,128)(2,1)} %get-tuple-element.74), channel_id=1, source_target_pairs={{0,2},{1,3},{2,0},{3,1},{4,6},{5,7},{6,4},{7,5},{8,10},{9,11},{10,... | collective-permute-start | bytes 589832 | tf_op jit(solution)/shard_map/ppermute | solution.py:464
  92.0 11.9 %collective-permute-start.15 = (bf16[256,384]{1,0:T(8,128)(2,1)}, bf16[256,384]{1,0:T(8,128)(2,1)S(1)}, u32[]{:S(2)}, u32[]{:S(2)}) collective-permute-start(bf16[256,384]{1,0:T(8,128)(2,1)} %get-tuple-element.75), channel_id=1, source_target_pairs={{0,3},{1,0},{2,1},{3,2},{4,7},{5,4},{6,5},{7,6},{8,11},{9,8},{10,9... | collective-permute-start | bytes 589832 | tf_op jit(solution)/shard_map/ppermute | solution.py:464
  99.4 8.3 %collective-permute-start.6 = (f32[48,384]{1,0:T(8,128)S(1)}, f32[48,384]{1,0:T(8,128)S(1)}, u32[]{:S(2)}, u32[]{:S(2)}) collective-permute-start(f32[48,384]{1,0:T(8,128)S(1)} %get-tuple-element.64), channel_id=1, source_target_pairs={{0,128},{128,0},{1,129},{129,1},{2,130},{130,2},{3,131},{131,3},{4... | collective-permute-start | bytes 221192 | tf_op jit(solution)/shard_map/ppermute | solution.py:592
  107.7 1.0 copy-start.8
  108.7 0.9 copy-start.9
  (1 other events, 0.6 us)

commit v8 on v7

--- a/solution.py
+++ b/solution.py
@@ -204,7 +204,7 @@
         rows = dot(pick, join_ref[:, pl.ds(pair * 384, 384)], NT).astype(bf16)
         z, core, x = pair // 4, (pair % 4) // 2, (pair % 2) * 2
         for step in range(2):
-            picked_ref[pl.ds((core * GRID + x + step) * 96 + z * 48, 48), :] = rows[
+            picked_ref[pl.ds((x + step) * 192 + (z * 2 + core) * 48, 48), :] = rows[
                 step * 48 : (step + 1) * 48
             ]
 
@@ -360,8 +360,18 @@
     sends_order = (2, 1, 3, 0)
     query_copies = fetch_halves(query_refs, 0, query_held, query_arrived)
     query_copies += fetch([grad_from], [grad_ref], grad_arrived)
-    key_copies = fetch_halves(pair_refs, 0, key_held, key_arrived)
-    value_copies = fetch_halves(pair_refs, 1, value_held, value_arrived)
+    key_copies, value_copies = (
+        [
+            pltpu.make_async_copy(
+                pair_refs[other].at[:, pl.ds(half * FEATS, FEATS)],
+                held.at[other],
+                arrived.at[other],
+            )
+            for other in range(GRID)
+        ]
+        for half, held, arrived in ((0, key_held, key_arrived), (1, value_held, value_arrived))
+    )
+    start([key_copies[sends_order[0]], value_copies[sends_order[0]]])
     root = math.sqrt(FRAMES * 64)
     totals = []
     for piece in range(GRID):
@@ -374,6 +384,8 @@
     totals = jnp.concatenate(totals, axis=1)
     for copy in query_copies:
         copy.wait()
+    for other in sends_order[1:]:
+        start([key_copies[other], value_copies[other]])
     sends = []
     for other in sends_order:
         key_copies[other].wait()
@@ -412,18 +424,12 @@
         send.wait()
 
 
-def half_kernel(parts_ref, kept_ref, sent_ref):
-    here_z = lax.axis_index("zh")
-    for out_ref, half in ((kept_ref, here_z), (sent_ref, 1 - here_z)):
-        out_ref[...] = sum(parts_ref[source, half].astype(f32) for source in range(2 * GRID))
-
-
-def sum_kernel(kept_ref, other_ref, *refs):
+def sum_kernel(parts_ref, *refs):
     pair_refs, query_refs = refs[:GRID], refs[GRID : 2 * GRID]
     query_out, key_out, value_out, weight_out, query_held, pair_held, *arrived = refs[2 * GRID :]
     pair_copies = fetch(pair_refs, [pair_held.at[step] for step in range(GRID)], arrived[1])
     query_copies = fetch(query_refs, [query_held.at[step] for step in range(GRID)], arrived[0])
-    weight_out[...] = kept_ref[...] + other_ref[...]
+    weight_out[...] = sum(parts_ref[source].astype(f32) for source in range(4))
     for copy in query_copies:
         copy.wait()
     query_out[0] = sum(query_held[step].astype(f32) for step in range(GRID)).astype(bf16)
@@ -448,6 +454,7 @@
 VMEM = pl.BlockSpec(memory_space=pltpu.VMEM)
 SMEM = pl.BlockSpec(memory_space=pltpu.SMEM)
 ANY = pl.BlockSpec(memory_space=pl.ANY)
+HBM = pl.BlockSpec(memory_space=pltpu.HBM)
 HELD = [pltpu.VMEM((GRID, ROWS_HERE, FEATS), bf16)]
 ARRIVED = [pltpu.SemaphoreType.DMA((GRID,))]
 
@@ -576,20 +583,14 @@
         out_spec=tuple([ANY] * (2 * GRID)),
     )(row_dots, *total_pieces, grad_out, *query_outs, *key_values)
     query_parts, pair_parts = outs[:GRID], outs[GRID:]
+    weight_part = lax.psum_scatter(weight_part, "hx", scatter_dimension=0, tiled=True)
     weight_parts = lax.all_to_all(
-        weight_part.reshape(8, 2, 48, FEATS),
-        ("core", "hx"),
+        weight_part.reshape(4, 48, FEATS),
+        ("zh", "core"),
         split_axis=0,
         concat_axis=0,
         tiled=True,
     )
-    weight_kept, weight_sent = call(
-        half_kernel,
-        (shape((48, FEATS), f32), shape((48, FEATS), f32)),
-        [VMEM],
-        limit=8,
-    )(weight_parts)
-    weight_other = lax.ppermute(weight_sent, "zh", [(0, 1), (1, 0)])
     pair_back = [pair_parts[0]] + [
         to_ahead(pair_parts[step], "hx", step) for step in range(1, GRID)
     ]
@@ -601,10 +602,10 @@
     return call(
         sum_kernel,
         (rows, rows, rows, shape((48, FEATS), f32)),
-        [VMEM] * 2 + [ANY] * (2 * GRID),
+        [VMEM] + ([HBM] + [ANY] * (GRID - 1)) * 2,
         scratch=HELD + [pltpu.VMEM((GRID, 2, ROWS_HERE, FEATS), bf16)] + ARRIVED * 2,
         limit=8,
-    )(weight_kept, weight_other, *pair_back, *query_back)
+    )(weight_parts, *pair_back, *query_back)
 
 
 def solution(mesh):

time: 113 us -> 123 us (1.088)
  between operations: 0.98 us -> 14.2 us
  starting transfers between devices: 40 us -> 35.2 us
    ppermute x1 -> x0, starting transfers between devices: 4.5 us -> none  [per_device(): weight_other = lax.ppermute(weight_sent, 'zh', [(0, 1), (1, 0)])]
    ppermute x6, waiting for transfers between devices: 7.8 us -> 10.8 us  [to_ahead(): lax.ppermute(block, axis, [(i, (i + step) % GRID) for i in range(GRID)])]
    ppermute x6, starting transfers between devices: 9.33 us -> 6.63 us  [to_ahead(): lax.ppermute(block, axis, [(i, (i + step) % GRID) for i in range(GRID)])]
    all_to_all x1, starting transfers between devices: 3.55 us -> 5.78 us  [per_device(): lax.all_to_all(weight_part.reshape(4, 48, FEATS), ('zh', 'core'), split_a...]
    ppermute x1 -> x0, waiting for transfers between devices: 1.93 us -> none  [per_device(): weight_other = lax.ppermute(weight_sent, 'zh', [(0, 1), (1, 0)])]
    pallas_call x2 -> x1, Pallas kernels: 2.9 us -> 2.83 us  [per_device(): call(sum_kernel, (rows, rows, rows, shape((48, FEATS), f32)), [VMEM] + ([...]
  transfers between devices with their start and end apart: 18 -> 18, of which waited for: 12 -> 11; matrix products, arithmetic and copies ran while one was open for 1% -> 1% of each run, Pallas kernels for 24% -> 22%
where the time goes in v8:
time: 123 us; the launch traced here: 121 us
  Pallas kernels  38.2 us (31%)
  starting transfers between devices  35.2 us (29%)
  waiting for transfers between devices  28.5 us (23%)
  between operations  14.2 us (12%)
  local copies, waits for them, and re-layouts  3.27 us (3%)
  other arithmetic  2.11 us (2%)
    ppermute x9, starting transfers between devices, from_ahead(): lax.ppermute(block, axis, [(i, (i - step) % GRID) for i in range(GRID)])  12.3 us
    ppermute x9, waiting for transfers between devices, from_ahead(): lax.ppermute(block, axis, [(i, (i - step) % GRID) for i in range(GRID)])  12.2 us
    pallas_call x1, Pallas kernels, per_device(): call(grads_kernel, tuple([shape((ROWS_HERE, FEATS), bf16)] * GRID) + tupl...  12 us
    ppermute x6, waiting for transfers between devices, to_ahead(): lax.ppermute(block, axis, [(i, (i + step) % GRID) for i in range(GRID)])  10.8 us
    all_to_all x1, starting transfers between devices, per_device(): lax.all_to_all(windows, ('tm', 'hx', 'hy'), split_axis=0, concat_axis=0,...  10.3 us
    pallas_call x1, Pallas kernels, per_device(): call(token_kernel, (shape((8, BLOCK), f32), shape((GRID, ROWS_HERE, FEATS...  8.46 us
    ppermute x6, starting transfers between devices, to_ahead(): lax.ppermute(block, axis, [(i, (i + step) % GRID) for i in range(GRID)])  6.63 us
    pallas_call x1, Pallas kernels, per_device(): call(weights_kernel, (shape((QUARTERS * LANES, FEATS), bf16), shape((768,...  6.16 us
  transfers between devices with their start and end apart: 18, of which 11 were waited for; matrix products, arithmetic and copies ran while one was open for 1% of the time, Pallas kernels for 22%

profile of v8, /device:TPU:24, one launch (start us, length us, event | category | flops | bytes accessed | tf_op | source)
XLA Modules:
  0.0 121.5 jit_solution(12286833922905141387)
XLA Ops:
  7.2 1.1 pad_maximum_fusion.refs_4_.refs_9_
  8.2 1.6 %collective-permute-start.1 = (bf16[256,768]{1,0:T(8,128)(2,1)S(1)}, bf16[256,768]{1,0:T(8,128)(2,1)S(1)}, u32[]{:S(2)}, u32[]{:S(2)}) collective-permute-start(bf16[256,768]{1,0:T(8,128)(2,1)S(1)} %pad_maximum_fusion.refs_4_.refs_9_), channel_id=1, source_target_pairs={{0,4},{4,8},{8,12},{12,0},{1,5},{5,9},{9,13},{13,1},{2,6},{6,10},{... | collective-permute-start | bytes 1179656 | tf_op jit(solution)/shard_map/ppermute | solution.py:467
  9.8 1.7 %collective-permute-start = (bf16[256,768]{1,0:T(8,128)(2,1)S(1)}, bf16[256,768]{1,0:T(8,128)(2,1)S(1)}, u32[]{:S(2)}, u32[]{:S(2)}) collective-permute-start(bf16[256,768]{1,0:T(8,128)(2,1)S(1)} %pad_maximum_fusion.refs_4_.refs_9_), channel_id=1, source_target_pairs={{0,12},{4,0},{8,4},{12,8},{1,13},{5,1},{9,5},{13,9},{2,14},{6,2},{... | collective-permute-start | bytes 1179656 | tf_op jit(solution)/shard_map/ppermute | solution.py:467
  11.5 1.1 pad_maximum_fusion.1.refs_0_.refs_3_.refs_5_
  12.6 2.0 %collective-permute-start.3 = (bf16[256,768]{1,0:T(8,128)(2,1)S(1)}, bf16[256,768]{1,0:T(8,128)(2,1)S(1)}, u32[]{:S(2)}, u32[]{:S(2)}) collective-permute-start(bf16[256,768]{1,0:T(8,128)(2,1)S(1)} %pad_maximum_fusion.1.refs_0_.refs_3_.refs_5_), channel_id=1, source_target_pairs={{0,1},{1,2},{2,3},{3,0},{4,5},{5,6},{6,7},{7,4},{8,9},{9,10},{10,1... | collective-permute-start | bytes 1179656 | tf_op jit(solution)/shard_map/ppermute | solution.py:467
  14.7 4.6 %shard_map.174 = bf16[64,16,128]{2,1,0:T(8,128)(2,1)} custom-call(bf16[1280]{0:T(1024)(128)(2,1)} %gain_ref.1, s32[1,64]{1,0:T(1,128)} %order_ref.1, bf16[256,1280]{1,0:T(8,128)(2,1)} %bitcast.7, bf16[256,1280]{1,0:T(8,128)(2,1)} %bitcast.8, bf16[128,588]{1,0:T(8,128)(2,1)} %constant.4.clone.refs_2_, bf16[588,1280]{1,0:T(8,128)(2,1)} %refs_3_.1, ...), custom_call_target="tpu_custom_call" | custom-call | flops 1000000 | bytes 100000 | tf_op jit(solution)/shard_map/pallas_call | solution.py:497
  19.3 1.1 collective-permute-done.1.refs_7_.refs_12_
  20.4 2.6 %collective-permute-done.3.refs_3_.refs_6_.refs_8_ = bf16[256,768]{1,0:T(8,128)(2,1)S(1)} collective-permute-done((bf16[256,768]{1,0:T(8,128)(2,1)S(1)}, bf16[256,768]{1,0:T(8,128)(2,1)S(1)}, u32[]{:S(2)}, u32[]{:S(2)}) %collective-permute-start.3) | collective-permute-done | bytes 393248 | tf_op jit(solution)/shard_map/ppermute | solution.py:467
  23.0 1.3 %collective-permute-done.2.refs_1_.refs_4_.refs_6_ = bf16[256,768]{1,0:T(8,128)(2,1)S(1)} collective-permute-done((bf16[256,768]{1,0:T(8,128)(2,1)S(1)}, bf16[256,768]{1,0:T(8,128)(2,1)S(1)}, u32[]{:S(2)}, u32[]{:S(2)}) %collective-permute-start.2) | collective-permute-done | bytes 393248 | tf_op jit(solution)/shard_map/ppermute | solution.py:467
  24.3 1.8 %collective-permute-start.4 = (bf16[256,768]{1,0:T(8,128)(2,1)S(1)}, bf16[256,768]{1,0:T(8,128)(2,1)S(1)}, u32[]{:S(2)}, u32[]{:S(2)}) collective-permute-start(bf16[256,768]{1,0:T(8,128)(2,1)S(1)} %pad_maximum_fusion.refs_4_.refs_9_), channel_id=1, source_target_pairs={{0,8},{4,12},{8,0},{12,4},{1,9},{5,13},{9,1},{13,5},{2,10},{6,14},... | collective-permute-start | bytes 1179656 | tf_op jit(solution)/shard_map/ppermute | solution.py:467
  26.1 1.2 %collective-permute-start.5 = (bf16[256,768]{1,0:T(8,128)(2,1)S(1)}, bf16[256,768]{1,0:T(8,128)(2,1)S(1)}, u32[]{:S(2)}, u32[]{:S(2)}) collective-permute-start(bf16[256,768]{1,0:T(8,128)(2,1)S(1)} %pad_maximum_fusion.1.refs_0_.refs_3_.refs_5_), channel_id=1, source_target_pairs={{0,2},{1,3},{2,0},{3,1},{4,6},{5,7},{6,4},{7,5},{8,10},{9,11},{10,... | collective-permute-start | bytes 1179656 | tf_op jit(solution)/shard_map/ppermute | solution.py:467
  27.3 6.2 %shard_map.175 = (bf16[512,384]{1,0:T(8,128)(2,1)}, bf16[768,512]{1,0:T(8,128)(2,1)}) custom-call(bf16[512,3072]{1,0:T(8,128)(2,1)} %join_from, bf16[384,3072]{1,0:T(8,128)(2,1)} %out_w_from.1), custom_call_target="tpu_custom_call" | custom-call | flops 1000000 | bytes 100000 | tf_op jit(solution)/shard_map/pallas_call | solution.py:524
  34.0 2.6 %collective-permute-done.5.refs_2_.refs_5_.refs_7_ = bf16[256,768]{1,0:T(8,128)(2,1)S(1)} collective-permute-done((bf16[256,768]{1,0:T(8,128)(2,1)S(1)}, bf16[256,768]{1,0:T(8,128)(2,1)S(1)}, u32[]{:S(2)}, u32[]{:S(2)}) %collective-permute-start.5) | collective-permute-done | bytes 393248 | tf_op jit(solution)/shard_map/ppermute | solution.py:467
  36.6 10.3 %all-to-all-start = ((bf16[64,16,128]{2,1,0:T(8,128)(2,1)}), bf16[64,16,128]{2,1,0:T(8,128)(2,1)S(1)}, u32[]{:S(2)}, u32[]{:S(2)}) async-start(bf16[64,16,128]{2,1,0:T(8,128)(2,1)} %shard_map.174), calls=%async_computation | async-start | bytes 524288 | tf_op jit(solution)/shard_map/all_to_all | solution.py:537
  47.1 4.1 %shard_map.176.refs_0_ = f32[8,1024]{1,0:T(8,128)S(1)} custom-call(bf16[256,768]{1,0:T(8,128)(2,1)S(1)} %pad_maximum_fusion.1.refs_0_.refs_3_.refs_5_, bf16[256,768]{1,0:T(8,128)(2,1)S(1)} %collective-permute-done.2.refs_1_.refs_4_.refs_6_, bf16[256,768]{1,0:T(8,128)(2,1)S(1)} %collective-permute-done.5.refs_2_.refs_5_.refs_7_, ...), custom_call_target="tpu_custom_call" | custom-call | flops 1000000 | bytes 100000 | tf_op jit(solution)/shard_map/pallas_call | solution.py:540
  51.3 5.5 %all-to-all-done.refs_0_ = bf16[64,16,128]{2,1,0:T(8,128)(2,1)S(1)} async-done(((bf16[64,16,128]{2,1,0:T(8,128)(2,1)}), bf16[64,16,128]{2,1,0:T(8,128)(2,1)S(1)}, u32[]{:S(2)}, u32[]{:S(2)}) %all-to-all-start) | async-done | bytes 262176 | tf_op jit(solution)/shard_map/all_to_all | solution.py:537
  57.5 8.5 %shard_map.177 = (f32[8,1024]{1,0:T(8,128)}, bf16[4,256,384]{2,1,0:T(8,128)(2,1)}, bf16[768,384]{1,0:T(8,128)(2,1)}) custom-call(s32[64]{0:T(128)} %owner_ref.1, bf16[81,128]{1,0:T(8,128)(2,1)} %conv_ref.1, bf16[64,16,128]{2,1,0:T(8,128)(2,1)} %copy-done.11, bf16[512,384]{1,0:T(8,128)(2,1)} %get-tuple-element.58.refs_1_, ...), custom_call_target="tpu_custom_call" | custom-call | flops 1000000 | bytes 100000 | tf_op jit(solution)/shard_map/pallas_call | solution.py:549
  66.0 2.4 %collective-permute-start.8 = (f32[8,1024]{1,0:T(8,128)S(1)}, f32[8,1024]{1,0:T(8,128)S(1)}, u32[]{:S(2)}, u32[]{:S(2)}) collective-permute-start(f32[8,1024]{1,0:T(8,128)S(1)} %shard_map.176.refs_0_), channel_id=1, source_target_pairs={{0,1},{1,2},{2,3},{3,0},{4,5},{5,6},{6,7},{7,4},{8,9},{9,10},{10,1... | collective-permute-start | bytes 98312 | tf_op jit(solution)/shard_map/ppermute | solution.py:467
  68.5 1.3 %collective-permute-start.6 = (f32[8,1024]{1,0:T(8,128)S(1)}, f32[8,1024]{1,0:T(8,128)S(1)}, u32[]{:S(2)}, u32[]{:S(2)}) collective-permute-start(f32[8,1024]{1,0:T(8,128)S(1)} %shard_map.176.refs_0_), channel_id=1, source_target_pairs={{0,3},{1,0},{2,1},{3,2},{4,7},{5,4},{6,5},{7,6},{8,11},{9,8},{10,9... | collective-permute-start | bytes 98312 | tf_op jit(solution)/shard_map/ppermute | solution.py:467
  70.0 3.9 %collective-permute-done.7.refs_2_ = f32[8,1024]{1,0:T(8,128)S(1)} collective-permute-done((f32[8,1024]{1,0:T(8,128)S(1)}, f32[8,1024]{1,0:T(8,128)S(1)}, u32[]{:S(2)}, u32[]{:S(2)}) %collective-permute-start.7) | collective-permute-done | bytes 32800 | tf_op jit(solution)/shard_map/ppermute | solution.py:467
  74.6 12.0 %shard_map.178 = (bf16[256,384]{1,0:T(8,128)(2,1)}, bf16[256,384]{1,0:T(8,128)(2,1)}, bf16[256,384]{1,0:T(8,128)(2,1)}, bf16[256,384]{1,0:T(8,128)(2,1)}, bf16[2...) custom-call(f32[8,1024]{1,0:T(8,128)} %get-tuple-element.61.dots_ref, ...), custom_call_target="tpu_custom_call" | custom-call | flops 1000000 | bytes 100000 | tf_op jit(solution)/shard_map/pallas_call | solution.py:572
  86.6 0.8 collective-permute-start.12
  88.1 1.3 %collective-permute-start.10 = (bf16[2,256,384]{2,1,0:T(8,128)(2,1)}, bf16[2,256,384]{2,1,0:T(8,128)(2,1)S(1)}, u32[]{:S(2)}, u32[]{:S(2)}) collective-permute-start(bf16[2,256,384]{2,1,0:T(8,128)(2,1)} %get-tuple-element.66), channel_id=1, source_target_pairs={{0,8},{4,12},{8,0},{12,4},{1,9},{5,13},{9,1},{13,5},{2,10},{6,14},... | collective-permute-start | bytes 1179656 | tf_op jit(solution)/shard_map/ppermute | solution.py:471
  89.4 1.4 %collective-permute-start.11 = (bf16[2,256,384]{2,1,0:T(8,128)(2,1)}, bf16[2,256,384]{2,1,0:T(8,128)(2,1)S(1)}, u32[]{:S(2)}, u32[]{:S(2)}) collective-permute-start(bf16[2,256,384]{2,1,0:T(8,128)(2,1)} %get-tuple-element.67), channel_id=1, source_target_pairs={{0,12},{4,0},{8,4},{12,8},{1,13},{5,1},{9,5},{13,9},{2,14},{6,2},{... | collective-permute-start | bytes 1179656 | tf_op jit(solution)/shard_map/ppermute | solution.py:471
  90.8 5.8 %all-to-all-start.1 = ((bf16[4,48,384]{2,1,0:T(8,128)(2,1)}), bf16[4,48,384]{2,1,0:T(8,128)(2,1)S(1)}, u32[]{:S(2)}, u32[]{:S(2)}) async-start(bf16[4,48,384]{2,1,0:T(8,128)(2,1)} %bitcast.13), calls=%async_computation.2 | async-start | bytes 294912 | tf_op jit(solution)/shard_map/all_to_all | solution.py:587
  96.6 1.2 %collective-permute-start.13 = (bf16[256,384]{1,0:T(8,128)(2,1)}, bf16[256,384]{1,0:T(8,128)(2,1)S(1)}, u32[]{:S(2)}, u32[]{:S(2)}) collective-permute-start(bf16[256,384]{1,0:T(8,128)(2,1)} %get-tuple-element.70), channel_id=1, source_target_pairs={{0,2},{1,3},{2,0},{3,1},{4,6},{5,7},{6,4},{7,5},{8,10},{9,11},{10,... | collective-permute-start | bytes 589832 | tf_op jit(solution)/shard_map/ppermute | solution.py:471
  97.8 1.2 %collective-permute-start.14 = (bf16[256,384]{1,0:T(8,128)(2,1)}, bf16[256,384]{1,0:T(8,128)(2,1)S(1)}, u32[]{:S(2)}, u32[]{:S(2)}) collective-permute-start(bf16[256,384]{1,0:T(8,128)(2,1)} %get-tuple-element.71), channel_id=1, source_target_pairs={{0,3},{1,0},{2,1},{3,2},{4,7},{5,4},{6,5},{7,6},{8,11},{9,8},{10,9... | collective-permute-start | bytes 589832 | tf_op jit(solution)/shard_map/ppermute | solution.py:471
  99.1 7.0 %collective-permute-done.13.refs_6_ = bf16[256,384]{1,0:T(8,128)(2,1)S(1)} collective-permute-done((bf16[256,384]{1,0:T(8,128)(2,1)}, bf16[256,384]{1,0:T(8,128)(2,1)S(1)}, u32[]{:S(2)}, u32[]{:S(2)}) %collective-permute-start.13) | collective-permute-done | bytes 196640 | tf_op jit(solution)/shard_map/ppermute | solution.py:471
  106.0 3.8 %collective-permute-done.14.refs_7_ = bf16[256,384]{1,0:T(8,128)(2,1)S(1)} collective-permute-done((bf16[256,384]{1,0:T(8,128)(2,1)}, bf16[256,384]{1,0:T(8,128)(2,1)S(1)}, u32[]{:S(2)}, u32[]{:S(2)}) %collective-permute-start.14) | collective-permute-done | bytes 196640 | tf_op jit(solution)/shard_map/ppermute | solution.py:471
  109.9 1.0 copy-done.8
  110.9 0.9 copy-done.9
  111.8 2.8 %shard_map.179 = (bf16[1,256,384]{2,1,0:T(8,128)(2,1)}, bf16[1,256,384]{2,1,0:T(8,128)(2,1)}, bf16[1,256,384]{2,1,0:T(8,128)(2,1)}, f32[48,384]{1,0:T(8,128)}) custom-call(bf16[4,48,384]{2,1,0:T(8,128)(2,1)S(1)} %all-to-all-done.1.parts_ref, bf16[2,256,384]{2,1,0:T(8,128)(2,1)S(1)} %copy-done.8, bf16[2,256,384]{2,1,0:T(8,128)(2,1)S(1)} %collective-permute-done.9.refs_1_, ...), custom_call_target="tpu_custom_call" | custom-call | flops 1000000 | bytes 100000 | tf_op jit(solution)/shard_map/pallas_call | solution.py:602
  (43 shorter events, 3.1 us)
Async XLA Ops:
  8.2 38.9 %copy-start.1 = (bf16[256,768]{1,0:T(8,128)(2,1)}, bf16[256,768]{1,0:T(8,128)(2,1)S(1)}, u32[]{:S(2)}) copy-start(bf16[256,768]{1,0:T(8,128)(2,1)S(1)} %pad_maximum_fusion.refs_4_.refs_9_) | copy-start | bytes 1179652
  8.2 12.1 %collective-permute-start.1 = (bf16[256,768]{1,0:T(8,128)(2,1)S(1)}, bf16[256,768]{1,0:T(8,128)(2,1)S(1)}, u32[]{:S(2)}, u32[]{:S(2)}) collective-permute-start(bf16[256,768]{1,0:T(8,128)(2,1)S(1)} %pad_maximum_fusion.refs_4_.refs_9_), channel_id=1, source_target_pairs={{0,4},{4,8},{8,12},{12,0},{1,5},{5,9},{9,13},{13,1},{2,6},{6,10},{... | collective-permute-start | bytes 1179656 | tf_op jit(solution)/shard_map/ppermute | solution.py:467
  9.8 10.6 %collective-permute-start = (bf16[256,768]{1,0:T(8,128)(2,1)S(1)}, bf16[256,768]{1,0:T(8,128)(2,1)S(1)}, u32[]{:S(2)}, u32[]{:S(2)}) collective-permute-start(bf16[256,768]{1,0:T(8,128)(2,1)S(1)} %pad_maximum_fusion.refs_4_.refs_9_), channel_id=1, source_target_pairs={{0,12},{4,0},{8,4},{12,8},{1,13},{5,1},{9,5},{13,9},{2,14},{6,2},{... | collective-permute-start | bytes 1179656 | tf_op jit(solution)/shard_map/ppermute | solution.py:467
  12.6 34.5 %copy-start = (bf16[256,768]{1,0:T(8,128)(2,1)}, bf16[256,768]{1,0:T(8,128)(2,1)S(1)}, u32[]{:S(2)}) copy-start(bf16[256,768]{1,0:T(8,128)(2,1)S(1)} %pad_maximum_fusion.1.refs_0_.refs_3_.refs_5_) | copy-start | bytes 1179652
  12.6 10.4 %collective-permute-start.3 = (bf16[256,768]{1,0:T(8,128)(2,1)S(1)}, bf16[256,768]{1,0:T(8,128)(2,1)S(1)}, u32[]{:S(2)}, u32[]{:S(2)}) collective-permute-start(bf16[256,768]{1,0:T(8,128)(2,1)S(1)} %pad_maximum_fusion.1.refs_0_.refs_3_.refs_5_), channel_id=1, source_target_pairs={{0,1},{1,2},{2,3},{3,0},{4,5},{5,6},{6,7},{7,4},{8,9},{9,10},{10,1... | collective-permute-start | bytes 1179656 | tf_op jit(solution)/shard_map/ppermute | solution.py:467
  14.7 9.6 %collective-permute-start.2 = (bf16[256,768]{1,0:T(8,128)(2,1)S(1)}, bf16[256,768]{1,0:T(8,128)(2,1)S(1)}, u32[]{:S(2)}, u32[]{:S(2)}) collective-permute-start(bf16[256,768]{1,0:T(8,128)(2,1)S(1)} %pad_maximum_fusion.1.refs_0_.refs_3_.refs_5_), channel_id=1, source_target_pairs={{0,3},{1,0},{2,1},{3,2},{4,7},{5,4},{6,5},{7,6},{8,11},{9,8},{10,9... | collective-permute-start | bytes 1179656 | tf_op jit(solution)/shard_map/ppermute | solution.py:467
  20.4 26.7 %copy-start.5 = (bf16[256,768]{1,0:T(8,128)(2,1)}, bf16[256,768]{1,0:T(8,128)(2,1)S(1)}, u32[]{:S(2)}) copy-start(bf16[256,768]{1,0:T(8,128)(2,1)S(1)} %collective-permute-done.1.refs_7_.refs_12_) | copy-start | bytes 1179652
  20.4 26.7 %copy-start.6 = (bf16[256,768]{1,0:T(8,128)(2,1)}, bf16[256,768]{1,0:T(8,128)(2,1)S(1)}, u32[]{:S(2)}) copy-start(bf16[256,768]{1,0:T(8,128)(2,1)S(1)} %collective-permute-done.refs_5_.refs_10_) | copy-start | bytes 1179652
  23.0 24.1 %copy-start.2 = (bf16[256,768]{1,0:T(8,128)(2,1)}, bf16[256,768]{1,0:T(8,128)(2,1)S(1)}, u32[]{:S(2)}) copy-start(bf16[256,768]{1,0:T(8,128)(2,1)S(1)} %collective-permute-done.3.refs_3_.refs_6_.refs_8_) | copy-start | bytes 1179652
  24.3 22.8 %copy-start.3 = (bf16[256,768]{1,0:T(8,128)(2,1)}, bf16[256,768]{1,0:T(8,128)(2,1)S(1)}, u32[]{:S(2)}) copy-start(bf16[256,768]{1,0:T(8,128)(2,1)S(1)} %collective-permute-done.2.refs_1_.refs_4_.refs_6_) | copy-start | bytes 1179652
  24.3 9.7 %collective-permute-start.4 = (bf16[256,768]{1,0:T(8,128)(2,1)S(1)}, bf16[256,768]{1,0:T(8,128)(2,1)S(1)}, u32[]{:S(2)}, u32[]{:S(2)}) collective-permute-start(bf16[256,768]{1,0:T(8,128)(2,1)S(1)} %pad_maximum_fusion.refs_4_.refs_9_), channel_id=1, source_target_pairs={{0,8},{4,12},{8,0},{12,4},{1,9},{5,13},{9,1},{13,5},{2,10},{6,14},... | collective-permute-start | bytes 1179656 | tf_op jit(solution)/shard_map/ppermute | solution.py:467
  26.1 10.5 %collective-permute-start.5 = (bf16[256,768]{1,0:T(8,128)(2,1)S(1)}, bf16[256,768]{1,0:T(8,128)(2,1)S(1)}, u32[]{:S(2)}, u32[]{:S(2)}) collective-permute-start(bf16[256,768]{1,0:T(8,128)(2,1)S(1)} %pad_maximum_fusion.1.refs_0_.refs_3_.refs_5_), channel_id=1, source_target_pairs={{0,2},{1,3},{2,0},{3,1},{4,6},{5,7},{6,4},{7,5},{8,10},{9,11},{10,... | collective-permute-start | bytes 1179656 | tf_op jit(solution)/shard_map/ppermute | solution.py:467
  34.0 32.0 %copy-start.7 = (bf16[256,768]{1,0:T(8,128)(2,1)}, bf16[256,768]{1,0:T(8,128)(2,1)S(1)}, u32[]{:S(2)}) copy-start(bf16[256,768]{1,0:T(8,128)(2,1)S(1)} %collective-permute-done.4.refs_6_.refs_11_) | copy-start | bytes 1179652
  36.6 20.2 %copy-start.4 = (bf16[256,768]{1,0:T(8,128)(2,1)}, bf16[256,768]{1,0:T(8,128)(2,1)S(1)}, u32[]{:S(2)}) copy-start(bf16[256,768]{1,0:T(8,128)(2,1)S(1)} %collective-permute-done.5.refs_2_.refs_5_.refs_7_) | copy-start | bytes 1179652
  36.6 20.2 %all-to-all-start = ((bf16[64,16,128]{2,1,0:T(8,128)(2,1)}), bf16[64,16,128]{2,1,0:T(8,128)(2,1)S(1)}, u32[]{:S(2)}, u32[]{:S(2)}) async-start(bf16[64,16,128]{2,1,0:T(8,128)(2,1)} %shard_map.174), calls=%async_computation | async-start | bytes 524288 | tf_op jit(solution)/shard_map/all_to_all | solution.py:537
  46.9 44.0 %reduce-scatter.2.cloned.1.call-start = ((), (), s32[]{:S(2)}) async-start(), calls=%async_computation.3 | async-start | bytes 737280 | tf_op jit(solution)/shard_map/reduce_scatter | solution.py:586
  51.3 22.7 %copy-start.10 = (f32[8,1024]{1,0:T(8,128)}, f32[8,1024]{1,0:T(8,128)S(1)}, u32[]{:S(2)}) copy-start(f32[8,1024]{1,0:T(8,128)S(1)} %shard_map.176.refs_0_) | copy-start | bytes 98308
  56.8 0.7 copy-start.11
  66.0 4.0 %collective-permute-start.8 = (f32[8,1024]{1,0:T(8,128)S(1)}, f32[8,1024]{1,0:T(8,128)S(1)}, u32[]{:S(2)}, u32[]{:S(2)}) collective-permute-start(f32[8,1024]{1,0:T(8,128)S(1)} %shard_map.176.refs_0_), channel_id=1, source_target_pairs={{0,1},{1,2},{2,3},{3,0},{4,5},{5,6},{6,7},{7,4},{8,9},{9,10},{10,1... | collective-permute-start | bytes 98312 | tf_op jit(solution)/shard_map/ppermute | solution.py:467
  68.4 5.5 %collective-permute-start.7 = (f32[8,1024]{1,0:T(8,128)S(1)}, f32[8,1024]{1,0:T(8,128)S(1)}, u32[]{:S(2)}, u32[]{:S(2)}) collective-permute-start(f32[8,1024]{1,0:T(8,128)S(1)} %shard_map.176.refs_0_), channel_id=1, source_target_pairs={{0,2},{1,3},{2,0},{3,1},{4,6},{5,7},{6,4},{7,5},{8,10},{9,11},{10,... | collective-permute-start | bytes 98312 | tf_op jit(solution)/shard_map/ppermute | solution.py:467
  68.5 5.5 %collective-permute-start.6 = (f32[8,1024]{1,0:T(8,128)S(1)}, f32[8,1024]{1,0:T(8,128)S(1)}, u32[]{:S(2)}, u32[]{:S(2)}) collective-permute-start(f32[8,1024]{1,0:T(8,128)S(1)} %shard_map.176.refs_0_), channel_id=1, source_target_pairs={{0,3},{1,0},{2,1},{3,2},{4,7},{5,4},{6,5},{7,6},{8,11},{9,8},{10,9... | collective-permute-start | bytes 98312 | tf_op jit(solution)/shard_map/ppermute | solution.py:467
  70.0 4.0 %copy-start.12 = (f32[8,1024]{1,0:T(8,128)}, f32[8,1024]{1,0:T(8,128)S(1)}, u32[]{:S(2)}) copy-start(f32[8,1024]{1,0:T(8,128)S(1)} %collective-permute-done.8.refs_3_) | copy-start | bytes 98308
  73.9 0.6 copy-start.13
  86.6 11.2 %collective-permute-start.12 = (bf16[256,384]{1,0:T(8,128)(2,1)}, bf16[256,384]{1,0:T(8,128)(2,1)S(1)}, u32[]{:S(2)}, u32[]{:S(2)}) collective-permute-start(bf16[256,384]{1,0:T(8,128)(2,1)} %get-tuple-element.69), channel_id=1, source_target_pairs={{0,1},{1,2},{2,3},{3,0},{4,5},{5,6},{6,7},{7,4},{8,9},{9,10},{10,1... | collective-permute-start | bytes 589832 | tf_op jit(solution)/shard_map/ppermute | solution.py:471
  87.5 22.4 %collective-permute-start.9 = (bf16[2,256,384]{2,1,0:T(8,128)(2,1)}, bf16[2,256,384]{2,1,0:T(8,128)(2,1)S(1)}, u32[]{:S(2)}, u32[]{:S(2)}) collective-permute-start(bf16[2,256,384]{2,1,0:T(8,128)(2,1)} %get-tuple-element.65), channel_id=1, source_target_pairs={{0,4},{4,8},{8,12},{12,0},{1,5},{5,9},{9,13},{13,1},{2,6},{6,10},{... | collective-permute-start | bytes 1179656 | tf_op jit(solution)/shard_map/ppermute | solution.py:471
  88.1 21.8 %collective-permute-start.10 = (bf16[2,256,384]{2,1,0:T(8,128)(2,1)}, bf16[2,256,384]{2,1,0:T(8,128)(2,1)S(1)}, u32[]{:S(2)}, u32[]{:S(2)}) collective-permute-start(bf16[2,256,384]{2,1,0:T(8,128)(2,1)} %get-tuple-element.66), channel_id=1, source_target_pairs={{0,8},{4,12},{8,0},{12,4},{1,9},{5,13},{9,1},{13,5},{2,10},{6,14},... | collective-permute-start | bytes 1179656 | tf_op jit(solution)/shard_map/ppermute | solution.py:471
  89.4 20.4 %collective-permute-start.11 = (bf16[2,256,384]{2,1,0:T(8,128)(2,1)}, bf16[2,256,384]{2,1,0:T(8,128)(2,1)S(1)}, u32[]{:S(2)}, u32[]{:S(2)}) collective-permute-start(bf16[2,256,384]{2,1,0:T(8,128)(2,1)} %get-tuple-element.67), channel_id=1, source_target_pairs={{0,12},{4,0},{8,4},{12,8},{1,13},{5,1},{9,5},{13,9},{2,14},{6,2},{... | collective-permute-start | bytes 1179656 | tf_op jit(solution)/shard_map/ppermute | solution.py:471
  90.8 19.0 %all-to-all-start.1 = ((bf16[4,48,384]{2,1,0:T(8,128)(2,1)}), bf16[4,48,384]{2,1,0:T(8,128)(2,1)S(1)}, u32[]{:S(2)}, u32[]{:S(2)}) async-start(bf16[4,48,384]{2,1,0:T(8,128)(2,1)} %bitcast.13), calls=%async_computation.2 | async-start | bytes 294912 | tf_op jit(solution)/shard_map/all_to_all | solution.py:587
  96.6 9.5 %collective-permute-start.13 = (bf16[256,384]{1,0:T(8,128)(2,1)}, bf16[256,384]{1,0:T(8,128)(2,1)S(1)}, u32[]{:S(2)}, u32[]{:S(2)}) collective-permute-start(bf16[256,384]{1,0:T(8,128)(2,1)} %get-tuple-element.70), channel_id=1, source_target_pairs={{0,2},{1,3},{2,0},{3,1},{4,6},{5,7},{6,4},{7,5},{8,10},{9,11},{10,... | collective-permute-start | bytes 589832 | tf_op jit(solution)/shard_map/ppermute | solution.py:471
  97.8 12.0 %collective-permute-start.14 = (bf16[256,384]{1,0:T(8,128)(2,1)}, bf16[256,384]{1,0:T(8,128)(2,1)S(1)}, u32[]{:S(2)}, u32[]{:S(2)}) collective-permute-start(bf16[256,384]{1,0:T(8,128)(2,1)} %get-tuple-element.71), channel_id=1, source_target_pairs={{0,3},{1,0},{2,1},{3,2},{4,7},{5,4},{6,5},{7,6},{8,11},{9,8},{10,9... | collective-permute-start | bytes 589832 | tf_op jit(solution)/shard_map/ppermute | solution.py:471
  109.9 1.0 copy-start.8
  110.9 0.9 copy-start.9
  (1 other events, 0.6 us)
Sparse Core Ops, SparseCore 0:
  66.1 22.1 reduce-scatter.1

commit v9 on v6

--- a/solution.py
+++ b/solution.py
@@ -210,18 +210,12 @@
 
 
 def totals_kernel(*refs):
-    out_ref, query_held, key_held, query_arrived, key_arrived = refs[2 * GRID :]
-    key_copies = fetch_halves(refs[GRID : 2 * GRID], 0, key_held, key_arrived)
-    query_copies = fetch_halves(refs[:GRID], 0, query_held, query_arrived)
-    for copy in key_copies:
-        copy.wait()
+    query_refs, key_refs, out_ref = refs[:GRID], refs[GRID : 2 * GRID], refs[2 * GRID]
     for head in range(HEADS_HERE):
         columns = pl.ds(head * HDIM, HDIM)
         for piece in range(GRID):
-            if head == 0:
-                query_copies[piece].wait()
-            query = query_held[piece, :, columns]
-            scores = [dot(key_held[other, :, columns], query, NT) for other in range(GRID)]
+            query = query_refs[piece][:, columns]
+            scores = [dot(key_ref[:, columns], query, NT) for key_ref in key_refs]
             top = functools.reduce(
                 jnp.maximum, [jnp.max(tile, axis=0, keepdims=True) for tile in scores]
             ) * (SCORE_SCALE * LOG2E)
@@ -281,11 +275,27 @@
             ]
 
 
-def grads_kernel(owner_ref, conv_ref, *refs):
+def block_grads(key, value, query, grad, totals, dots):
+    weights = jnp.exp2(dot(key, query, NT) * (SCORE_SCALE * LOG2E) - totals)
+    dscore = (weights * (dot(value, grad, NT) - dots)).astype(bf16)
+    root = math.sqrt(FRAMES * 64)
+    key_grad = (dot(dscore, query) * (root * SCORE_SCALE)).astype(bf16)
+    value_grad = (dot(weights.astype(bf16), grad) * root).astype(bf16)
+    return key_grad, value_grad, dot(key.T, dscore)
+
+
+def others_kernel(owner_ref, conv_ref, *refs):
     total_refs, (recv_from, joint_from, picked_from) = refs[:GRID], refs[GRID : GRID + 3]
-    query_refs, pair_refs = refs[GRID + 3 : 2 * GRID + 3], refs[2 * GRID + 3 : 3 * GRID + 3]
-    rest = refs[3 * GRID + 3 :]
-    query_out, pair_out, weight_out = rest[:GRID], rest[GRID : 2 * GRID], rest[2 * GRID]
+    query_refs, pair_refs = refs[GRID + 3 : 2 * GRID + 3], refs[2 * GRID + 3 : 3 * GRID + 2]
+    (
+        totals_ref,
+        dots_ref,
+        sums_out,
+        grad_out,
+        weight_out,
+        *rest,
+    ) = refs[3 * GRID + 2 :]
+    pair_out = rest[: GRID - 1]
     (
         frames,
         conv_big,
@@ -294,25 +304,22 @@
         joint_ref,
         picked_ref,
         weight_made,
-        dots_ref,
         sums,
         out_held,
         query_held,
         key_held,
         value_held,
         grad_ref,
-        query_made,
         pair_made,
         first_arrived,
         out_arrived,
         query_arrived,
         key_arrived,
         value_arrived,
-        query_sent,
         pair_sent,
         weight_sent,
-    ) = rest[2 * GRID + 1 :]
-    sends_order = (2, 1, 3, 0)
+        sums_sent,
+    ) = rest[GRID - 1 :]
     firsts = fetch(
         [recv_from, joint_from, picked_from], [recv_ref, joint_ref, picked_ref], first_arrived
     )
@@ -320,6 +327,15 @@
     query_copies = fetch_halves(query_refs, 0, query_held, query_arrived)
     key_copies = fetch_halves(pair_refs, 0, key_held, key_arrived)
     value_copies = fetch_halves(pair_refs, 1, value_held, value_arrived)
+    dots_ref[...] = jnp.zeros_like(dots_ref)
+    for piece in range(GRID):
+        columns = pl.ds(piece * ROWS_HERE, ROWS_HERE)
+        parts = [
+            total_refs[step][:, pl.ds(((piece - step) % GRID) * ROWS_HERE, ROWS_HERE)]
+            for step in range(GRID)
+        ]
+        top = functools.reduce(jnp.maximum, parts)
+        totals_ref[:, columns] = top + jnp.log2(sum(jnp.exp2(part - top) for part in parts))
     token_part(owner_ref, conv_ref, recv_ref, firsts[0], frames, conv_big, ordered)
     firsts[1].wait()
     ones = jnp.ones((8, 2 * HDIM), bf16)
@@ -336,59 +352,87 @@
         for head in range(HEADS_HERE):
             columns = slice(head * HDIM, (head + 1) * HDIM)
             both = jnp.concatenate([high[:, columns], low[:, columns]], axis=1)
-            dots_ref[head, :, pl.ds(piece * ROWS_HERE, ROWS_HERE)] = dot(ones, both, NT)
+            dots_ref[pl.ds(head, 1), pl.ds(piece * ROWS_HERE, ROWS_HERE)] = dot(ones, both, NT)[
+                0:1
+            ]
         outer = outer + dot(rows, outs, TN)
     firsts[2].wait()
     weight_made[...] = (
         dot(picked_ref[...], outer.astype(bf16)) * (1.0 / math.sqrt(FRAMES * 64 * 4))
     ).astype(bf16)
-    sends = fetch([weight_made], [weight_out], weight_sent)
-    root = math.sqrt(FRAMES * 64)
-    totals = []
-    for piece in range(GRID):
-        parts = [
-            total_refs[step][:, pl.ds(((piece - step) % GRID) * ROWS_HERE, ROWS_HERE)]
-            for step in range(GRID)
-        ]
-        top = functools.reduce(jnp.maximum, parts)
-        totals.append(top + jnp.log2(sum(jnp.exp2(part - top) for part in parts)))
-    totals = jnp.concatenate(totals, axis=1)
+    sends = fetch([weight_made, grad_ref], [weight_out, grad_out], weight_sent)
     for copy in query_copies:
         copy.wait()
-    for other in sends_order:
-        key_copies[other].wait()
-        value_copies[other].wait()
+    for place in (1, 0, 2):
+        key_copies[place].wait()
+        value_copies[place].wait()
         for head in range(HEADS_HERE):
             columns = pl.ds(head * HDIM, HDIM)
-            query = query_held[:, :, columns].reshape(BLOCK, HDIM)
-            grad = grad_ref[:, :, columns].reshape(BLOCK, HDIM)
-            key = key_held[other, :, columns]
-            value = value_held[other, :, columns]
-            weights = jnp.exp2(
-                dot(key, query, NT) * (SCORE_SCALE * LOG2E) - totals[head : head + 1]
+            key_grad, value_grad, part = block_grads(
+                key_held[place, :, columns],
+                value_held[place, :, columns],
+                query_held[:, :, columns].reshape(BLOCK, HDIM),
+                grad_ref[:, :, columns].reshape(BLOCK, HDIM),
+                totals_ref[pl.ds(head, 1), :],
+                dots_ref[pl.ds(head, 1), :],
             )
-            dscore = (weights * (dot(value, grad, NT) - dots_ref[head, 0:1, :])).astype(bf16)
-            pair_made[other, 1, :, columns] = (dot(weights.astype(bf16), grad) * root).astype(bf16)
-            pair_made[other, 0, :, columns] = (
-                dot(dscore, query) * (root * SCORE_SCALE)
-            ).astype(bf16)
-            part = dot(key.T, dscore)
-            if other == sends_order[0]:
+            pair_made[place, 0, :, columns] = key_grad
+            pair_made[place, 1, :, columns] = value_grad
+            if place == 1:
                 sums[head] = part
             else:
                 sums[head] += part
-        send = pltpu.make_async_copy(pair_made.at[other], pair_out[other], pair_sent.at[other])
-        send.start()
-        sends.append(send)
-    for piece in sends_order:
-        for head in range(HEADS_HERE):
-            query_made[piece, :, pl.ds(head * HDIM, HDIM)] = (
-                sums[head, :, pl.ds(piece * ROWS_HERE, ROWS_HERE)].T * (root * SCORE_SCALE)
-            ).astype(bf16)
-        send = pltpu.make_async_copy(query_made.at[piece], query_out[piece], query_sent.at[piece])
-        send.start()
-        sends.append(send)
+            if place == 2:
+                sends += fetch(
+                    [sums.at[head]], [sums_out.at[head]], sums_sent.at[pl.ds(head, 1)]
+                )
+        sends += fetch([pair_made.at[place]], [pair_out[place]], pair_sent.at[pl.ds(place, 1)])
     for send in sends:
+        send.wait()
+
+
+def own_kernel(totals_ref, dots_ref, sums_from, grad_from, pair_from, *refs):
+    query_refs, rest = refs[:GRID], refs[GRID:]
+    query_out, rest = rest[:GRID], rest[GRID:]
+    (
+        pair_out,
+        sums,
+        query_held,
+        grad_ref,
+        query_made,
+        pair_held,
+        sums_arrived,
+        grad_arrived,
+        pair_arrived,
+        query_arrived,
+        query_sent,
+    ) = rest
+    (pair_copy,) = fetch([pair_from], [pair_held], pair_arrived)
+    query_copies = fetch_halves(query_refs, 0, query_held, query_arrived)
+    (grad_copy,) = fetch([grad_from], [grad_ref], grad_arrived)
+    (sums_copy,) = fetch([sums_from], [sums], sums_arrived)
+    for copy in query_copies + [pair_copy, grad_copy]:
+        copy.wait()
+    for head in range(HEADS_HERE):
+        columns = pl.ds(head * HDIM, HDIM)
+        key_grad, value_grad, part = block_grads(
+            pair_held[:, columns],
+            pair_held[:, pl.ds(FEATS + head * HDIM, HDIM)],
+            query_held[:, :, columns].reshape(BLOCK, HDIM),
+            grad_ref[:, :, columns].reshape(BLOCK, HDIM),
+            totals_ref[pl.ds(head, 1), :],
+            dots_ref[pl.ds(head, 1), :],
+        )
+        pair_out[0, :, columns] = key_grad
+        pair_out[1, :, columns] = value_grad
+        if head == 0:
+            sums_copy.wait()
+        part = (sums[head] + part) * (math.sqrt(FRAMES * 64) * SCORE_SCALE)
+        for piece in range(GRID):
+            query_made[piece, :, columns] = part[
+                :, piece * ROWS_HERE : (piece + 1) * ROWS_HERE
+            ].T.astype(bf16)
+    for send in fetch([query_made.at[piece] for piece in range(GRID)], query_out, query_sent):
         send.wait()
 
 
@@ -400,28 +444,22 @@
 
 def sum_kernel(kept_ref, other_ref, *refs):
     pair_refs, query_refs = refs[:GRID], refs[GRID : 2 * GRID]
-    query_out, key_out, value_out, weight_out, query_held, pair_held, *arrived = refs[2 * GRID :]
-    pair_copies = fetch(pair_refs, [pair_held.at[step] for step in range(GRID)], arrived[1])
-    query_copies = fetch(query_refs, [query_held.at[step] for step in range(GRID)], arrived[0])
+    query_out, key_out, value_out, weight_out = refs[2 * GRID :]
     weight_out[...] = kept_ref[...] + other_ref[...]
-    for copy in query_copies:
-        copy.wait()
-    query_out[0] = sum(query_held[step].astype(f32) for step in range(GRID)).astype(bf16)
-    for copy in pair_copies:
-        copy.wait()
+    query_out[0] = sum(ref[...].astype(f32) for ref in query_refs).astype(bf16)
     for place, out_ref in enumerate((key_out, value_out)):
-        out_ref[0] = sum(pair_held[step, place].astype(f32) for step in range(GRID)).astype(bf16)
-
-
-def call(kernel, out_shape, in_specs, scratch=(), out_spec=None, limit=56):
+        out_ref[0] = sum(ref[place].astype(f32) for ref in pair_refs).astype(bf16)
+
+
+def call(kernel, out_shape, in_specs, scratch=(), out_spec=None, limit=56, flops=10**6):
     return pl.pallas_call(
         kernel,
         out_shape=out_shape,
         in_specs=in_specs,
-        out_specs=jax.tree.map(lambda _: out_spec or VMEM, out_shape),
+        out_specs=out_spec or jax.tree.map(lambda _: VMEM, out_shape),
         scratch_shapes=list(scratch),
         compiler_params=pltpu.CompilerParams(vmem_limit_bytes=limit * MIB),
-        cost_estimate=pl.CostEstimate(flops=10**6, bytes_accessed=10**5, transcendentals=0),
+        cost_estimate=pl.CostEstimate(flops=flops, bytes_accessed=10**5, transcendentals=0),
     )
 
 
@@ -513,17 +551,24 @@
     totals = call(
         totals_kernel,
         shape((8, BLOCK), f32),
-        [ANY] * (2 * GRID),
-        scratch=HELD * 2 + ARRIVED * 2,
+        [VMEM] * (2 * GRID),
         limit=24,
     )(*query_outs, *key_values)
     total_pieces = gather(totals, "hy")
-    outs = call(
-        grads_kernel,
-        tuple([shape((ROWS_HERE, FEATS), bf16)] * GRID)
-        + tuple([shape((2, ROWS_HERE, FEATS), bf16)] * GRID)
-        + (shape((768, FEATS), bf16),),
-        [SMEM] + [VMEM] * (1 + GRID) + [ANY] * (3 + 2 * GRID),
+    pair_shape = shape((2, ROWS_HERE, FEATS), bf16)
+    exact, row_dots, sums, grad_out, weight_part, *pair_others = call(
+        others_kernel,
+        (
+            shape((8, BLOCK), f32),
+            shape((8, BLOCK), f32),
+            shape((HEADS_HERE, HDIM, BLOCK), f32),
+            shape((GRID, ROWS_HERE, FEATS), bf16),
+            shape((768, FEATS), bf16),
+            pair_shape,
+            pair_shape,
+            pair_shape,
+        ),
+        [SMEM] + [VMEM] * (1 + GRID) + [ANY] * (2 + 2 * GRID),
         scratch=[
             pltpu.VMEM((FRAMES + 2, 16, LANES), bf16),
             pltpu.VMEM((3 * LANES, QUARTERS * LANES), bf16),
@@ -532,17 +577,27 @@
             pltpu.VMEM((QUARTERS * LANES, FEATS), bf16),
             pltpu.VMEM((768, QUARTERS * LANES), bf16),
             pltpu.VMEM((768, FEATS), bf16),
-            pltpu.VMEM((HEADS_HERE, 8, BLOCK), f32),
             pltpu.VMEM((HEADS_HERE, HDIM, BLOCK), f32),
         ]
-        + HELD * 6
-        + [pltpu.VMEM((GRID, 2, ROWS_HERE, FEATS), bf16), pltpu.SemaphoreType.DMA((3,))]
-        + ARRIVED * 6
-        + [pltpu.SemaphoreType.DMA((1,))],
-        out_spec=ANY,
-        limit=56,
-    )(frame_owner, conv_w, *total_pieces, received, joint, picked, *query_outs, *key_values)
-    query_parts, pair_parts, weight_part = outs[:GRID], outs[GRID : 2 * GRID], outs[2 * GRID]
+        + HELD * 5
+        + [pltpu.VMEM((GRID - 1, 2, ROWS_HERE, FEATS), bf16), pltpu.SemaphoreType.DMA((3,))]
+        + ARRIVED * 5
+        + [pltpu.SemaphoreType.DMA((2,)), pltpu.SemaphoreType.DMA((HEADS_HERE,))],
+        out_spec=(VMEM, VMEM) + (ANY,) * 6,
+    )(frame_owner, conv_w, *total_pieces, received, joint, picked, *query_outs, *key_values[1:])
+    *query_parts, pair_own = call(
+        own_kernel,
+        tuple([shape((ROWS_HERE, FEATS), bf16)] * GRID) + (pair_shape,),
+        [VMEM] * 2 + [ANY] * (3 + GRID),
+        scratch=[pltpu.VMEM((HEADS_HERE, HDIM, BLOCK), f32)]
+        + HELD * 3
+        + [pltpu.VMEM((ROWS_HERE, 2 * FEATS), bf16)]
+        + [pltpu.SemaphoreType.DMA((1,))] * 3
+        + ARRIVED * 2,
+        out_spec=(ANY,) * GRID + (VMEM,),
+        flops=10**6,
+    )(exact, row_dots, sums, grad_out, key_values[0], *query_outs)
+    pair_parts = [pair_own] + pair_others
     weight_parts = lax.all_to_all(
         weight_part.reshape(8, 2, 48, FEATS),
         ("core", "hx"),
@@ -568,9 +623,8 @@
     return call(
         sum_kernel,
         (rows, rows, rows, shape((48, FEATS), f32)),
-        [VMEM] * 2 + [ANY] * (2 * GRID),
-        scratch=HELD + [pltpu.VMEM((GRID, 2, ROWS_HERE, FEATS), bf16)] + ARRIVED * 2,
-        limit=8,
+        [VMEM] * (2 + 2 * GRID),
+        limit=16,
     )(weight_kept, weight_other, *pair_back, *query_back)
 
 

time: 110 us -> 108 us (0.982); the launches traced: 108 us -> 107 us
  waiting for transfers between devices: 28.4 us -> 25.7 us
  Pallas kernels: 34.7 us -> 36.6 us
    ppermute x6, waiting for transfers between devices: 12.9 us -> 9.78 us  [to_ahead(): lax.ppermute(block, axis, [(i, (i + step) % GRID) for i in range(GRID)])]
    ppermute x1, waiting for transfers between devices: 0.01 us -> 2.73 us  [per_device(): weight_other = lax.ppermute(weight_sent, 'zh', [(0, 1), (1, 0)])]
    all_to_all x1, waiting for transfers between devices: 2.24 us -> 0.01 us  [per_device(): lax.all_to_all(weight_part.reshape(8, 2, 48, FEATS), ('core', 'hx'), spli...]
    pallas_call x3 -> x4, Pallas kernels: 23.9 us -> 25.8 us  [the longest x1 15.2 us: per_device(): call(others_kernel, (shape((8, BLOCK), f32), shape((8, BLOCK), f32), shap...]
    unnamed x30 -> x36, local copies, waits for them, and re-layouts: 3.24 us -> 3.26 us
  transfers between devices with their start and end apart: 18 -> 18, of which waited for: 11 -> 11; matrix products, arithmetic and copies ran while one was open for 1% -> 1% of each run, Pallas kernels for 14% -> 19%
where the time goes in v9:
time: 108 us; the launch traced here: 107 us
  starting transfers between devices  38.9 us (36%)
  Pallas kernels  36.6 us (34%)
  waiting for transfers between devices  25.7 us (24%)
  local copies, waits for them, and re-layouts  3.26 us (3%)
  other arithmetic  2.11 us (2%)
    pallas_call x1, Pallas kernels, per_device(): call(others_kernel, (shape((8, BLOCK), f32), shape((8, BLOCK), f32), shap...  15.2 us
    ppermute x9, waiting for transfers between devices, from_ahead(): lax.ppermute(block, axis, [(i, (i - step) % GRID) for i in range(GRID)])  13.2 us
    ppermute x9, starting transfers between devices, from_ahead(): lax.ppermute(block, axis, [(i, (i - step) % GRID) for i in range(GRID)])  11.6 us
    all_to_all x1, starting transfers between devices, per_device(): lax.all_to_all(windows, ('tm', 'hx', 'hy'), split_axis=0, concat_axis=0,...  10.3 us
    ppermute x6, waiting for transfers between devices, to_ahead(): lax.ppermute(block, axis, [(i, (i + step) % GRID) for i in range(GRID)])  9.78 us
    ppermute x6, starting transfers between devices, to_ahead(): lax.ppermute(block, axis, [(i, (i + step) % GRID) for i in range(GRID)])  8.25 us
    pallas_call x1, Pallas kernels, per_device(): call(own_kernel, tuple([shape((ROWS_HERE, FEATS), bf16)] * GRID) + (pair_...  6.5 us
    pallas_call x1, Pallas kernels, per_device(): call(weights_kernel, (shape((QUARTERS * LANES, FEATS), bf16), shape((768,...  6.15 us
  transfers between devices with their start and end apart: 18, of which 11 were waited for; matrix products, arithmetic and copies ran while one was open for 1% of the time, Pallas kernels for 19%

profile of v9, /device:TPU:24, one launch (start us, length us, event | category | flops | bytes accessed | tf_op | source)
XLA Modules:
  0.0 107.5 jit_solution(8519345042926690205)
XLA Ops:
  0.6 1.1 pad_maximum_fusion.refs_4_.pair_from
  1.7 1.6 %collective-permute-start.1 = (bf16[256,768]{1,0:T(8,128)(2,1)S(1)}, bf16[256,768]{1,0:T(8,128)(2,1)S(1)}, u32[]{:S(2)}, u32[]{:S(2)}) collective-permute-start(bf16[256,768]{1,0:T(8,128)(2,1)S(1)} %pad_maximum_fusion.refs_4_.pair_from), channel_id=1, source_target_pairs={{0,4},{4,8},{8,12},{12,0},{1,5},{5,9},{9,13},{13,1},{2,6},{6,10},{... | collective-permute-start | bytes 1179656 | tf_op jit(solution)/shard_map/ppermute | solution.py:478
  3.3 1.7 %collective-permute-start = (bf16[256,768]{1,0:T(8,128)(2,1)S(1)}, bf16[256,768]{1,0:T(8,128)(2,1)S(1)}, u32[]{:S(2)}, u32[]{:S(2)}) collective-permute-start(bf16[256,768]{1,0:T(8,128)(2,1)S(1)} %pad_maximum_fusion.refs_4_.pair_from), channel_id=1, source_target_pairs={{0,12},{4,0},{8,4},{12,8},{1,13},{5,1},{9,5},{13,9},{2,14},{6,2},{... | collective-permute-start | bytes 1179656 | tf_op jit(solution)/shard_map/ppermute | solution.py:478
  5.0 1.1 pad_maximum_fusion.1.refs_0_.refs_7_
  6.1 2.0 %collective-permute-start.3 = (bf16[256,768]{1,0:T(8,128)(2,1)S(1)}, bf16[256,768]{1,0:T(8,128)(2,1)S(1)}, u32[]{:S(2)}, u32[]{:S(2)}) collective-permute-start(bf16[256,768]{1,0:T(8,128)(2,1)S(1)} %pad_maximum_fusion.1.refs_0_.refs_7_), channel_id=1, source_target_pairs={{0,1},{1,2},{2,3},{3,0},{4,5},{5,6},{6,7},{7,4},{8,9},{9,10},{10,1... | collective-permute-start | bytes 1179656 | tf_op jit(solution)/shard_map/ppermute | solution.py:478
  8.2 4.6 %shard_map.174 = bf16[64,16,128]{2,1,0:T(8,128)(2,1)} custom-call(bf16[1280]{0:T(1024)(128)(2,1)} %gain_ref.1, s32[1,64]{1,0:T(1,128)} %order_ref.1, bf16[256,1280]{1,0:T(8,128)(2,1)} %bitcast.7, bf16[256,1280]{1,0:T(8,128)(2,1)} %bitcast.8, bf16[128,588]{1,0:T(8,128)(2,1)} %constant.4.clone.refs_2_, bf16[588,1280]{1,0:T(8,128)(2,1)} %refs_3_.1, ...), custom_call_target="tpu_custom_call" | custom-call | flops 1000000 | bytes 100000 | tf_op jit(solution)/shard_map/pallas_call | solution.py:508
  12.8 1.1 %collective-permute-done.1.refs_7_.refs_13_ = bf16[256,768]{1,0:T(8,128)(2,1)S(1)} collective-permute-done((bf16[256,768]{1,0:T(8,128)(2,1)S(1)}, bf16[256,768]{1,0:T(8,128)(2,1)S(1)}, u32[]{:S(2)}, u32[]{:S(2)}) %collective-permute-start.1) | collective-permute-done | bytes 393248 | tf_op jit(solution)/shard_map/ppermute | solution.py:478
  13.9 2.6 %collective-permute-done.3.refs_3_.refs_10_ = bf16[256,768]{1,0:T(8,128)(2,1)S(1)} collective-permute-done((bf16[256,768]{1,0:T(8,128)(2,1)S(1)}, bf16[256,768]{1,0:T(8,128)(2,1)S(1)}, u32[]{:S(2)}, u32[]{:S(2)}) %collective-permute-start.3) | collective-permute-done | bytes 393248 | tf_op jit(solution)/shard_map/ppermute | solution.py:478
  16.5 1.3 %collective-permute-done.2.refs_1_.refs_8_ = bf16[256,768]{1,0:T(8,128)(2,1)S(1)} collective-permute-done((bf16[256,768]{1,0:T(8,128)(2,1)S(1)}, bf16[256,768]{1,0:T(8,128)(2,1)S(1)}, u32[]{:S(2)}, u32[]{:S(2)}) %collective-permute-start.2) | collective-permute-done | bytes 393248 | tf_op jit(solution)/shard_map/ppermute | solution.py:478
  17.8 1.8 %collective-permute-start.4 = (bf16[256,768]{1,0:T(8,128)(2,1)S(1)}, bf16[256,768]{1,0:T(8,128)(2,1)S(1)}, u32[]{:S(2)}, u32[]{:S(2)}) collective-permute-start(bf16[256,768]{1,0:T(8,128)(2,1)S(1)} %pad_maximum_fusion.refs_4_.pair_from), channel_id=1, source_target_pairs={{0,8},{4,12},{8,0},{12,4},{1,9},{5,13},{9,1},{13,5},{2,10},{6,14},... | collective-permute-start | bytes 1179656 | tf_op jit(solution)/shard_map/ppermute | solution.py:478
  19.6 1.2 %collective-permute-start.5 = (bf16[256,768]{1,0:T(8,128)(2,1)S(1)}, bf16[256,768]{1,0:T(8,128)(2,1)S(1)}, u32[]{:S(2)}, u32[]{:S(2)}) collective-permute-start(bf16[256,768]{1,0:T(8,128)(2,1)S(1)} %pad_maximum_fusion.1.refs_0_.refs_7_), channel_id=1, source_target_pairs={{0,2},{1,3},{2,0},{3,1},{4,6},{5,7},{6,4},{7,5},{8,10},{9,11},{10,... | collective-permute-start | bytes 1179656 | tf_op jit(solution)/shard_map/ppermute | solution.py:478
  20.8 6.1 %shard_map.175 = (bf16[512,384]{1,0:T(8,128)(2,1)}, bf16[768,512]{1,0:T(8,128)(2,1)}) custom-call(bf16[512,3072]{1,0:T(8,128)(2,1)} %join_from, bf16[384,3072]{1,0:T(8,128)(2,1)} %out_w_from.1), custom_call_target="tpu_custom_call" | custom-call | flops 1000000 | bytes 100000 | tf_op jit(solution)/shard_map/pallas_call | solution.py:535
  27.4 2.6 %collective-permute-done.5.refs_2_.refs_9_ = bf16[256,768]{1,0:T(8,128)(2,1)S(1)} collective-permute-done((bf16[256,768]{1,0:T(8,128)(2,1)S(1)}, bf16[256,768]{1,0:T(8,128)(2,1)S(1)}, u32[]{:S(2)}, u32[]{:S(2)}) %collective-permute-start.5) | collective-permute-done | bytes 393248 | tf_op jit(solution)/shard_map/ppermute | solution.py:478
  30.0 10.3 %all-to-all-start = ((bf16[64,16,128]{2,1,0:T(8,128)(2,1)}), bf16[64,16,128]{2,1,0:T(8,128)(2,1)S(1)}, u32[]{:S(2)}, u32[]{:S(2)}) async-start(bf16[64,16,128]{2,1,0:T(8,128)(2,1)} %shard_map.174), calls=%async_computation | async-start | bytes 524288 | tf_op jit(solution)/shard_map/all_to_all | solution.py:548
  40.4 3.2 %shard_map.176.refs_0_ = f32[8,1024]{1,0:T(8,128)S(1)} custom-call(bf16[256,768]{1,0:T(8,128)(2,1)S(1)} %pad_maximum_fusion.1.refs_0_.refs_7_, bf16[256,768]{1,0:T(8,128)(2,1)S(1)} %collective-permute-done.2.refs_1_.refs_8_, bf16[256,768]{1,0:T(8,128)(2,1)S(1)} %collective-permute-done.5.refs_2_.refs_9_, ...), custom_call_target="tpu_custom_call" | custom-call | flops 1000000 | bytes 100000 | tf_op jit(solution)/shard_map/pallas_call | solution.py:551
  44.3 2.5 %collective-permute-start.7 = (f32[8,1024]{1,0:T(8,128)S(1)}, f32[8,1024]{1,0:T(8,128)S(1)}, u32[]{:S(2)}, u32[]{:S(2)}) collective-permute-start(f32[8,1024]{1,0:T(8,128)S(1)} %shard_map.176.refs_0_), channel_id=1, source_target_pairs={{0,2},{1,3},{2,0},{3,1},{4,6},{5,7},{6,4},{7,5},{8,10},{9,11},{10,... | collective-permute-start | bytes 98312 | tf_op jit(solution)/shard_map/ppermute | solution.py:478
  46.8 1.0 collective-permute-done.8.refs_3_
  47.8 1.9 %collective-permute-done.7.refs_2_ = f32[8,1024]{1,0:T(8,128)S(1)} collective-permute-done((f32[8,1024]{1,0:T(8,128)S(1)}, f32[8,1024]{1,0:T(8,128)S(1)}, u32[]{:S(2)}, u32[]{:S(2)}) %collective-permute-start.7) | collective-permute-done | bytes 32800 | tf_op jit(solution)/shard_map/ppermute | solution.py:478
  49.7 2.2 %collective-permute-done.6.refs_1_ = f32[8,1024]{1,0:T(8,128)S(1)} collective-permute-done((f32[8,1024]{1,0:T(8,128)S(1)}, f32[8,1024]{1,0:T(8,128)S(1)}, u32[]{:S(2)}, u32[]{:S(2)}) %collective-permute-start.6) | collective-permute-done | bytes 32800 | tf_op jit(solution)/shard_map/ppermute | solution.py:478
  53.2 15.2 %shard_map.177 = (f32[8,1024]{1,0:T(8,128)}, f32[8,1024]{1,0:T(8,128)}, f32[3,128,1024]{2,1,0:T(8,128)}, bf16[4,256,384]{2,1,0:T(8,128)(2,1)}, bf16[768,384]{1,0...) custom-call(s32[64]{0:T(128)} %owner_ref.1, ...), custom_call_target="tpu_custom_call" | custom-call | flops 1000000 | bytes 100000 | tf_op jit(solution)/shard_map/pallas_call | solution.py:559
  68.4 4.3 %all-to-all-start.1 = ((bf16[8,2,48,384]{3,2,1,0:T(8,128)(2,1)}), bf16[8,2,48,384]{3,2,1,0:T(8,128)(2,1)S(1)}, u32[]{:S(2)}, u32[]{:S(2)}) async-start(bf16[8,2,48,384]{3,2,1,0:T(8,128)(2,1)} %bitcast.9), calls=%async_computation.1 | async-start | bytes 1179648 | tf_op jit(solution)/shard_map/all_to_all | solution.py:601
  72.7 6.5 %shard_map.179 = (bf16[256,384]{1,0:T(8,128)(2,1)}, bf16[256,384]{1,0:T(8,128)(2,1)}, bf16[256,384]{1,0:T(8,128)(2,1)}, bf16[256,384]{1,0:T(8,128)(2,1)}, bf16[2,256,384]{2,1,0:T(8,128)(2,1)}) custom-call(f32[8,1024]{1,0:T(8,128)} %get-tuple-element.64.totals_ref, f32[8,1024]{1,0:T(8,128)} %get-tuple-element.65.dots_ref, ...), custom_call_target="tpu_custom_call" | custom-call | flops 1000000 | bytes 100000 | tf_op jit(solution)/shard_map/pallas_call | solution.py:588
  79.9 2.0 %collective-permute-start.10 = (bf16[2,256,384]{2,1,0:T(8,128)(2,1)S(1)}, bf16[2,256,384]{2,1,0:T(8,128)(2,1)S(1)}, u32[]{:S(2)}, u32[]{:S(2)}) collective-permute-start(bf16[2,256,384]{2,1,0:T(8,128)(2,1)S(1)} %copy-done.17), channel_id=1, source_target_pairs={{0,4},{4,8},{8,12},{12,0},{1,5},{5,9},{9,13},{13,1},{2,6},{6,10},{... | collective-permute-start | bytes 1179656 | tf_op jit(solution)/shard_map/ppermute | solution.py:482
  81.9 2.7 %collective-permute-start.11 = (bf16[2,256,384]{2,1,0:T(8,128)(2,1)S(1)}, bf16[2,256,384]{2,1,0:T(8,128)(2,1)S(1)}, u32[]{:S(2)}, u32[]{:S(2)}) collective-permute-start(bf16[2,256,384]{2,1,0:T(8,128)(2,1)S(1)} %copy-done.16), channel_id=1, source_target_pairs={{0,8},{4,12},{8,0},{12,4},{1,9},{5,13},{9,1},{13,5},{2,10},{6,14},... | collective-permute-start | bytes 1179656 | tf_op jit(solution)/shard_map/ppermute | solution.py:482
  84.5 1.5 %collective-permute-start.12 = (bf16[2,256,384]{2,1,0:T(8,128)(2,1)S(1)}, bf16[2,256,384]{2,1,0:T(8,128)(2,1)S(1)}, u32[]{:S(2)}, u32[]{:S(2)}) collective-permute-start(bf16[2,256,384]{2,1,0:T(8,128)(2,1)S(1)} %copy-done.15), channel_id=1, source_target_pairs={{0,12},{4,0},{8,4},{12,8},{1,13},{5,1},{9,5},{13,9},{2,14},{6,2},{... | collective-permute-start | bytes 1179656 | tf_op jit(solution)/shard_map/ppermute | solution.py:482
  87.6 8.0 %collective-permute-done.14.refs_6_ = bf16[256,384]{1,0:T(8,128)(2,1)S(1)} collective-permute-done((bf16[256,384]{1,0:T(8,128)(2,1)}, bf16[256,384]{1,0:T(8,128)(2,1)S(1)}, u32[]{:S(2)}, u32[]{:S(2)}) %collective-permute-start.14) | collective-permute-done | bytes 196640 | tf_op jit(solution)/shard_map/ppermute | solution.py:482
  95.6 4.5 %collective-permute-start.9 = (f32[48,384]{1,0:T(8,128)S(1)}, f32[48,384]{1,0:T(8,128)S(1)}, u32[]{:S(2)}, u32[]{:S(2)}) collective-permute-start(f32[48,384]{1,0:T(8,128)S(1)} %get-tuple-element.63), channel_id=1, source_target_pairs={{0,128},{128,0},{1,129},{129,1},{2,130},{130,2},{3,131},{131,3},{4... | collective-permute-start | bytes 221192 | tf_op jit(solution)/shard_map/ppermute | solution.py:614
  100.1 1.8 %collective-permute-done.11.refs_2_ = bf16[2,256,384]{2,1,0:T(8,128)(2,1)S(1)} collective-permute-done((bf16[2,256,384]{2,1,0:T(8,128)(2,1)S(1)}, bf16[2,256,384]{2,1,0:T(8,128)(2,1)S(1)}, u32[]{:S(2)}, u32[]{:S(2)}) %collective-permute-start.11) | collective-permute-done | bytes 393248 | tf_op jit(solution)/shard_map/ppermute | solution.py:482
  101.8 2.7 %collective-permute-done.9.other_ref = f32[48,384]{1,0:T(8,128)S(1)} collective-permute-done((f32[48,384]{1,0:T(8,128)S(1)}, f32[48,384]{1,0:T(8,128)S(1)}, u32[]{:S(2)}, u32[]{:S(2)}) %collective-permute-start.9) | collective-permute-done | bytes 73760 | tf_op jit(solution)/shard_map/ppermute | solution.py:614
  104.6 1.0 copy-done.8
  105.6 0.9 copy-done.9
  106.5 1.0 shard_map.180
  (49 shorter events, 4.8 us)
Async XLA Ops:
  1.7 38.6 %copy-start.4 = (bf16[256,768]{1,0:T(8,128)(2,1)}, bf16[256,768]{1,0:T(8,128)(2,1)S(1)}, u32[]{:S(2)}) copy-start(bf16[256,768]{1,0:T(8,128)(2,1)S(1)} %pad_maximum_fusion.refs_4_.pair_from) | copy-start | bytes 1179652
  1.7 12.1 %collective-permute-start.1 = (bf16[256,768]{1,0:T(8,128)(2,1)S(1)}, bf16[256,768]{1,0:T(8,128)(2,1)S(1)}, u32[]{:S(2)}, u32[]{:S(2)}) collective-permute-start(bf16[256,768]{1,0:T(8,128)(2,1)S(1)} %pad_maximum_fusion.refs_4_.pair_from), channel_id=1, source_target_pairs={{0,4},{4,8},{8,12},{12,0},{1,5},{5,9},{9,13},{13,1},{2,6},{6,10},{... | collective-permute-start | bytes 1179656 | tf_op jit(solution)/shard_map/ppermute | solution.py:478
  3.3 10.6 %collective-permute-start = (bf16[256,768]{1,0:T(8,128)(2,1)S(1)}, bf16[256,768]{1,0:T(8,128)(2,1)S(1)}, u32[]{:S(2)}, u32[]{:S(2)}) collective-permute-start(bf16[256,768]{1,0:T(8,128)(2,1)S(1)} %pad_maximum_fusion.refs_4_.pair_from), channel_id=1, source_target_pairs={{0,12},{4,0},{8,4},{12,8},{1,13},{5,1},{9,5},{13,9},{2,14},{6,2},{... | collective-permute-start | bytes 1179656 | tf_op jit(solution)/shard_map/ppermute | solution.py:478
  6.1 34.3 %copy-start = (bf16[256,768]{1,0:T(8,128)(2,1)}, bf16[256,768]{1,0:T(8,128)(2,1)S(1)}, u32[]{:S(2)}) copy-start(bf16[256,768]{1,0:T(8,128)(2,1)S(1)} %pad_maximum_fusion.1.refs_0_.refs_7_) | copy-start | bytes 1179652
  6.1 10.4 %collective-permute-start.3 = (bf16[256,768]{1,0:T(8,128)(2,1)S(1)}, bf16[256,768]{1,0:T(8,128)(2,1)S(1)}, u32[]{:S(2)}, u32[]{:S(2)}) collective-permute-start(bf16[256,768]{1,0:T(8,128)(2,1)S(1)} %pad_maximum_fusion.1.refs_0_.refs_7_), channel_id=1, source_target_pairs={{0,1},{1,2},{2,3},{3,0},{4,5},{5,6},{6,7},{7,4},{8,9},{9,10},{10,1... | collective-permute-start | bytes 1179656 | tf_op jit(solution)/shard_map/ppermute | solution.py:478
  8.1 9.6 %collective-permute-start.2 = (bf16[256,768]{1,0:T(8,128)(2,1)S(1)}, bf16[256,768]{1,0:T(8,128)(2,1)S(1)}, u32[]{:S(2)}, u32[]{:S(2)}) collective-permute-start(bf16[256,768]{1,0:T(8,128)(2,1)S(1)} %pad_maximum_fusion.1.refs_0_.refs_7_), channel_id=1, source_target_pairs={{0,3},{1,0},{2,1},{3,2},{4,7},{5,4},{6,5},{7,6},{8,11},{9,8},{10,9... | collective-permute-start | bytes 1179656 | tf_op jit(solution)/shard_map/ppermute | solution.py:478
  13.8 26.5 %copy-start.5 = (bf16[256,768]{1,0:T(8,128)(2,1)}, bf16[256,768]{1,0:T(8,128)(2,1)S(1)}, u32[]{:S(2)}) copy-start(bf16[256,768]{1,0:T(8,128)(2,1)S(1)} %collective-permute-done.1.refs_7_.refs_13_) | copy-start | bytes 1179652
  13.8 26.5 %copy-start.6 = (bf16[256,768]{1,0:T(8,128)(2,1)}, bf16[256,768]{1,0:T(8,128)(2,1)S(1)}, u32[]{:S(2)}) copy-start(bf16[256,768]{1,0:T(8,128)(2,1)S(1)} %collective-permute-done.refs_5_.refs_11_) | copy-start | bytes 1179652
  16.5 23.9 %copy-start.1 = (bf16[256,768]{1,0:T(8,128)(2,1)}, bf16[256,768]{1,0:T(8,128)(2,1)S(1)}, u32[]{:S(2)}) copy-start(bf16[256,768]{1,0:T(8,128)(2,1)S(1)} %collective-permute-done.3.refs_3_.refs_10_) | copy-start | bytes 1179652
  17.8 22.6 %copy-start.2 = (bf16[256,768]{1,0:T(8,128)(2,1)}, bf16[256,768]{1,0:T(8,128)(2,1)S(1)}, u32[]{:S(2)}) copy-start(bf16[256,768]{1,0:T(8,128)(2,1)S(1)} %collective-permute-done.2.refs_1_.refs_8_) | copy-start | bytes 1179652
  17.8 9.7 %collective-permute-start.4 = (bf16[256,768]{1,0:T(8,128)(2,1)S(1)}, bf16[256,768]{1,0:T(8,128)(2,1)S(1)}, u32[]{:S(2)}, u32[]{:S(2)}) collective-permute-start(bf16[256,768]{1,0:T(8,128)(2,1)S(1)} %pad_maximum_fusion.refs_4_.pair_from), channel_id=1, source_target_pairs={{0,8},{4,12},{8,0},{12,4},{1,9},{5,13},{9,1},{13,5},{2,10},{6,14},... | collective-permute-start | bytes 1179656 | tf_op jit(solution)/shard_map/ppermute | solution.py:478
  19.6 10.5 %collective-permute-start.5 = (bf16[256,768]{1,0:T(8,128)(2,1)S(1)}, bf16[256,768]{1,0:T(8,128)(2,1)S(1)}, u32[]{:S(2)}, u32[]{:S(2)}) collective-permute-start(bf16[256,768]{1,0:T(8,128)(2,1)S(1)} %pad_maximum_fusion.1.refs_0_.refs_7_), channel_id=1, source_target_pairs={{0,2},{1,3},{2,0},{3,1},{4,6},{5,7},{6,4},{7,5},{8,10},{9,11},{10,... | collective-permute-start | bytes 1179656 | tf_op jit(solution)/shard_map/ppermute | solution.py:478
  27.4 24.5 %copy-start.7 = (bf16[256,768]{1,0:T(8,128)(2,1)}, bf16[256,768]{1,0:T(8,128)(2,1)S(1)}, u32[]{:S(2)}) copy-start(bf16[256,768]{1,0:T(8,128)(2,1)S(1)} %collective-permute-done.4.refs_6_.refs_12_) | copy-start | bytes 1179652
  30.0 21.9 %copy-start.3 = (bf16[256,768]{1,0:T(8,128)(2,1)}, bf16[256,768]{1,0:T(8,128)(2,1)S(1)}, u32[]{:S(2)}) copy-start(bf16[256,768]{1,0:T(8,128)(2,1)S(1)} %collective-permute-done.5.refs_2_.refs_9_) | copy-start | bytes 1179652
  30.0 21.9 %all-to-all-start = ((bf16[64,16,128]{2,1,0:T(8,128)(2,1)}), bf16[64,16,128]{2,1,0:T(8,128)(2,1)S(1)}, u32[]{:S(2)}, u32[]{:S(2)}) async-start(bf16[64,16,128]{2,1,0:T(8,128)(2,1)} %shard_map.174), calls=%async_computation | async-start | bytes 524288 | tf_op jit(solution)/shard_map/all_to_all | solution.py:548
  43.6 8.3 %copy-start.10 = (f32[8,1024]{1,0:T(8,128)}, f32[8,1024]{1,0:T(8,128)S(1)}, u32[]{:S(2)}) copy-start(f32[8,1024]{1,0:T(8,128)S(1)} %shard_map.176.refs_0_) | copy-start | bytes 98308
  43.6 4.2 %collective-permute-start.8 = (f32[8,1024]{1,0:T(8,128)S(1)}, f32[8,1024]{1,0:T(8,128)S(1)}, u32[]{:S(2)}, u32[]{:S(2)}) collective-permute-start(f32[8,1024]{1,0:T(8,128)S(1)} %shard_map.176.refs_0_), channel_id=1, source_target_pairs={{0,1},{1,2},{2,3},{3,0},{4,5},{5,6},{6,7},{7,4},{8,9},{9,10},{10,1... | collective-permute-start | bytes 98312 | tf_op jit(solution)/shard_map/ppermute | solution.py:478
  44.3 5.4 %collective-permute-start.7 = (f32[8,1024]{1,0:T(8,128)S(1)}, f32[8,1024]{1,0:T(8,128)S(1)}, u32[]{:S(2)}, u32[]{:S(2)}) collective-permute-start(f32[8,1024]{1,0:T(8,128)S(1)} %shard_map.176.refs_0_), channel_id=1, source_target_pairs={{0,2},{1,3},{2,0},{3,1},{4,6},{5,7},{6,4},{7,5},{8,10},{9,11},{10,... | collective-permute-start | bytes 98312 | tf_op jit(solution)/shard_map/ppermute | solution.py:478
  46.8 5.1 %collective-permute-start.6 = (f32[8,1024]{1,0:T(8,128)S(1)}, f32[8,1024]{1,0:T(8,128)S(1)}, u32[]{:S(2)}, u32[]{:S(2)}) collective-permute-start(f32[8,1024]{1,0:T(8,128)S(1)} %shard_map.176.refs_0_), channel_id=1, source_target_pairs={{0,3},{1,0},{2,1},{3,2},{4,7},{5,4},{6,5},{7,6},{8,11},{9,8},{10,9... | collective-permute-start | bytes 98312 | tf_op jit(solution)/shard_map/ppermute | solution.py:478
  47.8 4.1 %copy-start.12 = (f32[8,1024]{1,0:T(8,128)}, f32[8,1024]{1,0:T(8,128)S(1)}, u32[]{:S(2)}) copy-start(f32[8,1024]{1,0:T(8,128)S(1)} %collective-permute-done.8.refs_3_) | copy-start | bytes 98308
  49.7 2.2 %copy-start.13 = (f32[8,1024]{1,0:T(8,128)}, f32[8,1024]{1,0:T(8,128)S(1)}, u32[]{:S(2)}) copy-start(f32[8,1024]{1,0:T(8,128)S(1)} %collective-permute-done.7.refs_2_) | copy-start | bytes 98308
  68.4 19.1 %all-to-all-start.1 = ((bf16[8,2,48,384]{3,2,1,0:T(8,128)(2,1)}), bf16[8,2,48,384]{3,2,1,0:T(8,128)(2,1)S(1)}, u32[]{:S(2)}, u32[]{:S(2)}) async-start(bf16[8,2,48,384]{3,2,1,0:T(8,128)(2,1)} %bitcast.9), calls=%async_computation.1 | async-start | bytes 1179648 | tf_op jit(solution)/shard_map/all_to_all | solution.py:601
  72.7 7.2 %copy-start.17 = (bf16[2,256,384]{2,1,0:T(8,128)(2,1)S(1)}, bf16[2,256,384]{2,1,0:T(8,128)(2,1)}, u32[]{:S(2)}) copy-start(bf16[2,256,384]{2,1,0:T(8,128)(2,1)} %get-tuple-element.69) | copy-start | bytes 1179652
  72.7 9.2 %copy-start.16 = (bf16[2,256,384]{2,1,0:T(8,128)(2,1)S(1)}, bf16[2,256,384]{2,1,0:T(8,128)(2,1)}, u32[]{:S(2)}) copy-start(bf16[2,256,384]{2,1,0:T(8,128)(2,1)} %get-tuple-element.70) | copy-start | bytes 1179652
  72.7 11.9 %copy-start.15 = (bf16[2,256,384]{2,1,0:T(8,128)(2,1)S(1)}, bf16[2,256,384]{2,1,0:T(8,128)(2,1)}, u32[]{:S(2)}) copy-start(bf16[2,256,384]{2,1,0:T(8,128)(2,1)} %get-tuple-element.71) | copy-start | bytes 1179652
  79.2 7.7 %collective-permute-start.13 = (bf16[256,384]{1,0:T(8,128)(2,1)}, bf16[256,384]{1,0:T(8,128)(2,1)S(1)}, u32[]{:S(2)}, u32[]{:S(2)}) collective-permute-start(bf16[256,384]{1,0:T(8,128)(2,1)} %get-tuple-element.73), channel_id=1, source_target_pairs={{0,1},{1,2},{2,3},{3,0},{4,5},{5,6},{6,7},{7,4},{8,9},{9,10},{10,1... | collective-permute-start | bytes 589832 | tf_op jit(solution)/shard_map/ppermute | solution.py:482
  79.9 20.2 %collective-permute-start.10 = (bf16[2,256,384]{2,1,0:T(8,128)(2,1)S(1)}, bf16[2,256,384]{2,1,0:T(8,128)(2,1)S(1)}, u32[]{:S(2)}, u32[]{:S(2)}) collective-permute-start(bf16[2,256,384]{2,1,0:T(8,128)(2,1)S(1)} %copy-done.17), channel_id=1, source_target_pairs={{0,4},{4,8},{8,12},{12,0},{1,5},{5,9},{9,13},{13,1},{2,6},{6,10},{... | collective-permute-start | bytes 1179656 | tf_op jit(solution)/shard_map/ppermute | solution.py:482
  81.9 20.0 %collective-permute-start.11 = (bf16[2,256,384]{2,1,0:T(8,128)(2,1)S(1)}, bf16[2,256,384]{2,1,0:T(8,128)(2,1)S(1)}, u32[]{:S(2)}, u32[]{:S(2)}) collective-permute-start(bf16[2,256,384]{2,1,0:T(8,128)(2,1)S(1)} %copy-done.16), channel_id=1, source_target_pairs={{0,8},{4,12},{8,0},{12,4},{1,9},{5,13},{9,1},{13,5},{2,10},{6,14},... | collective-permute-start | bytes 1179656 | tf_op jit(solution)/shard_map/ppermute | solution.py:482
  84.5 17.3 %collective-permute-start.12 = (bf16[2,256,384]{2,1,0:T(8,128)(2,1)S(1)}, bf16[2,256,384]{2,1,0:T(8,128)(2,1)S(1)}, u32[]{:S(2)}, u32[]{:S(2)}) collective-permute-start(bf16[2,256,384]{2,1,0:T(8,128)(2,1)S(1)} %copy-done.15), channel_id=1, source_target_pairs={{0,12},{4,0},{8,4},{12,8},{1,13},{5,1},{9,5},{13,9},{2,14},{6,2},{... | collective-permute-start | bytes 1179656 | tf_op jit(solution)/shard_map/ppermute | solution.py:482
  86.0 9.6 %collective-permute-start.14 = (bf16[256,384]{1,0:T(8,128)(2,1)}, bf16[256,384]{1,0:T(8,128)(2,1)S(1)}, u32[]{:S(2)}, u32[]{:S(2)}) collective-permute-start(bf16[256,384]{1,0:T(8,128)(2,1)} %get-tuple-element.74), channel_id=1, source_target_pairs={{0,2},{1,3},{2,0},{3,1},{4,6},{5,7},{6,4},{7,5},{8,10},{9,11},{10,... | collective-permute-start | bytes 589832 | tf_op jit(solution)/shard_map/ppermute | solution.py:482
  86.9 13.1 %collective-permute-start.15 = (bf16[256,384]{1,0:T(8,128)(2,1)}, bf16[256,384]{1,0:T(8,128)(2,1)S(1)}, u32[]{:S(2)}, u32[]{:S(2)}) collective-permute-start(bf16[256,384]{1,0:T(8,128)(2,1)} %get-tuple-element.75), channel_id=1, source_target_pairs={{0,3},{1,0},{2,1},{3,2},{4,7},{5,4},{6,5},{7,6},{8,11},{9,8},{10,9... | collective-permute-start | bytes 589832 | tf_op jit(solution)/shard_map/ppermute | solution.py:482
  95.6 9.0 %collective-permute-start.9 = (f32[48,384]{1,0:T(8,128)S(1)}, f32[48,384]{1,0:T(8,128)S(1)}, u32[]{:S(2)}, u32[]{:S(2)}) collective-permute-start(f32[48,384]{1,0:T(8,128)S(1)} %get-tuple-element.63), channel_id=1, source_target_pairs={{0,128},{128,0},{1,129},{129,1},{2,130},{130,2},{3,131},{131,3},{4... | collective-permute-start | bytes 221192 | tf_op jit(solution)/shard_map/ppermute | solution.py:614
  (4 other events, 3.3 us)

commit v10 on v6

--- a/solution.py
+++ b/solution.py
@@ -204,24 +204,18 @@
         rows = dot(pick, join_ref[:, pl.ds(pair * 384, 384)], NT).astype(bf16)
         z, core, x = pair // 4, (pair % 4) // 2, (pair % 2) * 2
         for step in range(2):
-            picked_ref[pl.ds((core * GRID + x + step) * 96 + z * 48, 48), :] = rows[
+            picked_ref[pl.ds((z * 2 + core) * 192 + (x + step) * 48, 48), :] = rows[
                 step * 48 : (step + 1) * 48
             ]
 
 
 def totals_kernel(*refs):
-    out_ref, query_held, key_held, query_arrived, key_arrived = refs[2 * GRID :]
-    key_copies = fetch_halves(refs[GRID : 2 * GRID], 0, key_held, key_arrived)
-    query_copies = fetch_halves(refs[:GRID], 0, query_held, query_arrived)
-    for copy in key_copies:
-        copy.wait()
+    query_refs, key_refs, out_ref = refs[:GRID], refs[GRID : 2 * GRID], refs[2 * GRID]
     for head in range(HEADS_HERE):
         columns = pl.ds(head * HDIM, HDIM)
         for piece in range(GRID):
-            if head == 0:
-                query_copies[piece].wait()
-            query = query_held[piece, :, columns]
-            scores = [dot(key_held[other, :, columns], query, NT) for other in range(GRID)]
+            query = query_refs[piece][:, columns]
+            scores = [dot(key_ref[:, columns], query, NT) for key_ref in key_refs]
             top = functools.reduce(
                 jnp.maximum, [jnp.max(tile, axis=0, keepdims=True) for tile in scores]
             ) * (SCORE_SCALE * LOG2E)
@@ -392,25 +386,17 @@
         send.wait()
 
 
-def half_kernel(parts_ref, kept_ref, sent_ref):
-    here_z = lax.axis_index("zh")
-    for out_ref, half in ((kept_ref, here_z), (sent_ref, 1 - here_z)):
-        out_ref[...] = sum(parts_ref[source, half].astype(f32) for source in range(2 * GRID))
-
-
-def sum_kernel(kept_ref, other_ref, *refs):
+def weight_kernel(parts_ref, out_ref):
+    out_ref[...] = sum(parts_ref[source].astype(f32) for source in range(4)).astype(bf16)
+
+
+def sum_kernel(parts_ref, *refs):
     pair_refs, query_refs = refs[:GRID], refs[GRID : 2 * GRID]
-    query_out, key_out, value_out, weight_out, query_held, pair_held, *arrived = refs[2 * GRID :]
-    pair_copies = fetch(pair_refs, [pair_held.at[step] for step in range(GRID)], arrived[1])
-    query_copies = fetch(query_refs, [query_held.at[step] for step in range(GRID)], arrived[0])
-    weight_out[...] = kept_ref[...] + other_ref[...]
-    for copy in query_copies:
-        copy.wait()
-    query_out[0] = sum(query_held[step].astype(f32) for step in range(GRID)).astype(bf16)
-    for copy in pair_copies:
-        copy.wait()
+    query_out, key_out, value_out, weight_out = refs[2 * GRID :]
+    weight_out[...] = sum(parts_ref[source].astype(f32) for source in range(GRID))
+    query_out[0] = sum(ref[...].astype(f32) for ref in query_refs).astype(bf16)
     for place, out_ref in enumerate((key_out, value_out)):
-        out_ref[0] = sum(pair_held[step, place].astype(f32) for step in range(GRID)).astype(bf16)
+        out_ref[0] = sum(ref[place].astype(f32) for ref in pair_refs).astype(bf16)
 
 
 def call(kernel, out_shape, in_specs, scratch=(), out_spec=None, limit=56):
@@ -513,8 +499,7 @@
     totals = call(
         totals_kernel,
         shape((8, BLOCK), f32),
-        [ANY] * (2 * GRID),
-        scratch=HELD * 2 + ARRIVED * 2,
+        [VMEM] * (2 * GRID),
         limit=24,
     )(*query_outs, *key_values)
     total_pieces = gather(totals, "hy")
@@ -544,19 +529,16 @@
     )(frame_owner, conv_w, *total_pieces, received, joint, picked, *query_outs, *key_values)
     query_parts, pair_parts, weight_part = outs[:GRID], outs[GRID : 2 * GRID], outs[2 * GRID]
     weight_parts = lax.all_to_all(
-        weight_part.reshape(8, 2, 48, FEATS),
-        ("core", "hx"),
+        weight_part.reshape(4, 4 * 48, FEATS),
+        ("zh", "core"),
         split_axis=0,
         concat_axis=0,
         tiled=True,
     )
-    weight_kept, weight_sent = call(
-        half_kernel,
-        (shape((48, FEATS), f32), shape((48, FEATS), f32)),
-        [VMEM],
-        limit=8,
-    )(weight_parts)
-    weight_other = lax.ppermute(weight_sent, "zh", [(0, 1), (1, 0)])
+    weight_blocks = call(weight_kernel, shape((4 * 48, FEATS), bf16), [VMEM], limit=8)(weight_parts)
+    weight_parts = lax.all_to_all(
+        weight_blocks.reshape(4, 48, FEATS), "hx", split_axis=0, concat_axis=0, tiled=True
+    )
     pair_back = [pair_parts[0]] + [
         to_ahead(pair_parts[step], "hx", step) for step in range(1, GRID)
     ]
@@ -568,10 +550,9 @@
     return call(
         sum_kernel,
         (rows, rows, rows, shape((48, FEATS), f32)),
-        [VMEM] * 2 + [ANY] * (2 * GRID),
-        scratch=HELD + [pltpu.VMEM((GRID, 2, ROWS_HERE, FEATS), bf16)] + ARRIVED * 2,
-        limit=8,
-    )(weight_kept, weight_other, *pair_back, *query_back)
+        [VMEM] * (1 + 2 * GRID),
+        limit=16,
+    )(weight_parts, *pair_back, *query_back)
 
 
 def solution(mesh):

time: 110 us -> 108 us (0.982); the launches traced: 108 us -> 108 us
  waiting for transfers between devices: 28.4 us -> 31.8 us
  Pallas kernels: 34.7 us -> 32.6 us
  local copies, waits for them, and re-layouts: 3.24 us -> 1.33 us
    all_to_all x1 -> x2, waiting for transfers between devices: 2.24 us -> 18.2 us  [the longest x1 12.2 us: per_device(): lax.all_to_all(weight_part.reshape(4, 4 * 48, FEATS), ('zh', 'core'), spl...]
    ppermute x6, waiting for transfers between devices: 12.9 us -> 0.45 us  [to_ahead(): lax.ppermute(block, axis, [(i, (i + step) % GRID) for i in range(GRID)])]
    all_to_all x1 -> x2, starting transfers between devices: 4.25 us -> 10.1 us  [the longest x1 5.9 us: per_device(): lax.all_to_all(weight_part.reshape(4, 4 * 48, FEATS), ('zh', 'core'), spl...]
    ppermute x1 -> x0, starting transfers between devices: 4.5 us -> none  [per_device(): weight_other = lax.ppermute(weight_sent, 'zh', [(0, 1), (1, 0)])]
    pallas_call x3, Pallas kernels: 7.05 us -> 4.93 us  [the longest x1 3.2 us: per_device(): call(totals_kernel, shape((8, BLOCK), f32), [VMEM] * (2 * GRID), limit=24)]
    unnamed x30, local copies, waits for them, and re-layouts: 3.24 us -> 1.33 us
where the time goes in v10:
time: 108 us
  starting transfers between devices  39 us (36%)
  Pallas kernels  32.6 us (30%)
  waiting for transfers between devices  31.8 us (29%)
  other arithmetic  2.11 us (2%)
  local copies, waits for them, and re-layouts  1.33 us (1%)
    pallas_call x1, Pallas kernels, per_device(): call(grads_kernel, tuple([shape((ROWS_HERE, FEATS), bf16)] * GRID) + tupl...  16.9 us
    ppermute x9, waiting for transfers between devices, from_ahead(): lax.ppermute(block, axis, [(i, (i - step) % GRID) for i in range(GRID)])  13.2 us
    all_to_all x1, waiting for transfers between devices, per_device(): lax.all_to_all(weight_part.reshape(4, 4 * 48, FEATS), ('zh', 'core'), spl...  12.2 us
    ppermute x9, starting transfers between devices, from_ahead(): lax.ppermute(block, axis, [(i, (i - step) % GRID) for i in range(GRID)])  11.5 us
    all_to_all x1, starting transfers between devices, per_device(): lax.all_to_all(windows, ('tm', 'hx', 'hy'), split_axis=0, concat_axis=0,...  10.3 us
    ppermute x6, starting transfers between devices, to_ahead(): lax.ppermute(block, axis, [(i, (i + step) % GRID) for i in range(GRID)])  7.17 us
    pallas_call x1, Pallas kernels, per_device(): call(weights_kernel, (shape((QUARTERS * LANES, FEATS), bf16), shape((768,...  6.14 us
    all_to_all x1, waiting for transfers between devices, per_device(): lax.all_to_all(weight_blocks.reshape(4, 48, FEATS), 'hx', split_axis=0, c...  6.02 us
  transfers between devices with their start and end apart: 18, of which 11 were waited for; matrix products, arithmetic and copies ran while one was open for 1% of the time, Pallas kernels for 14%

profile of v10, /device:TPU:24, one launch (start us, length us, event | category | flops | bytes accessed | tf_op | source)
XLA Modules:
  0.0 107.7 jit_solution(1633531756551125244)
XLA Ops:
  0.6 1.1 pad_maximum_fusion.refs_4_.refs_11_
  1.7 1.6 %collective-permute-start.1 = (bf16[256,768]{1,0:T(8,128)(2,1)S(1)}, bf16[256,768]{1,0:T(8,128)(2,1)S(1)}, u32[]{:S(2)}, u32[]{:S(2)}) collective-permute-start(bf16[256,768]{1,0:T(8,128)(2,1)S(1)} %pad_maximum_fusion.refs_4_.refs_11_), channel_id=1, source_target_pairs={{0,4},{4,8},{8,12},{12,0},{1,5},{5,9},{9,13},{13,1},{2,6},{6,10},{... | collective-permute-start | bytes 1179656 | tf_op jit(solution)/shard_map/ppermute | solution.py:426
  3.3 1.7 %collective-permute-start = (bf16[256,768]{1,0:T(8,128)(2,1)S(1)}, bf16[256,768]{1,0:T(8,128)(2,1)S(1)}, u32[]{:S(2)}, u32[]{:S(2)}) collective-permute-start(bf16[256,768]{1,0:T(8,128)(2,1)S(1)} %pad_maximum_fusion.refs_4_.refs_11_), channel_id=1, source_target_pairs={{0,12},{4,0},{8,4},{12,8},{1,13},{5,1},{9,5},{13,9},{2,14},{6,2},{... | collective-permute-start | bytes 1179656 | tf_op jit(solution)/shard_map/ppermute | solution.py:426
  5.0 1.1 pad_maximum_fusion.1.refs_0_.refs_7_
  6.1 2.0 %collective-permute-start.3 = (bf16[256,768]{1,0:T(8,128)(2,1)S(1)}, bf16[256,768]{1,0:T(8,128)(2,1)S(1)}, u32[]{:S(2)}, u32[]{:S(2)}) collective-permute-start(bf16[256,768]{1,0:T(8,128)(2,1)S(1)} %pad_maximum_fusion.1.refs_0_.refs_7_), channel_id=1, source_target_pairs={{0,1},{1,2},{2,3},{3,0},{4,5},{5,6},{6,7},{7,4},{8,9},{9,10},{10,1... | collective-permute-start | bytes 1179656 | tf_op jit(solution)/shard_map/ppermute | solution.py:426
  8.2 4.6 %shard_map.174 = bf16[64,16,128]{2,1,0:T(8,128)(2,1)} custom-call(bf16[1280]{0:T(1024)(128)(2,1)} %gain_ref.1, s32[1,64]{1,0:T(1,128)} %order_ref.1, bf16[256,1280]{1,0:T(8,128)(2,1)} %bitcast.8, bf16[256,1280]{1,0:T(8,128)(2,1)} %bitcast.9, bf16[128,588]{1,0:T(8,128)(2,1)} %constant.4.clone.refs_2_, bf16[588,1280]{1,0:T(8,128)(2,1)} %refs_3_.1, ...), custom_call_target="tpu_custom_call" | custom-call | flops 1000000 | bytes 100000 | tf_op jit(solution)/shard_map/pallas_call | solution.py:456
  12.8 1.1 %collective-permute-done.1.refs_7_.refs_14_ = bf16[256,768]{1,0:T(8,128)(2,1)S(1)} collective-permute-done((bf16[256,768]{1,0:T(8,128)(2,1)S(1)}, bf16[256,768]{1,0:T(8,128)(2,1)S(1)}, u32[]{:S(2)}, u32[]{:S(2)}) %collective-permute-start.1) | collective-permute-done | bytes 393248 | tf_op jit(solution)/shard_map/ppermute | solution.py:426
  13.9 2.6 %collective-permute-done.3.refs_3_.refs_10_ = bf16[256,768]{1,0:T(8,128)(2,1)S(1)} collective-permute-done((bf16[256,768]{1,0:T(8,128)(2,1)S(1)}, bf16[256,768]{1,0:T(8,128)(2,1)S(1)}, u32[]{:S(2)}, u32[]{:S(2)}) %collective-permute-start.3) | collective-permute-done | bytes 393248 | tf_op jit(solution)/shard_map/ppermute | solution.py:426
  16.5 1.3 %collective-permute-done.2.refs_1_.refs_8_ = bf16[256,768]{1,0:T(8,128)(2,1)S(1)} collective-permute-done((bf16[256,768]{1,0:T(8,128)(2,1)S(1)}, bf16[256,768]{1,0:T(8,128)(2,1)S(1)}, u32[]{:S(2)}, u32[]{:S(2)}) %collective-permute-start.2) | collective-permute-done | bytes 393248 | tf_op jit(solution)/shard_map/ppermute | solution.py:426
  17.8 1.8 %collective-permute-start.4 = (bf16[256,768]{1,0:T(8,128)(2,1)S(1)}, bf16[256,768]{1,0:T(8,128)(2,1)S(1)}, u32[]{:S(2)}, u32[]{:S(2)}) collective-permute-start(bf16[256,768]{1,0:T(8,128)(2,1)S(1)} %pad_maximum_fusion.refs_4_.refs_11_), channel_id=1, source_target_pairs={{0,8},{4,12},{8,0},{12,4},{1,9},{5,13},{9,1},{13,5},{2,10},{6,14},... | collective-permute-start | bytes 1179656 | tf_op jit(solution)/shard_map/ppermute | solution.py:426
  19.6 1.2 %collective-permute-start.5 = (bf16[256,768]{1,0:T(8,128)(2,1)S(1)}, bf16[256,768]{1,0:T(8,128)(2,1)S(1)}, u32[]{:S(2)}, u32[]{:S(2)}) collective-permute-start(bf16[256,768]{1,0:T(8,128)(2,1)S(1)} %pad_maximum_fusion.1.refs_0_.refs_7_), channel_id=1, source_target_pairs={{0,2},{1,3},{2,0},{3,1},{4,6},{5,7},{6,4},{7,5},{8,10},{9,11},{10,... | collective-permute-start | bytes 1179656 | tf_op jit(solution)/shard_map/ppermute | solution.py:426
  20.8 6.1 %shard_map.175 = (bf16[512,384]{1,0:T(8,128)(2,1)}, bf16[768,512]{1,0:T(8,128)(2,1)}) custom-call(bf16[512,3072]{1,0:T(8,128)(2,1)} %join_from, bf16[384,3072]{1,0:T(8,128)(2,1)} %out_w_from.1), custom_call_target="tpu_custom_call" | custom-call | flops 1000000 | bytes 100000 | tf_op jit(solution)/shard_map/pallas_call | solution.py:483
  27.4 2.6 %collective-permute-done.5.refs_2_.refs_9_ = bf16[256,768]{1,0:T(8,128)(2,1)S(1)} collective-permute-done((bf16[256,768]{1,0:T(8,128)(2,1)S(1)}, bf16[256,768]{1,0:T(8,128)(2,1)S(1)}, u32[]{:S(2)}, u32[]{:S(2)}) %collective-permute-start.5) | collective-permute-done | bytes 393248 | tf_op jit(solution)/shard_map/ppermute | solution.py:426
  30.0 10.3 %all-to-all-start = ((bf16[64,16,128]{2,1,0:T(8,128)(2,1)}), bf16[64,16,128]{2,1,0:T(8,128)(2,1)S(1)}, u32[]{:S(2)}, u32[]{:S(2)}) async-start(bf16[64,16,128]{2,1,0:T(8,128)(2,1)} %shard_map.174), calls=%async_computation | async-start | bytes 524288 | tf_op jit(solution)/shard_map/all_to_all | solution.py:496
  40.4 3.2 %shard_map.176.refs_0_ = f32[8,1024]{1,0:T(8,128)S(1)} custom-call(bf16[256,768]{1,0:T(8,128)(2,1)S(1)} %pad_maximum_fusion.1.refs_0_.refs_7_, bf16[256,768]{1,0:T(8,128)(2,1)S(1)} %collective-permute-done.2.refs_1_.refs_8_, bf16[256,768]{1,0:T(8,128)(2,1)S(1)} %collective-permute-done.5.refs_2_.refs_9_, ...), custom_call_target="tpu_custom_call" | custom-call | flops 1000000 | bytes 100000 | tf_op jit(solution)/shard_map/pallas_call | solution.py:499
  44.1 2.5 %collective-permute-start.7 = (f32[8,1024]{1,0:T(8,128)S(1)}, f32[8,1024]{1,0:T(8,128)S(1)}, u32[]{:S(2)}, u32[]{:S(2)}) collective-permute-start(f32[8,1024]{1,0:T(8,128)S(1)} %shard_map.176.refs_0_), channel_id=1, source_target_pairs={{0,2},{1,3},{2,0},{3,1},{4,6},{5,7},{6,4},{7,5},{8,10},{9,11},{10,... | collective-permute-start | bytes 98312 | tf_op jit(solution)/shard_map/ppermute | solution.py:426
  46.6 1.1 collective-permute-done.8.refs_3_
  47.7 1.9 %collective-permute-done.7.refs_2_ = f32[8,1024]{1,0:T(8,128)S(1)} collective-permute-done((f32[8,1024]{1,0:T(8,128)S(1)}, f32[8,1024]{1,0:T(8,128)S(1)}, u32[]{:S(2)}, u32[]{:S(2)}) %collective-permute-start.7) | collective-permute-done | bytes 32800 | tf_op jit(solution)/shard_map/ppermute | solution.py:426
  49.5 2.2 %collective-permute-done.6.refs_1_ = f32[8,1024]{1,0:T(8,128)S(1)} collective-permute-done((f32[8,1024]{1,0:T(8,128)S(1)}, f32[8,1024]{1,0:T(8,128)S(1)}, u32[]{:S(2)}, u32[]{:S(2)}) %collective-permute-start.6) | collective-permute-done | bytes 32800 | tf_op jit(solution)/shard_map/ppermute | solution.py:426
  52.3 0.7 copy-done.11
  53.1 16.9 %shard_map.177 = (bf16[256,384]{1,0:T(8,128)(2,1)}, bf16[256,384]{1,0:T(8,128)(2,1)}, bf16[256,384]{1,0:T(8,128)(2,1)}, bf16[256,384]{1,0:T(8,128)(2,1)}, bf16[2...) custom-call(s32[64]{0:T(128)} %owner_ref.1, ...), custom_call_target="tpu_custom_call" | custom-call | flops 1000000 | bytes 100000 | tf_op jit(solution)/shard_map/pallas_call | solution.py:506
  70.0 5.9 %all-to-all-start.1 = ((bf16[4,192,384]{2,1,0:T(8,128)(2,1)}), bf16[4,192,384]{2,1,0:T(8,128)(2,1)S(1)}, u32[]{:S(2)}, u32[]{:S(2)}) async-start(bf16[4,192,384]{2,1,0:T(8,128)(2,1)} %bitcast.10), calls=%async_computation.1 | async-start | bytes 1179648 | tf_op jit(solution)/shard_map/all_to_all | solution.py:531
  75.9 0.6 collective-permute-start.12
  76.5 1.5 %collective-permute-start.9 = (bf16[2,256,384]{2,1,0:T(8,128)(2,1)}, bf16[2,256,384]{2,1,0:T(8,128)(2,1)S(1)}, u32[]{:S(2)}, u32[]{:S(2)}) collective-permute-start(bf16[2,256,384]{2,1,0:T(8,128)(2,1)} %get-tuple-element.57), channel_id=1, source_target_pairs={{0,4},{4,8},{8,12},{12,0},{1,5},{5,9},{9,13},{13,1},{2,6},{6,10},{... | collective-permute-start | bytes 1179656 | tf_op jit(solution)/shard_map/ppermute | solution.py:430
  78.0 2.7 %collective-permute-start.10 = (bf16[2,256,384]{2,1,0:T(8,128)(2,1)}, bf16[2,256,384]{2,1,0:T(8,128)(2,1)S(1)}, u32[]{:S(2)}, u32[]{:S(2)}) collective-permute-start(bf16[2,256,384]{2,1,0:T(8,128)(2,1)} %get-tuple-element.58), channel_id=1, source_target_pairs={{0,8},{4,12},{8,0},{12,4},{1,9},{5,13},{9,1},{13,5},{2,10},{6,14},... | collective-permute-start | bytes 1179656 | tf_op jit(solution)/shard_map/ppermute | solution.py:430
  80.6 1.5 %collective-permute-start.11 = (bf16[2,256,384]{2,1,0:T(8,128)(2,1)}, bf16[2,256,384]{2,1,0:T(8,128)(2,1)S(1)}, u32[]{:S(2)}, u32[]{:S(2)}) collective-permute-start(bf16[2,256,384]{2,1,0:T(8,128)(2,1)} %get-tuple-element.59), channel_id=1, source_target_pairs={{0,12},{4,0},{8,4},{12,8},{1,13},{5,1},{9,5},{13,9},{2,14},{6,2},{... | collective-permute-start | bytes 1179656 | tf_op jit(solution)/shard_map/ppermute | solution.py:430
  82.1 0.9 collective-permute-start.13
  83.5 12.2 %all-to-all-done.1.parts_ref = bf16[4,192,384]{2,1,0:T(8,128)(2,1)S(1)} async-done(((bf16[4,192,384]{2,1,0:T(8,128)(2,1)}), bf16[4,192,384]{2,1,0:T(8,128)(2,1)S(1)}, u32[]{:S(2)}, u32[]{:S(2)}) %all-to-all-start.1) | async-done | bytes 589856 | tf_op jit(solution)/shard_map/all_to_all | solution.py:531
  95.7 0.7 shard_map.178
  96.5 4.2 %all-to-all-start.2 = ((bf16[4,48,384]{2,1,0:T(8,128)(2,1)}), bf16[4,48,384]{2,1,0:T(8,128)(2,1)S(1)}, u32[]{:S(2)}, u32[]{:S(2)}) async-start(bf16[4,48,384]{2,1,0:T(8,128)(2,1)} %bitcast.7), calls=%async_computation.2 | async-start | bytes 294912 | tf_op jit(solution)/shard_map/all_to_all | solution.py:539
  100.7 6.0 %all-to-all-done.2.parts_ref = bf16[4,48,384]{2,1,0:T(8,128)(2,1)S(1)} async-done(((bf16[4,48,384]{2,1,0:T(8,128)(2,1)}), bf16[4,48,384]{2,1,0:T(8,128)(2,1)S(1)}, u32[]{:S(2)}, u32[]{:S(2)}) %all-to-all-start.2) | async-done | bytes 147488 | tf_op jit(solution)/shard_map/all_to_all | solution.py:539
  106.7 1.0 shard_map.179
  (42 shorter events, 2.2 us)
Async XLA Ops:
  1.7 38.6 %copy-start = (bf16[256,768]{1,0:T(8,128)(2,1)}, bf16[256,768]{1,0:T(8,128)(2,1)S(1)}, u32[]{:S(2)}) copy-start(bf16[256,768]{1,0:T(8,128)(2,1)S(1)} %pad_maximum_fusion.refs_4_.refs_11_) | copy-start | bytes 1179652
  1.7 12.1 %collective-permute-start.1 = (bf16[256,768]{1,0:T(8,128)(2,1)S(1)}, bf16[256,768]{1,0:T(8,128)(2,1)S(1)}, u32[]{:S(2)}, u32[]{:S(2)}) collective-permute-start(bf16[256,768]{1,0:T(8,128)(2,1)S(1)} %pad_maximum_fusion.refs_4_.refs_11_), channel_id=1, source_target_pairs={{0,4},{4,8},{8,12},{12,0},{1,5},{5,9},{9,13},{13,1},{2,6},{6,10},{... | collective-permute-start | bytes 1179656 | tf_op jit(solution)/shard_map/ppermute | solution.py:426
  3.3 10.6 %collective-permute-start = (bf16[256,768]{1,0:T(8,128)(2,1)S(1)}, bf16[256,768]{1,0:T(8,128)(2,1)S(1)}, u32[]{:S(2)}, u32[]{:S(2)}) collective-permute-start(bf16[256,768]{1,0:T(8,128)(2,1)S(1)} %pad_maximum_fusion.refs_4_.refs_11_), channel_id=1, source_target_pairs={{0,12},{4,0},{8,4},{12,8},{1,13},{5,1},{9,5},{13,9},{2,14},{6,2},{... | collective-permute-start | bytes 1179656 | tf_op jit(solution)/shard_map/ppermute | solution.py:426
  6.1 34.3 %copy-start.1 = (bf16[256,768]{1,0:T(8,128)(2,1)}, bf16[256,768]{1,0:T(8,128)(2,1)S(1)}, u32[]{:S(2)}) copy-start(bf16[256,768]{1,0:T(8,128)(2,1)S(1)} %pad_maximum_fusion.1.refs_0_.refs_7_) | copy-start | bytes 1179652
  6.1 10.4 %collective-permute-start.3 = (bf16[256,768]{1,0:T(8,128)(2,1)S(1)}, bf16[256,768]{1,0:T(8,128)(2,1)S(1)}, u32[]{:S(2)}, u32[]{:S(2)}) collective-permute-start(bf16[256,768]{1,0:T(8,128)(2,1)S(1)} %pad_maximum_fusion.1.refs_0_.refs_7_), channel_id=1, source_target_pairs={{0,1},{1,2},{2,3},{3,0},{4,5},{5,6},{6,7},{7,4},{8,9},{9,10},{10,1... | collective-permute-start | bytes 1179656 | tf_op jit(solution)/shard_map/ppermute | solution.py:426
  8.1 9.6 %collective-permute-start.2 = (bf16[256,768]{1,0:T(8,128)(2,1)S(1)}, bf16[256,768]{1,0:T(8,128)(2,1)S(1)}, u32[]{:S(2)}, u32[]{:S(2)}) collective-permute-start(bf16[256,768]{1,0:T(8,128)(2,1)S(1)} %pad_maximum_fusion.1.refs_0_.refs_7_), channel_id=1, source_target_pairs={{0,3},{1,0},{2,1},{3,2},{4,7},{5,4},{6,5},{7,6},{8,11},{9,8},{10,9... | collective-permute-start | bytes 1179656 | tf_op jit(solution)/shard_map/ppermute | solution.py:426
  13.8 26.5 %copy-start.2 = (bf16[256,768]{1,0:T(8,128)(2,1)}, bf16[256,768]{1,0:T(8,128)(2,1)S(1)}, u32[]{:S(2)}) copy-start(bf16[256,768]{1,0:T(8,128)(2,1)S(1)} %collective-permute-done.1.refs_7_.refs_14_) | copy-start | bytes 1179652
  13.8 26.5 %copy-start.3 = (bf16[256,768]{1,0:T(8,128)(2,1)}, bf16[256,768]{1,0:T(8,128)(2,1)S(1)}, u32[]{:S(2)}) copy-start(bf16[256,768]{1,0:T(8,128)(2,1)S(1)} %collective-permute-done.refs_5_.refs_12_) | copy-start | bytes 1179652
  16.5 23.9 %copy-start.4 = (bf16[256,768]{1,0:T(8,128)(2,1)}, bf16[256,768]{1,0:T(8,128)(2,1)S(1)}, u32[]{:S(2)}) copy-start(bf16[256,768]{1,0:T(8,128)(2,1)S(1)} %collective-permute-done.3.refs_3_.refs_10_) | copy-start | bytes 1179652
  17.8 22.6 %copy-start.5 = (bf16[256,768]{1,0:T(8,128)(2,1)}, bf16[256,768]{1,0:T(8,128)(2,1)S(1)}, u32[]{:S(2)}) copy-start(bf16[256,768]{1,0:T(8,128)(2,1)S(1)} %collective-permute-done.2.refs_1_.refs_8_) | copy-start | bytes 1179652
  17.8 9.7 %collective-permute-start.4 = (bf16[256,768]{1,0:T(8,128)(2,1)S(1)}, bf16[256,768]{1,0:T(8,128)(2,1)S(1)}, u32[]{:S(2)}, u32[]{:S(2)}) collective-permute-start(bf16[256,768]{1,0:T(8,128)(2,1)S(1)} %pad_maximum_fusion.refs_4_.refs_11_), channel_id=1, source_target_pairs={{0,8},{4,12},{8,0},{12,4},{1,9},{5,13},{9,1},{13,5},{2,10},{6,14},... | collective-permute-start | bytes 1179656 | tf_op jit(solution)/shard_map/ppermute | solution.py:426
  19.6 10.5 %collective-permute-start.5 = (bf16[256,768]{1,0:T(8,128)(2,1)S(1)}, bf16[256,768]{1,0:T(8,128)(2,1)S(1)}, u32[]{:S(2)}, u32[]{:S(2)}) collective-permute-start(bf16[256,768]{1,0:T(8,128)(2,1)S(1)} %pad_maximum_fusion.1.refs_0_.refs_7_), channel_id=1, source_target_pairs={{0,2},{1,3},{2,0},{3,1},{4,6},{5,7},{6,4},{7,5},{8,10},{9,11},{10,... | collective-permute-start | bytes 1179656 | tf_op jit(solution)/shard_map/ppermute | solution.py:426
  27.4 24.3 %copy-start.6 = (bf16[256,768]{1,0:T(8,128)(2,1)}, bf16[256,768]{1,0:T(8,128)(2,1)S(1)}, u32[]{:S(2)}) copy-start(bf16[256,768]{1,0:T(8,128)(2,1)S(1)} %collective-permute-done.4.refs_6_.refs_13_) | copy-start | bytes 1179652
  30.0 21.7 %copy-start.7 = (bf16[256,768]{1,0:T(8,128)(2,1)}, bf16[256,768]{1,0:T(8,128)(2,1)S(1)}, u32[]{:S(2)}) copy-start(bf16[256,768]{1,0:T(8,128)(2,1)S(1)} %collective-permute-done.5.refs_2_.refs_9_) | copy-start | bytes 1179652
  30.0 21.7 %all-to-all-start = ((bf16[64,16,128]{2,1,0:T(8,128)(2,1)}), bf16[64,16,128]{2,1,0:T(8,128)(2,1)S(1)}, u32[]{:S(2)}, u32[]{:S(2)}) async-start(bf16[64,16,128]{2,1,0:T(8,128)(2,1)} %shard_map.174), calls=%async_computation | async-start | bytes 524288 | tf_op jit(solution)/shard_map/all_to_all | solution.py:496
  43.6 8.2 %copy-start.10 = (f32[8,1024]{1,0:T(8,128)}, f32[8,1024]{1,0:T(8,128)S(1)}, u32[]{:S(2)}) copy-start(f32[8,1024]{1,0:T(8,128)S(1)} %shard_map.176.refs_0_) | copy-start | bytes 98308
  43.6 4.1 %collective-permute-start.8 = (f32[8,1024]{1,0:T(8,128)S(1)}, f32[8,1024]{1,0:T(8,128)S(1)}, u32[]{:S(2)}, u32[]{:S(2)}) collective-permute-start(f32[8,1024]{1,0:T(8,128)S(1)} %shard_map.176.refs_0_), channel_id=1, source_target_pairs={{0,1},{1,2},{2,3},{3,0},{4,5},{5,6},{6,7},{7,4},{8,9},{9,10},{10,1... | collective-permute-start | bytes 98312 | tf_op jit(solution)/shard_map/ppermute | solution.py:426
  44.1 5.4 %collective-permute-start.7 = (f32[8,1024]{1,0:T(8,128)S(1)}, f32[8,1024]{1,0:T(8,128)S(1)}, u32[]{:S(2)}, u32[]{:S(2)}) collective-permute-start(f32[8,1024]{1,0:T(8,128)S(1)} %shard_map.176.refs_0_), channel_id=1, source_target_pairs={{0,2},{1,3},{2,0},{3,1},{4,6},{5,7},{6,4},{7,5},{8,10},{9,11},{10,... | collective-permute-start | bytes 98312 | tf_op jit(solution)/shard_map/ppermute | solution.py:426
  46.6 5.1 %collective-permute-start.6 = (f32[8,1024]{1,0:T(8,128)S(1)}, f32[8,1024]{1,0:T(8,128)S(1)}, u32[]{:S(2)}, u32[]{:S(2)}) collective-permute-start(f32[8,1024]{1,0:T(8,128)S(1)} %shard_map.176.refs_0_), channel_id=1, source_target_pairs={{0,3},{1,0},{2,1},{3,2},{4,7},{5,4},{6,5},{7,6},{8,11},{9,8},{10,9... | collective-permute-start | bytes 98312 | tf_op jit(solution)/shard_map/ppermute | solution.py:426
  47.7 4.1 %copy-start.12 = (f32[8,1024]{1,0:T(8,128)}, f32[8,1024]{1,0:T(8,128)S(1)}, u32[]{:S(2)}) copy-start(f32[8,1024]{1,0:T(8,128)S(1)} %collective-permute-done.8.refs_3_) | copy-start | bytes 98308
  49.5 2.2 %copy-start.13 = (f32[8,1024]{1,0:T(8,128)}, f32[8,1024]{1,0:T(8,128)S(1)}, u32[]{:S(2)}) copy-start(f32[8,1024]{1,0:T(8,128)S(1)} %collective-permute-done.7.refs_2_) | copy-start | bytes 98308
  52.3 0.7 copy-start.11
  70.0 36.7 %copy-start.8 = (bf16[2,256,384]{2,1,0:T(8,128)(2,1)S(1)}, bf16[2,256,384]{2,1,0:T(8,128)(2,1)}, u32[]{:S(2)}) copy-start(bf16[2,256,384]{2,1,0:T(8,128)(2,1)} %get-tuple-element.56.refs_0_) | copy-start | bytes 1179652
  70.0 36.7 %copy-start.9 = (bf16[256,384]{1,0:T(8,128)(2,1)S(1)}, bf16[256,384]{1,0:T(8,128)(2,1)}, u32[]{:S(2)}) copy-start(bf16[256,384]{1,0:T(8,128)(2,1)} %get-tuple-element.60.refs_4_) | copy-start | bytes 589828
  70.0 25.7 %all-to-all-start.1 = ((bf16[4,192,384]{2,1,0:T(8,128)(2,1)}), bf16[4,192,384]{2,1,0:T(8,128)(2,1)S(1)}, u32[]{:S(2)}, u32[]{:S(2)}) async-start(bf16[4,192,384]{2,1,0:T(8,128)(2,1)} %bitcast.10), calls=%async_computation.1 | async-start | bytes 1179648 | tf_op jit(solution)/shard_map/all_to_all | solution.py:531
  75.9 7.5 %collective-permute-start.12 = (bf16[256,384]{1,0:T(8,128)(2,1)}, bf16[256,384]{1,0:T(8,128)(2,1)S(1)}, u32[]{:S(2)}, u32[]{:S(2)}) collective-permute-start(bf16[256,384]{1,0:T(8,128)(2,1)} %get-tuple-element.61), channel_id=1, source_target_pairs={{0,1},{1,2},{2,3},{3,0},{4,5},{5,6},{6,7},{7,4},{8,9},{9,10},{10,1... | collective-permute-start | bytes 589832 | tf_op jit(solution)/shard_map/ppermute | solution.py:430
  76.5 24.2 %collective-permute-start.9 = (bf16[2,256,384]{2,1,0:T(8,128)(2,1)}, bf16[2,256,384]{2,1,0:T(8,128)(2,1)S(1)}, u32[]{:S(2)}, u32[]{:S(2)}) collective-permute-start(bf16[2,256,384]{2,1,0:T(8,128)(2,1)} %get-tuple-element.57), channel_id=1, source_target_pairs={{0,4},{4,8},{8,12},{12,0},{1,5},{5,9},{9,13},{13,1},{2,6},{6,10},{... | collective-permute-start | bytes 1179656 | tf_op jit(solution)/shard_map/ppermute | solution.py:430
  78.0 22.7 %collective-permute-start.10 = (bf16[2,256,384]{2,1,0:T(8,128)(2,1)}, bf16[2,256,384]{2,1,0:T(8,128)(2,1)S(1)}, u32[]{:S(2)}, u32[]{:S(2)}) collective-permute-start(bf16[2,256,384]{2,1,0:T(8,128)(2,1)} %get-tuple-element.58), channel_id=1, source_target_pairs={{0,8},{4,12},{8,0},{12,4},{1,9},{5,13},{9,1},{13,5},{2,10},{6,14},... | collective-permute-start | bytes 1179656 | tf_op jit(solution)/shard_map/ppermute | solution.py:430
  80.6 20.1 %collective-permute-start.11 = (bf16[2,256,384]{2,1,0:T(8,128)(2,1)}, bf16[2,256,384]{2,1,0:T(8,128)(2,1)S(1)}, u32[]{:S(2)}, u32[]{:S(2)}) collective-permute-start(bf16[2,256,384]{2,1,0:T(8,128)(2,1)} %get-tuple-element.59), channel_id=1, source_target_pairs={{0,12},{4,0},{8,4},{12,8},{1,13},{5,1},{9,5},{13,9},{2,14},{6,2},{... | collective-permute-start | bytes 1179656 | tf_op jit(solution)/shard_map/ppermute | solution.py:430
  82.1 18.6 %collective-permute-start.13 = (bf16[256,384]{1,0:T(8,128)(2,1)}, bf16[256,384]{1,0:T(8,128)(2,1)S(1)}, u32[]{:S(2)}, u32[]{:S(2)}) collective-permute-start(bf16[256,384]{1,0:T(8,128)(2,1)} %get-tuple-element.62), channel_id=1, source_target_pairs={{0,2},{1,3},{2,0},{3,1},{4,6},{5,7},{6,4},{7,5},{8,10},{9,11},{10,... | collective-permute-start | bytes 589832 | tf_op jit(solution)/shard_map/ppermute | solution.py:430
  83.5 17.2 %collective-permute-start.14 = (bf16[256,384]{1,0:T(8,128)(2,1)}, bf16[256,384]{1,0:T(8,128)(2,1)S(1)}, u32[]{:S(2)}, u32[]{:S(2)}) collective-permute-start(bf16[256,384]{1,0:T(8,128)(2,1)} %get-tuple-element.63), channel_id=1, source_target_pairs={{0,3},{1,0},{2,1},{3,2},{4,7},{5,4},{6,5},{7,6},{8,11},{9,8},{10,9... | collective-permute-start | bytes 589832 | tf_op jit(solution)/shard_map/ppermute | solution.py:430
  96.5 10.3 %all-to-all-start.2 = ((bf16[4,48,384]{2,1,0:T(8,128)(2,1)}), bf16[4,48,384]{2,1,0:T(8,128)(2,1)S(1)}, u32[]{:S(2)}, u32[]{:S(2)}) async-start(bf16[4,48,384]{2,1,0:T(8,128)(2,1)} %bitcast.7), calls=%async_computation.2 | async-start | bytes 294912 | tf_op jit(solution)/shard_map/all_to_all | solution.py:539
  (1 other events, 0.6 us)

commit v11 on v7

--- a/solution.py
+++ b/solution.py
@@ -204,24 +204,18 @@
         rows = dot(pick, join_ref[:, pl.ds(pair * 384, 384)], NT).astype(bf16)
         z, core, x = pair // 4, (pair % 4) // 2, (pair % 2) * 2
         for step in range(2):
-            picked_ref[pl.ds((core * GRID + x + step) * 96 + z * 48, 48), :] = rows[
+            picked_ref[pl.ds((z * 2 + core) * 192 + (x + step) * 48, 48), :] = rows[
                 step * 48 : (step + 1) * 48
             ]
 
 
 def totals_kernel(*refs):
-    out_ref, query_held, key_held, query_arrived, key_arrived = refs[2 * GRID :]
-    key_copies = fetch_halves(refs[GRID : 2 * GRID], 0, key_held, key_arrived)
-    query_copies = fetch_halves(refs[:GRID], 0, query_held, query_arrived)
-    for copy in key_copies:
-        copy.wait()
+    query_refs, key_refs, out_ref = refs[:GRID], refs[GRID : 2 * GRID], refs[2 * GRID]
     for head in range(HEADS_HERE):
         columns = pl.ds(head * HDIM, HDIM)
         for piece in range(GRID):
-            if head == 0:
-                query_copies[piece].wait()
-            query = query_held[piece, :, columns]
-            scores = [dot(key_held[other, :, columns], query, NT) for other in range(GRID)]
+            query = query_refs[piece][:, columns]
+            scores = [dot(key_ref[:, columns], query, NT) for key_ref in key_refs]
             top = functools.reduce(
                 jnp.maximum, [jnp.max(tile, axis=0, keepdims=True) for tile in scores]
             ) * (SCORE_SCALE * LOG2E)
@@ -412,25 +406,17 @@
         send.wait()
 
 
-def half_kernel(parts_ref, kept_ref, sent_ref):
-    here_z = lax.axis_index("zh")
-    for out_ref, half in ((kept_ref, here_z), (sent_ref, 1 - here_z)):
-        out_ref[...] = sum(parts_ref[source, half].astype(f32) for source in range(2 * GRID))
-
-
-def sum_kernel(kept_ref, other_ref, *refs):
+def weight_kernel(parts_ref, out_ref):
+    out_ref[...] = sum(parts_ref[source].astype(f32) for source in range(4)).astype(bf16)
+
+
+def sum_kernel(parts_ref, *refs):
     pair_refs, query_refs = refs[:GRID], refs[GRID : 2 * GRID]
-    query_out, key_out, value_out, weight_out, query_held, pair_held, *arrived = refs[2 * GRID :]
-    pair_copies = fetch(pair_refs, [pair_held.at[step] for step in range(GRID)], arrived[1])
-    query_copies = fetch(query_refs, [query_held.at[step] for step in range(GRID)], arrived[0])
-    weight_out[...] = kept_ref[...] + other_ref[...]
-    for copy in query_copies:
-        copy.wait()
-    query_out[0] = sum(query_held[step].astype(f32) for step in range(GRID)).astype(bf16)
-    for copy in pair_copies:
-        copy.wait()
+    query_out, key_out, value_out, weight_out = refs[2 * GRID :]
+    weight_out[...] = sum(parts_ref[source].astype(f32) for source in range(GRID))
+    query_out[0] = sum(ref[...].astype(f32) for ref in query_refs).astype(bf16)
     for place, out_ref in enumerate((key_out, value_out)):
-        out_ref[0] = sum(pair_held[step, place].astype(f32) for step in range(GRID)).astype(bf16)
+        out_ref[0] = sum(ref[place].astype(f32) for ref in pair_refs).astype(bf16)
 
 
 def call(kernel, out_shape, in_specs, scratch=(), out_spec=None, limit=56):
@@ -533,12 +519,11 @@
     totals = call(
         totals_kernel,
         shape((8, BLOCK), f32),
-        [ANY] * (2 * GRID),
-        scratch=HELD * 2 + ARRIVED * 2,
+        [VMEM] * (2 * GRID),
         limit=24,
     )(*query_outs, *key_values)
-    totals, received = lax.optimization_barrier((totals, received))
     total_pieces = gather(totals, "hy")
+    total_pieces, received = lax.optimization_barrier((total_pieces, received))
     row_dots, grad_out, weight_part = call(
         token_kernel,
         (
@@ -561,6 +546,7 @@
         + ARRIVED * 2
         + [pltpu.SemaphoreType.DMA((1,))],
         out_spec=(VMEM, ANY, ANY),
+        limit=56,
     )(frame_owner, conv_w, received, joint, picked, *query_outs)
     outs = call(
         grads_kernel,
@@ -574,22 +560,20 @@
         + [pltpu.SemaphoreType.DMA((1,))]
         + ARRIVED * 2,
         out_spec=tuple([ANY] * (2 * GRID)),
+        limit=56,
     )(row_dots, *total_pieces, grad_out, *query_outs, *key_values)
     query_parts, pair_parts = outs[:GRID], outs[GRID:]
     weight_parts = lax.all_to_all(
-        weight_part.reshape(8, 2, 48, FEATS),
-        ("core", "hx"),
+        weight_part.reshape(4, 4 * 48, FEATS),
+        ("zh", "core"),
         split_axis=0,
         concat_axis=0,
         tiled=True,
     )
-    weight_kept, weight_sent = call(
-        half_kernel,
-        (shape((48, FEATS), f32), shape((48, FEATS), f32)),
-        [VMEM],
-        limit=8,
-    )(weight_parts)
-    weight_other = lax.ppermute(weight_sent, "zh", [(0, 1), (1, 0)])
+    weight_blocks = call(weight_kernel, shape((4 * 48, FEATS), bf16), [VMEM], limit=8)(weight_parts)
+    weight_parts = lax.all_to_all(
+        weight_blocks.reshape(4, 48, FEATS), "hx", split_axis=0, concat_axis=0, tiled=True
+    )
     pair_back = [pair_parts[0]] + [
         to_ahead(pair_parts[step], "hx", step) for step in range(1, GRID)
     ]
@@ -601,10 +585,9 @@
     return call(
         sum_kernel,
         (rows, rows, rows, shape((48, FEATS), f32)),
-        [VMEM] * 2 + [ANY] * (2 * GRID),
-        scratch=HELD + [pltpu.VMEM((GRID, 2, ROWS_HERE, FEATS), bf16)] + ARRIVED * 2,
-        limit=8,
-    )(weight_kept, weight_other, *pair_back, *query_back)
+        [VMEM] * (1 + 2 * GRID),
+        limit=16,
+    )(weight_parts, *pair_back, *query_back)
 
 
 def solution(mesh):

time: 113 us -> 109 us (0.965); the launches traced: 113 us -> 107 us
  waiting for transfers between devices: 27.6 us -> 18.6 us
  starting transfers between devices: 40 us -> 46.6 us
  Pallas kernels: 38.6 us -> 36.5 us
    all_to_all x1 -> x2, starting transfers between devices: 3.55 us -> 12.8 us  [the longest x1 7.06 us: per_device(): lax.all_to_all(weight_blocks.reshape(4, 48, FEATS), 'hx', split_axis=0, c...]
    all_to_all x1, waiting for transfers between devices: 5.69 us -> 0.01 us  [per_device(): lax.all_to_all(windows, ('tm', 'hx', 'hy'), split_axis=0, concat_axis=0,...]
    ppermute x1 -> x0, starting transfers between devices: 4.5 us -> none  [per_device(): weight_other = lax.ppermute(weight_sent, 'zh', [(0, 1), (1, 0)])]
    ppermute x9, waiting for transfers between devices: 12.2 us -> 9.27 us  [from_ahead(): lax.ppermute(block, axis, [(i, (i - step) % GRID) for i in range(GRID)])]
    pallas_call x3, Pallas kernels: 7.05 us -> 4.93 us  [the longest x1 3.21 us: per_device(): call(totals_kernel, shape((8, BLOCK), f32), [VMEM] * (2 * GRID), limit=24)]
    ppermute x1 -> x0, waiting for transfers between devices: 1.93 us -> none  [per_device(): weight_other = lax.ppermute(weight_sent, 'zh', [(0, 1), (1, 0)])]
    ppermute x9, starting transfers between devices: 12.3 us -> 14 us  [from_ahead(): lax.ppermute(block, axis, [(i, (i - step) % GRID) for i in range(GRID)])]
  transfers between devices with their start and end apart: 18 -> 18, of which waited for: 12 -> 11; matrix products, arithmetic and copies ran while one was open for 1% -> 1% of each run, Pallas kernels for 24% -> 25%
where the time goes in v11:
time: 109 us; the launch traced here: 107 us
  starting transfers between devices  46.6 us (43%)
  Pallas kernels  36.5 us (33%)
  waiting for transfers between devices  18.6 us (17%)
  local copies, waits for them, and re-layouts  2.67 us (2%)
  other arithmetic  2.11 us (2%)
    ppermute x9, starting transfers between devices, from_ahead(): lax.ppermute(block, axis, [(i, (i - step) % GRID) for i in range(GRID)])  14 us
    pallas_call x1, Pallas kernels, per_device(): call(grads_kernel, tuple([shape((ROWS_HERE, FEATS), bf16)] * GRID) + tupl...  12.4 us
    all_to_all x1, starting transfers between devices, per_device(): lax.all_to_all(windows, ('tm', 'hx', 'hy'), split_axis=0, concat_axis=0,...  10.4 us
    ppermute x6, starting transfers between devices, to_ahead(): lax.ppermute(block, axis, [(i, (i + step) % GRID) for i in range(GRID)])  9.46 us
    ppermute x9, waiting for transfers between devices, from_ahead(): lax.ppermute(block, axis, [(i, (i - step) % GRID) for i in range(GRID)])  9.27 us
    pallas_call x1, Pallas kernels, per_device(): call(token_kernel, (shape((8, BLOCK), f32), shape((GRID, ROWS_HERE, FEATS...  8.46 us
    ppermute x6, waiting for transfers between devices, to_ahead(): lax.ppermute(block, axis, [(i, (i + step) % GRID) for i in range(GRID)])  8.44 us
    all_to_all x1, starting transfers between devices, per_device(): lax.all_to_all(weight_blocks.reshape(4, 48, FEATS), 'hx', split_axis=0, c...  7.06 us
  transfers between devices with their start and end apart: 18, of which 11 were waited for; matrix products, arithmetic and copies ran while one was open for 1% of the time, Pallas kernels for 25%

profile of v11, /device:TPU:24, one launch (start us, length us, event | category | flops | bytes accessed | tf_op | source)
XLA Modules:
  0.0 107.4 jit_solution(12515456047237316545)
XLA Ops:
  0.6 1.1 pad_maximum_fusion.refs_4_.refs_9_
  1.7 2.8 %collective-permute-start = (bf16[256,768]{1,0:T(8,128)(2,1)S(1)}, bf16[256,768]{1,0:T(8,128)(2,1)S(1)}, u32[]{:S(2)}, u32[]{:S(2)}) collective-permute-start(bf16[256,768]{1,0:T(8,128)(2,1)S(1)} %pad_maximum_fusion.refs_4_.refs_9_), channel_id=1, source_target_pairs={{0,12},{4,0},{8,4},{12,8},{1,13},{5,1},{9,5},{13,9},{2,14},{6,2},{... | collective-permute-start | bytes 1179656 | tf_op jit(solution)/shard_map/ppermute | solution.py:446
  4.5 1.1 pad_maximum_fusion.1.refs_0_.refs_3_.refs_5_
  6.4 2.5 %collective-permute-start.3 = (bf16[256,768]{1,0:T(8,128)(2,1)S(1)}, bf16[256,768]{1,0:T(8,128)(2,1)S(1)}, u32[]{:S(2)}, u32[]{:S(2)}) collective-permute-start(bf16[256,768]{1,0:T(8,128)(2,1)S(1)} %pad_maximum_fusion.1.refs_0_.refs_3_.refs_5_), channel_id=1, source_target_pairs={{0,1},{1,2},{2,3},{3,0},{4,5},{5,6},{6,7},{7,4},{8,9},{9,10},{10,1... | collective-permute-start | bytes 1179656 | tf_op jit(solution)/shard_map/ppermute | solution.py:446
  8.9 4.6 %shard_map.174 = bf16[64,16,128]{2,1,0:T(8,128)(2,1)} custom-call(bf16[1280]{0:T(1024)(128)(2,1)} %gain_ref.1, s32[1,64]{1,0:T(1,128)} %order_ref.1, bf16[256,1280]{1,0:T(8,128)(2,1)} %bitcast.8, bf16[256,1280]{1,0:T(8,128)(2,1)} %bitcast.9, bf16[128,588]{1,0:T(8,128)(2,1)} %constant.4.clone.refs_2_, bf16[588,1280]{1,0:T(8,128)(2,1)} %refs_3_.1, ...), custom_call_target="tpu_custom_call" | custom-call | flops 1000000 | bytes 100000 | tf_op jit(solution)/shard_map/pallas_call | solution.py:476
  13.5 2.8 %collective-permute-done.1.refs_7_.refs_12_ = bf16[256,768]{1,0:T(8,128)(2,1)S(1)} collective-permute-done((bf16[256,768]{1,0:T(8,128)(2,1)S(1)}, bf16[256,768]{1,0:T(8,128)(2,1)S(1)}, u32[]{:S(2)}, u32[]{:S(2)}) %collective-permute-start.1) | collective-permute-done | bytes 393248 | tf_op jit(solution)/shard_map/ppermute | solution.py:446
  16.3 1.1 %collective-permute-done.2.refs_1_.refs_4_.refs_6_ = bf16[256,768]{1,0:T(8,128)(2,1)S(1)} collective-permute-done((bf16[256,768]{1,0:T(8,128)(2,1)S(1)}, bf16[256,768]{1,0:T(8,128)(2,1)S(1)}, u32[]{:S(2)}, u32[]{:S(2)}) %collective-permute-start.2) | collective-permute-done | bytes 393248 | tf_op jit(solution)/shard_map/ppermute | solution.py:446
  17.5 2.1 %collective-permute-start.4 = (bf16[256,768]{1,0:T(8,128)(2,1)S(1)}, bf16[256,768]{1,0:T(8,128)(2,1)S(1)}, u32[]{:S(2)}, u32[]{:S(2)}) collective-permute-start(bf16[256,768]{1,0:T(8,128)(2,1)S(1)} %pad_maximum_fusion.refs_4_.refs_9_), channel_id=1, source_target_pairs={{0,8},{4,12},{8,0},{12,4},{1,9},{5,13},{9,1},{13,5},{2,10},{6,14},... | collective-permute-start | bytes 1179656 | tf_op jit(solution)/shard_map/ppermute | solution.py:446
  19.6 1.4 %collective-permute-start.5 = (bf16[256,768]{1,0:T(8,128)(2,1)S(1)}, bf16[256,768]{1,0:T(8,128)(2,1)S(1)}, u32[]{:S(2)}, u32[]{:S(2)}) collective-permute-start(bf16[256,768]{1,0:T(8,128)(2,1)S(1)} %pad_maximum_fusion.1.refs_0_.refs_3_.refs_5_), channel_id=1, source_target_pairs={{0,2},{1,3},{2,0},{3,1},{4,6},{5,7},{6,4},{7,5},{8,10},{9,11},{10,... | collective-permute-start | bytes 1179656 | tf_op jit(solution)/shard_map/ppermute | solution.py:446
  20.9 6.2 %shard_map.175 = (bf16[512,384]{1,0:T(8,128)(2,1)}, bf16[768,512]{1,0:T(8,128)(2,1)}) custom-call(bf16[512,3072]{1,0:T(8,128)(2,1)} %join_from, bf16[384,3072]{1,0:T(8,128)(2,1)} %out_w_from.1), custom_call_target="tpu_custom_call" | custom-call | flops 1000000 | bytes 100000 | tf_op jit(solution)/shard_map/pallas_call | solution.py:503
  27.1 1.6 %collective-permute-done.4.refs_6_.refs_11_ = bf16[256,768]{1,0:T(8,128)(2,1)S(1)} collective-permute-done((bf16[256,768]{1,0:T(8,128)(2,1)S(1)}, bf16[256,768]{1,0:T(8,128)(2,1)S(1)}, u32[]{:S(2)}, u32[]{:S(2)}) %collective-permute-start.4) | collective-permute-done | bytes 393248 | tf_op jit(solution)/shard_map/ppermute | solution.py:446
  28.7 1.4 %collective-permute-done.5.refs_2_.refs_5_.refs_7_ = bf16[256,768]{1,0:T(8,128)(2,1)S(1)} collective-permute-done((bf16[256,768]{1,0:T(8,128)(2,1)S(1)}, bf16[256,768]{1,0:T(8,128)(2,1)S(1)}, u32[]{:S(2)}, u32[]{:S(2)}) %collective-permute-start.5) | collective-permute-done | bytes 393248 | tf_op jit(solution)/shard_map/ppermute | solution.py:446
  30.2 10.4 %all-to-all-start = ((bf16[64,16,128]{2,1,0:T(8,128)(2,1)}), bf16[64,16,128]{2,1,0:T(8,128)(2,1)S(1)}, u32[]{:S(2)}, u32[]{:S(2)}) async-start(bf16[64,16,128]{2,1,0:T(8,128)(2,1)} %shard_map.174), calls=%async_computation | async-start | bytes 524288 | tf_op jit(solution)/shard_map/all_to_all | solution.py:516
  40.6 3.2 %shard_map.176.refs_0_ = f32[8,1024]{1,0:T(8,128)S(1)} custom-call(bf16[256,768]{1,0:T(8,128)(2,1)S(1)} %pad_maximum_fusion.1.refs_0_.refs_3_.refs_5_, bf16[256,768]{1,0:T(8,128)(2,1)S(1)} %collective-permute-done.2.refs_1_.refs_4_.refs_6_, bf16[256,768]{1,0:T(8,128)(2,1)S(1)} %collective-permute-done.5.refs_2_.refs_5_.refs_7_, ...), custom_call_target="tpu_custom_call" | custom-call | flops 1000000 | bytes 100000 | tf_op jit(solution)/shard_map/pallas_call | solution.py:519
  43.8 1.1 %collective-permute-start.6 = (f32[8,1024]{1,0:T(8,128)S(1)}, f32[8,1024]{1,0:T(8,128)S(1)}, u32[]{:S(2)}, u32[]{:S(2)}) collective-permute-start(f32[8,1024]{1,0:T(8,128)S(1)} %shard_map.176.refs_0_), channel_id=1, source_target_pairs={{0,3},{1,0},{2,1},{3,2},{4,7},{5,4},{6,5},{7,6},{8,11},{9,8},{10,9... | collective-permute-start | bytes 98312 | tf_op jit(solution)/shard_map/ppermute | solution.py:446
  44.9 1.1 collective-permute-start.7
  46.0 2.2 %collective-permute-start.8 = (f32[8,1024]{1,0:T(8,128)S(1)}, f32[8,1024]{1,0:T(8,128)S(1)}, u32[]{:S(2)}, u32[]{:S(2)}) collective-permute-start(f32[8,1024]{1,0:T(8,128)S(1)} %shard_map.176.refs_0_), channel_id=1, source_target_pairs={{0,1},{1,2},{2,3},{3,0},{4,5},{5,6},{6,7},{7,4},{8,9},{9,10},{10,1... | collective-permute-start | bytes 98312 | tf_op jit(solution)/shard_map/ppermute | solution.py:446
  48.2 1.0 collective-permute-done.6.refs_1_
  49.2 1.1 %collective-permute-done.7.refs_2_ = f32[8,1024]{1,0:T(8,128)S(1)} collective-permute-done((f32[8,1024]{1,0:T(8,128)S(1)}, f32[8,1024]{1,0:T(8,128)S(1)}, u32[]{:S(2)}, u32[]{:S(2)}) %collective-permute-start.7) | collective-permute-done | bytes 32800 | tf_op jit(solution)/shard_map/ppermute | solution.py:446
  51.2 8.5 %shard_map.177 = (f32[8,1024]{1,0:T(8,128)}, bf16[4,256,384]{2,1,0:T(8,128)(2,1)}, bf16[768,384]{1,0:T(8,128)(2,1)}) custom-call(s32[64]{0:T(128)} %owner_ref.1, bf16[81,128]{1,0:T(8,128)(2,1)} %conv_ref.1, bf16[64,16,128]{2,1,0:T(8,128)(2,1)} %copy-done.11, bf16[512,384]{1,0:T(8,128)(2,1)} %get-tuple-element.61.refs_1_, ...), custom_call_target="tpu_custom_call" | custom-call | flops 1000000 | bytes 100000 | tf_op jit(solution)/shard_map/pallas_call | solution.py:527
  59.7 5.8 %all-to-all-start.1 = ((bf16[4,192,384]{2,1,0:T(8,128)(2,1)}), bf16[4,192,384]{2,1,0:T(8,128)(2,1)S(1)}, u32[]{:S(2)}, u32[]{:S(2)}) async-start(bf16[4,192,384]{2,1,0:T(8,128)(2,1)} %bitcast.10), calls=%async_computation.1 | async-start | bytes 1179648 | tf_op jit(solution)/shard_map/all_to_all | solution.py:566
  65.5 12.4 %shard_map.179 = (bf16[256,384]{1,0:T(8,128)(2,1)}, bf16[256,384]{1,0:T(8,128)(2,1)}, bf16[256,384]{1,0:T(8,128)(2,1)}, bf16[256,384]{1,0:T(8,128)(2,1)}, bf16[2...) custom-call(f32[8,1024]{1,0:T(8,128)} %get-tuple-element.64.dots_ref, ...), custom_call_target="tpu_custom_call" | custom-call | flops 1000000 | bytes 100000 | tf_op jit(solution)/shard_map/pallas_call | solution.py:551
  77.9 2.9 %collective-permute-start.12 = (bf16[256,384]{1,0:T(8,128)(2,1)}, bf16[256,384]{1,0:T(8,128)(2,1)S(1)}, u32[]{:S(2)}, u32[]{:S(2)}) collective-permute-start(bf16[256,384]{1,0:T(8,128)(2,1)} %get-tuple-element.75), channel_id=1, source_target_pairs={{0,1},{1,2},{2,3},{3,0},{4,5},{5,6},{6,7},{7,4},{8,9},{9,10},{10,1... | collective-permute-start | bytes 589832 | tf_op jit(solution)/shard_map/ppermute | solution.py:450
  80.8 1.5 %collective-permute-start.9 = (bf16[2,256,384]{2,1,0:T(8,128)(2,1)}, bf16[2,256,384]{2,1,0:T(8,128)(2,1)S(1)}, u32[]{:S(2)}, u32[]{:S(2)}) collective-permute-start(bf16[2,256,384]{2,1,0:T(8,128)(2,1)} %get-tuple-element.71), channel_id=1, source_target_pairs={{0,4},{4,8},{8,12},{12,0},{1,5},{5,9},{9,13},{13,1},{2,6},{6,10},{... | collective-permute-start | bytes 1179656 | tf_op jit(solution)/shard_map/ppermute | solution.py:450
  82.3 2.7 %collective-permute-start.10 = (bf16[2,256,384]{2,1,0:T(8,128)(2,1)}, bf16[2,256,384]{2,1,0:T(8,128)(2,1)S(1)}, u32[]{:S(2)}, u32[]{:S(2)}) collective-permute-start(bf16[2,256,384]{2,1,0:T(8,128)(2,1)} %get-tuple-element.72), channel_id=1, source_target_pairs={{0,8},{4,12},{8,0},{12,4},{1,9},{5,13},{9,1},{13,5},{2,10},{6,14},... | collective-permute-start | bytes 1179656 | tf_op jit(solution)/shard_map/ppermute | solution.py:450
  84.9 1.5 %collective-permute-start.11 = (bf16[2,256,384]{2,1,0:T(8,128)(2,1)}, bf16[2,256,384]{2,1,0:T(8,128)(2,1)S(1)}, u32[]{:S(2)}, u32[]{:S(2)}) collective-permute-start(bf16[2,256,384]{2,1,0:T(8,128)(2,1)} %get-tuple-element.73), channel_id=1, source_target_pairs={{0,12},{4,0},{8,4},{12,8},{1,13},{5,1},{9,5},{13,9},{2,14},{6,2},{... | collective-permute-start | bytes 1179656 | tf_op jit(solution)/shard_map/ppermute | solution.py:450
  88.1 7.1 %all-to-all-start.2 = ((bf16[4,48,384]{2,1,0:T(8,128)(2,1)}), bf16[4,48,384]{2,1,0:T(8,128)(2,1)S(1)}, u32[]{:S(2)}, u32[]{:S(2)}) async-start(bf16[4,48,384]{2,1,0:T(8,128)(2,1)} %bitcast.7), calls=%async_computation.2 | async-start | bytes 294912 | tf_op jit(solution)/shard_map/all_to_all | solution.py:574
  96.0 2.5 %collective-permute-done.14.refs_7_ = bf16[256,384]{1,0:T(8,128)(2,1)S(1)} collective-permute-done((bf16[256,384]{1,0:T(8,128)(2,1)}, bf16[256,384]{1,0:T(8,128)(2,1)S(1)}, u32[]{:S(2)}, u32[]{:S(2)}) %collective-permute-start.14) | collective-permute-done | bytes 196640 | tf_op jit(solution)/shard_map/ppermute | solution.py:450
  98.5 5.1 %collective-permute-done.10.refs_2_ = bf16[2,256,384]{2,1,0:T(8,128)(2,1)S(1)} collective-permute-done((bf16[2,256,384]{2,1,0:T(8,128)(2,1)}, bf16[2,256,384]{2,1,0:T(8,128)(2,1)S(1)}, u32[]{:S(2)}, u32[]{:S(2)}) %collective-permute-start.10) | collective-permute-done | bytes 393248 | tf_op jit(solution)/shard_map/ppermute | solution.py:450
  104.4 1.0 copy-done.8
  105.4 0.9 copy-done.9
  106.4 1.0 shard_map.180
  (43 shorter events, 5.1 us)
Async XLA Ops:
  1.7 38.9 %copy-start.1 = (bf16[256,768]{1,0:T(8,128)(2,1)}, bf16[256,768]{1,0:T(8,128)(2,1)S(1)}, u32[]{:S(2)}) copy-start(bf16[256,768]{1,0:T(8,128)(2,1)S(1)} %pad_maximum_fusion.refs_4_.refs_9_) | copy-start | bytes 1179652
  1.7 11.8 %collective-permute-start = (bf16[256,768]{1,0:T(8,128)(2,1)S(1)}, bf16[256,768]{1,0:T(8,128)(2,1)S(1)}, u32[]{:S(2)}, u32[]{:S(2)}) collective-permute-start(bf16[256,768]{1,0:T(8,128)(2,1)S(1)} %pad_maximum_fusion.refs_4_.refs_9_), channel_id=1, source_target_pairs={{0,12},{4,0},{8,4},{12,8},{1,13},{5,1},{9,5},{13,9},{2,14},{6,2},{... | collective-permute-start | bytes 1179656 | tf_op jit(solution)/shard_map/ppermute | solution.py:446
  4.5 11.8 %collective-permute-start.1 = (bf16[256,768]{1,0:T(8,128)(2,1)S(1)}, bf16[256,768]{1,0:T(8,128)(2,1)S(1)}, u32[]{:S(2)}, u32[]{:S(2)}) collective-permute-start(bf16[256,768]{1,0:T(8,128)(2,1)S(1)} %pad_maximum_fusion.refs_4_.refs_9_), channel_id=1, source_target_pairs={{0,4},{4,8},{8,12},{12,0},{1,5},{5,9},{9,13},{13,1},{2,6},{6,10},{... | collective-permute-start | bytes 1179656 | tf_op jit(solution)/shard_map/ppermute | solution.py:446
  5.6 35.0 %copy-start = (bf16[256,768]{1,0:T(8,128)(2,1)}, bf16[256,768]{1,0:T(8,128)(2,1)S(1)}, u32[]{:S(2)}) copy-start(bf16[256,768]{1,0:T(8,128)(2,1)S(1)} %pad_maximum_fusion.1.refs_0_.refs_3_.refs_5_) | copy-start | bytes 1179652
  5.6 11.9 %collective-permute-start.2 = (bf16[256,768]{1,0:T(8,128)(2,1)S(1)}, bf16[256,768]{1,0:T(8,128)(2,1)S(1)}, u32[]{:S(2)}, u32[]{:S(2)}) collective-permute-start(bf16[256,768]{1,0:T(8,128)(2,1)S(1)} %pad_maximum_fusion.1.refs_0_.refs_3_.refs_5_), channel_id=1, source_target_pairs={{0,3},{1,0},{2,1},{3,2},{4,7},{5,4},{6,5},{7,6},{8,11},{9,8},{10,9... | collective-permute-start | bytes 1179656 | tf_op jit(solution)/shard_map/ppermute | solution.py:446
  6.4 11.0 %collective-permute-start.3 = (bf16[256,768]{1,0:T(8,128)(2,1)S(1)}, bf16[256,768]{1,0:T(8,128)(2,1)S(1)}, u32[]{:S(2)}, u32[]{:S(2)}) collective-permute-start(bf16[256,768]{1,0:T(8,128)(2,1)S(1)} %pad_maximum_fusion.1.refs_0_.refs_3_.refs_5_), channel_id=1, source_target_pairs={{0,1},{1,2},{2,3},{3,0},{4,5},{5,6},{6,7},{7,4},{8,9},{9,10},{10,1... | collective-permute-start | bytes 1179656 | tf_op jit(solution)/shard_map/ppermute | solution.py:446
  13.5 27.1 %copy-start.5 = (bf16[256,768]{1,0:T(8,128)(2,1)}, bf16[256,768]{1,0:T(8,128)(2,1)S(1)}, u32[]{:S(2)}) copy-start(bf16[256,768]{1,0:T(8,128)(2,1)S(1)} %collective-permute-done.refs_5_.refs_10_) | copy-start | bytes 1179652
  16.3 24.3 %copy-start.6 = (bf16[256,768]{1,0:T(8,128)(2,1)}, bf16[256,768]{1,0:T(8,128)(2,1)S(1)}, u32[]{:S(2)}) copy-start(bf16[256,768]{1,0:T(8,128)(2,1)S(1)} %collective-permute-done.1.refs_7_.refs_12_) | copy-start | bytes 1179652
  17.5 23.1 %copy-start.2 = (bf16[256,768]{1,0:T(8,128)(2,1)}, bf16[256,768]{1,0:T(8,128)(2,1)S(1)}, u32[]{:S(2)}) copy-start(bf16[256,768]{1,0:T(8,128)(2,1)S(1)} %collective-permute-done.2.refs_1_.refs_4_.refs_6_) | copy-start | bytes 1179652
  17.5 23.1 %copy-start.3 = (bf16[256,768]{1,0:T(8,128)(2,1)}, bf16[256,768]{1,0:T(8,128)(2,1)S(1)}, u32[]{:S(2)}) copy-start(bf16[256,768]{1,0:T(8,128)(2,1)S(1)} %collective-permute-done.3.refs_3_.refs_6_.refs_8_) | copy-start | bytes 1179652
  17.5 11.3 %collective-permute-start.4 = (bf16[256,768]{1,0:T(8,128)(2,1)S(1)}, bf16[256,768]{1,0:T(8,128)(2,1)S(1)}, u32[]{:S(2)}, u32[]{:S(2)}) collective-permute-start(bf16[256,768]{1,0:T(8,128)(2,1)S(1)} %pad_maximum_fusion.refs_4_.refs_9_), channel_id=1, source_target_pairs={{0,8},{4,12},{8,0},{12,4},{1,9},{5,13},{9,1},{13,5},{2,10},{6,14},... | collective-permute-start | bytes 1179656 | tf_op jit(solution)/shard_map/ppermute | solution.py:446
  19.6 10.6 %collective-permute-start.5 = (bf16[256,768]{1,0:T(8,128)(2,1)S(1)}, bf16[256,768]{1,0:T(8,128)(2,1)S(1)}, u32[]{:S(2)}, u32[]{:S(2)}) collective-permute-start(bf16[256,768]{1,0:T(8,128)(2,1)S(1)} %pad_maximum_fusion.1.refs_0_.refs_3_.refs_5_), channel_id=1, source_target_pairs={{0,2},{1,3},{2,0},{3,1},{4,6},{5,7},{6,4},{7,5},{8,10},{9,11},{10,... | collective-permute-start | bytes 1179656 | tf_op jit(solution)/shard_map/ppermute | solution.py:446
  28.7 30.9 %copy-start.7 = (bf16[256,768]{1,0:T(8,128)(2,1)}, bf16[256,768]{1,0:T(8,128)(2,1)S(1)}, u32[]{:S(2)}) copy-start(bf16[256,768]{1,0:T(8,128)(2,1)S(1)} %collective-permute-done.4.refs_6_.refs_11_) | copy-start | bytes 1179652
  30.2 20.3 %copy-start.4 = (bf16[256,768]{1,0:T(8,128)(2,1)}, bf16[256,768]{1,0:T(8,128)(2,1)S(1)}, u32[]{:S(2)}) copy-start(bf16[256,768]{1,0:T(8,128)(2,1)S(1)} %collective-permute-done.5.refs_2_.refs_5_.refs_7_) | copy-start | bytes 1179652
  30.2 20.3 %all-to-all-start = ((bf16[64,16,128]{2,1,0:T(8,128)(2,1)}), bf16[64,16,128]{2,1,0:T(8,128)(2,1)S(1)}, u32[]{:S(2)}, u32[]{:S(2)}) async-start(bf16[64,16,128]{2,1,0:T(8,128)(2,1)} %shard_map.174), calls=%async_computation | async-start | bytes 524288 | tf_op jit(solution)/shard_map/all_to_all | solution.py:516
  43.8 21.6 %copy-start.10 = (f32[8,1024]{1,0:T(8,128)}, f32[8,1024]{1,0:T(8,128)S(1)}, u32[]{:S(2)}) copy-start(f32[8,1024]{1,0:T(8,128)S(1)} %shard_map.176.refs_0_) | copy-start | bytes 98308
  43.8 5.4 %collective-permute-start.6 = (f32[8,1024]{1,0:T(8,128)S(1)}, f32[8,1024]{1,0:T(8,128)S(1)}, u32[]{:S(2)}, u32[]{:S(2)}) collective-permute-start(f32[8,1024]{1,0:T(8,128)S(1)} %shard_map.176.refs_0_), channel_id=1, source_target_pairs={{0,3},{1,0},{2,1},{3,2},{4,7},{5,4},{6,5},{7,6},{8,11},{9,8},{10,9... | collective-permute-start | bytes 98312 | tf_op jit(solution)/shard_map/ppermute | solution.py:446
  44.9 5.4 %collective-permute-start.7 = (f32[8,1024]{1,0:T(8,128)S(1)}, f32[8,1024]{1,0:T(8,128)S(1)}, u32[]{:S(2)}, u32[]{:S(2)}) collective-permute-start(f32[8,1024]{1,0:T(8,128)S(1)} %shard_map.176.refs_0_), channel_id=1, source_target_pairs={{0,2},{1,3},{2,0},{3,1},{4,6},{5,7},{6,4},{7,5},{8,10},{9,11},{10,... | collective-permute-start | bytes 98312 | tf_op jit(solution)/shard_map/ppermute | solution.py:446
  46.0 4.5 %collective-permute-start.8 = (f32[8,1024]{1,0:T(8,128)S(1)}, f32[8,1024]{1,0:T(8,128)S(1)}, u32[]{:S(2)}, u32[]{:S(2)}) collective-permute-start(f32[8,1024]{1,0:T(8,128)S(1)} %shard_map.176.refs_0_), channel_id=1, source_target_pairs={{0,1},{1,2},{2,3},{3,0},{4,5},{5,6},{6,7},{7,4},{8,9},{9,10},{10,1... | collective-permute-start | bytes 98312 | tf_op jit(solution)/shard_map/ppermute | solution.py:446
  49.2 16.2 %copy-start.12 = (f32[8,1024]{1,0:T(8,128)}, f32[8,1024]{1,0:T(8,128)S(1)}, u32[]{:S(2)}) copy-start(f32[8,1024]{1,0:T(8,128)S(1)} %collective-permute-done.6.refs_1_) | copy-start | bytes 98308
  50.4 15.1 %copy-start.13 = (f32[8,1024]{1,0:T(8,128)}, f32[8,1024]{1,0:T(8,128)S(1)}, u32[]{:S(2)}) copy-start(f32[8,1024]{1,0:T(8,128)S(1)} %collective-permute-done.7.refs_2_) | copy-start | bytes 98308
  50.5 15.0 %copy-start.14 = (f32[8,1024]{1,0:T(8,128)}, f32[8,1024]{1,0:T(8,128)S(1)}, u32[]{:S(2)}) copy-start(f32[8,1024]{1,0:T(8,128)S(1)} %collective-permute-done.8.refs_3_) | copy-start | bytes 98308
  59.7 27.7 %all-to-all-start.1 = ((bf16[4,192,384]{2,1,0:T(8,128)(2,1)}), bf16[4,192,384]{2,1,0:T(8,128)(2,1)S(1)}, u32[]{:S(2)}, u32[]{:S(2)}) async-start(bf16[4,192,384]{2,1,0:T(8,128)(2,1)} %bitcast.10), calls=%async_computation.1 | async-start | bytes 1179648 | tf_op jit(solution)/shard_map/all_to_all | solution.py:566
  77.9 9.4 %collective-permute-start.12 = (bf16[256,384]{1,0:T(8,128)(2,1)}, bf16[256,384]{1,0:T(8,128)(2,1)S(1)}, u32[]{:S(2)}, u32[]{:S(2)}) collective-permute-start(bf16[256,384]{1,0:T(8,128)(2,1)} %get-tuple-element.75), channel_id=1, source_target_pairs={{0,1},{1,2},{2,3},{3,0},{4,5},{5,6},{6,7},{7,4},{8,9},{9,10},{10,1... | collective-permute-start | bytes 589832 | tf_op jit(solution)/shard_map/ppermute | solution.py:450
  80.8 17.7 %collective-permute-start.9 = (bf16[2,256,384]{2,1,0:T(8,128)(2,1)}, bf16[2,256,384]{2,1,0:T(8,128)(2,1)S(1)}, u32[]{:S(2)}, u32[]{:S(2)}) collective-permute-start(bf16[2,256,384]{2,1,0:T(8,128)(2,1)} %get-tuple-element.71), channel_id=1, source_target_pairs={{0,4},{4,8},{8,12},{12,0},{1,5},{5,9},{9,13},{13,1},{2,6},{6,10},{... | collective-permute-start | bytes 1179656 | tf_op jit(solution)/shard_map/ppermute | solution.py:450
  82.3 21.3 %collective-permute-start.10 = (bf16[2,256,384]{2,1,0:T(8,128)(2,1)}, bf16[2,256,384]{2,1,0:T(8,128)(2,1)S(1)}, u32[]{:S(2)}, u32[]{:S(2)}) collective-permute-start(bf16[2,256,384]{2,1,0:T(8,128)(2,1)} %get-tuple-element.72), channel_id=1, source_target_pairs={{0,8},{4,12},{8,0},{12,4},{1,9},{5,13},{9,1},{13,5},{2,10},{6,14},... | collective-permute-start | bytes 1179656 | tf_op jit(solution)/shard_map/ppermute | solution.py:450
  84.9 18.7 %collective-permute-start.11 = (bf16[2,256,384]{2,1,0:T(8,128)(2,1)}, bf16[2,256,384]{2,1,0:T(8,128)(2,1)S(1)}, u32[]{:S(2)}, u32[]{:S(2)}) collective-permute-start(bf16[2,256,384]{2,1,0:T(8,128)(2,1)} %get-tuple-element.73), channel_id=1, source_target_pairs={{0,12},{4,0},{8,4},{12,8},{1,13},{5,1},{9,5},{13,9},{2,14},{6,2},{... | collective-permute-start | bytes 1179656 | tf_op jit(solution)/shard_map/ppermute | solution.py:450
  86.4 9.6 %collective-permute-start.13 = (bf16[256,384]{1,0:T(8,128)(2,1)}, bf16[256,384]{1,0:T(8,128)(2,1)S(1)}, u32[]{:S(2)}, u32[]{:S(2)}) collective-permute-start(bf16[256,384]{1,0:T(8,128)(2,1)} %get-tuple-element.76), channel_id=1, source_target_pairs={{0,2},{1,3},{2,0},{3,1},{4,6},{5,7},{6,4},{7,5},{8,10},{9,11},{10,... | collective-permute-start | bytes 589832 | tf_op jit(solution)/shard_map/ppermute | solution.py:450
  87.3 11.3 %collective-permute-start.14 = (bf16[256,384]{1,0:T(8,128)(2,1)}, bf16[256,384]{1,0:T(8,128)(2,1)S(1)}, u32[]{:S(2)}, u32[]{:S(2)}) collective-permute-start(bf16[256,384]{1,0:T(8,128)(2,1)} %get-tuple-element.77), channel_id=1, source_target_pairs={{0,3},{1,0},{2,1},{3,2},{4,7},{5,4},{6,5},{7,6},{8,11},{9,8},{10,9... | collective-permute-start | bytes 589832 | tf_op jit(solution)/shard_map/ppermute | solution.py:450
  88.1 16.3 %all-to-all-start.2 = ((bf16[4,48,384]{2,1,0:T(8,128)(2,1)}), bf16[4,48,384]{2,1,0:T(8,128)(2,1)S(1)}, u32[]{:S(2)}, u32[]{:S(2)}) async-start(bf16[4,48,384]{2,1,0:T(8,128)(2,1)} %bitcast.7), calls=%async_computation.2 | async-start | bytes 294912 | tf_op jit(solution)/shard_map/all_to_all | solution.py:574
  104.4 1.0 copy-start.8
  105.4 0.9 copy-start.9
  (1 other events, 0.7 us)

commit v12 on v10

--- a/solution.py
+++ b/solution.py
@@ -204,7 +204,7 @@
         rows = dot(pick, join_ref[:, pl.ds(pair * 384, 384)], NT).astype(bf16)
         z, core, x = pair // 4, (pair % 4) // 2, (pair % 2) * 2
         for step in range(2):
-            picked_ref[pl.ds((z * 2 + core) * 192 + (x + step) * 48, 48), :] = rows[
+            picked_ref[pl.ds((core * 2 + z) * 192 + (x + step) * 48, 48), :] = rows[
                 step * 48 : (step + 1) * 48
             ]
 
@@ -279,7 +279,8 @@
     total_refs, (recv_from, joint_from, picked_from) = refs[:GRID], refs[GRID : GRID + 3]
     query_refs, pair_refs = refs[GRID + 3 : 2 * GRID + 3], refs[2 * GRID + 3 : 3 * GRID + 3]
     rest = refs[3 * GRID + 3 :]
-    query_out, pair_out, weight_out = rest[:GRID], rest[GRID : 2 * GRID], rest[2 * GRID]
+    query_out, pair_out = rest[:GRID], rest[GRID : 2 * GRID]
+    weight_outs = rest[2 * GRID : 2 * GRID + 2]
     (
         frames,
         conv_big,
@@ -305,7 +306,7 @@
         query_sent,
         pair_sent,
         weight_sent,
-    ) = rest[2 * GRID + 1 :]
+    ) = rest[2 * GRID + 2 :]
     sends_order = (2, 1, 3, 0)
     firsts = fetch(
         [recv_from, joint_from, picked_from], [recv_ref, joint_ref, picked_ref], first_arrived
@@ -336,7 +337,15 @@
     weight_made[...] = (
         dot(picked_ref[...], outer.astype(bf16)) * (1.0 / math.sqrt(FRAMES * 64 * 4))
     ).astype(bf16)
-    sends = fetch([weight_made], [weight_out], weight_sent)
+    here_core = lax.axis_index("core")
+    sends = fetch(
+        [
+            weight_made.at[pl.ds(pl.multiple_of(half * 384, 384), 384)]
+            for half in (here_core, 1 - here_core)
+        ],
+        weight_outs,
+        weight_sent,
+    )
     root = math.sqrt(FRAMES * 64)
     totals = []
     for piece in range(GRID):
@@ -386,8 +395,17 @@
         send.wait()
 
 
-def weight_kernel(parts_ref, out_ref):
-    out_ref[...] = sum(parts_ref[source].astype(f32) for source in range(4)).astype(bf16)
+def half_kernel(kept_ref, got_ref, kept_out, sent_out):
+    here_z = lax.axis_index("zh")
+    for out_ref, half in ((kept_out, here_z), (sent_out, 1 - here_z)):
+        rows = pl.ds(pl.multiple_of(half * 192, 192), 192)
+        out_ref[...] = (kept_ref[rows, :].astype(f32) + got_ref[rows, :].astype(f32)).astype(
+            out_ref.dtype
+        )
+
+
+def weight_kernel(kept_ref, got_ref, out_ref):
+    out_ref[...] = (kept_ref[...] + got_ref[...].astype(f32)).astype(bf16)
 
 
 def sum_kernel(parts_ref, *refs):
@@ -507,7 +525,7 @@
         grads_kernel,
         tuple([shape((ROWS_HERE, FEATS), bf16)] * GRID)
         + tuple([shape((2, ROWS_HERE, FEATS), bf16)] * GRID)
-        + (shape((768, FEATS), bf16),),
+        + (shape((384, FEATS), bf16),) * 2,
         [SMEM] + [VMEM] * (1 + GRID) + [ANY] * (3 + 2 * GRID),
         scratch=[
             pltpu.VMEM((FRAMES + 2, 16, LANES), bf16),
@@ -523,19 +541,20 @@
         + HELD * 6
         + [pltpu.VMEM((GRID, 2, ROWS_HERE, FEATS), bf16), pltpu.SemaphoreType.DMA((3,))]
         + ARRIVED * 6
-        + [pltpu.SemaphoreType.DMA((1,))],
+        + [pltpu.SemaphoreType.DMA((2,))],
         out_spec=ANY,
         limit=56,
     )(frame_owner, conv_w, *total_pieces, received, joint, picked, *query_outs, *key_values)
-    query_parts, pair_parts, weight_part = outs[:GRID], outs[GRID : 2 * GRID], outs[2 * GRID]
-    weight_parts = lax.all_to_all(
-        weight_part.reshape(4, 4 * 48, FEATS),
-        ("zh", "core"),
-        split_axis=0,
-        concat_axis=0,
-        tiled=True,
-    )
-    weight_blocks = call(weight_kernel, shape((4 * 48, FEATS), bf16), [VMEM], limit=8)(weight_parts)
+    query_parts, pair_parts = outs[:GRID], outs[GRID : 2 * GRID]
+    weight_kept, weight_sent = outs[2 * GRID :]
+    weight_got = lax.ppermute(weight_sent, "core", [(0, 1), (1, 0)])
+    weight_kept, weight_sent = call(
+        half_kernel, (shape((192, FEATS), f32), shape((192, FEATS), bf16)), [VMEM] * 2, limit=8
+    )(weight_kept, weight_got)
+    weight_got = lax.ppermute(weight_sent, "zh", [(0, 1), (1, 0)])
+    weight_blocks = call(weight_kernel, shape((192, FEATS), bf16), [VMEM] * 2, limit=8)(
+        weight_kept, weight_got
+    )
     weight_parts = lax.all_to_all(
         weight_blocks.reshape(4, 48, FEATS), "hx", split_axis=0, concat_axis=0, tiled=True
     )

time: 108 us -> 105 us (0.972)
  the two profiles are of different devices: /device:TPU:24 before, /device:TPU:64 now
where the time goes in v12:
time: 105 us
  starting transfers between devices  47.8 us (46%)
  Pallas kernels  32.5 us (31%)
  waiting for transfers between devices  17.5 us (17%)
  local copies, waits for them, and re-layouts  4.2 us (4%)
  other arithmetic  2.11 us (2%)
    ppermute x9, starting transfers between devices, from_ahead(): lax.ppermute(block, axis, [(i, (i - step) % GRID) for i in range(GRID)])  17.2 us
    pallas_call x1, Pallas kernels, per_device(): call(grads_kernel, tuple([shape((ROWS_HERE, FEATS), bf16)] * GRID) + tupl...  16.8 us
    ppermute x6, starting transfers between devices, to_ahead(): lax.ppermute(block, axis, [(i, (i + step) % GRID) for i in range(GRID)])  12.8 us
    all_to_all x1, starting transfers between devices, per_device(): lax.all_to_all(windows, ('tm', 'hx', 'hy'), split_axis=0, concat_axis=0,...  9.55 us
    ppermute x9, waiting for transfers between devices, from_ahead(): lax.ppermute(block, axis, [(i, (i - step) % GRID) for i in range(GRID)])  7.84 us
    pallas_call x1, Pallas kernels, per_device(): call(weights_kernel, (shape((QUARTERS * LANES, FEATS), bf16), shape((768,...  6.14 us
    all_to_all x1, waiting for transfers between devices, per_device(): lax.all_to_all(weight_blocks.reshape(4, 48, FEATS), 'hx', split_axis=0, c...  5.39 us
    pallas_call x1, Pallas kernels, per_device(): call(window_kernel, shape((FRAMES, 16, LANES), bf16), [VMEM] * 2 + [ANY]...  4.59 us
  transfers between devices with their start and end apart: 19, of which 8 were waited for; matrix products, arithmetic and copies ran while one was open for 1% of the time, Pallas kernels for 14%

profile of v12, /device:TPU:64, one launch (start us, length us, event | category | flops | bytes accessed | tf_op | source)
XLA Modules:
  0.0 105.0 jit_solution(282263552760730823)
XLA Ops:
  0.6 1.1 %pad_maximum_fusion.refs_4_.refs_11_ = bf16[256,768]{1,0:T(8,128)(2,1)S(1)} fusion(bf16[256,384]{1,0:T(8,128)(2,1)} %bitcast.9, bf16[256,384]{1,0:T(8,128)(2,1)} %bitcast.10), kind=kLoop, calls=%fused_computation | loop fusion | flops 786432 | bytes 786432 | tf_op jit(solution)/shard_map/concatenate | solution.py:470
  1.7 1.6 %collective-permute-start.1 = (bf16[256,768]{1,0:T(8,128)(2,1)S(1)}, bf16[256,768]{1,0:T(8,128)(2,1)S(1)}, u32[]{:S(2)}, u32[]{:S(2)}) collective-permute-start(bf16[256,768]{1,0:T(8,128)(2,1)S(1)} %pad_maximum_fusion.refs_4_.refs_11_), channel_id=1, source_target_pairs={{0,4},{4,8},{8,12},{12,0},{1,5},{5,9},{9,13},{13,1},{2,6},{6,10},{... | collective-permute-start | bytes 1179656 | tf_op jit(solution)/shard_map/ppermute | solution.py:444
  3.3 1.7 %collective-permute-start = (bf16[256,768]{1,0:T(8,128)(2,1)S(1)}, bf16[256,768]{1,0:T(8,128)(2,1)S(1)}, u32[]{:S(2)}, u32[]{:S(2)}) collective-permute-start(bf16[256,768]{1,0:T(8,128)(2,1)S(1)} %pad_maximum_fusion.refs_4_.refs_11_), channel_id=1, source_target_pairs={{0,12},{4,0},{8,4},{12,8},{1,13},{5,1},{9,5},{13,9},{2,14},{6,2},{... | collective-permute-start | bytes 1179656 | tf_op jit(solution)/shard_map/ppermute | solution.py:444
  5.0 1.1 %pad_maximum_fusion.1.refs_0_.refs_7_ = bf16[256,768]{1,0:T(8,128)(2,1)S(1)} fusion(bf16[256,384]{1,0:T(8,128)(2,1)} %bitcast.11, bf16[256,384]{1,0:T(8,128)(2,1)} %bitcast.12), kind=kLoop, calls=%fused_computation.1 | loop fusion | flops 786432 | bytes 786432 | tf_op jit(solution)/shard_map/concatenate | solution.py:471
  6.1 1.7 %collective-permute-start.3 = (bf16[256,768]{1,0:T(8,128)(2,1)S(1)}, bf16[256,768]{1,0:T(8,128)(2,1)S(1)}, u32[]{:S(2)}, u32[]{:S(2)}) collective-permute-start(bf16[256,768]{1,0:T(8,128)(2,1)S(1)} %pad_maximum_fusion.1.refs_0_.refs_7_), channel_id=1, source_target_pairs={{0,1},{1,2},{2,3},{3,0},{4,5},{5,6},{6,7},{7,4},{8,9},{9,10},{10,1... | collective-permute-start | bytes 1179656 | tf_op jit(solution)/shard_map/ppermute | solution.py:444
  7.7 1.7 %collective-permute-start.2 = (bf16[256,768]{1,0:T(8,128)(2,1)S(1)}, bf16[256,768]{1,0:T(8,128)(2,1)S(1)}, u32[]{:S(2)}, u32[]{:S(2)}) collective-permute-start(bf16[256,768]{1,0:T(8,128)(2,1)S(1)} %pad_maximum_fusion.1.refs_0_.refs_7_), channel_id=1, source_target_pairs={{0,3},{1,0},{2,1},{3,2},{4,7},{5,4},{6,5},{7,6},{8,11},{9,8},{10,9... | collective-permute-start | bytes 1179656 | tf_op jit(solution)/shard_map/ppermute | solution.py:444
  9.4 4.6 %shard_map.174 = bf16[64,16,128]{2,1,0:T(8,128)(2,1)} custom-call(bf16[1280]{0:T(1024)(128)(2,1)} %gain_ref.1, s32[1,64]{1,0:T(1,128)} %order_ref.1, bf16[256,1280]{1,0:T(8,128)(2,1)} %bitcast.7, bf16[256,1280]{1,0:T(8,128)(2,1)} %bitcast.8, bf16[128,588]{1,0:T(8,128)(2,1)} %constant.4.clone.refs_2_, bf16[588,1280]{1,0:T(8,128)(2,1)} %refs_3_.1, ...), custom_call_target="tpu_custom_call" | custom-call | flops 1000000 | bytes 100000 | tf_op jit(solution)/shard_map/pallas_call | solution.py:474
  14.0 3.7 %collective-permute-done.3.refs_3_.refs_10_ = bf16[256,768]{1,0:T(8,128)(2,1)S(1)} collective-permute-done((bf16[256,768]{1,0:T(8,128)(2,1)S(1)}, bf16[256,768]{1,0:T(8,128)(2,1)S(1)}, u32[]{:S(2)}, u32[]{:S(2)}) %collective-permute-start.3) | collective-permute-done | bytes 393248 | tf_op jit(solution)/shard_map/ppermute | solution.py:444
  17.8 1.9 %collective-permute-start.4 = (bf16[256,768]{1,0:T(8,128)(2,1)S(1)}, bf16[256,768]{1,0:T(8,128)(2,1)S(1)}, u32[]{:S(2)}, u32[]{:S(2)}) collective-permute-start(bf16[256,768]{1,0:T(8,128)(2,1)S(1)} %pad_maximum_fusion.refs_4_.refs_11_), channel_id=1, source_target_pairs={{0,8},{4,12},{8,0},{12,4},{1,9},{5,13},{9,1},{13,5},{2,10},{6,14},... | collective-permute-start | bytes 1179656 | tf_op jit(solution)/shard_map/ppermute | solution.py:444
  19.6 2.8 %collective-permute-start.5 = (bf16[256,768]{1,0:T(8,128)(2,1)S(1)}, bf16[256,768]{1,0:T(8,128)(2,1)S(1)}, u32[]{:S(2)}, u32[]{:S(2)}) collective-permute-start(bf16[256,768]{1,0:T(8,128)(2,1)S(1)} %pad_maximum_fusion.1.refs_0_.refs_7_), channel_id=1, source_target_pairs={{0,2},{1,3},{2,0},{3,1},{4,6},{5,7},{6,4},{7,5},{8,10},{9,11},{10,... | collective-permute-start | bytes 1179656 | tf_op jit(solution)/shard_map/ppermute | solution.py:444
  22.5 6.1 %shard_map.175 = (bf16[512,384]{1,0:T(8,128)(2,1)}, bf16[768,512]{1,0:T(8,128)(2,1)}) custom-call(bf16[512,3072]{1,0:T(8,128)(2,1)} %join_from, bf16[384,3072]{1,0:T(8,128)(2,1)} %out_w_from.1), custom_call_target="tpu_custom_call" | custom-call | flops 1000000 | bytes 100000 | tf_op jit(solution)/shard_map/pallas_call | solution.py:501
  28.8 1.5 %collective-permute-done.5.refs_2_.refs_9_ = bf16[256,768]{1,0:T(8,128)(2,1)S(1)} collective-permute-done((bf16[256,768]{1,0:T(8,128)(2,1)S(1)}, bf16[256,768]{1,0:T(8,128)(2,1)S(1)}, u32[]{:S(2)}, u32[]{:S(2)}) %collective-permute-start.5) | collective-permute-done | bytes 393248 | tf_op jit(solution)/shard_map/ppermute | solution.py:444
  30.3 9.6 %all-to-all-start = ((bf16[64,16,128]{2,1,0:T(8,128)(2,1)}), bf16[64,16,128]{2,1,0:T(8,128)(2,1)S(1)}, u32[]{:S(2)}, u32[]{:S(2)}) async-start(bf16[64,16,128]{2,1,0:T(8,128)(2,1)} %shard_map.174), calls=%async_computation | async-start | bytes 524288 | tf_op jit(solution)/shard_map/all_to_all | solution.py:514
  39.9 3.2 %shard_map.176.refs_0_ = f32[8,1024]{1,0:T(8,128)S(1)} custom-call(bf16[256,768]{1,0:T(8,128)(2,1)S(1)} %pad_maximum_fusion.1.refs_0_.refs_7_, bf16[256,768]{1,0:T(8,128)(2,1)S(1)} %collective-permute-done.2.refs_1_.refs_8_, bf16[256,768]{1,0:T(8,128)(2,1)S(1)} %collective-permute-done.5.refs_2_.refs_9_, ...), custom_call_target="tpu_custom_call" | custom-call | flops 1000000 | bytes 100000 | tf_op jit(solution)/shard_map/pallas_call | solution.py:517
  43.1 1.7 %collective-permute-start.8 = (f32[8,1024]{1,0:T(8,128)S(1)}, f32[8,1024]{1,0:T(8,128)S(1)}, u32[]{:S(2)}, u32[]{:S(2)}) collective-permute-start(f32[8,1024]{1,0:T(8,128)S(1)} %shard_map.176.refs_0_), channel_id=1, source_target_pairs={{0,1},{1,2},{2,3},{3,0},{4,5},{5,6},{6,7},{7,4},{8,9},{9,10},{10,1... | collective-permute-start | bytes 98312 | tf_op jit(solution)/shard_map/ppermute | solution.py:444
  44.9 2.7 %collective-permute-start.7 = (f32[8,1024]{1,0:T(8,128)S(1)}, f32[8,1024]{1,0:T(8,128)S(1)}, u32[]{:S(2)}, u32[]{:S(2)}) collective-permute-start(f32[8,1024]{1,0:T(8,128)S(1)} %shard_map.176.refs_0_), channel_id=1, source_target_pairs={{0,2},{1,3},{2,0},{3,1},{4,6},{5,7},{6,4},{7,5},{8,10},{9,11},{10,... | collective-permute-start | bytes 98312 | tf_op jit(solution)/shard_map/ppermute | solution.py:444
  47.5 1.5 %collective-permute-start.6 = (f32[8,1024]{1,0:T(8,128)S(1)}, f32[8,1024]{1,0:T(8,128)S(1)}, u32[]{:S(2)}, u32[]{:S(2)}) collective-permute-start(f32[8,1024]{1,0:T(8,128)S(1)} %shard_map.176.refs_0_), channel_id=1, source_target_pairs={{0,3},{1,0},{2,1},{3,2},{4,7},{5,4},{6,5},{7,6},{8,11},{9,8},{10,9... | collective-permute-start | bytes 98312 | tf_op jit(solution)/shard_map/ppermute | solution.py:444
  49.0 1.3 %collective-permute-done.7.refs_2_ = f32[8,1024]{1,0:T(8,128)S(1)} collective-permute-done((f32[8,1024]{1,0:T(8,128)S(1)}, f32[8,1024]{1,0:T(8,128)S(1)}, u32[]{:S(2)}, u32[]{:S(2)}) %collective-permute-start.7) | collective-permute-done | bytes 32800 | tf_op jit(solution)/shard_map/ppermute | solution.py:444
  50.3 1.2 %collective-permute-done.6.refs_1_ = f32[8,1024]{1,0:T(8,128)S(1)} collective-permute-done((f32[8,1024]{1,0:T(8,128)S(1)}, f32[8,1024]{1,0:T(8,128)S(1)}, u32[]{:S(2)}, u32[]{:S(2)}) %collective-permute-start.6) | collective-permute-done | bytes 32800 | tf_op jit(solution)/shard_map/ppermute | solution.py:444
  52.8 16.8 %shard_map.177 = (bf16[256,384]{1,0:T(8,128)(2,1)}, bf16[256,384]{1,0:T(8,128)(2,1)}, bf16[256,384]{1,0:T(8,128)(2,1)}, bf16[256,384]{1,0:T(8,128)(2,1)}, bf16[2...) custom-call(s32[64]{0:T(128)} %owner_ref.1, ...), custom_call_target="tpu_custom_call" | custom-call | flops 1000000 | bytes 100000 | tf_op jit(solution)/shard_map/pallas_call | solution.py:524
  70.3 1.5 %collective-permute-start.11 = (bf16[2,256,384]{2,1,0:T(8,128)(2,1)}, bf16[2,256,384]{2,1,0:T(8,128)(2,1)S(1)}, u32[]{:S(2)}, u32[]{:S(2)}) collective-permute-start(bf16[2,256,384]{2,1,0:T(8,128)(2,1)} %get-tuple-element.63), channel_id=1, source_target_pairs={{0,4},{4,8},{8,12},{12,0},{1,5},{5,9},{9,13},{13,1},{2,6},{6,10},{... | collective-permute-start | bytes 1179656 | tf_op jit(solution)/shard_map/ppermute | solution.py:448
  71.8 2.7 %collective-permute-start.12 = (bf16[2,256,384]{2,1,0:T(8,128)(2,1)}, bf16[2,256,384]{2,1,0:T(8,128)(2,1)S(1)}, u32[]{:S(2)}, u32[]{:S(2)}) collective-permute-start(bf16[2,256,384]{2,1,0:T(8,128)(2,1)} %get-tuple-element.64), channel_id=1, source_target_pairs={{0,8},{4,12},{8,0},{12,4},{1,9},{5,13},{9,1},{13,5},{2,10},{6,14},... | collective-permute-start | bytes 1179656 | tf_op jit(solution)/shard_map/ppermute | solution.py:448
  74.5 1.5 %collective-permute-start.13 = (bf16[2,256,384]{2,1,0:T(8,128)(2,1)}, bf16[2,256,384]{2,1,0:T(8,128)(2,1)S(1)}, u32[]{:S(2)}, u32[]{:S(2)}) collective-permute-start(bf16[2,256,384]{2,1,0:T(8,128)(2,1)} %get-tuple-element.65), channel_id=1, source_target_pairs={{0,12},{4,0},{8,4},{12,8},{1,13},{5,1},{9,5},{13,9},{2,14},{6,2},{... | collective-permute-start | bytes 1179656 | tf_op jit(solution)/shard_map/ppermute | solution.py:448
  76.0 1.0 copy-done.9
  77.0 4.6 %collective-permute-start.10 = (bf16[192,384]{1,0:T(8,128)(2,1)S(1)}, bf16[192,384]{1,0:T(8,128)(2,1)S(1)}, u32[]{:S(2)}, u32[]{:S(2)}) collective-permute-start(bf16[192,384]{1,0:T(8,128)(2,1)S(1)} %get-tuple-element.61), channel_id=1, source_target_pairs={{0,128},{128,0},{1,129},{129,1},{2,130},{130,2},{3,131},{131,3},{4... | collective-permute-start | bytes 442376 | tf_op jit(solution)/shard_map/ppermute | solution.py:554
  81.6 3.8 %collective-permute-start.15 = (bf16[256,384]{1,0:T(8,128)(2,1)}, bf16[256,384]{1,0:T(8,128)(2,1)S(1)}, u32[]{:S(2)}, u32[]{:S(2)}) collective-permute-start(bf16[256,384]{1,0:T(8,128)(2,1)} %get-tuple-element.68), channel_id=1, source_target_pairs={{0,2},{1,3},{2,0},{3,1},{4,6},{5,7},{6,4},{7,5},{8,10},{9,11},{10,... | collective-permute-start | bytes 589832 | tf_op jit(solution)/shard_map/ppermute | solution.py:448
  85.4 3.6 %collective-permute-done.10.got_ref = bf16[192,384]{1,0:T(8,128)(2,1)S(1)} collective-permute-done((bf16[192,384]{1,0:T(8,128)(2,1)S(1)}, bf16[192,384]{1,0:T(8,128)(2,1)S(1)}, u32[]{:S(2)}, u32[]{:S(2)}) %collective-permute-start.10) | collective-permute-done | bytes 147488 | tf_op jit(solution)/shard_map/ppermute | solution.py:554
  89.1 2.9 %collective-permute-start.16 = (bf16[256,384]{1,0:T(8,128)(2,1)}, bf16[256,384]{1,0:T(8,128)(2,1)S(1)}, u32[]{:S(2)}, u32[]{:S(2)}) collective-permute-start(bf16[256,384]{1,0:T(8,128)(2,1)} %get-tuple-element.69), channel_id=1, source_target_pairs={{0,3},{1,0},{2,1},{3,2},{4,7},{5,4},{6,5},{7,6},{8,11},{9,8},{10,9... | collective-permute-start | bytes 589832 | tf_op jit(solution)/shard_map/ppermute | solution.py:448
  92.7 3.3 %all-to-all-start.1 = ((bf16[4,48,384]{2,1,0:T(8,128)(2,1)}), bf16[4,48,384]{2,1,0:T(8,128)(2,1)S(1)}, u32[]{:S(2)}, u32[]{:S(2)}) async-start(bf16[4,48,384]{2,1,0:T(8,128)(2,1)} %bitcast.6), calls=%async_computation.1 | async-start | bytes 294912 | tf_op jit(solution)/shard_map/all_to_all | solution.py:558
  96.7 5.4 %all-to-all-done.1.parts_ref = bf16[4,48,384]{2,1,0:T(8,128)(2,1)S(1)} async-done(((bf16[4,48,384]{2,1,0:T(8,128)(2,1)}), bf16[4,48,384]{2,1,0:T(8,128)(2,1)S(1)}, u32[]{:S(2)}, u32[]{:S(2)}) %all-to-all-start.1) | async-done | bytes 147488 | tf_op jit(solution)/shard_map/all_to_all | solution.py:558
  102.1 1.0 copy-done.8
  104.0 1.0 shard_map.180
  (47 shorter events, 4.5 us)
Async XLA Ops:
  1.7 38.2 %copy-start = (bf16[256,768]{1,0:T(8,128)(2,1)}, bf16[256,768]{1,0:T(8,128)(2,1)S(1)}, u32[]{:S(2)}) copy-start(bf16[256,768]{1,0:T(8,128)(2,1)S(1)} %pad_maximum_fusion.refs_4_.refs_11_) | copy-start | bytes 1179652
  1.7 12.3 %collective-permute-start.1 = (bf16[256,768]{1,0:T(8,128)(2,1)S(1)}, bf16[256,768]{1,0:T(8,128)(2,1)S(1)}, u32[]{:S(2)}, u32[]{:S(2)}) collective-permute-start(bf16[256,768]{1,0:T(8,128)(2,1)S(1)} %pad_maximum_fusion.refs_4_.refs_11_), channel_id=1, source_target_pairs={{0,4},{4,8},{8,12},{12,0},{1,5},{5,9},{9,13},{13,1},{2,6},{6,10},{... | collective-permute-start | bytes 1179656 | tf_op jit(solution)/shard_map/ppermute | solution.py:444
  3.3 10.7 %collective-permute-start = (bf16[256,768]{1,0:T(8,128)(2,1)S(1)}, bf16[256,768]{1,0:T(8,128)(2,1)S(1)}, u32[]{:S(2)}, u32[]{:S(2)}) collective-permute-start(bf16[256,768]{1,0:T(8,128)(2,1)S(1)} %pad_maximum_fusion.refs_4_.refs_11_), channel_id=1, source_target_pairs={{0,12},{4,0},{8,4},{12,8},{1,13},{5,1},{9,5},{13,9},{2,14},{6,2},{... | collective-permute-start | bytes 1179656 | tf_op jit(solution)/shard_map/ppermute | solution.py:444
  6.1 33.8 %copy-start.1 = (bf16[256,768]{1,0:T(8,128)(2,1)}, bf16[256,768]{1,0:T(8,128)(2,1)S(1)}, u32[]{:S(2)}) copy-start(bf16[256,768]{1,0:T(8,128)(2,1)S(1)} %pad_maximum_fusion.1.refs_0_.refs_7_) | copy-start | bytes 1179652
  6.1 11.6 %collective-permute-start.3 = (bf16[256,768]{1,0:T(8,128)(2,1)S(1)}, bf16[256,768]{1,0:T(8,128)(2,1)S(1)}, u32[]{:S(2)}, u32[]{:S(2)}) collective-permute-start(bf16[256,768]{1,0:T(8,128)(2,1)S(1)} %pad_maximum_fusion.1.refs_0_.refs_7_), channel_id=1, source_target_pairs={{0,1},{1,2},{2,3},{3,0},{4,5},{5,6},{6,7},{7,4},{8,9},{9,10},{10,1... | collective-permute-start | bytes 1179656 | tf_op jit(solution)/shard_map/ppermute | solution.py:444
  7.7 10.0 %collective-permute-start.2 = (bf16[256,768]{1,0:T(8,128)(2,1)S(1)}, bf16[256,768]{1,0:T(8,128)(2,1)S(1)}, u32[]{:S(2)}, u32[]{:S(2)}) collective-permute-start(bf16[256,768]{1,0:T(8,128)(2,1)S(1)} %pad_maximum_fusion.1.refs_0_.refs_7_), channel_id=1, source_target_pairs={{0,3},{1,0},{2,1},{3,2},{4,7},{5,4},{6,5},{7,6},{8,11},{9,8},{10,9... | collective-permute-start | bytes 1179656 | tf_op jit(solution)/shard_map/ppermute | solution.py:444
  14.0 25.9 %copy-start.2 = (bf16[256,768]{1,0:T(8,128)(2,1)}, bf16[256,768]{1,0:T(8,128)(2,1)S(1)}, u32[]{:S(2)}) copy-start(bf16[256,768]{1,0:T(8,128)(2,1)S(1)} %collective-permute-done.1.refs_7_.refs_14_) | copy-start | bytes 1179652
  14.0 25.9 %copy-start.3 = (bf16[256,768]{1,0:T(8,128)(2,1)}, bf16[256,768]{1,0:T(8,128)(2,1)S(1)}, u32[]{:S(2)}) copy-start(bf16[256,768]{1,0:T(8,128)(2,1)S(1)} %collective-permute-done.refs_5_.refs_12_) | copy-start | bytes 1179652
  17.7 22.2 %copy-start.4 = (bf16[256,768]{1,0:T(8,128)(2,1)}, bf16[256,768]{1,0:T(8,128)(2,1)S(1)}, u32[]{:S(2)}) copy-start(bf16[256,768]{1,0:T(8,128)(2,1)S(1)} %collective-permute-done.3.refs_3_.refs_10_) | copy-start | bytes 1179652
  17.8 22.2 %copy-start.5 = (bf16[256,768]{1,0:T(8,128)(2,1)}, bf16[256,768]{1,0:T(8,128)(2,1)S(1)}, u32[]{:S(2)}) copy-start(bf16[256,768]{1,0:T(8,128)(2,1)S(1)} %collective-permute-done.2.refs_1_.refs_8_) | copy-start | bytes 1179652
  17.8 11.0 %collective-permute-start.4 = (bf16[256,768]{1,0:T(8,128)(2,1)S(1)}, bf16[256,768]{1,0:T(8,128)(2,1)S(1)}, u32[]{:S(2)}, u32[]{:S(2)}) collective-permute-start(bf16[256,768]{1,0:T(8,128)(2,1)S(1)} %pad_maximum_fusion.refs_4_.refs_11_), channel_id=1, source_target_pairs={{0,8},{4,12},{8,0},{12,4},{1,9},{5,13},{9,1},{13,5},{2,10},{6,14},... | collective-permute-start | bytes 1179656 | tf_op jit(solution)/shard_map/ppermute | solution.py:444
  19.6 10.7 %collective-permute-start.5 = (bf16[256,768]{1,0:T(8,128)(2,1)S(1)}, bf16[256,768]{1,0:T(8,128)(2,1)S(1)}, u32[]{:S(2)}, u32[]{:S(2)}) collective-permute-start(bf16[256,768]{1,0:T(8,128)(2,1)S(1)} %pad_maximum_fusion.1.refs_0_.refs_7_), channel_id=1, source_target_pairs={{0,2},{1,3},{2,0},{3,1},{4,6},{5,7},{6,4},{7,5},{8,10},{9,11},{10,... | collective-permute-start | bytes 1179656 | tf_op jit(solution)/shard_map/ppermute | solution.py:444
  28.8 22.7 %copy-start.6 = (bf16[256,768]{1,0:T(8,128)(2,1)}, bf16[256,768]{1,0:T(8,128)(2,1)S(1)}, u32[]{:S(2)}) copy-start(bf16[256,768]{1,0:T(8,128)(2,1)S(1)} %collective-permute-done.4.refs_6_.refs_13_) | copy-start | bytes 1179652
  30.3 21.2 %copy-start.7 = (bf16[256,768]{1,0:T(8,128)(2,1)}, bf16[256,768]{1,0:T(8,128)(2,1)S(1)}, u32[]{:S(2)}) copy-start(bf16[256,768]{1,0:T(8,128)(2,1)S(1)} %collective-permute-done.5.refs_2_.refs_9_) | copy-start | bytes 1179652
  30.3 21.2 %all-to-all-start = ((bf16[64,16,128]{2,1,0:T(8,128)(2,1)}), bf16[64,16,128]{2,1,0:T(8,128)(2,1)S(1)}, u32[]{:S(2)}, u32[]{:S(2)}) async-start(bf16[64,16,128]{2,1,0:T(8,128)(2,1)} %shard_map.174), calls=%async_computation | async-start | bytes 524288 | tf_op jit(solution)/shard_map/all_to_all | solution.py:514
  43.1 8.4 %copy-start.11 = (f32[8,1024]{1,0:T(8,128)}, f32[8,1024]{1,0:T(8,128)S(1)}, u32[]{:S(2)}) copy-start(f32[8,1024]{1,0:T(8,128)S(1)} %shard_map.176.refs_0_) | copy-start | bytes 98308
  43.1 5.9 %collective-permute-start.8 = (f32[8,1024]{1,0:T(8,128)S(1)}, f32[8,1024]{1,0:T(8,128)S(1)}, u32[]{:S(2)}, u32[]{:S(2)}) collective-permute-start(f32[8,1024]{1,0:T(8,128)S(1)} %shard_map.176.refs_0_), channel_id=1, source_target_pairs={{0,1},{1,2},{2,3},{3,0},{4,5},{5,6},{6,7},{7,4},{8,9},{9,10},{10,1... | collective-permute-start | bytes 98312 | tf_op jit(solution)/shard_map/ppermute | solution.py:444
  44.9 5.4 %collective-permute-start.7 = (f32[8,1024]{1,0:T(8,128)S(1)}, f32[8,1024]{1,0:T(8,128)S(1)}, u32[]{:S(2)}, u32[]{:S(2)}) collective-permute-start(f32[8,1024]{1,0:T(8,128)S(1)} %shard_map.176.refs_0_), channel_id=1, source_target_pairs={{0,2},{1,3},{2,0},{3,1},{4,6},{5,7},{6,4},{7,5},{8,10},{9,11},{10,... | collective-permute-start | bytes 98312 | tf_op jit(solution)/shard_map/ppermute | solution.py:444
  47.5 3.9 %collective-permute-start.6 = (f32[8,1024]{1,0:T(8,128)S(1)}, f32[8,1024]{1,0:T(8,128)S(1)}, u32[]{:S(2)}, u32[]{:S(2)}) collective-permute-start(f32[8,1024]{1,0:T(8,128)S(1)} %shard_map.176.refs_0_), channel_id=1, source_target_pairs={{0,3},{1,0},{2,1},{3,2},{4,7},{5,4},{6,5},{7,6},{8,11},{9,8},{10,9... | collective-permute-start | bytes 98312 | tf_op jit(solution)/shard_map/ppermute | solution.py:444
  49.0 2.5 %copy-start.13 = (f32[8,1024]{1,0:T(8,128)}, f32[8,1024]{1,0:T(8,128)S(1)}, u32[]{:S(2)}) copy-start(f32[8,1024]{1,0:T(8,128)S(1)} %collective-permute-done.8.refs_3_) | copy-start | bytes 98308
  50.3 1.2 %copy-start.14 = (f32[8,1024]{1,0:T(8,128)}, f32[8,1024]{1,0:T(8,128)S(1)}, u32[]{:S(2)}) copy-start(f32[8,1024]{1,0:T(8,128)S(1)} %collective-permute-done.7.refs_2_) | copy-start | bytes 98308
  69.6 6.4 %collective-permute-start.9 = (bf16[384,384]{1,0:T(8,128)(2,1)}, bf16[384,384]{1,0:T(8,128)(2,1)S(1)}, u32[]{:S(2)}, u32[]{:S(2)}) collective-permute-start(bf16[384,384]{1,0:T(8,128)(2,1)} %get-tuple-element.59), channel_id=1, source_target_pairs={{0,64},{64,0},{1,65},{65,1},{2,66},{66,2},{3,67},{67,3},{4,68},{68... | collective-permute-start | bytes 884744 | tf_op jit(solution)/shard_map/ppermute | solution.py:550
  69.9 11.7 %collective-permute-start.14 = (bf16[256,384]{1,0:T(8,128)(2,1)}, bf16[256,384]{1,0:T(8,128)(2,1)S(1)}, u32[]{:S(2)}, u32[]{:S(2)}) collective-permute-start(bf16[256,384]{1,0:T(8,128)(2,1)} %get-tuple-element.67), channel_id=1, source_target_pairs={{0,1},{1,2},{2,3},{3,0},{4,5},{5,6},{6,7},{7,4},{8,9},{9,10},{10,1... | collective-permute-start | bytes 589832 | tf_op jit(solution)/shard_map/ppermute | solution.py:448
  70.3 26.3 %collective-permute-start.11 = (bf16[2,256,384]{2,1,0:T(8,128)(2,1)}, bf16[2,256,384]{2,1,0:T(8,128)(2,1)S(1)}, u32[]{:S(2)}, u32[]{:S(2)}) collective-permute-start(bf16[2,256,384]{2,1,0:T(8,128)(2,1)} %get-tuple-element.63), channel_id=1, source_target_pairs={{0,4},{4,8},{8,12},{12,0},{1,5},{5,9},{9,13},{13,1},{2,6},{6,10},{... | collective-permute-start | bytes 1179656 | tf_op jit(solution)/shard_map/ppermute | solution.py:448
  71.8 24.9 %collective-permute-start.12 = (bf16[2,256,384]{2,1,0:T(8,128)(2,1)}, bf16[2,256,384]{2,1,0:T(8,128)(2,1)S(1)}, u32[]{:S(2)}, u32[]{:S(2)}) collective-permute-start(bf16[2,256,384]{2,1,0:T(8,128)(2,1)} %get-tuple-element.64), channel_id=1, source_target_pairs={{0,8},{4,12},{8,0},{12,4},{1,9},{5,13},{9,1},{13,5},{2,10},{6,14},... | collective-permute-start | bytes 1179656 | tf_op jit(solution)/shard_map/ppermute | solution.py:448
  74.5 22.1 %collective-permute-start.13 = (bf16[2,256,384]{2,1,0:T(8,128)(2,1)}, bf16[2,256,384]{2,1,0:T(8,128)(2,1)S(1)}, u32[]{:S(2)}, u32[]{:S(2)}) collective-permute-start(bf16[2,256,384]{2,1,0:T(8,128)(2,1)} %get-tuple-element.65), channel_id=1, source_target_pairs={{0,12},{4,0},{8,4},{12,8},{1,13},{5,1},{9,5},{13,9},{2,14},{6,2},{... | collective-permute-start | bytes 1179656 | tf_op jit(solution)/shard_map/ppermute | solution.py:448
  76.0 1.0 copy-start.9
  77.0 12.1 %collective-permute-start.10 = (bf16[192,384]{1,0:T(8,128)(2,1)S(1)}, bf16[192,384]{1,0:T(8,128)(2,1)S(1)}, u32[]{:S(2)}, u32[]{:S(2)}) collective-permute-start(bf16[192,384]{1,0:T(8,128)(2,1)S(1)} %get-tuple-element.61), channel_id=1, source_target_pairs={{0,128},{128,0},{1,129},{129,1},{2,130},{130,2},{3,131},{131,3},{4... | collective-permute-start | bytes 442376 | tf_op jit(solution)/shard_map/ppermute | solution.py:554
  81.6 14.4 %collective-permute-start.15 = (bf16[256,384]{1,0:T(8,128)(2,1)}, bf16[256,384]{1,0:T(8,128)(2,1)S(1)}, u32[]{:S(2)}, u32[]{:S(2)}) collective-permute-start(bf16[256,384]{1,0:T(8,128)(2,1)} %get-tuple-element.68), channel_id=1, source_target_pairs={{0,2},{1,3},{2,0},{3,1},{4,6},{5,7},{6,4},{7,5},{8,10},{9,11},{10,... | collective-permute-start | bytes 589832 | tf_op jit(solution)/shard_map/ppermute | solution.py:448
  89.1 7.6 %collective-permute-start.16 = (bf16[256,384]{1,0:T(8,128)(2,1)}, bf16[256,384]{1,0:T(8,128)(2,1)S(1)}, u32[]{:S(2)}, u32[]{:S(2)}) collective-permute-start(bf16[256,384]{1,0:T(8,128)(2,1)} %get-tuple-element.69), channel_id=1, source_target_pairs={{0,3},{1,0},{2,1},{3,2},{4,7},{5,4},{6,5},{7,6},{8,11},{9,8},{10,9... | collective-permute-start | bytes 589832 | tf_op jit(solution)/shard_map/ppermute | solution.py:448
  92.7 9.4 %all-to-all-start.1 = ((bf16[4,48,384]{2,1,0:T(8,128)(2,1)}), bf16[4,48,384]{2,1,0:T(8,128)(2,1)S(1)}, u32[]{:S(2)}, u32[]{:S(2)}) async-start(bf16[4,48,384]{2,1,0:T(8,128)(2,1)} %bitcast.6), calls=%async_computation.1 | async-start | bytes 294912 | tf_op jit(solution)/shard_map/all_to_all | solution.py:558
  102.1 1.0 copy-start.8
  (3 other events, 2.2 us)

commit v13 on v12

--- a/solution.py
+++ b/solution.py
@@ -408,10 +408,13 @@
     out_ref[...] = (kept_ref[...] + got_ref[...].astype(f32)).astype(bf16)
 
 
-def sum_kernel(parts_ref, *refs):
+def last_kernel(parts_ref, out_ref):
+    out_ref[...] = sum(parts_ref[source].astype(f32) for source in range(GRID))
+
+
+def sum_kernel(*refs):
     pair_refs, query_refs = refs[:GRID], refs[GRID : 2 * GRID]
-    query_out, key_out, value_out, weight_out = refs[2 * GRID :]
-    weight_out[...] = sum(parts_ref[source].astype(f32) for source in range(GRID))
+    query_out, key_out, value_out = refs[2 * GRID :]
     query_out[0] = sum(ref[...].astype(f32) for ref in query_refs).astype(bf16)
     for place, out_ref in enumerate((key_out, value_out)):
         out_ref[0] = sum(ref[place].astype(f32) for ref in pair_refs).astype(bf16)
@@ -566,12 +569,11 @@
     ]
 
     rows = shape((1, ROWS_HERE, FEATS), bf16)
-    return call(
-        sum_kernel,
-        (rows, rows, rows, shape((48, FEATS), f32)),
-        [VMEM] * (1 + 2 * GRID),
-        limit=16,
-    )(weight_parts, *pair_back, *query_back)
+    query_grad, key_grad, value_grad = call(
+        sum_kernel, (rows, rows, rows), [VMEM] * (2 * GRID), limit=16
+    )(*pair_back, *query_back)
+    weight_grad = call(last_kernel, shape((48, FEATS), f32), [VMEM], limit=8)(weight_parts)
+    return query_grad, key_grad, value_grad, weight_grad
 
 
 def solution(mesh):

time: 105 us -> 103 us (0.981)
  waiting for transfers between devices: 17.5 us -> 14.6 us
    all_to_all x1, waiting for transfers between devices: 5.39 us -> 2.46 us  [per_device(): lax.all_to_all(weight_blocks.reshape(4, 48, FEATS), 'hx', split_axis=0, c...]
  transfers between devices with their start and end apart: 19 -> 19, of which waited for: 8 -> 8; matrix products, arithmetic and copies ran while one was open for 1% -> 1% of each run, Pallas kernels for 14% -> 15%
where the time goes in v13:
time: 103 us
  starting transfers between devices  47.8 us (46%)
  Pallas kernels  33.1 us (32%)
  waiting for transfers between devices  14.6 us (14%)
  local copies, waits for them, and re-layouts  4.19 us (4%)
  other arithmetic  2.11 us (2%)
    ppermute x9, starting transfers between devices, from_ahead(): lax.ppermute(block, axis, [(i, (i - step) % GRID) for i in range(GRID)])  17.2 us
    pallas_call x1, Pallas kernels, per_device(): call(grads_kernel, tuple([shape((ROWS_HERE, FEATS), bf16)] * GRID) + tupl...  16.8 us
    ppermute x6, starting transfers between devices, to_ahead(): lax.ppermute(block, axis, [(i, (i + step) % GRID) for i in range(GRID)])  12.8 us
    all_to_all x1, starting transfers between devices, per_device(): lax.all_to_all(windows, ('tm', 'hx', 'hy'), split_axis=0, concat_axis=0,...  9.55 us
    ppermute x9, waiting for transfers between devices, from_ahead(): lax.ppermute(block, axis, [(i, (i - step) % GRID) for i in range(GRID)])  7.85 us
    pallas_call x1, Pallas kernels, per_device(): call(weights_kernel, (shape((QUARTERS * LANES, FEATS), bf16), shape((768,...  6.15 us
    pallas_call x1, Pallas kernels, per_device(): call(window_kernel, shape((FRAMES, 16, LANES), bf16), [VMEM] * 2 + [ANY]...  4.58 us
    ppermute x1, starting transfers between devices, per_device(): weight_got = lax.ppermute(weight_sent, 'zh', [(0, 1), (1, 0)])  4.58 us
  transfers between devices with their start and end apart: 19, of which 8 were waited for; matrix products, arithmetic and copies ran while one was open for 1% of the time, Pallas kernels for 15%

profile of v13, /device:TPU:64, one launch (start us, length us, event | category | flops | bytes accessed | tf_op | source)
XLA Modules:
  0.0 102.7 jit_solution(5837314715940677917)
XLA Ops:
  0.6 1.1 %pad_maximum_fusion.refs_4_.refs_11_ = bf16[256,768]{1,0:T(8,128)(2,1)S(1)} fusion(bf16[256,384]{1,0:T(8,128)(2,1)} %bitcast.9, bf16[256,384]{1,0:T(8,128)(2,1)} %bitcast.10), kind=kLoop, calls=%fused_computation | loop fusion | flops 786432 | bytes 786432 | tf_op jit(solution)/shard_map/concatenate | solution.py:473
  1.7 1.6 %collective-permute-start.1 = (bf16[256,768]{1,0:T(8,128)(2,1)S(1)}, bf16[256,768]{1,0:T(8,128)(2,1)S(1)}, u32[]{:S(2)}, u32[]{:S(2)}) collective-permute-start(bf16[256,768]{1,0:T(8,128)(2,1)S(1)} %pad_maximum_fusion.refs_4_.refs_11_), channel_id=1, source_target_pairs={{0,4},{4,8},{8,12},{12,0},{1,5},{5,9},{9,13},{13,1},{2,6},{6,10},{... | collective-permute-start | bytes 1179656 | tf_op jit(solution)/shard_map/ppermute | solution.py:447
  3.3 1.7 %collective-permute-start = (bf16[256,768]{1,0:T(8,128)(2,1)S(1)}, bf16[256,768]{1,0:T(8,128)(2,1)S(1)}, u32[]{:S(2)}, u32[]{:S(2)}) collective-permute-start(bf16[256,768]{1,0:T(8,128)(2,1)S(1)} %pad_maximum_fusion.refs_4_.refs_11_), channel_id=1, source_target_pairs={{0,12},{4,0},{8,4},{12,8},{1,13},{5,1},{9,5},{13,9},{2,14},{6,2},{... | collective-permute-start | bytes 1179656 | tf_op jit(solution)/shard_map/ppermute | solution.py:447
  5.0 1.1 %pad_maximum_fusion.1.refs_0_.refs_7_ = bf16[256,768]{1,0:T(8,128)(2,1)S(1)} fusion(bf16[256,384]{1,0:T(8,128)(2,1)} %bitcast.11, bf16[256,384]{1,0:T(8,128)(2,1)} %bitcast.12), kind=kLoop, calls=%fused_computation.1 | loop fusion | flops 786432 | bytes 786432 | tf_op jit(solution)/shard_map/concatenate | solution.py:474
  6.1 1.7 %collective-permute-start.3 = (bf16[256,768]{1,0:T(8,128)(2,1)S(1)}, bf16[256,768]{1,0:T(8,128)(2,1)S(1)}, u32[]{:S(2)}, u32[]{:S(2)}) collective-permute-start(bf16[256,768]{1,0:T(8,128)(2,1)S(1)} %pad_maximum_fusion.1.refs_0_.refs_7_), channel_id=1, source_target_pairs={{0,1},{1,2},{2,3},{3,0},{4,5},{5,6},{6,7},{7,4},{8,9},{9,10},{10,1... | collective-permute-start | bytes 1179656 | tf_op jit(solution)/shard_map/ppermute | solution.py:447
  7.7 1.7 %collective-permute-start.2 = (bf16[256,768]{1,0:T(8,128)(2,1)S(1)}, bf16[256,768]{1,0:T(8,128)(2,1)S(1)}, u32[]{:S(2)}, u32[]{:S(2)}) collective-permute-start(bf16[256,768]{1,0:T(8,128)(2,1)S(1)} %pad_maximum_fusion.1.refs_0_.refs_7_), channel_id=1, source_target_pairs={{0,3},{1,0},{2,1},{3,2},{4,7},{5,4},{6,5},{7,6},{8,11},{9,8},{10,9... | collective-permute-start | bytes 1179656 | tf_op jit(solution)/shard_map/ppermute | solution.py:447
  9.4 4.6 %shard_map.174 = bf16[64,16,128]{2,1,0:T(8,128)(2,1)} custom-call(bf16[1280]{0:T(1024)(128)(2,1)} %gain_ref.1, s32[1,64]{1,0:T(1,128)} %order_ref.1, bf16[256,1280]{1,0:T(8,128)(2,1)} %bitcast.7, bf16[256,1280]{1,0:T(8,128)(2,1)} %bitcast.8, bf16[128,588]{1,0:T(8,128)(2,1)} %constant.4.clone.refs_2_, bf16[588,1280]{1,0:T(8,128)(2,1)} %refs_3_.1, ...), custom_call_target="tpu_custom_call" | custom-call | flops 1000000 | bytes 100000 | tf_op jit(solution)/shard_map/pallas_call | solution.py:477
  14.0 3.7 %collective-permute-done.3.refs_3_.refs_10_ = bf16[256,768]{1,0:T(8,128)(2,1)S(1)} collective-permute-done((bf16[256,768]{1,0:T(8,128)(2,1)S(1)}, bf16[256,768]{1,0:T(8,128)(2,1)S(1)}, u32[]{:S(2)}, u32[]{:S(2)}) %collective-permute-start.3) | collective-permute-done | bytes 393248 | tf_op jit(solution)/shard_map/ppermute | solution.py:447
  17.8 1.9 %collective-permute-start.4 = (bf16[256,768]{1,0:T(8,128)(2,1)S(1)}, bf16[256,768]{1,0:T(8,128)(2,1)S(1)}, u32[]{:S(2)}, u32[]{:S(2)}) collective-permute-start(bf16[256,768]{1,0:T(8,128)(2,1)S(1)} %pad_maximum_fusion.refs_4_.refs_11_), channel_id=1, source_target_pairs={{0,8},{4,12},{8,0},{12,4},{1,9},{5,13},{9,1},{13,5},{2,10},{6,14},... | collective-permute-start | bytes 1179656 | tf_op jit(solution)/shard_map/ppermute | solution.py:447
  19.6 2.8 %collective-permute-start.5 = (bf16[256,768]{1,0:T(8,128)(2,1)S(1)}, bf16[256,768]{1,0:T(8,128)(2,1)S(1)}, u32[]{:S(2)}, u32[]{:S(2)}) collective-permute-start(bf16[256,768]{1,0:T(8,128)(2,1)S(1)} %pad_maximum_fusion.1.refs_0_.refs_7_), channel_id=1, source_target_pairs={{0,2},{1,3},{2,0},{3,1},{4,6},{5,7},{6,4},{7,5},{8,10},{9,11},{10,... | collective-permute-start | bytes 1179656 | tf_op jit(solution)/shard_map/ppermute | solution.py:447
  22.5 6.1 %shard_map.175 = (bf16[512,384]{1,0:T(8,128)(2,1)}, bf16[768,512]{1,0:T(8,128)(2,1)}) custom-call(bf16[512,3072]{1,0:T(8,128)(2,1)} %join_from, bf16[384,3072]{1,0:T(8,128)(2,1)} %out_w_from.1), custom_call_target="tpu_custom_call" | custom-call | flops 1000000 | bytes 100000 | tf_op jit(solution)/shard_map/pallas_call | solution.py:504
  28.8 1.5 %collective-permute-done.5.refs_2_.refs_9_ = bf16[256,768]{1,0:T(8,128)(2,1)S(1)} collective-permute-done((bf16[256,768]{1,0:T(8,128)(2,1)S(1)}, bf16[256,768]{1,0:T(8,128)(2,1)S(1)}, u32[]{:S(2)}, u32[]{:S(2)}) %collective-permute-start.5) | collective-permute-done | bytes 393248 | tf_op jit(solution)/shard_map/ppermute | solution.py:447
  30.3 9.6 %all-to-all-start = ((bf16[64,16,128]{2,1,0:T(8,128)(2,1)}), bf16[64,16,128]{2,1,0:T(8,128)(2,1)S(1)}, u32[]{:S(2)}, u32[]{:S(2)}) async-start(bf16[64,16,128]{2,1,0:T(8,128)(2,1)} %shard_map.174), calls=%async_computation | async-start | bytes 524288 | tf_op jit(solution)/shard_map/all_to_all | solution.py:517
  39.9 3.2 %shard_map.176.refs_0_ = f32[8,1024]{1,0:T(8,128)S(1)} custom-call(bf16[256,768]{1,0:T(8,128)(2,1)S(1)} %pad_maximum_fusion.1.refs_0_.refs_7_, bf16[256,768]{1,0:T(8,128)(2,1)S(1)} %collective-permute-done.2.refs_1_.refs_8_, bf16[256,768]{1,0:T(8,128)(2,1)S(1)} %collective-permute-done.5.refs_2_.refs_9_, ...), custom_call_target="tpu_custom_call" | custom-call | flops 1000000 | bytes 100000 | tf_op jit(solution)/shard_map/pallas_call | solution.py:520
  43.1 1.7 %collective-permute-start.8 = (f32[8,1024]{1,0:T(8,128)S(1)}, f32[8,1024]{1,0:T(8,128)S(1)}, u32[]{:S(2)}, u32[]{:S(2)}) collective-permute-start(f32[8,1024]{1,0:T(8,128)S(1)} %shard_map.176.refs_0_), channel_id=1, source_target_pairs={{0,1},{1,2},{2,3},{3,0},{4,5},{5,6},{6,7},{7,4},{8,9},{9,10},{10,1... | collective-permute-start | bytes 98312 | tf_op jit(solution)/shard_map/ppermute | solution.py:447
  44.9 2.7 %collective-permute-start.7 = (f32[8,1024]{1,0:T(8,128)S(1)}, f32[8,1024]{1,0:T(8,128)S(1)}, u32[]{:S(2)}, u32[]{:S(2)}) collective-permute-start(f32[8,1024]{1,0:T(8,128)S(1)} %shard_map.176.refs_0_), channel_id=1, source_target_pairs={{0,2},{1,3},{2,0},{3,1},{4,6},{5,7},{6,4},{7,5},{8,10},{9,11},{10,... | collective-permute-start | bytes 98312 | tf_op jit(solution)/shard_map/ppermute | solution.py:447
  47.5 1.5 %collective-permute-start.6 = (f32[8,1024]{1,0:T(8,128)S(1)}, f32[8,1024]{1,0:T(8,128)S(1)}, u32[]{:S(2)}, u32[]{:S(2)}) collective-permute-start(f32[8,1024]{1,0:T(8,128)S(1)} %shard_map.176.refs_0_), channel_id=1, source_target_pairs={{0,3},{1,0},{2,1},{3,2},{4,7},{5,4},{6,5},{7,6},{8,11},{9,8},{10,9... | collective-permute-start | bytes 98312 | tf_op jit(solution)/shard_map/ppermute | solution.py:447
  49.0 1.3 %collective-permute-done.7.refs_2_ = f32[8,1024]{1,0:T(8,128)S(1)} collective-permute-done((f32[8,1024]{1,0:T(8,128)S(1)}, f32[8,1024]{1,0:T(8,128)S(1)}, u32[]{:S(2)}, u32[]{:S(2)}) %collective-permute-start.7) | collective-permute-done | bytes 32800 | tf_op jit(solution)/shard_map/ppermute | solution.py:447
  50.3 1.2 %collective-permute-done.6.refs_1_ = f32[8,1024]{1,0:T(8,128)S(1)} collective-permute-done((f32[8,1024]{1,0:T(8,128)S(1)}, f32[8,1024]{1,0:T(8,128)S(1)}, u32[]{:S(2)}, u32[]{:S(2)}) %collective-permute-start.6) | collective-permute-done | bytes 32800 | tf_op jit(solution)/shard_map/ppermute | solution.py:447
  52.8 16.8 %shard_map.177 = (bf16[256,384]{1,0:T(8,128)(2,1)}, bf16[256,384]{1,0:T(8,128)(2,1)}, bf16[256,384]{1,0:T(8,128)(2,1)}, bf16[256,384]{1,0:T(8,128)(2,1)}, bf16[2...) custom-call(s32[64]{0:T(128)} %owner_ref.1, ...), custom_call_target="tpu_custom_call" | custom-call | flops 1000000 | bytes 100000 | tf_op jit(solution)/shard_map/pallas_call | solution.py:527
  70.3 1.5 %collective-permute-start.9 = (bf16[2,256,384]{2,1,0:T(8,128)(2,1)}, bf16[2,256,384]{2,1,0:T(8,128)(2,1)S(1)}, u32[]{:S(2)}, u32[]{:S(2)}) collective-permute-start(bf16[2,256,384]{2,1,0:T(8,128)(2,1)} %get-tuple-element.62), channel_id=1, source_target_pairs={{0,4},{4,8},{8,12},{12,0},{1,5},{5,9},{9,13},{13,1},{2,6},{6,10},{... | collective-permute-start | bytes 1179656 | tf_op jit(solution)/shard_map/ppermute | solution.py:451
  71.8 2.7 %collective-permute-start.10 = (bf16[2,256,384]{2,1,0:T(8,128)(2,1)}, bf16[2,256,384]{2,1,0:T(8,128)(2,1)S(1)}, u32[]{:S(2)}, u32[]{:S(2)}) collective-permute-start(bf16[2,256,384]{2,1,0:T(8,128)(2,1)} %get-tuple-element.63), channel_id=1, source_target_pairs={{0,8},{4,12},{8,0},{12,4},{1,9},{5,13},{9,1},{13,5},{2,10},{6,14},... | collective-permute-start | bytes 1179656 | tf_op jit(solution)/shard_map/ppermute | solution.py:451
  74.5 1.4 %collective-permute-start.11 = (bf16[2,256,384]{2,1,0:T(8,128)(2,1)}, bf16[2,256,384]{2,1,0:T(8,128)(2,1)S(1)}, u32[]{:S(2)}, u32[]{:S(2)}) collective-permute-start(bf16[2,256,384]{2,1,0:T(8,128)(2,1)} %get-tuple-element.64), channel_id=1, source_target_pairs={{0,12},{4,0},{8,4},{12,8},{1,13},{5,1},{9,5},{13,9},{2,14},{6,2},{... | collective-permute-start | bytes 1179656 | tf_op jit(solution)/shard_map/ppermute | solution.py:451
  76.0 1.0 copy-done.9
  77.0 4.6 %collective-permute-start.16 = (bf16[192,384]{1,0:T(8,128)(2,1)S(1)}, bf16[192,384]{1,0:T(8,128)(2,1)S(1)}, u32[]{:S(2)}, u32[]{:S(2)}) collective-permute-start(bf16[192,384]{1,0:T(8,128)(2,1)S(1)} %get-tuple-element.75), channel_id=1, source_target_pairs={{0,128},{128,0},{1,129},{129,1},{2,130},{130,2},{3,131},{131,3},{4... | collective-permute-start | bytes 442376 | tf_op jit(solution)/shard_map/ppermute | solution.py:557
  81.6 3.8 %collective-permute-start.13 = (bf16[256,384]{1,0:T(8,128)(2,1)}, bf16[256,384]{1,0:T(8,128)(2,1)S(1)}, u32[]{:S(2)}, u32[]{:S(2)}) collective-permute-start(bf16[256,384]{1,0:T(8,128)(2,1)} %get-tuple-element.67), channel_id=1, source_target_pairs={{0,2},{1,3},{2,0},{3,1},{4,6},{5,7},{6,4},{7,5},{8,10},{9,11},{10,... | collective-permute-start | bytes 589832 | tf_op jit(solution)/shard_map/ppermute | solution.py:451
  85.4 3.6 %collective-permute-done.16.got_ref = bf16[192,384]{1,0:T(8,128)(2,1)S(1)} collective-permute-done((bf16[192,384]{1,0:T(8,128)(2,1)S(1)}, bf16[192,384]{1,0:T(8,128)(2,1)S(1)}, u32[]{:S(2)}, u32[]{:S(2)}) %collective-permute-start.16) | collective-permute-done | bytes 147488 | tf_op jit(solution)/shard_map/ppermute | solution.py:557
  89.1 2.9 %collective-permute-start.14 = (bf16[256,384]{1,0:T(8,128)(2,1)}, bf16[256,384]{1,0:T(8,128)(2,1)S(1)}, u32[]{:S(2)}, u32[]{:S(2)}) collective-permute-start(bf16[256,384]{1,0:T(8,128)(2,1)} %get-tuple-element.68), channel_id=1, source_target_pairs={{0,3},{1,0},{2,1},{3,2},{4,7},{5,4},{6,5},{7,6},{8,11},{9,8},{10,9... | collective-permute-start | bytes 589832 | tf_op jit(solution)/shard_map/ppermute | solution.py:451
  92.7 3.3 %all-to-all-start.1 = ((bf16[4,48,384]{2,1,0:T(8,128)(2,1)}), bf16[4,48,384]{2,1,0:T(8,128)(2,1)S(1)}, u32[]{:S(2)}, u32[]{:S(2)}) async-start(bf16[4,48,384]{2,1,0:T(8,128)(2,1)} %bitcast.6), calls=%async_computation.1 | async-start | bytes 294912 | tf_op jit(solution)/shard_map/all_to_all | solution.py:561
  96.7 1.0 copy-done.8
  98.6 1.0 shard_map.178
  99.6 2.5 %all-to-all-done.1.parts_ref = bf16[4,48,384]{2,1,0:T(8,128)(2,1)S(1)} async-done(((bf16[4,48,384]{2,1,0:T(8,128)(2,1)}), bf16[4,48,384]{2,1,0:T(8,128)(2,1)S(1)}, u32[]{:S(2)}, u32[]{:S(2)}) %all-to-all-start.1) | async-done | bytes 147488 | tf_op jit(solution)/shard_map/all_to_all | solution.py:561
  (48 shorter events, 5.1 us)
Async XLA Ops:
  1.7 38.2 %copy-start = (bf16[256,768]{1,0:T(8,128)(2,1)}, bf16[256,768]{1,0:T(8,128)(2,1)S(1)}, u32[]{:S(2)}) copy-start(bf16[256,768]{1,0:T(8,128)(2,1)S(1)} %pad_maximum_fusion.refs_4_.refs_11_) | copy-start | bytes 1179652
  1.7 12.3 %collective-permute-start.1 = (bf16[256,768]{1,0:T(8,128)(2,1)S(1)}, bf16[256,768]{1,0:T(8,128)(2,1)S(1)}, u32[]{:S(2)}, u32[]{:S(2)}) collective-permute-start(bf16[256,768]{1,0:T(8,128)(2,1)S(1)} %pad_maximum_fusion.refs_4_.refs_11_), channel_id=1, source_target_pairs={{0,4},{4,8},{8,12},{12,0},{1,5},{5,9},{9,13},{13,1},{2,6},{6,10},{... | collective-permute-start | bytes 1179656 | tf_op jit(solution)/shard_map/ppermute | solution.py:447
  3.3 10.7 %collective-permute-start = (bf16[256,768]{1,0:T(8,128)(2,1)S(1)}, bf16[256,768]{1,0:T(8,128)(2,1)S(1)}, u32[]{:S(2)}, u32[]{:S(2)}) collective-permute-start(bf16[256,768]{1,0:T(8,128)(2,1)S(1)} %pad_maximum_fusion.refs_4_.refs_11_), channel_id=1, source_target_pairs={{0,12},{4,0},{8,4},{12,8},{1,13},{5,1},{9,5},{13,9},{2,14},{6,2},{... | collective-permute-start | bytes 1179656 | tf_op jit(solution)/shard_map/ppermute | solution.py:447
  6.1 33.8 %copy-start.1 = (bf16[256,768]{1,0:T(8,128)(2,1)}, bf16[256,768]{1,0:T(8,128)(2,1)S(1)}, u32[]{:S(2)}) copy-start(bf16[256,768]{1,0:T(8,128)(2,1)S(1)} %pad_maximum_fusion.1.refs_0_.refs_7_) | copy-start | bytes 1179652
  6.1 11.6 %collective-permute-start.3 = (bf16[256,768]{1,0:T(8,128)(2,1)S(1)}, bf16[256,768]{1,0:T(8,128)(2,1)S(1)}, u32[]{:S(2)}, u32[]{:S(2)}) collective-permute-start(bf16[256,768]{1,0:T(8,128)(2,1)S(1)} %pad_maximum_fusion.1.refs_0_.refs_7_), channel_id=1, source_target_pairs={{0,1},{1,2},{2,3},{3,0},{4,5},{5,6},{6,7},{7,4},{8,9},{9,10},{10,1... | collective-permute-start | bytes 1179656 | tf_op jit(solution)/shard_map/ppermute | solution.py:447
  7.7 10.0 %collective-permute-start.2 = (bf16[256,768]{1,0:T(8,128)(2,1)S(1)}, bf16[256,768]{1,0:T(8,128)(2,1)S(1)}, u32[]{:S(2)}, u32[]{:S(2)}) collective-permute-start(bf16[256,768]{1,0:T(8,128)(2,1)S(1)} %pad_maximum_fusion.1.refs_0_.refs_7_), channel_id=1, source_target_pairs={{0,3},{1,0},{2,1},{3,2},{4,7},{5,4},{6,5},{7,6},{8,11},{9,8},{10,9... | collective-permute-start | bytes 1179656 | tf_op jit(solution)/shard_map/ppermute | solution.py:447
  14.0 25.9 %copy-start.2 = (bf16[256,768]{1,0:T(8,128)(2,1)}, bf16[256,768]{1,0:T(8,128)(2,1)S(1)}, u32[]{:S(2)}) copy-start(bf16[256,768]{1,0:T(8,128)(2,1)S(1)} %collective-permute-done.1.refs_7_.refs_14_) | copy-start | bytes 1179652
  14.0 25.9 %copy-start.3 = (bf16[256,768]{1,0:T(8,128)(2,1)}, bf16[256,768]{1,0:T(8,128)(2,1)S(1)}, u32[]{:S(2)}) copy-start(bf16[256,768]{1,0:T(8,128)(2,1)S(1)} %collective-permute-done.refs_5_.refs_12_) | copy-start | bytes 1179652
  17.7 22.2 %copy-start.4 = (bf16[256,768]{1,0:T(8,128)(2,1)}, bf16[256,768]{1,0:T(8,128)(2,1)S(1)}, u32[]{:S(2)}) copy-start(bf16[256,768]{1,0:T(8,128)(2,1)S(1)} %collective-permute-done.3.refs_3_.refs_10_) | copy-start | bytes 1179652
  17.8 22.2 %copy-start.5 = (bf16[256,768]{1,0:T(8,128)(2,1)}, bf16[256,768]{1,0:T(8,128)(2,1)S(1)}, u32[]{:S(2)}) copy-start(bf16[256,768]{1,0:T(8,128)(2,1)S(1)} %collective-permute-done.2.refs_1_.refs_8_) | copy-start | bytes 1179652
  17.8 11.0 %collective-permute-start.4 = (bf16[256,768]{1,0:T(8,128)(2,1)S(1)}, bf16[256,768]{1,0:T(8,128)(2,1)S(1)}, u32[]{:S(2)}, u32[]{:S(2)}) collective-permute-start(bf16[256,768]{1,0:T(8,128)(2,1)S(1)} %pad_maximum_fusion.refs_4_.refs_11_), channel_id=1, source_target_pairs={{0,8},{4,12},{8,0},{12,4},{1,9},{5,13},{9,1},{13,5},{2,10},{6,14},... | collective-permute-start | bytes 1179656 | tf_op jit(solution)/shard_map/ppermute | solution.py:447
  19.6 10.7 %collective-permute-start.5 = (bf16[256,768]{1,0:T(8,128)(2,1)S(1)}, bf16[256,768]{1,0:T(8,128)(2,1)S(1)}, u32[]{:S(2)}, u32[]{:S(2)}) collective-permute-start(bf16[256,768]{1,0:T(8,128)(2,1)S(1)} %pad_maximum_fusion.1.refs_0_.refs_7_), channel_id=1, source_target_pairs={{0,2},{1,3},{2,0},{3,1},{4,6},{5,7},{6,4},{7,5},{8,10},{9,11},{10,... | collective-permute-start | bytes 1179656 | tf_op jit(solution)/shard_map/ppermute | solution.py:447
  28.8 22.7 %copy-start.6 = (bf16[256,768]{1,0:T(8,128)(2,1)}, bf16[256,768]{1,0:T(8,128)(2,1)S(1)}, u32[]{:S(2)}) copy-start(bf16[256,768]{1,0:T(8,128)(2,1)S(1)} %collective-permute-done.4.refs_6_.refs_13_) | copy-start | bytes 1179652
  30.3 21.2 %copy-start.7 = (bf16[256,768]{1,0:T(8,128)(2,1)}, bf16[256,768]{1,0:T(8,128)(2,1)S(1)}, u32[]{:S(2)}) copy-start(bf16[256,768]{1,0:T(8,128)(2,1)S(1)} %collective-permute-done.5.refs_2_.refs_9_) | copy-start | bytes 1179652
  30.3 21.2 %all-to-all-start = ((bf16[64,16,128]{2,1,0:T(8,128)(2,1)}), bf16[64,16,128]{2,1,0:T(8,128)(2,1)S(1)}, u32[]{:S(2)}, u32[]{:S(2)}) async-start(bf16[64,16,128]{2,1,0:T(8,128)(2,1)} %shard_map.174), calls=%async_computation | async-start | bytes 524288 | tf_op jit(solution)/shard_map/all_to_all | solution.py:517
  43.1 8.4 %copy-start.11 = (f32[8,1024]{1,0:T(8,128)}, f32[8,1024]{1,0:T(8,128)S(1)}, u32[]{:S(2)}) copy-start(f32[8,1024]{1,0:T(8,128)S(1)} %shard_map.176.refs_0_) | copy-start | bytes 98308
  43.1 5.9 %collective-permute-start.8 = (f32[8,1024]{1,0:T(8,128)S(1)}, f32[8,1024]{1,0:T(8,128)S(1)}, u32[]{:S(2)}, u32[]{:S(2)}) collective-permute-start(f32[8,1024]{1,0:T(8,128)S(1)} %shard_map.176.refs_0_), channel_id=1, source_target_pairs={{0,1},{1,2},{2,3},{3,0},{4,5},{5,6},{6,7},{7,4},{8,9},{9,10},{10,1... | collective-permute-start | bytes 98312 | tf_op jit(solution)/shard_map/ppermute | solution.py:447
  44.9 5.4 %collective-permute-start.7 = (f32[8,1024]{1,0:T(8,128)S(1)}, f32[8,1024]{1,0:T(8,128)S(1)}, u32[]{:S(2)}, u32[]{:S(2)}) collective-permute-start(f32[8,1024]{1,0:T(8,128)S(1)} %shard_map.176.refs_0_), channel_id=1, source_target_pairs={{0,2},{1,3},{2,0},{3,1},{4,6},{5,7},{6,4},{7,5},{8,10},{9,11},{10,... | collective-permute-start | bytes 98312 | tf_op jit(solution)/shard_map/ppermute | solution.py:447
  47.5 3.9 %collective-permute-start.6 = (f32[8,1024]{1,0:T(8,128)S(1)}, f32[8,1024]{1,0:T(8,128)S(1)}, u32[]{:S(2)}, u32[]{:S(2)}) collective-permute-start(f32[8,1024]{1,0:T(8,128)S(1)} %shard_map.176.refs_0_), channel_id=1, source_target_pairs={{0,3},{1,0},{2,1},{3,2},{4,7},{5,4},{6,5},{7,6},{8,11},{9,8},{10,9... | collective-permute-start | bytes 98312 | tf_op jit(solution)/shard_map/ppermute | solution.py:447
  49.0 2.5 %copy-start.13 = (f32[8,1024]{1,0:T(8,128)}, f32[8,1024]{1,0:T(8,128)S(1)}, u32[]{:S(2)}) copy-start(f32[8,1024]{1,0:T(8,128)S(1)} %collective-permute-done.8.refs_3_) | copy-start | bytes 98308
  50.3 1.2 %copy-start.14 = (f32[8,1024]{1,0:T(8,128)}, f32[8,1024]{1,0:T(8,128)S(1)}, u32[]{:S(2)}) copy-start(f32[8,1024]{1,0:T(8,128)S(1)} %collective-permute-done.7.refs_2_) | copy-start | bytes 98308
  69.6 6.4 %collective-permute-start.15 = (bf16[384,384]{1,0:T(8,128)(2,1)}, bf16[384,384]{1,0:T(8,128)(2,1)S(1)}, u32[]{:S(2)}, u32[]{:S(2)}) collective-permute-start(bf16[384,384]{1,0:T(8,128)(2,1)} %get-tuple-element.73), channel_id=1, source_target_pairs={{0,64},{64,0},{1,65},{65,1},{2,66},{66,2},{3,67},{67,3},{4,68},{68... | collective-permute-start | bytes 884744 | tf_op jit(solution)/shard_map/ppermute | solution.py:553
  69.9 11.7 %collective-permute-start.12 = (bf16[256,384]{1,0:T(8,128)(2,1)}, bf16[256,384]{1,0:T(8,128)(2,1)S(1)}, u32[]{:S(2)}, u32[]{:S(2)}) collective-permute-start(bf16[256,384]{1,0:T(8,128)(2,1)} %get-tuple-element.66), channel_id=1, source_target_pairs={{0,1},{1,2},{2,3},{3,0},{4,5},{5,6},{6,7},{7,4},{8,9},{9,10},{10,1... | collective-permute-start | bytes 589832 | tf_op jit(solution)/shard_map/ppermute | solution.py:451
  70.3 26.3 %collective-permute-start.9 = (bf16[2,256,384]{2,1,0:T(8,128)(2,1)}, bf16[2,256,384]{2,1,0:T(8,128)(2,1)S(1)}, u32[]{:S(2)}, u32[]{:S(2)}) collective-permute-start(bf16[2,256,384]{2,1,0:T(8,128)(2,1)} %get-tuple-element.62), channel_id=1, source_target_pairs={{0,4},{4,8},{8,12},{12,0},{1,5},{5,9},{9,13},{13,1},{2,6},{6,10},{... | collective-permute-start | bytes 1179656 | tf_op jit(solution)/shard_map/ppermute | solution.py:451
  71.8 24.9 %collective-permute-start.10 = (bf16[2,256,384]{2,1,0:T(8,128)(2,1)}, bf16[2,256,384]{2,1,0:T(8,128)(2,1)S(1)}, u32[]{:S(2)}, u32[]{:S(2)}) collective-permute-start(bf16[2,256,384]{2,1,0:T(8,128)(2,1)} %get-tuple-element.63), channel_id=1, source_target_pairs={{0,8},{4,12},{8,0},{12,4},{1,9},{5,13},{9,1},{13,5},{2,10},{6,14},... | collective-permute-start | bytes 1179656 | tf_op jit(solution)/shard_map/ppermute | solution.py:451
  74.5 22.1 %collective-permute-start.11 = (bf16[2,256,384]{2,1,0:T(8,128)(2,1)}, bf16[2,256,384]{2,1,0:T(8,128)(2,1)S(1)}, u32[]{:S(2)}, u32[]{:S(2)}) collective-permute-start(bf16[2,256,384]{2,1,0:T(8,128)(2,1)} %get-tuple-element.64), channel_id=1, source_target_pairs={{0,12},{4,0},{8,4},{12,8},{1,13},{5,1},{9,5},{13,9},{2,14},{6,2},{... | collective-permute-start | bytes 1179656 | tf_op jit(solution)/shard_map/ppermute | solution.py:451
  76.0 1.0 copy-start.9
  77.0 12.1 %collective-permute-start.16 = (bf16[192,384]{1,0:T(8,128)(2,1)S(1)}, bf16[192,384]{1,0:T(8,128)(2,1)S(1)}, u32[]{:S(2)}, u32[]{:S(2)}) collective-permute-start(bf16[192,384]{1,0:T(8,128)(2,1)S(1)} %get-tuple-element.75), channel_id=1, source_target_pairs={{0,128},{128,0},{1,129},{129,1},{2,130},{130,2},{3,131},{131,3},{4... | collective-permute-start | bytes 442376 | tf_op jit(solution)/shard_map/ppermute | solution.py:557
  81.6 14.4 %collective-permute-start.13 = (bf16[256,384]{1,0:T(8,128)(2,1)}, bf16[256,384]{1,0:T(8,128)(2,1)S(1)}, u32[]{:S(2)}, u32[]{:S(2)}) collective-permute-start(bf16[256,384]{1,0:T(8,128)(2,1)} %get-tuple-element.67), channel_id=1, source_target_pairs={{0,2},{1,3},{2,0},{3,1},{4,6},{5,7},{6,4},{7,5},{8,10},{9,11},{10,... | collective-permute-start | bytes 589832 | tf_op jit(solution)/shard_map/ppermute | solution.py:451
  89.1 7.6 %collective-permute-start.14 = (bf16[256,384]{1,0:T(8,128)(2,1)}, bf16[256,384]{1,0:T(8,128)(2,1)S(1)}, u32[]{:S(2)}, u32[]{:S(2)}) collective-permute-start(bf16[256,384]{1,0:T(8,128)(2,1)} %get-tuple-element.68), channel_id=1, source_target_pairs={{0,3},{1,0},{2,1},{3,2},{4,7},{5,4},{6,5},{7,6},{8,11},{9,8},{10,9... | collective-permute-start | bytes 589832 | tf_op jit(solution)/shard_map/ppermute | solution.py:451
  92.7 9.4 %all-to-all-start.1 = ((bf16[4,48,384]{2,1,0:T(8,128)(2,1)}), bf16[4,48,384]{2,1,0:T(8,128)(2,1)S(1)}, u32[]{:S(2)}, u32[]{:S(2)}) async-start(bf16[4,48,384]{2,1,0:T(8,128)(2,1)} %bitcast.6), calls=%async_computation.1 | async-start | bytes 294912 | tf_op jit(solution)/shard_map/all_to_all | solution.py:561
  96.7 1.0 copy-start.8
  (3 other events, 2.2 us)
